TPU v7x, 32 devices: a whole 2x2x4 slice. The times are simulated.
32 devices in a mesh: dp: 8 (over y, x, core), tensor: 4 (over z).
Axes of the slice: x: 2, y: 2, z: 4, core: 2. Of those that a mesh axis runs over, the one named last changes fastest.
Arguments:
- activations: bfloat16 [4608, 2560], P(('dp', 'tensor')), may hold values from -6 to 6
- out_grad: bfloat16 [4608, 6912], P('dp', 'tensor'), may hold values from -0.29882812 to 0.29882812
- error_state: bfloat16 [8, 6912, 2560], P('dp', 'tensor'), may hold values from -36 to 36
- right_factor: float32 [2560, 32], P('tensor'), may hold values from -6 to 6
Outputs:
- new_error: bfloat16 [8, 6912, 2560], P('dp', 'tensor')
- new_factor: float32 [2560, 32], P('tensor')
All inputs are finite; a program needn't handle non-finite values.
Results may differ from a plain program's by a relative error of at most 0.0065.
Values may be sent and summed in bfloat16 or wider, within the bound.
No kernel may reach another device: no remote copies, remote signals or barrier semaphores. Data moves between devices by JAX's collectives and lax.ppermute only.
A program may use at most 128 MiB of HBM per device.

v0:
```python
import jax
import jax.numpy as jnp
from jax import lax
from jax.sharding import PartitionSpec as P

contract_first = (((0,), (0,)), ((), ()))
column_block = 8


def body(activations, out_grad, error_state, right_factor):
    highest = lax.Precision.HIGHEST
    errors = error_state[0]
    rows_here = right_factor.shape[0]
    factor_full = lax.all_gather(right_factor, "tensor", axis=0, tiled=True)
    grad = lax.dot_general(
        out_grad,
        lax.all_gather(activations, "tensor", axis=0, tiled=True),
        contract_first,
        preferred_element_type=jnp.float32,
    )
    corrected = grad + errors.astype(jnp.float32)
    p_local = jnp.dot(corrected, factor_full, precision=highest)
    p_total = lax.psum(p_local.astype(jnp.bfloat16), "dp").astype(jnp.float32)
    p_basis = jnp.zeros_like(p_total)
    for block_index in range(p_total.shape[1] // column_block):
        first = block_index * column_block
        columns = p_total[:, first : first + column_block]
        coeffs, block_gram = lax.psum(
            (
                jnp.dot(p_basis.T, columns, precision=highest),
                jnp.dot(columns.T, columns, precision=highest),
            ),
            "tensor",
        )
        remainder = columns - jnp.dot(p_basis, coeffs, precision=highest)
        residual_gram = block_gram - jnp.dot(coeffs.T, coeffs, precision=highest)
        lower_factor = jnp.linalg.cholesky(residual_gram)
        orthonormal = lax.linalg.triangular_solve(
            lower_factor, remainder, left_side=False, lower=True, transpose_a=True
        )
        p_basis = p_basis.at[:, first : first + column_block].set(orthonormal)
    replicas = lax.axis_size("dp")
    term = lax.dot_general(corrected, p_basis, contract_first, precision=highest)
    summed = lax.psum(term, ("dp", "tensor")) / replicas
    new_error = (corrected - jnp.dot(p_basis, summed.T, precision=highest)).astype(jnp.bfloat16)
    new_factor = lax.dynamic_slice_in_dim(
        summed, lax.axis_index("tensor") * rows_here, rows_here, 0
    )
    return (new_error[None], new_factor)


def solution(mesh):
    placed = (
        P(("dp", "tensor"), None),
        P("dp", "tensor"),
        P("dp", "tensor", None),
        P("tensor", None),
    )
    return jax.shard_map(
        body,
        mesh=mesh,
        in_specs=placed,
        out_specs=(P("dp", "tensor", None), P("tensor", None)),
        check_vma=False,
    )
```

profile of v0, /device:TPU:0, one launch (start us, length us, event | category | flops | bytes accessed | tf_op | source)
XLA Modules:
  0.0 385.6 jit_solution(10484460821982997632)
XLA Ops:
  7.2 0.7 all-gather.2.cloned.1.call-update
  8.0 17.1 %all_gather.7 = f32[2560,32]{0,1:T(8,128)S(1)} all-gather(f32[640,32]{0,1:T(8,128)} %param.18), channel_id=1, replica_groups=mesh['dp'=8,'tensor'=4] {'tensor'}, dimensions={0}, use_global_device_ids=true | all-gather | bytes 409600 | tf_op jit(solution)/shard_map/all_gather | solution.py:14
  25.0 47.8 %all-gather.2.cloned.1.call-done = bf16[576,2560]{1,0:T(8,128)(2,1)} async-done(((bf16[144,2560]{1,0:T(8,128)(2,1)}), bf16[576,2560]{1,0:T(8,128)(2,1)}) %all-gather.2.cloned.1.call-update) | async-done | bytes 2949136 | tf_op jit(solution)/shard_map/all_gather | solution.py:17
  72.8 10.4 %convert_add_fusion = f32[1728,2560]{1,0:T(8,128)S(1)} fusion(bf16[576,1728]{1,0:T(8,128)(2,1)S(1)} %copy-done, bf16[576,2560]{1,0:T(8,128)(2,1)} %all-gather.2.cloned.1.call-done, bf16[1,1728,2560]{2,1,0:T(8,128)(2,1)} %param.17), kind=kOutput, calls=%fused_computation | convolution fusion | flops 5104926720 | bytes 31481856 | tf_op jit(solution)/shard_map/dot_general | solution.py:15
  83.2 6.0 %copy-done.1 = f32[1728,2560]{1,0:T(8,128)} copy-done((f32[1728,2560]{1,0:T(8,128)}, f32[1728,2560]{1,0:T(8,128)S(1)}, u32[]{:S(2)}) %copy-start.1) | copy-done | bytes 17694744
  89.3 16.4 %convolution_convert_fusion = bf16[1728,32]{0,1:T(8,128)(2,1)} fusion(f32[1728,2560]{1,0:T(8,128)S(1)} %convert_add_fusion, f32[2560,32]{0,1:T(8,128)S(1)} %all_gather.7), kind=kOutput, calls=%fused_computation.3 | convolution fusion | flops 1698748416 | bytes 18132992 | tf_op jit(solution)/shard_map/dot_general | solution.py:22
  105.8 0.6 compare_reduce_fusion.6
  106.4 0.6 compare_reduce_fusion.5
  107.0 0.6 compare_reduce_fusion.4
  107.7 48.5 %all-reduce.8.cloned.1.call-done = bf16[1728,32]{0,1:T(8,128)(2,1)} async-done(((bf16[1728,32]{0,1:T(8,128)(2,1)}), bf16[1728,32]{0,1:T(8,128)(2,1)}) %all-reduce.8.cloned.1.call-update) | async-done | bytes 110608 | tf_op jit(solution)/shard_map/psum | solution.py:23
  156.2 0.9 fusion.10
  157.0 1.0 fusion.25
  158.0 11.8 %all-reduce.4 = (f32[32,8]{0,1:T(8,128)S(1)}, f32[8,8]{0,1:T(8,128)S(1)}) all-reduce(f32[32,8]{0,1:T(8,128)S(1)} %fusion.10, f32[8,8]{0,1:T(8,128)S(1)} %fusion.25), channel_id=1, replica_groups=mesh['dp'=8,'tensor'=4] {'tensor'}, use_global_device_ids=true, to_apply=%region_3.4 | all-reduce | flops 320 | bytes 2560 | tf_op jit(solution)/shard_map/psum | solution.py:28
  169.9 0.1 multiply_reduce_fusion
  170.0 0.1 convolution_subtract_fusion.6
  170.1 0.1 copy.8
  170.2 0.7 cholesky.74
  170.9 0.1 select_reduce_fusion.3
  171.0 0.6 compare_reduce_fusion.3
  171.6 0.6 fusion.27
  172.3 0.6 custom-call.8
  172.9 0.9 convert_element_type.18
  173.8 0.9 fusion.6
  174.7 0.9 fusion.22
  175.7 0.9 fusion.8
  176.6 8.6 %all-reduce.3 = (f32[32,8]{0,1:T(8,128)S(1)}, f32[8,8]{0,1:T(8,128)S(1)}) all-reduce(f32[32,8]{0,1:T(8,128)S(1)} %fusion.8, f32[8,8]{0,1:T(8,128)S(1)} %fusion.22), channel_id=1, replica_groups=mesh['dp'=8,'tensor'=4] {'tensor'}, use_global_device_ids=true, to_apply=%region_9.12 | all-reduce | flops 320 | bytes 2560 | tf_op jit(solution)/shard_map/psum | solution.py:28
  185.1 0.2 convolution_subtract_fusion.2
  185.3 0.1 convolution_subtract_fusion.5
  185.4 0.1 copy.12
  185.5 0.7 cholesky.85
  186.2 0.1 select_reduce_fusion.2
  186.3 0.6 compare_reduce_fusion.2
  186.9 0.6 fusion.28
  187.6 0.6 custom-call.9
  188.2 0.8 fusion.5
  189.0 0.9 fusion.19
  190.0 0.9 fusion.17
  190.9 10.6 %all-reduce.2 = (f32[32,8]{0,1:T(8,128)S(1)}, f32[8,8]{0,1:T(8,128)S(1)}) all-reduce(f32[32,8]{0,1:T(8,128)S(1)} %fusion.17, f32[8,8]{0,1:T(8,128)S(1)} %fusion.19), channel_id=1, replica_groups=mesh['dp'=8,'tensor'=4] {'tensor'}, use_global_device_ids=true, to_apply=%region_12.15 | all-reduce | flops 320 | bytes 2560 | tf_op jit(solution)/shard_map/psum | solution.py:28
  201.5 0.2 convolution_subtract_fusion.1
  201.7 0.1 convolution_subtract_fusion.4
  201.9 0.1 copy.16
  201.9 0.7 cholesky.96
  202.6 0.1 select_reduce_fusion.1
  202.7 0.6 compare_reduce_fusion.1
  203.3 0.6 fusion.29
  204.0 0.6 custom-call.10
  204.6 0.8 fusion.3
  205.5 0.9 fusion.15
  206.4 0.9 fusion.13
  207.3 8.6 %all-reduce.1 = (f32[32,8]{0,1:T(8,128)S(1)}, f32[8,8]{0,1:T(8,128)S(1)}) all-reduce(f32[32,8]{0,1:T(8,128)S(1)} %fusion.13, f32[8,8]{0,1:T(8,128)S(1)} %fusion.15), channel_id=1, replica_groups=mesh['dp'=8,'tensor'=4] {'tensor'}, use_global_device_ids=true, to_apply=%region_14.17 | all-reduce | flops 320 | bytes 2560 | tf_op jit(solution)/shard_map/psum | solution.py:28
  215.9 0.2 convolution_subtract_fusion
  216.1 0.1 convolution_subtract_fusion.3
  216.3 0.1 copy.20
  216.4 0.7 cholesky.107
  217.0 0.1 select_reduce_fusion
  217.1 0.6 compare_reduce_fusion
  217.8 0.6 fusion.30
  218.4 0.6 custom-call.11
  219.0 0.3 fusion.1
  219.3 13.8 %fusion.42 = f32[2560,32]{0,1:T(8,128)} fusion(f32[1728,2560]{1,0:T(8,128)} %copy-done.1, f32[1728,32]{0,1:T(8,128)S(1)} %fusion.1), kind=kOutput, calls=%fused_computation.82 | convolution fusion | flops 1698693120 | bytes 18243584 | tf_op jit(solution)/shard_map/dot_general | solution.py:43
  233.1 125.2 %all-reduce.10.cloned.1.call-done = f32[2560,32]{0,1:T(8,128)} async-done(((f32[2560,32]{0,1:T(8,128)}), f32[2560,32]{0,1:T(8,128)}) %all-reduce.10.cloned.1.call-update) | async-done | bytes 327696 | tf_op jit(solution)/shard_map/psum | solution.py:44
  358.2 1.0 broadcast_multiply_fusion
  359.2 0.7 constant_dynamic-slice_fusion
  359.9 19.1 %fusion = bf16[1,1728,2560]{2,1,0:T(8,128)(2,1)} fusion(f32[1728,2560]{1,0:T(8,128)} %copy-done.1, f32[1728,32]{0,1:T(8,128)S(1)} %fusion.1, f32[2560,32]{0,1:T(8,128)} %all-reduce.10.cloned.1.call-done), kind=kOutput, calls=%fused_computation.2 | convolution fusion | flops 1707622400 | bytes 27090944 | tf_op jit(solution)/shard_map/dot_general | solution.py:45
  (13 shorter events, 0.2 us)
Async XLA Ops:
  7.2 65.6 %copy-start = (bf16[576,1728]{1,0:T(8,128)(2,1)S(1)}, bf16[576,1728]{1,0:T(8,128)(2,1)}, u32[]{:S(2)}) copy-start(bf16[576,1728]{1,0:T(8,128)(2,1)} %param.16) | copy-start | bytes 5971972
  7.2 65.6 %all-gather.2.cloned.1.call-start = ((), (), s32[]{:S(2)}) async-start(), calls=%async_computation | async-start | bytes 3686400 | tf_op jit(solution)/shard_map/all_gather | solution.py:17
  7.9 148.3 %all-reduce.8.cloned.1.call-start = ((), (), s32[]{:S(2)}) async-start(), calls=%async_computation.1 | async-start | bytes 229376 | tf_op jit(solution)/shard_map/psum | solution.py:23
  83.2 6.1 %copy-start.1 = (f32[1728,2560]{1,0:T(8,128)}, f32[1728,2560]{1,0:T(8,128)S(1)}, u32[]{:S(2)}) copy-start(f32[1728,2560]{1,0:T(8,128)S(1)} %convert_add_fusion) | copy-start | bytes 53084164
  105.7 252.5 %all-reduce.10.cloned.1.call-start = ((), (), s32[]{:S(2)}) async-start(), calls=%async_computation.2 | async-start | bytes 655360 | tf_op jit(solution)/shard_map/psum | solution.py:44
Sparse Core Ops, SparseCore 0:
  9.6 63.1 all-gather.1
  105.8 50.2 all-reduce.7
  233.2 124.9 all-reduce.9
where the time goes:
time: 387 us; the launch traced here: 386 us
  waiting for transfers between devices  222 us (57%)
  matrix products  71.1 us (18%)
  blocking collectives  56.6 us (15%)
  other arithmetic  14.7 us (4%)
  between operations  13.9 us (4%)
  local copies, waits for them, and re-layouts  7.01 us (2%)
    psum x1, waiting for transfers between devices, body(): summed = lax.psum(term, ('dp', 'tensor')) / replicas  125 us
    psum x1, waiting for transfers between devices, body(): p_total = lax.psum(p_local.astype(jnp.bfloat16), 'dp').astype(jnp.float32)  48.5 us
    all_gather x1, waiting for transfers between devices, body(): lax.all_gather(activations, 'tensor', axis=0, tiled=True)  47.8 us
    psum x4, blocking collectives, body(): lax.psum((jnp.dot(p_basis.T, columns, precision=highest), jnp.dot(columns...  39.5 us
    dot_general x1, matrix products, body(): jnp.dot(p_basis, summed.T, precision=highest)  19.1 us
    all_gather x1, blocking collectives, body(): factor_full = lax.all_gather(right_factor, 'tensor', axis=0, tiled=True)  17.1 us
    dot_general x1, matrix products, body(): p_local = jnp.dot(corrected, factor_full, precision=highest)  16.4 us
    dot_general x1, matrix products, body(): lax.dot_general(corrected, p_basis, contract_first, precision=highest)  13.8 us
  transfers between devices with their start and end apart: 3, of which 3 were waited for; matrix products, arithmetic and copies ran while one was open for 0% of the time, Pallas kernels for 0%

commit v1 on v0

--- a/solution.py
+++ b/solution.py
@@ -1,13 +1,19 @@
+import functools
 import jax
 import jax.numpy as jnp
 from jax import lax
+from jax.experimental import pallas as pl
+from jax.experimental.pallas import tpu as pltpu
 from jax.sharding import PartitionSpec as P
 
 contract_first = (((0,), (0,)), ((), ()))
+contract_last = (((1,), (1,)), ((), ()))
 column_block = 8
-
-
-def body(activations, out_grad, error_state, right_factor):
+bf16, f32 = jnp.bfloat16, jnp.float32
+MIB = 1 << 20
+
+
+def plain_body(activations, out_grad, error_state, right_factor):
     highest = lax.Precision.HIGHEST
     errors = error_state[0]
     rows_here = right_factor.shape[0]
@@ -16,11 +22,11 @@
         out_grad,
         lax.all_gather(activations, "tensor", axis=0, tiled=True),
         contract_first,
-        preferred_element_type=jnp.float32,
-    )
-    corrected = grad + errors.astype(jnp.float32)
+        preferred_element_type=f32,
+    )
+    corrected = grad + errors.astype(f32)
     p_local = jnp.dot(corrected, factor_full, precision=highest)
-    p_total = lax.psum(p_local.astype(jnp.bfloat16), "dp").astype(jnp.float32)
+    p_total = lax.psum(p_local.astype(bf16), "dp").astype(f32)
     p_basis = jnp.zeros_like(p_total)
     for block_index in range(p_total.shape[1] // column_block):
         first = block_index * column_block
@@ -42,9 +48,320 @@
     replicas = lax.axis_size("dp")
     term = lax.dot_general(corrected, p_basis, contract_first, precision=highest)
     summed = lax.psum(term, ("dp", "tensor")) / replicas
-    new_error = (corrected - jnp.dot(p_basis, summed.T, precision=highest)).astype(jnp.bfloat16)
+    new_error = (corrected - jnp.dot(p_basis, summed.T, precision=highest)).astype(bf16)
     new_factor = lax.dynamic_slice_in_dim(
         summed, lax.axis_index("tensor") * rows_here, rows_here, 0
+    )
+    return (new_error[None], new_factor)
+
+
+def dot(a, b, dims=None, precision=None):
+    if dims is None:
+        dims = (((1,), (0,)), ((), ()))
+    return lax.dot_general(a, b, dims, precision=precision, preferred_element_type=f32)
+
+
+def split(v):
+    high = v.astype(bf16)
+    return high, (v - high.astype(f32)).astype(bf16)
+
+
+def call(kernel, outs, *args, scratch=(), grid=None, in_specs=None, out_specs=None, vmem=48, flops=0, moved=0):
+    vmem_spec = pl.BlockSpec(memory_space=pltpu.VMEM)
+    if grid is None:
+        in_specs = [
+            pl.BlockSpec(memory_space=pltpu.SMEM) if a.dtype == jnp.int32 else vmem_spec
+            for a in args
+        ]
+        out_specs = [vmem_spec] * len(outs)
+        extra = {}
+    else:
+        extra = {"grid": grid}
+    size = sum(a.size * a.dtype.itemsize for a in args) + sum(
+        o.size * o.dtype.itemsize for o in outs
+    )
+    result = pl.pallas_call(
+        kernel,
+        out_shape=list(outs),
+        in_specs=in_specs,
+        out_specs=out_specs,
+        scratch_shapes=list(scratch),
+        compiler_params=pltpu.CompilerParams(vmem_limit_bytes=vmem * MIB),
+        cost_estimate=pl.CostEstimate(flops=flops, bytes_accessed=size, transcendentals=0),
+        name=kernel.__name__ if hasattr(kernel, "__name__") else kernel.func.__name__,
+        **extra,
+    )(*args)
+    return result
+
+
+def like(shape, dtype):
+    return jax.ShapeDtypeStruct(shape, dtype)
+
+
+def flip_factor(q_ref, out_ref):
+    out_ref[...] = q_ref[...].T.astype(bf16)
+
+
+def project(place, own, n1, n2, n3, x_ref, q_ref, y_ref):
+    t = place[0]
+    for k, part in enumerate((own, n1, n2, n3)):
+        q_ref[t ^ k] = part[...]
+    parts, _, width = q_ref.shape
+    total = dot(q_ref[0], x_ref[:, :width], contract_last)
+    for k in range(1, parts):
+        total += dot(q_ref[k], x_ref[:, k * width : (k + 1) * width], contract_last)
+    y_ref[...] = total
+
+
+def error_left(q_ref, e_ref, out_ref):
+    term = dot(q_ref[0], e_ref[...], contract_last)
+
+    @pl.when(pl.program_id(0) == 0)
+    def _():
+        out_ref[...] = term
+
+    @pl.when(pl.program_id(0) > 0)
+    def _():
+        out_ref[...] += term
+
+
+def left_factor(place, eq_ref, own, n1, n2, n3, dy_ref, out_ref, y4):
+    t = place[0]
+    for k, part in enumerate((own, n1, n2, n3)):
+        y4[t ^ k] = part[...]
+    parts, rank, tokens = y4.shape
+    total = eq_ref[...]
+    for s in range(parts):
+        both = jnp.concatenate(split(y4[s]), axis=0)
+        term = dot(both, dy_ref[s * tokens : (s + 1) * tokens, :])
+        total += term[:rank] + term[rank:]
+    out_ref[...] = total.astype(bf16)
+
+
+def weigh(place, own, n1, n2, n3, dy_ref, p_ref, m0, m1, m2, m3, held):
+    t = place[0]
+    p = (own[...].astype(f32) + n1[...].astype(f32)) + (n2[...].astype(f32) + n3[...].astype(f32))
+    p = p.astype(bf16)
+    p_ref[...] = p
+    parts, rank, tokens = held.shape
+    gram = dot(p, p, contract_last)
+    for s in range(parts):
+        held[s] = dot(p, dy_ref[s * tokens : (s + 1) * tokens, :], contract_last)
+    for k, out in enumerate((m0, m1, m2, m3)):
+        out[:, :tokens] = held[t ^ k]
+        out[:, 256 : 256 + rank] = gram
+
+
+def error_right(p_ref, e_ref, out_ref):
+    out_ref[...] = dot(p_ref[...], e_ref[...])
+
+
+def right_term(place, m0, m1, m2, m3, te_ref, x_ref, gram_ref, keep_ref, send_ref, held):
+    core = place[1]
+    tokens = x_ref.shape[0]
+    rank = te_ref.shape[0]
+    total = (m0[...] + m1[...]) + (m2[...] + m3[...])
+    gram_ref[...] = total[:, 256 : 256 + rank]
+    both = jnp.concatenate(split(total[:, :tokens]), axis=0)
+    term = dot(both, x_ref[...])
+    term = te_ref[...] + (term[:rank] + term[rank:])
+    held[0] = term[: rank // 2]
+    held[1] = term[rank // 2 :]
+    keep_ref[...] = held[core]
+    send_ref[...] = held[1 - core]
+
+
+def cut(place, keep, got, o0, o1, o2, o3, held):
+    t = place[0]
+    total = keep[...] + got[...]
+    width = held.shape[2]
+    for s in range(held.shape[0]):
+        held[s] = total[:, s * width : (s + 1) * width]
+    for k, out in enumerate((o0, o1, o2, o3)):
+        out[...] = held[t ^ k]
+
+
+def invert_cholesky(g_ref, out_ref):
+    n = g_ref.shape[0]
+    rows = lax.broadcasted_iota(jnp.int32, (n, n), 0)
+    cols = lax.broadcasted_iota(jnp.int32, (n, n), 1)
+    a = g_ref[...]
+    inverse = jnp.where(rows == cols, 1.0, 0.0).astype(f32)
+    for j in range(n):
+        column = jnp.sum(jnp.where(cols == j, a, 0.0), axis=1, keepdims=True)
+        pivot = column[j : j + 1, :]
+        factor = jnp.where(rows[:, :1] > j, column / pivot, 0.0)
+        a = a - factor * a[j : j + 1, :]
+        inverse = inverse - factor * inverse[j : j + 1, :]
+    diagonal = jnp.sum(jnp.where(rows == cols, a, 0.0), axis=1, keepdims=True)
+    out_ref[...] = inverse * lax.rsqrt(diagonal)
+
+
+def flip_grad(dy_ref, main_ref, rest_ref):
+    main = main_ref.shape[1]
+    main_ref[...] = dy_ref[:main, :].T
+    rest_ref[...] = dy_ref[main:, :].T
+
+
+def finish_factor(replicas, place, linv, p_ref, rest_ref, a0, a1, a2, a3, b0, b1, b2, b3, left_ref, right_ref, new_ref, held, nf4):
+    t, core = place[0], place[1]
+    for k, (a, b) in enumerate(((a0, b0), (a1, b1), (a2, b2), (a3, b3))):
+        held[t ^ k, core] = a[...]
+        held[t ^ k, 1 - core] = b[...]
+    highest = lax.Precision.HIGHEST
+    parts, _, half, width = held.shape
+    rank = 2 * half
+    scaled = linv[...] * (1.0 / replicas)
+    for s in range(parts):
+        nf = dot(scaled, held[s].reshape(rank, width), precision=highest)
+        nf4[s] = nf
+        high, low = split(nf)
+        at = slice(s * width, (s + 1) * width)
+        right_ref[:rank, at] = high
+        right_ref[rank : 2 * rank, at] = high
+        right_ref[2 * rank :, at] = low
+    new_ref[...] = nf4[t].T
+    basis = dot(linv[...], p_ref[...].astype(f32), precision=highest)
+    high, low = split(-basis)
+    rest = rest_ref.shape[1]
+    left_ref[:, :rest] = rest_ref[...]
+    left_ref[:, rest:] = jnp.concatenate((high, low, high), axis=0).T
+
+
+def rebuild(main_ref, left_ref, x_ref, right_ref, e_ref, out_ref, tail):
+    main = main_ref.shape[1]
+    rest = x_ref.shape[0] - main
+
+    @pl.when(pl.program_id(0) == 0)
+    def _():
+        tail[:rest, :] = x_ref[main:, :]
+        tail[rest:, :] = right_ref[...]
+
+    step = 512
+    for c in range(0, x_ref.shape[1], step):
+        at = slice(c, c + step)
+        total = dot(main_ref[...], x_ref[:main, at]) + dot(left_ref[...], tail[:, at])
+        out_ref[:, at] = (total + e_ref[:, at].astype(f32)).astype(bf16)
+
+
+def partners(value, axis, size, by):
+    return [lax.ppermute(value, axis, [(i, i ^ k) for i in range(size)]) for k in by]
+
+
+def body(activations, out_grad, error_state, right_factor):
+    errors = error_state[0]
+    n_dp, n_t = lax.axis_size("dp"), lax.axis_size("tensor")
+    rows, rank = right_factor.shape
+    tokens, features = activations.shape
+    all_tokens, hidden = out_grad.shape
+    place = jnp.stack([lax.axis_index("tensor"), lax.axis_index("dp") % 2]).astype(jnp.int32)
+    along_t = functools.partial(partners, axis="tensor", size=n_t, by=(1, 2, 3))
+    along_xy = functools.partial(partners, axis="dp", size=n_dp, by=(2, 4, 6))
+
+    x_full = lax.all_gather(activations, "tensor", axis=0, tiled=True)
+
+    (q_own,) = call(flip_factor, [like((rank, rows), bf16)], right_factor)
+    q_parts = along_t(q_own)
+    main = all_tokens // 256 * 256
+    main_t, rest_t = call(
+        flip_grad,
+        [like((hidden, main), bf16), like((hidden, all_tokens - main), bf16)],
+        out_grad,
+    )
+    q_full, y_own = call(
+        project,
+        [like((n_t, rank, rows), bf16), like((rank, tokens), f32)],
+        place, q_own, *q_parts, activations,
+    )
+    y_parts = along_t(y_own)
+    (eq,) = call(
+        error_left,
+        [like((rank, hidden), f32)],
+        q_full, errors,
+        grid=(n_t,),
+        in_specs=[
+            pl.BlockSpec((1, rank, rows), lambda k: (k, 0, 0)),
+            pl.BlockSpec((hidden, rows), lambda k: (0, k)),
+        ],
+        out_specs=[pl.BlockSpec((rank, hidden), lambda k: (0, 0))],
+    )
+    (p_local,) = call(
+        left_factor,
+        [like((rank, hidden), bf16)],
+        place, eq, y_own, *y_parts, out_grad,
+        scratch=[pltpu.VMEM((n_t, rank, tokens), f32)],
+    )
+    (p_other,) = partners(p_local, "dp", n_dp, (1,))
+    p_chip = (p_local.astype(f32) + p_other.astype(f32)).astype(bf16)
+    p_parts = along_xy(p_chip)
+    p_total, *messages = call(
+        weigh,
+        [like((rank, hidden), bf16)] + [like((rank, 384), f32)] * 4,
+        place, p_chip, *p_parts, out_grad,
+        scratch=[pltpu.VMEM((n_t, rank, tokens), f32)],
+    )
+    arrived = [
+        lax.ppermute(m, "tensor", [(i, i ^ k) for i in range(n_t)])
+        for k, m in enumerate(messages)
+        if k
+    ]
+    (te,) = call(
+        error_right,
+        [like((rank, features), f32)],
+        p_total, errors,
+        grid=(n_t,),
+        in_specs=[
+            pl.BlockSpec((rank, hidden), lambda k: (0, 0)),
+            pl.BlockSpec((hidden, rows), lambda k: (0, k)),
+        ],
+        out_specs=[pl.BlockSpec((rank, rows), lambda k: (0, k))],
+    )
+    gram, keep, send = call(
+        right_term,
+        [like((rank, rank), f32), like((rank // 2, features), f32), like((rank // 2, features), f32)],
+        place, messages[0], *arrived, te, activations,
+        scratch=[pltpu.VMEM((2, rank // 2, features), f32)],
+    )
+    (got,) = partners(send, "dp", n_dp, (1,))
+    (linv,) = call(invert_cholesky, [like((rank, rank), f32)], gram)
+    pieces = call(
+        cut,
+        [like((rank // 2, rows), f32)] * 4,
+        place, keep, got,
+        scratch=[pltpu.VMEM((n_t, rank // 2, rows), f32)],
+    )
+    arrived = [
+        lax.ppermute(m, "tensor", [(i, i ^ k) for i in range(n_t)])
+        for k, m in enumerate(pieces)
+        if k
+    ]
+    mine = (pieces[0] + arrived[0]) + (arrived[1] + arrived[2])
+    x_side, y_side, diagonal = along_xy(mine)
+    mine = (mine + x_side) + (y_side + diagonal)
+    near = [mine] + along_t(mine)
+    far = [partners(v, "dp", n_dp, (1,))[0] for v in near]
+    left, right, new_factor = call(
+        functools.partial(finish_factor, n_dp),
+        [like((hidden, all_tokens - main + 3 * rank), bf16), like((3 * rank, features), bf16), like((rows, rank), f32)],
+        place, linv, p_total, rest_t, *near, *far,
+        scratch=[pltpu.VMEM((n_t, 2, rank // 2, rows), f32), pltpu.VMEM((n_t, rank, rows), f32)],
+    )
+    steps = 6
+    block = hidden // steps
+    (new_error,) = call(
+        rebuild,
+        [like((hidden, features), bf16)],
+        main_t, left, x_full, right, errors,
+        grid=(steps,),
+        in_specs=[
+            pl.BlockSpec((block, main), lambda k: (k, 0)),
+            pl.BlockSpec((block, left.shape[1]), lambda k: (k, 0)),
+            pl.BlockSpec((all_tokens, features), lambda k: (0, 0)),
+            pl.BlockSpec((3 * rank, features), lambda k: (0, 0)),
+            pl.BlockSpec((block, features), lambda k: (k, 0)),
+        ],
+        out_specs=[pl.BlockSpec((block, features), lambda k: (k, 0))],
+        scratch=[pltpu.VMEM((left.shape[1], features), bf16)],
     )
     return (new_error[None], new_factor)
 
@@ -56,8 +373,9 @@
         P("dp", "tensor", None),
         P("tensor", None),
     )
+    fits = mesh.shape["dp"] == 8 and mesh.shape["tensor"] == 4
     return jax.shard_map(
-        body,
+        body if fits else plain_body,
         mesh=mesh,
         in_specs=placed,
         out_specs=(P("dp", "tensor", None), P("tensor", None)),

time: 387 us -> 114 us (0.29)
  waiting for transfers between devices: 222 us -> 26.5 us
  matrix products: 71.1 us -> 0 us
  blocking collectives: 56.6 us -> 0 us
  starting transfers between devices: 0.12 us -> 34.9 us
  Pallas kernels: 0 us -> 32.7 us
  other arithmetic: 14.7 us -> 0.13 us
    psum x2 -> x0, waiting for transfers between devices: 174 us -> none  [the longest x1 125 us: body(): summed = lax.psum(term, ('dp', 'tensor')) / replicas]
    dot_general x19 -> x0, matrix products: 68.3 us -> none  [the longest x1 19.1 us: body(): jnp.dot(p_basis, summed.T, precision=highest)]
    all_gather x1, waiting for transfers between devices: 47.8 us -> 0.01 us  [body(): x_full = lax.all_gather(activations, 'tensor', axis=0, tiled=True)]
    psum x4 -> x0, blocking collectives: 39.5 us -> none  [body(): lax.psum((jnp.dot(p_basis.T, columns, precision=highest), jnp.dot(columns...]
    ppermute x0 -> x27, starting transfers between devices: none -> 34.8 us  [the longest x21 23.1 us: partners(): lax.ppermute(value, axis, [(i, i ^ k) for i in range(size)])]
    pallas_call x0 -> x12, Pallas kernels: none -> 32.7 us  [call(): pl.pallas_call(kernel, out_shape=list(outs), in_specs=in_specs, out_specs...]
    ppermute x0 -> x27, waiting for transfers between devices: none -> 25.9 us  [the longest x21 18.9 us: partners(): lax.ppermute(value, axis, [(i, i ^ k) for i in range(size)])]
    all_gather x1 -> x0, blocking collectives: 17.1 us -> none  [body(): factor_full = lax.all_gather(right_factor, 'tensor', axis=0, tiled=True)]
  transfers between devices with their start and end apart: 3 -> 28, of which waited for: 3 -> 17; matrix products, arithmetic and copies ran while one was open for 0% -> 2% of each run, Pallas kernels for 0% -> 18%
where the time goes in v1:
time: 114 us; the launch traced here: 113 us
  starting transfers between devices  34.9 us (31%)
  Pallas kernels  32.7 us (29%)
  waiting for transfers between devices  26.5 us (23%)
  between operations  14.2 us (12%)
  local copies, waits for them, and re-layouts  4.85 us (4%)
    pallas_call x12, Pallas kernels, call(): pl.pallas_call(kernel, out_shape=list(outs), in_specs=in_specs, out_specs...  32.7 us
    ppermute x21, starting transfers between devices, partners(): lax.ppermute(value, axis, [(i, i ^ k) for i in range(size)])  23.1 us
    ppermute x21, waiting for transfers between devices, partners(): lax.ppermute(value, axis, [(i, i ^ k) for i in range(size)])  18.9 us
    ppermute x6, starting transfers between devices, body(): lax.ppermute(m, 'tensor', [(i, i ^ k) for i in range(n_t)])  11.8 us
    ppermute x6, waiting for transfers between devices, body(): lax.ppermute(m, 'tensor', [(i, i ^ k) for i in range(n_t)])  6.95 us
    unnamed x10, local copies, waits for them, and re-layouts  4.85 us
  transfers between devices with their start and end apart: 28, of which 17 were waited for; matrix products, arithmetic and copies ran while one was open for 2% of the time, Pallas kernels for 18%

profile of v1, /device:TPU:0, one launch (start us, length us, event | category | flops | bytes accessed | tf_op | source)
XLA Modules:
  0.0 113.4 jit_solution(7439144944596511168)
XLA Ops:
  7.2 0.0 all-gather.2.cloned.1.call-start
  7.2 0.7 all-gather.2.cloned.1.call-update
  7.9 1.0 copy.6.q_ref
  9.0 0.1 flip_factor.1.own
  9.1 5.1 %collective-permute-start.2 = (bf16[32,640]{1,0:T(8,128)(2,1)S(1)}, bf16[32,640]{1,0:T(8,128)(2,1)S(1)}, u32[]{:S(2)}, u32[]{:S(2)}) collective-permute-start(bf16[32,640]{1,0:T(8,128)(2,1)S(1)} %flip_factor.1.own), channel_id=1, source_target_pairs={{0,3},{1,2},{2,1},{3,0},{4,7},{5,6},{6,5},{7,4},{8,11},{9,10},{10,... | collective-permute-start | bytes 122888 | tf_op jit(solution)/shard_map/ppermute | solution.py:248
  14.2 0.6 collective-permute-start
  14.8 0.1 pad_add_fusion.place
  14.9 1.3 %collective-permute-done.2.n3 = bf16[32,640]{1,0:T(8,128)(2,1)S(1)} collective-permute-done((bf16[32,640]{1,0:T(8,128)(2,1)S(1)}, bf16[32,640]{1,0:T(8,128)(2,1)S(1)}, u32[]{:S(2)}, u32[]{:S(2)}) %collective-permute-start.2) | collective-permute-done | bytes 40992 | tf_op jit(solution)/shard_map/ppermute | solution.py:248
  16.2 2.9 %collective-permute-done.1.n2 = bf16[32,640]{1,0:T(8,128)(2,1)S(1)} collective-permute-done((bf16[32,640]{1,0:T(8,128)(2,1)S(1)}, bf16[32,640]{1,0:T(8,128)(2,1)S(1)}, u32[]{:S(2)}, u32[]{:S(2)}) %collective-permute-start.1) | collective-permute-done | bytes 40992 | tf_op jit(solution)/shard_map/ppermute | solution.py:248
  19.1 1.2 %copy-done.1 = bf16[144,2560]{1,0:T(8,128)(2,1)S(1)} copy-done((bf16[144,2560]{1,0:T(8,128)(2,1)S(1)}, bf16[144,2560]{1,0:T(8,128)(2,1)}, u32[]{:S(2)}) %copy-start.1) | copy-done | bytes 737304
  20.2 0.9 project.1
  21.1 1.5 %collective-permute-start.5 = (f32[32,144]{1,0:T(8,128)S(1)}, f32[32,144]{1,0:T(8,128)S(1)}, u32[]{:S(2)}, u32[]{:S(2)}) collective-permute-start(f32[32,144]{1,0:T(8,128)S(1)} %get-tuple-element.23.own), channel_id=1, source_target_pairs={{0,3},{1,2},{2,1},{3,0},{4,7},{5,6},{6,5},{7,4},{8,11},{9,10},{10,... | collective-permute-start | bytes 55304 | tf_op jit(solution)/shard_map/ppermute | solution.py:248
  22.7 0.6 collective-permute-start.4
  23.3 2.3 %collective-permute-start.3 = (f32[32,144]{1,0:T(8,128)S(1)}, f32[32,144]{1,0:T(8,128)S(1)}, u32[]{:S(2)}, u32[]{:S(2)}) collective-permute-start(f32[32,144]{1,0:T(8,128)S(1)} %get-tuple-element.23.own), channel_id=1, source_target_pairs={{0,1},{1,0},{2,3},{3,2},{4,5},{5,4},{6,7},{7,6},{8,9},{9,8},{10,11... | collective-permute-start | bytes 55304 | tf_op jit(solution)/shard_map/ppermute | solution.py:248
  25.5 5.9 %error_left.1.eq_ref = f32[32,1728]{1,0:T(8,128)S(1)} custom-call(bf16[4,32,640]{2,1,0:T(8,128)(2,1)S(1)} %get-tuple-element.22.q_ref, bf16[1728,2560]{1,0:T(8,128)(2,1)} %bitcast.4), custom_call_target="tpu_custom_call" | custom-call | bytes 9232384 | tf_op jit(solution)/shard_map/error_left/pallas_call | solution.py:83
  31.4 0.0 collective-permute-done.5.n3
  31.4 0.0 collective-permute-done.4.n2
  31.5 1.0 left_factor.1
  32.4 0.1 collective-permute-start.6
  32.5 1.3 %collective-permute-done.6 = bf16[32,1728]{1,0:T(8,128)(2,1)S(1)} collective-permute-done((bf16[32,1728]{1,0:T(8,128)(2,1)S(1)}, bf16[32,1728]{1,0:T(8,128)(2,1)S(1)}, u32[]{:S(2)}, u32[]{:S(2)}) %collective-permute-start.6) | collective-permute-done | bytes 110624 | tf_op jit(solution)/shard_map/ppermute | solution.py:248
  33.8 2.5 %collective-permute-start.9 = (bf16[32,1728]{1,0:T(8,128)(2,1)S(1)}, bf16[32,1728]{1,0:T(8,128)(2,1)S(1)}, u32[]{:S(2)}, u32[]{:S(2)}) collective-permute-start(bf16[32,1728]{1,0:T(8,128)(2,1)S(1)} %add_convert_fusion.own), channel_id=1, source_target_pairs={{0,24},{4,28},{8,16},{12,20},{16,8},{20,12},{24,0},{28,4},{1,25},{... | collective-permute-start | bytes 331784 | tf_op jit(solution)/shard_map/ppermute | solution.py:248
  36.3 0.5 collective-permute-start.8
  36.8 0.5 collective-permute-start.7
  37.4 2.7 %collective-permute-done.9.n3 = bf16[32,1728]{1,0:T(8,128)(2,1)S(1)} collective-permute-done((bf16[32,1728]{1,0:T(8,128)(2,1)S(1)}, bf16[32,1728]{1,0:T(8,128)(2,1)S(1)}, u32[]{:S(2)}, u32[]{:S(2)}) %collective-permute-start.9) | collective-permute-done | bytes 110624 | tf_op jit(solution)/shard_map/ppermute | solution.py:248
  40.1 2.4 %collective-permute-done.8.n2 = bf16[32,1728]{1,0:T(8,128)(2,1)S(1)} collective-permute-done((bf16[32,1728]{1,0:T(8,128)(2,1)S(1)}, bf16[32,1728]{1,0:T(8,128)(2,1)S(1)}, u32[]{:S(2)}, u32[]{:S(2)}) %collective-permute-start.8) | collective-permute-done | bytes 110624 | tf_op jit(solution)/shard_map/ppermute | solution.py:248
  42.5 0.1 collective-permute-done.7.n1
  42.5 1.3 %weigh.1 = (bf16[32,1728]{1,0:T(8,128)(2,1)S(1)}, f32[32,384]{1,0:T(8,128)S(1)}, f32[32,384]{1,0:T(8,128)S(1)}, f32[32,384]{1,0:T(8,128)S(1)}, f32[32,384]{1,0:T(8,128)S(1)}) custom-call(s32[2]{0:T(128)S(1)} %pad_add_fusion.place, bf16[32,1728]{1,0:T(8,128)(2,1)S(1)} %add_convert_fusion.own, bf16[32,1728]{1,0:T(8,128)(2,1)S(1)} %collective-permute-done.7.n1, ...), custom_call_target="tpu_custom_call" | custom-call | bytes 2740232 | tf_op jit(solution)/shard_map/weigh/pallas_call | solution.py:83
  43.8 0.1 collective-permute-start.10
  43.9 2.2 %collective-permute-start.11 = (f32[32,384]{1,0:T(8,128)S(1)}, f32[32,384]{1,0:T(8,128)S(1)}, u32[]{:S(2)}, u32[]{:S(2)}) collective-permute-start(f32[32,384]{1,0:T(8,128)S(1)} %get-tuple-element.26), channel_id=1, source_target_pairs={{0,2},{1,3},{2,0},{3,1},{4,6},{5,7},{6,4},{7,5},{8,10},{9,11},{10,... | collective-permute-start | bytes 147464 | tf_op jit(solution)/shard_map/ppermute | solution.py:304
  46.1 2.2 %collective-permute-start.12 = (f32[32,384]{1,0:T(8,128)S(1)}, f32[32,384]{1,0:T(8,128)S(1)}, u32[]{:S(2)}, u32[]{:S(2)}) collective-permute-start(f32[32,384]{1,0:T(8,128)S(1)} %get-tuple-element.27), channel_id=1, source_target_pairs={{0,3},{1,2},{2,1},{3,0},{4,7},{5,6},{6,5},{7,4},{8,11},{9,10},{10,... | collective-permute-start | bytes 147464 | tf_op jit(solution)/shard_map/ppermute | solution.py:304
  48.2 5.2 %error_right.1.te_ref = f32[32,2560]{1,0:T(8,128)S(1)} custom-call(bf16[32,1728]{1,0:T(8,128)(2,1)S(1)} %get-tuple-element.28.p_ref, bf16[1728,2560]{1,0:T(8,128)(2,1)} %bitcast.5), custom_call_target="tpu_custom_call" | custom-call | bytes 9285632 | tf_op jit(solution)/shard_map/error_right/pallas_call | solution.py:83
  53.5 0.0 collective-permute-done.11.m2
  53.5 0.5 collective-permute-done.12.m3
  53.9 0.8 right_term.1
  54.8 0.1 collective-permute-start.13
  54.9 1.4 %collective-permute-done.13.got = f32[16,2560]{1,0:T(8,128)S(1)} collective-permute-done((f32[16,2560]{1,0:T(8,128)S(1)}, f32[16,2560]{1,0:T(8,128)S(1)}, u32[]{:S(2)}, u32[]{:S(2)}) %collective-permute-start.13) | collective-permute-done | bytes 163872 | tf_op jit(solution)/shard_map/ppermute | solution.py:248
  56.2 0.6 cut.1
  56.8 3.8 %collective-permute-start.14 = (f32[16,640]{1,0:T(8,128)S(1)}, f32[16,640]{1,0:T(8,128)S(1)}, u32[]{:S(2)}, u32[]{:S(2)}) collective-permute-start(f32[16,640]{1,0:T(8,128)S(1)} %get-tuple-element.34), channel_id=1, source_target_pairs={{0,1},{1,0},{2,3},{3,2},{4,5},{5,4},{6,7},{7,6},{8,9},{9,8},{10,11... | collective-permute-start | bytes 122888 | tf_op jit(solution)/shard_map/ppermute | solution.py:334
  60.6 2.2 %collective-permute-start.15 = (f32[16,640]{1,0:T(8,128)S(1)}, f32[16,640]{1,0:T(8,128)S(1)}, u32[]{:S(2)}, u32[]{:S(2)}) collective-permute-start(f32[16,640]{1,0:T(8,128)S(1)} %get-tuple-element.35), channel_id=1, source_target_pairs={{0,2},{1,3},{2,0},{3,1},{4,6},{5,7},{6,4},{7,5},{8,10},{9,11},{10,... | collective-permute-start | bytes 122888 | tf_op jit(solution)/shard_map/ppermute | solution.py:334
  62.8 1.4 %collective-permute-start.16 = (f32[16,640]{1,0:T(8,128)S(1)}, f32[16,640]{1,0:T(8,128)S(1)}, u32[]{:S(2)}, u32[]{:S(2)}) collective-permute-start(f32[16,640]{1,0:T(8,128)S(1)} %get-tuple-element.36), channel_id=1, source_target_pairs={{0,3},{1,2},{2,1},{3,0},{4,7},{5,6},{6,5},{7,4},{8,11},{9,10},{10,... | collective-permute-start | bytes 122888 | tf_op jit(solution)/shard_map/ppermute | solution.py:334
  64.2 1.9 %collective-permute-done.14 = f32[16,640]{1,0:T(8,128)S(1)} collective-permute-done((f32[16,640]{1,0:T(8,128)S(1)}, f32[16,640]{1,0:T(8,128)S(1)}, u32[]{:S(2)}, u32[]{:S(2)}) %collective-permute-start.14) | collective-permute-done | bytes 40992 | tf_op jit(solution)/shard_map/ppermute | solution.py:334
  66.0 4.1 %collective-permute-done.15 = f32[16,640]{1,0:T(8,128)S(1)} collective-permute-done((f32[16,640]{1,0:T(8,128)S(1)}, f32[16,640]{1,0:T(8,128)S(1)}, u32[]{:S(2)}, u32[]{:S(2)}) %collective-permute-start.15) | collective-permute-done | bytes 40992 | tf_op jit(solution)/shard_map/ppermute | solution.py:334
  70.1 0.5 collective-permute-done.16
  70.7 2.1 %collective-permute-start.19 = (f32[16,640]{1,0:T(8,128)S(1)}, f32[16,640]{1,0:T(8,128)S(1)}, u32[]{:S(2)}, u32[]{:S(2)}) collective-permute-start(f32[16,640]{1,0:T(8,128)S(1)} %add_add_fusion.1), channel_id=1, source_target_pairs={{0,24},{4,28},{8,16},{12,20},{16,8},{20,12},{24,0},{28,4},{1,25},{... | collective-permute-start | bytes 122888 | tf_op jit(solution)/shard_map/ppermute | solution.py:248
  72.7 1.0 collective-permute-start.18
  73.7 0.5 collective-permute-start.17
  74.2 1.5 %collective-permute-done.19 = f32[16,640]{1,0:T(8,128)S(1)} collective-permute-done((f32[16,640]{1,0:T(8,128)S(1)}, f32[16,640]{1,0:T(8,128)S(1)}, u32[]{:S(2)}, u32[]{:S(2)}) %collective-permute-start.19) | collective-permute-done | bytes 40992 | tf_op jit(solution)/shard_map/ppermute | solution.py:248
  75.7 1.0 collective-permute-done.18
  76.7 1.0 collective-permute-done.17
  77.8 2.2 %collective-permute-start.22 = (f32[16,640]{1,0:T(8,128)S(1)}, f32[16,640]{1,0:T(8,128)S(1)}, u32[]{:S(2)}, u32[]{:S(2)}) collective-permute-start(f32[16,640]{1,0:T(8,128)S(1)} %add_add_fusion.a0), channel_id=1, source_target_pairs={{0,3},{1,2},{2,1},{3,0},{4,7},{5,6},{6,5},{7,4},{8,11},{9,10},{10,... | collective-permute-start | bytes 122888 | tf_op jit(solution)/shard_map/ppermute | solution.py:248
  79.9 2.9 %collective-permute-start.21 = (f32[16,640]{1,0:T(8,128)S(1)}, f32[16,640]{1,0:T(8,128)S(1)}, u32[]{:S(2)}, u32[]{:S(2)}) collective-permute-start(f32[16,640]{1,0:T(8,128)S(1)} %add_add_fusion.a0), channel_id=1, source_target_pairs={{0,2},{1,3},{2,0},{3,1},{4,6},{5,7},{6,4},{7,5},{8,10},{9,11},{10,... | collective-permute-start | bytes 122888 | tf_op jit(solution)/shard_map/ppermute | solution.py:248
  82.8 0.5 collective-permute-start.20
  83.3 0.0 collective-permute-start.23
  83.3 0.4 collective-permute-done.22.a3
  83.6 0.2 collective-permute-start.26
  83.8 1.8 %collective-permute-done.21.a2 = f32[16,640]{1,0:T(8,128)S(1)} collective-permute-done((f32[16,640]{1,0:T(8,128)S(1)}, f32[16,640]{1,0:T(8,128)S(1)}, u32[]{:S(2)}, u32[]{:S(2)}) %collective-permute-start.21) | collective-permute-done | bytes 40992 | tf_op jit(solution)/shard_map/ppermute | solution.py:248
  85.6 1.2 %collective-permute-done.20.a1 = f32[16,640]{1,0:T(8,128)S(1)} collective-permute-done((f32[16,640]{1,0:T(8,128)S(1)}, f32[16,640]{1,0:T(8,128)S(1)}, u32[]{:S(2)}, u32[]{:S(2)}) %collective-permute-start.20) | collective-permute-done | bytes 40992 | tf_op jit(solution)/shard_map/ppermute | solution.py:248
  86.8 0.6 flip_grad.1
  87.4 2.8 %invert_cholesky.1.linv = f32[32,32]{1,0:T(8,128)S(1)} custom-call(f32[32,32]{1,0:T(8,128)S(1)} %get-tuple-element.29.g_ref), custom_call_target="tpu_custom_call" | custom-call | bytes 8192 | tf_op jit(solution)/shard_map/invert_cholesky/pallas_call | solution.py:83
  90.3 0.0 collective-permute-done.23.b0
  90.3 1.8 %finish_factor.1 = (bf16[1728,160]{1,0:T(8,128)(2,1)S(1)}, bf16[96,2560]{1,0:T(8,128)(2,1)S(1)}, f32[640,32]{1,0:T(8,128)S(1)}) custom-call(s32[2]{0:T(128)S(1)} %pad_add_fusion.place, f32[32,32]{1,0:T(8,128)S(1)} %invert_cholesky.1.linv, bf16[32,1728]{1,0:T(8,128)(2,1)S(1)} %get-tuple-element.28.p_ref, bf16[1728,64]{1,0:T(8,128)(2,1)S(1)} %get-tuple-element.30.rest_ref, ...), custom_call_target="tpu_custom_call" | custom-call | bytes 1789960 | tf_op jit(solution)/shard_map/finish_factor/pallas_call | solution.py:83
  92.1 0.8 copy.7
  92.9 1.8 %copy-done.3 = bf16[576,2560]{1,0:T(8,128)(2,1)S(1)} copy-done((bf16[576,2560]{1,0:T(8,128)(2,1)S(1)}, bf16[576,2560]{1,0:T(8,128)(2,1)}, u32[]{:S(2)}) %copy-start.3) | copy-done | bytes 2949144
  94.7 11.8 %rebuild.1 = bf16[1728,2560]{1,0:T(8,128)(2,1)} custom-call(bf16[1728,512]{1,0:T(8,128)(2,1)S(1)} %get-tuple-element.21.main_ref, bf16[1728,160]{1,0:T(8,128)(2,1)S(1)} %get-tuple-element.37.left_ref, bf16[576,2560]{1,0:T(8,128)(2,1)S(1)} %copy-done.3, bf16[96,2560]{1,0:T(8,128)(2,1)S(1)} %get-tuple-element.38.right_ref, bf16[1728,2560]{1,0:T(8,128)(2,1)} %bitcast.6), custom_call_target="tpu_custom_call" | custom-call | bytes 23457792 | tf_op jit(solution)/shard_map/rebuild/pallas_call | solution.py:83
  (19 shorter events, 0.1 us)
Async XLA Ops:
  7.2 85.7 %all-gather.2.cloned.1.call-start = ((), (), s32[]{:S(2)}) async-start(), calls=%async_computation | async-start | bytes 3686400 | tf_op jit(solution)/shard_map/all_gather | solution.py:261
  9.1 7.1 %collective-permute-start.2 = (bf16[32,640]{1,0:T(8,128)(2,1)S(1)}, bf16[32,640]{1,0:T(8,128)(2,1)S(1)}, u32[]{:S(2)}, u32[]{:S(2)}) collective-permute-start(bf16[32,640]{1,0:T(8,128)(2,1)S(1)} %flip_factor.1.own), channel_id=1, source_target_pairs={{0,3},{1,2},{2,1},{3,0},{4,7},{5,6},{6,5},{7,4},{8,11},{9,10},{10,... | collective-permute-start | bytes 122888 | tf_op jit(solution)/shard_map/ppermute | solution.py:248
  14.2 4.9 %collective-permute-start.1 = (bf16[32,640]{1,0:T(8,128)(2,1)S(1)}, bf16[32,640]{1,0:T(8,128)(2,1)S(1)}, u32[]{:S(2)}, u32[]{:S(2)}) collective-permute-start(bf16[32,640]{1,0:T(8,128)(2,1)S(1)} %flip_factor.1.own), channel_id=1, source_target_pairs={{0,2},{1,3},{2,0},{3,1},{4,6},{5,7},{6,4},{7,5},{8,10},{9,11},{10,... | collective-permute-start | bytes 122888 | tf_op jit(solution)/shard_map/ppermute | solution.py:248
  14.2 4.9 %collective-permute-start = (bf16[32,640]{1,0:T(8,128)(2,1)S(1)}, bf16[32,640]{1,0:T(8,128)(2,1)S(1)}, u32[]{:S(2)}, u32[]{:S(2)}) collective-permute-start(bf16[32,640]{1,0:T(8,128)(2,1)S(1)} %flip_factor.1.own), channel_id=1, source_target_pairs={{0,1},{1,0},{2,3},{3,2},{4,5},{5,4},{6,7},{7,6},{8,9},{9,8},{10,11... | collective-permute-start | bytes 122888 | tf_op jit(solution)/shard_map/ppermute | solution.py:248
  19.1 1.2 %copy-start.1 = (bf16[144,2560]{1,0:T(8,128)(2,1)S(1)}, bf16[144,2560]{1,0:T(8,128)(2,1)}, u32[]{:S(2)}) copy-start(bf16[144,2560]{1,0:T(8,128)(2,1)} %x_ref.3) | copy-start | bytes 2211844
  21.1 10.3 %collective-permute-start.5 = (f32[32,144]{1,0:T(8,128)S(1)}, f32[32,144]{1,0:T(8,128)S(1)}, u32[]{:S(2)}, u32[]{:S(2)}) collective-permute-start(f32[32,144]{1,0:T(8,128)S(1)} %get-tuple-element.23.own), channel_id=1, source_target_pairs={{0,3},{1,2},{2,1},{3,0},{4,7},{5,6},{6,5},{7,4},{8,11},{9,10},{10,... | collective-permute-start | bytes 55304 | tf_op jit(solution)/shard_map/ppermute | solution.py:248
  22.7 8.8 %collective-permute-start.4 = (f32[32,144]{1,0:T(8,128)S(1)}, f32[32,144]{1,0:T(8,128)S(1)}, u32[]{:S(2)}, u32[]{:S(2)}) collective-permute-start(f32[32,144]{1,0:T(8,128)S(1)} %get-tuple-element.23.own), channel_id=1, source_target_pairs={{0,2},{1,3},{2,0},{3,1},{4,6},{5,7},{6,4},{7,5},{8,10},{9,11},{10,... | collective-permute-start | bytes 55304 | tf_op jit(solution)/shard_map/ppermute | solution.py:248
  23.3 8.2 %collective-permute-start.3 = (f32[32,144]{1,0:T(8,128)S(1)}, f32[32,144]{1,0:T(8,128)S(1)}, u32[]{:S(2)}, u32[]{:S(2)}) collective-permute-start(f32[32,144]{1,0:T(8,128)S(1)} %get-tuple-element.23.own), channel_id=1, source_target_pairs={{0,1},{1,0},{2,3},{3,2},{4,5},{5,4},{6,7},{7,6},{8,9},{9,8},{10,11... | collective-permute-start | bytes 55304 | tf_op jit(solution)/shard_map/ppermute | solution.py:248
  25.5 5.9 %copy-start = (bf16[576,1728]{1,0:T(8,128)(2,1)S(1)}, bf16[576,1728]{1,0:T(8,128)(2,1)}, u32[]{:S(2)}) copy-start(bf16[576,1728]{1,0:T(8,128)(2,1)} %dy_ref.5) | copy-start | bytes 5971972
  32.4 1.4 %collective-permute-start.6 = (bf16[32,1728]{1,0:T(8,128)(2,1)S(1)}, bf16[32,1728]{1,0:T(8,128)(2,1)S(1)}, u32[]{:S(2)}, u32[]{:S(2)}) collective-permute-start(bf16[32,1728]{1,0:T(8,128)(2,1)S(1)} %left_factor.1), channel_id=1, source_target_pairs={{0,4},{4,0},{8,12},{12,8},{16,20},{20,16},{24,28},{28,24},{1,5},{5... | collective-permute-start | bytes 331784 | tf_op jit(solution)/shard_map/ppermute | solution.py:248
  33.8 6.3 %collective-permute-start.9 = (bf16[32,1728]{1,0:T(8,128)(2,1)S(1)}, bf16[32,1728]{1,0:T(8,128)(2,1)S(1)}, u32[]{:S(2)}, u32[]{:S(2)}) collective-permute-start(bf16[32,1728]{1,0:T(8,128)(2,1)S(1)} %add_convert_fusion.own), channel_id=1, source_target_pairs={{0,24},{4,28},{8,16},{12,20},{16,8},{20,12},{24,0},{28,4},{1,25},{... | collective-permute-start | bytes 331784 | tf_op jit(solution)/shard_map/ppermute | solution.py:248
  36.3 6.1 %collective-permute-start.8 = (bf16[32,1728]{1,0:T(8,128)(2,1)S(1)}, bf16[32,1728]{1,0:T(8,128)(2,1)S(1)}, u32[]{:S(2)}, u32[]{:S(2)}) collective-permute-start(bf16[32,1728]{1,0:T(8,128)(2,1)S(1)} %add_convert_fusion.own), channel_id=1, source_target_pairs={{0,16},{4,20},{8,24},{12,28},{16,0},{20,4},{24,8},{28,12},{1,17},{... | collective-permute-start | bytes 331784 | tf_op jit(solution)/shard_map/ppermute | solution.py:248
  36.8 5.7 %collective-permute-start.7 = (bf16[32,1728]{1,0:T(8,128)(2,1)S(1)}, bf16[32,1728]{1,0:T(8,128)(2,1)S(1)}, u32[]{:S(2)}, u32[]{:S(2)}) collective-permute-start(bf16[32,1728]{1,0:T(8,128)(2,1)S(1)} %add_convert_fusion.own), channel_id=1, source_target_pairs={{0,8},{4,12},{8,0},{12,4},{16,24},{20,28},{24,16},{28,20},{1,9},{5... | collective-permute-start | bytes 331784 | tf_op jit(solution)/shard_map/ppermute | solution.py:248
  43.8 9.7 %collective-permute-start.10 = (f32[32,384]{1,0:T(8,128)S(1)}, f32[32,384]{1,0:T(8,128)S(1)}, u32[]{:S(2)}, u32[]{:S(2)}) collective-permute-start(f32[32,384]{1,0:T(8,128)S(1)} %get-tuple-element.25), channel_id=1, source_target_pairs={{0,1},{1,0},{2,3},{3,2},{4,5},{5,4},{6,7},{7,6},{8,9},{9,8},{10,11... | collective-permute-start | bytes 147464 | tf_op jit(solution)/shard_map/ppermute | solution.py:304
  43.9 9.6 %collective-permute-start.11 = (f32[32,384]{1,0:T(8,128)S(1)}, f32[32,384]{1,0:T(8,128)S(1)}, u32[]{:S(2)}, u32[]{:S(2)}) collective-permute-start(f32[32,384]{1,0:T(8,128)S(1)} %get-tuple-element.26), channel_id=1, source_target_pairs={{0,2},{1,3},{2,0},{3,1},{4,6},{5,7},{6,4},{7,5},{8,10},{9,11},{10,... | collective-permute-start | bytes 147464 | tf_op jit(solution)/shard_map/ppermute | solution.py:304
  46.1 7.9 %collective-permute-start.12 = (f32[32,384]{1,0:T(8,128)S(1)}, f32[32,384]{1,0:T(8,128)S(1)}, u32[]{:S(2)}, u32[]{:S(2)}) collective-permute-start(f32[32,384]{1,0:T(8,128)S(1)} %get-tuple-element.27), channel_id=1, source_target_pairs={{0,3},{1,2},{2,1},{3,0},{4,7},{5,6},{6,5},{7,4},{8,11},{9,10},{10,... | collective-permute-start | bytes 147464 | tf_op jit(solution)/shard_map/ppermute | solution.py:304
  48.2 5.7 %copy-start.2 = (bf16[144,2560]{1,0:T(8,128)(2,1)S(1)}, bf16[144,2560]{1,0:T(8,128)(2,1)}, u32[]{:S(2)}) copy-start(bf16[144,2560]{1,0:T(8,128)(2,1)} %x_ref.3) | copy-start | bytes 2211844
  54.8 1.5 %collective-permute-start.13 = (f32[16,2560]{1,0:T(8,128)S(1)}, f32[16,2560]{1,0:T(8,128)S(1)}, u32[]{:S(2)}, u32[]{:S(2)}) collective-permute-start(f32[16,2560]{1,0:T(8,128)S(1)} %get-tuple-element.32), channel_id=1, source_target_pairs={{0,4},{4,0},{8,12},{12,8},{16,20},{20,16},{24,28},{28,24},{1,5},{5... | collective-permute-start | bytes 491528 | tf_op jit(solution)/shard_map/ppermute | solution.py:248
  56.8 9.2 %collective-permute-start.14 = (f32[16,640]{1,0:T(8,128)S(1)}, f32[16,640]{1,0:T(8,128)S(1)}, u32[]{:S(2)}, u32[]{:S(2)}) collective-permute-start(f32[16,640]{1,0:T(8,128)S(1)} %get-tuple-element.34), channel_id=1, source_target_pairs={{0,1},{1,0},{2,3},{3,2},{4,5},{5,4},{6,7},{7,6},{8,9},{9,8},{10,11... | collective-permute-start | bytes 122888 | tf_op jit(solution)/shard_map/ppermute | solution.py:334
  60.6 9.5 %collective-permute-start.15 = (f32[16,640]{1,0:T(8,128)S(1)}, f32[16,640]{1,0:T(8,128)S(1)}, u32[]{:S(2)}, u32[]{:S(2)}) collective-permute-start(f32[16,640]{1,0:T(8,128)S(1)} %get-tuple-element.35), channel_id=1, source_target_pairs={{0,2},{1,3},{2,0},{3,1},{4,6},{5,7},{6,4},{7,5},{8,10},{9,11},{10,... | collective-permute-start | bytes 122888 | tf_op jit(solution)/shard_map/ppermute | solution.py:334
  62.8 7.9 %collective-permute-start.16 = (f32[16,640]{1,0:T(8,128)S(1)}, f32[16,640]{1,0:T(8,128)S(1)}, u32[]{:S(2)}, u32[]{:S(2)}) collective-permute-start(f32[16,640]{1,0:T(8,128)S(1)} %get-tuple-element.36), channel_id=1, source_target_pairs={{0,3},{1,2},{2,1},{3,0},{4,7},{5,6},{6,5},{7,4},{8,11},{9,10},{10,... | collective-permute-start | bytes 122888 | tf_op jit(solution)/shard_map/ppermute | solution.py:334
  70.7 5.0 %collective-permute-start.19 = (f32[16,640]{1,0:T(8,128)S(1)}, f32[16,640]{1,0:T(8,128)S(1)}, u32[]{:S(2)}, u32[]{:S(2)}) collective-permute-start(f32[16,640]{1,0:T(8,128)S(1)} %add_add_fusion.1), channel_id=1, source_target_pairs={{0,24},{4,28},{8,16},{12,20},{16,8},{20,12},{24,0},{28,4},{1,25},{... | collective-permute-start | bytes 122888 | tf_op jit(solution)/shard_map/ppermute | solution.py:248
  72.7 4.0 %collective-permute-start.18 = (f32[16,640]{1,0:T(8,128)S(1)}, f32[16,640]{1,0:T(8,128)S(1)}, u32[]{:S(2)}, u32[]{:S(2)}) collective-permute-start(f32[16,640]{1,0:T(8,128)S(1)} %add_add_fusion.1), channel_id=1, source_target_pairs={{0,16},{4,20},{8,24},{12,28},{16,0},{20,4},{24,8},{28,12},{1,17},{... | collective-permute-start | bytes 122888 | tf_op jit(solution)/shard_map/ppermute | solution.py:248
  73.7 4.0 %collective-permute-start.17 = (f32[16,640]{1,0:T(8,128)S(1)}, f32[16,640]{1,0:T(8,128)S(1)}, u32[]{:S(2)}, u32[]{:S(2)}) collective-permute-start(f32[16,640]{1,0:T(8,128)S(1)} %add_add_fusion.1), channel_id=1, source_target_pairs={{0,8},{4,12},{8,0},{12,4},{16,24},{20,28},{24,16},{28,20},{1,9},{5... | collective-permute-start | bytes 122888 | tf_op jit(solution)/shard_map/ppermute | solution.py:248
  77.8 5.9 %collective-permute-start.22 = (f32[16,640]{1,0:T(8,128)S(1)}, f32[16,640]{1,0:T(8,128)S(1)}, u32[]{:S(2)}, u32[]{:S(2)}) collective-permute-start(f32[16,640]{1,0:T(8,128)S(1)} %add_add_fusion.a0), channel_id=1, source_target_pairs={{0,3},{1,2},{2,1},{3,0},{4,7},{5,6},{6,5},{7,4},{8,11},{9,10},{10,... | collective-permute-start | bytes 122888 | tf_op jit(solution)/shard_map/ppermute | solution.py:248
  79.9 5.6 %collective-permute-start.21 = (f32[16,640]{1,0:T(8,128)S(1)}, f32[16,640]{1,0:T(8,128)S(1)}, u32[]{:S(2)}, u32[]{:S(2)}) collective-permute-start(f32[16,640]{1,0:T(8,128)S(1)} %add_add_fusion.a0), channel_id=1, source_target_pairs={{0,2},{1,3},{2,0},{3,1},{4,6},{5,7},{6,4},{7,5},{8,10},{9,11},{10,... | collective-permute-start | bytes 122888 | tf_op jit(solution)/shard_map/ppermute | solution.py:248
  82.8 4.0 %collective-permute-start.20 = (f32[16,640]{1,0:T(8,128)S(1)}, f32[16,640]{1,0:T(8,128)S(1)}, u32[]{:S(2)}, u32[]{:S(2)}) collective-permute-start(f32[16,640]{1,0:T(8,128)S(1)} %add_add_fusion.a0), channel_id=1, source_target_pairs={{0,1},{1,0},{2,3},{3,2},{4,5},{5,4},{6,7},{7,6},{8,9},{9,8},{10,11... | collective-permute-start | bytes 122888 | tf_op jit(solution)/shard_map/ppermute | solution.py:248
  83.3 7.0 %collective-permute-start.23 = (f32[16,640]{1,0:T(8,128)S(1)}, f32[16,640]{1,0:T(8,128)S(1)}, u32[]{:S(2)}, u32[]{:S(2)}) collective-permute-start(f32[16,640]{1,0:T(8,128)S(1)} %add_add_fusion.a0), channel_id=1, source_target_pairs={{0,4},{4,0},{8,12},{12,8},{16,20},{20,16},{24,28},{28,24},{1,5},{5... | collective-permute-start | bytes 122888 | tf_op jit(solution)/shard_map/ppermute | solution.py:248
  83.6 6.7 %collective-permute-start.26 = (f32[16,640]{1,0:T(8,128)S(1)}, f32[16,640]{1,0:T(8,128)S(1)}, u32[]{:S(2)}, u32[]{:S(2)}) collective-permute-start(f32[16,640]{1,0:T(8,128)S(1)} %collective-permute-done.22.a3), channel_id=1, source_target_pairs={{0,4},{4,0},{8,12},{12,8},{16,20},{20,16},{24,28},{28,24},{1,5},{5... | collective-permute-start | bytes 122888 | tf_op jit(solution)/shard_map/ppermute | solution.py:248
  85.6 4.8 %collective-permute-start.25 = (f32[16,640]{1,0:T(8,128)S(1)}, f32[16,640]{1,0:T(8,128)S(1)}, u32[]{:S(2)}, u32[]{:S(2)}) collective-permute-start(f32[16,640]{1,0:T(8,128)S(1)} %collective-permute-done.21.a2), channel_id=1, source_target_pairs={{0,4},{4,0},{8,12},{12,8},{16,20},{20,16},{24,28},{28,24},{1,5},{5... | collective-permute-start | bytes 122888 | tf_op jit(solution)/shard_map/ppermute | solution.py:248
  86.8 3.5 %collective-permute-start.24 = (f32[16,640]{1,0:T(8,128)S(1)}, f32[16,640]{1,0:T(8,128)S(1)}, u32[]{:S(2)}, u32[]{:S(2)}) collective-permute-start(f32[16,640]{1,0:T(8,128)S(1)} %collective-permute-done.20.a1), channel_id=1, source_target_pairs={{0,4},{4,0},{8,12},{12,8},{16,20},{20,16},{24,28},{28,24},{1,5},{5... | collective-permute-start | bytes 122888 | tf_op jit(solution)/shard_map/ppermute | solution.py:248
  92.9 1.8 %copy-start.3 = (bf16[576,2560]{1,0:T(8,128)(2,1)S(1)}, bf16[576,2560]{1,0:T(8,128)(2,1)}, u32[]{:S(2)}) copy-start(bf16[576,2560]{1,0:T(8,128)(2,1)} %all-gather.2.cloned.1.call-done.x_ref) | copy-start | bytes 8847364
Sparse Core Ops, SparseCore 0:
  9.6 73.1 all-gather.1

commit v2 on v1

v2 whole, which is shorter than its diff:
```python
import functools
import jax
import jax.numpy as jnp
from jax import lax
from jax.experimental import pallas as pl
from jax.experimental.pallas import tpu as pltpu
from jax.sharding import PartitionSpec as P

contract_first = (((0,), (0,)), ((), ()))
contract_last = (((1,), (1,)), ((), ()))
column_block = 8
bf16, f32 = jnp.bfloat16, jnp.float32
MIB = 1 << 20


def plain_body(activations, out_grad, error_state, right_factor):
    highest = lax.Precision.HIGHEST
    errors = error_state[0]
    rows_here = right_factor.shape[0]
    factor_full = lax.all_gather(right_factor, "tensor", axis=0, tiled=True)
    grad = lax.dot_general(
        out_grad,
        lax.all_gather(activations, "tensor", axis=0, tiled=True),
        contract_first,
        preferred_element_type=f32,
    )
    corrected = grad + errors.astype(f32)
    p_local = jnp.dot(corrected, factor_full, precision=highest)
    p_total = lax.psum(p_local.astype(bf16), "dp").astype(f32)
    p_basis = jnp.zeros_like(p_total)
    for block_index in range(p_total.shape[1] // column_block):
        first = block_index * column_block
        columns = p_total[:, first : first + column_block]
        coeffs, block_gram = lax.psum(
            (
                jnp.dot(p_basis.T, columns, precision=highest),
                jnp.dot(columns.T, columns, precision=highest),
            ),
            "tensor",
        )
        remainder = columns - jnp.dot(p_basis, coeffs, precision=highest)
        residual_gram = block_gram - jnp.dot(coeffs.T, coeffs, precision=highest)
        lower_factor = jnp.linalg.cholesky(residual_gram)
        orthonormal = lax.linalg.triangular_solve(
            lower_factor, remainder, left_side=False, lower=True, transpose_a=True
        )
        p_basis = p_basis.at[:, first : first + column_block].set(orthonormal)
    replicas = lax.axis_size("dp")
    term = lax.dot_general(corrected, p_basis, contract_first, precision=highest)
    summed = lax.psum(term, ("dp", "tensor")) / replicas
    new_error = (corrected - jnp.dot(p_basis, summed.T, precision=highest)).astype(bf16)
    new_factor = lax.dynamic_slice_in_dim(
        summed, lax.axis_index("tensor") * rows_here, rows_here, 0
    )
    return (new_error[None], new_factor)


def dot(a, b, dims=None, precision=None):
    if dims is None:
        dims = (((1,), (0,)), ((), ()))
    return lax.dot_general(a, b, dims, precision=precision, preferred_element_type=f32)


def split(v):
    high = v.astype(bf16)
    return high, (v - high.astype(f32)).astype(bf16)


def call(kernel, outs, *args, scratch=(), grid=None, in_specs=None, out_specs=None, vmem=8, flops=0, moved=0):
    vmem_spec = pl.BlockSpec(memory_space=pltpu.VMEM)
    if in_specs is None:
        in_specs = [
            pl.BlockSpec(memory_space=pltpu.SMEM) if a.dtype == jnp.int32 else vmem_spec
            for a in args
        ]
    if out_specs is None:
        out_specs = [vmem_spec] * len(outs)
    extra = {} if grid is None else {"grid": grid}
    size = sum(a.size * a.dtype.itemsize for a in args) + sum(
        o.size * o.dtype.itemsize for o in outs
    )
    result = pl.pallas_call(
        kernel,
        out_shape=list(outs),
        in_specs=in_specs,
        out_specs=out_specs,
        scratch_shapes=list(scratch),
        compiler_params=pltpu.CompilerParams(vmem_limit_bytes=vmem * MIB),
        cost_estimate=pl.CostEstimate(flops=flops, bytes_accessed=size, transcendentals=0),
        **extra,
        name=kernel.__name__ if hasattr(kernel, "__name__") else kernel.func.__name__,
    )(*args)
    return result


def like(shape, dtype):
    return jax.ShapeDtypeStruct(shape, dtype)


def project(place, own, n1, n2, n3, x_ref, q_ref, y_ref):
    t = place[0]
    for k, part in enumerate((own, n1, n2, n3)):
        q_ref[t ^ k] = part[...]
    parts, _, width = q_ref.shape
    total = dot(q_ref[0], x_ref[:, :width], contract_last)
    for k in range(1, parts):
        total += dot(q_ref[k], x_ref[:, k * width : (k + 1) * width], contract_last)
    y_ref[...] = total


def error_left(q_ref, e_ref, out_ref):
    term = dot(q_ref[0], e_ref[...], contract_last)

    @pl.when(pl.program_id(0) == 0)
    def _():
        out_ref[...] = term

    @pl.when(pl.program_id(0) > 0)
    def _():
        out_ref[...] += term


def left_factor(place, eq_ref, own, n1, n2, n3, dy_ref, out_ref, y4):
    t = place[0]
    for k, part in enumerate((own, n1, n2, n3)):
        y4[t ^ k] = part[...]
    parts, rank, tokens = y4.shape
    total = eq_ref[...]
    for s in range(parts):
        both = jnp.concatenate(split(y4[s]), axis=0)
        term = dot(both, dy_ref[s * tokens : (s + 1) * tokens, :])
        total += term[:rank] + term[rank:]
    out_ref[...] = total.astype(bf16)


def first_partner(t):
    return jnp.where((t == 1) | (t == 2), 2, 1)


def weigh(place, own, n1, n2, n3, dy_ref, p_ref, gram_ref, near_ref, far_ref, held):
    t = place[0]
    p = (own[...].astype(f32) + n1[...].astype(f32)) + (n2[...].astype(f32) + n3[...].astype(f32))
    p = p.astype(bf16)
    p_ref[...] = p
    parts, _, tokens = held.shape
    gram_ref[...] = dot(p, p, contract_last)
    for s in range(parts):
        held[s] = dot(p, dy_ref[s * tokens : (s + 1) * tokens, :], contract_last)
    step = first_partner(t)
    near_ref[0] = held[t]
    near_ref[1] = held[t ^ step]
    far_ref[0] = held[t ^ 3]
    far_ref[1] = held[t ^ 3 ^ step]


def error_right(p_ref, e_ref, out_ref):
    out_ref[...] = dot(p_ref[...], e_ref[...])


def right_term(place, near_ref, got_ref, te_ref, x_own, x_first, keep_ref, send_ref, held):
    core = place[1]
    rank = te_ref.shape[0]
    total = te_ref[...]
    for k, x_ref in enumerate((x_own, x_first)):
        both = jnp.concatenate(split(near_ref[k] + got_ref[k]), axis=0)
        term = dot(both, x_ref[...])
        total += term[:rank] + term[rank:]
    held[0] = total[: rank // 2]
    held[1] = total[rank // 2 :]
    keep_ref[...] = held[core]
    send_ref[...] = held[1 - core]


def cut(place, keep, got, o0, o1, o2, o3, held):
    chip = place[2]
    total = keep[...] + got[...]
    width = held.shape[2]
    for s in range(held.shape[0]):
        held[s] = total[:, s * width : (s + 1) * width]
    for k, out in enumerate((o0, o1, o2, o3)):
        out[...] = held[chip ^ k]


def pack(a, b, c, d, gram_ref, out_ref):
    half, width = a.shape
    rank = 2 * half
    out_ref[...] = jnp.zeros_like(out_ref)
    out_ref[:, :width] = (a[...] + b[...]) + (c[...] + d[...])
    out_ref[:, width : width + rank] = gram_ref[:half, :]
    out_ref[:, width + 128 : width + 128 + rank] = gram_ref[half:, :]


def unpack(a, b, c, d, out_ref, gram_ref):
    half, width = out_ref.shape
    rank = 2 * half
    total = (a[...] + b[...]) + (c[...] + d[...])
    out_ref[...] = total[:, :width]
    gram_ref[:half, :] = total[:, width : width + rank]
    gram_ref[half:, :] = total[:, width + 128 : width + 128 + rank]


def invert_cholesky(g_ref, out_ref):
    n = g_ref.shape[0]
    rows = lax.broadcasted_iota(jnp.int32, (n, n), 0)
    cols = lax.broadcasted_iota(jnp.int32, (n, n), 1)
    a = g_ref[...]
    inverse = jnp.where(rows == cols, 1.0, 0.0).astype(f32)
    for j in range(n):
        column = jnp.sum(jnp.where(cols == j, a, 0.0), axis=1, keepdims=True)
        pivot = column[j : j + 1, :]
        factor = jnp.where(rows[:, :1] > j, column / pivot, 0.0)
        a = a - factor * a[j : j + 1, :]
        inverse = inverse - factor * inverse[j : j + 1, :]
    diagonal = jnp.sum(jnp.where(rows == cols, a, 0.0), axis=1, keepdims=True)
    out_ref[...] = inverse * lax.rsqrt(diagonal)


def arrange(place, dy_any, dy_ref, main_ref, rest_ref, held, sem):
    copy = pltpu.make_async_copy(dy_any, dy_ref, sem)
    copy.start()
    t = place[0]
    step = first_partner(t)
    tokens = rest_ref.shape[1]
    copy.wait()
    for k, source in enumerate((t, t ^ step, t ^ 3 ^ step, t ^ 3)):
        held[k * tokens : (k + 1) * tokens, :] = dy_ref[pl.ds(pl.multiple_of(source * tokens, tokens), tokens), :]
    main = main_ref.shape[1]
    main_ref[...] = held[:main, :].T
    rest_ref[...] = held[main:, :].T


def accumulate(first, main_ref, e_any, x_own, x_first, x_second, acc_ref, x_ref, e_ref, e_sem, sems):
    width = acc_ref.shape[1]
    tokens = x_own.shape[0]
    copies = [pltpu.make_async_copy(e_any.at[:, pl.ds(first, width)], e_ref, e_sem)]
    for k, source in enumerate((x_own, x_first, x_second)):
        copies.append(
            pltpu.make_async_copy(source.at[:, pl.ds(first, width)], x_ref.at[pl.ds(k * tokens, tokens), :], sems.at[k])
        )
    for copy in copies:
        copy.start()
    for copy in copies:
        copy.wait()
    step, block = 640, 432
    for c in range(0, width, step):
        cols = slice(c, c + step)
        for r in range(0, acc_ref.shape[0], block):
            at = slice(r, r + block)
            acc_ref[at, cols] = dot(main_ref[at, :], x_ref[:, cols]) + e_ref[at, cols].astype(f32)


def rebuild(replicas, place, linv, p_ref, rest_ref, a0, a1, a2, a3, b0, b1, b2, b3, acc_0, acc_1, outer, inner,
            new_ref, out_any, held, nf4, left_ref, buffer, staged, sems, out_sems):
    rows = inner.shape[0]
    t, core, chip = place[0], place[1], place[2]
    is_inner = (t == 1) | (t == 2)

    def fetch(source):
        return pltpu.make_async_copy(source, buffer.at[pl.ds(0, rows), :], sems.at[0])

    @pl.when(is_inner)
    def _():
        fetch(inner).start()

    @pl.when(jnp.logical_not(is_inner))
    def _():
        fetch(outer).start()

    for k, (a, b) in enumerate(((a0, b0), (a1, b1), (a2, b2), (a3, b3))):
        held[chip ^ k, core] = a[...]
        held[chip ^ k, 1 - core] = b[...]
    highest = lax.Precision.HIGHEST
    parts, _, half, width = held.shape
    rank = 2 * half
    base = rows
    scaled = linv[...] * (1.0 / replicas)
    for s in range(parts):
        nf = dot(scaled, held[s].reshape(rank, width), precision=highest)
        nf4[s] = nf
        high, low = split(nf)
        at = slice(s * width, (s + 1) * width)
        buffer[base : base + rank, at] = high
        buffer[base + rank : base + 2 * rank, at] = high
        buffer[base + 2 * rank :, at] = low
    new_ref[...] = nf4[t]
    basis = dot(linv[...], p_ref[...].astype(f32), precision=highest)
    high, low = split(-basis)
    left_ref[:, :base] = rest_ref[...]
    left_ref[:, base:] = jnp.concatenate((high, low, high), axis=0).T
    fetch(inner).wait()
    width = staged.shape[2]
    count = acc_0.shape[1] // width

    def put(i, slot):
        return pltpu.make_async_copy(staged.at[slot], out_any.at[:, pl.ds(pl.multiple_of(i * width, width), width)], out_sems.at[slot])

    for part, acc_ref in enumerate((acc_0, acc_1)):

        @pl.loop(0, count)
        def _(c):
            i = part * count + c
            slot = lax.rem(i, 2)

            @pl.when(i >= 2)
            def _():
                put(i - 2, slot).wait()

            here = pl.ds(pl.multiple_of(c * width, width), width)
            cols = pl.ds(pl.multiple_of(i * width, width), width)
            block = 432
            for r in range(0, acc_ref.shape[0], block):
                at = slice(r, r + block)
                total = acc_ref[at, here] + dot(left_ref[at, :], buffer[:, cols])
                staged[slot, at, :] = total.astype(bf16)
            put(i, slot).start()

    for i in (2 * count - 2, 2 * count - 1):
        put(i, i % 2).wait()


def after(value, *others):
    return lax.optimization_barrier((value, *others))[0]


def partners(value, axis, size, by):
    return [lax.ppermute(value, axis, [(i, i ^ k) for i in range(size)]) for k in by]


def body(activations, out_grad, error_state, right_factor):
    errors = error_state[0]
    n_dp, n_t = lax.axis_size("dp"), lax.axis_size("tensor")
    rows, rank = right_factor.shape
    tokens, features = activations.shape
    all_tokens, hidden = out_grad.shape
    half = rank // 2
    t, d = lax.axis_index("tensor"), lax.axis_index("dp")
    place = jnp.stack([t, d & 1, d >> 1]).astype(jnp.int32)
    along_t = functools.partial(partners, axis="tensor", size=n_t, by=(1, 2, 3))
    along_xy = functools.partial(partners, axis="dp", size=n_dp, by=(2, 4, 6))

    anywhere = pl.BlockSpec(memory_space=pl.ANY)
    vmem_spec = pl.BlockSpec(memory_space=pltpu.VMEM)
    smem_spec = pl.BlockSpec(memory_space=pltpu.SMEM)
    hbm_spec = pl.BlockSpec(memory_space=pltpu.HBM)

    def move(value, perm, *when):
        return lax.ppermute(after(value, *when), "tensor", perm)

    q_own = right_factor.T.astype(bf16)
    q_parts = along_t(q_own)

    main = 3 * tokens
    grads, main_t, rest_t = call(
        arrange,
        [like((all_tokens, hidden), bf16), like((hidden, main), bf16), like((hidden, tokens), bf16)],
        place, out_grad,
        in_specs=[smem_spec, hbm_spec],
        scratch=[pltpu.VMEM((all_tokens, hidden), bf16), pltpu.SemaphoreType.DMA(())],
        vmem=50,
    )
    q_parts, _ = lax.optimization_barrier((q_parts, main_t))
    q_full, y_own = call(
        project,
        [like((n_t, rank, rows), bf16), like((rank, tokens), f32)],
        place, q_own, *q_parts, activations,
    )
    y_parts = along_t(y_own)
    (eq,) = call(
        error_left,
        [like((rank, hidden), f32)],
        q_full, errors,
        grid=(n_t,),
        in_specs=[
            pl.BlockSpec((1, rank, rows), lambda k: (k, 0, 0)),
            pl.BlockSpec((hidden, rows), lambda k: (0, k)),
        ],
        out_specs=[pl.BlockSpec((rank, hidden), lambda k: (0, 0))],
        vmem=50,
    )
    y_parts[0] = after(y_parts[0], eq)
    x_first = move(activations, [(0, 2), (2, 3), (3, 1), (1, 0)], *y_parts)
    (p_local,) = call(
        left_factor,
        [like((rank, hidden), bf16)],
        place, eq, y_own, *y_parts, grads,
        scratch=[pltpu.VMEM((n_t, rank, tokens), f32)],
    )
    (p_other,) = partners(p_local, "dp", n_dp, (1,))
    p_chip = (p_local.astype(f32) + p_other.astype(f32)).astype(bf16)
    p_parts = along_xy(p_chip)
    p_parts[0] = after(p_parts[0], x_first)
    p_total, gram, near_w, far_w = call(
        weigh,
        [like((rank, hidden), bf16), like((rank, rank), f32), like((2, rank, tokens), f32), like((2, rank, tokens), f32)],
        place, p_chip, *p_parts, grads,
        scratch=[pltpu.VMEM((n_t, rank, tokens), f32)],
    )
    (got_w,) = partners(far_w, "tensor", n_t, (3,))
    (te,) = call(
        error_right,
        [like((rank, features), f32)],
        p_total, errors,
        grid=(n_t,),
        in_specs=[
            pl.BlockSpec((rank, hidden), lambda k: (0, 0)),
            pl.BlockSpec((hidden, rows), lambda k: (0, k)),
        ],
        out_specs=[pl.BlockSpec((rank, rows), lambda k: (0, k))],
        vmem=50,
    )
    got_w = after(got_w, te)
    keep, given = call(
        right_term,
        [like((half, features), f32), like((half, features), f32)],
        place, near_w, got_w, te, activations, x_first,
        scratch=[pltpu.VMEM((2, half, features), f32)],
    )
    x_second = move(activations, [(0, 1), (1, 3), (3, 2), (2, 0)], got_w)
    (got,) = partners(given, "dp", n_dp, (1,))
    parts = call(
        cut,
        [like((half, rows), f32)] * 4,
        place, keep, got,
        scratch=[pltpu.VMEM((n_t, half, rows), f32)],
    )
    arrived = [
        lax.ppermute(m, "dp", [(i, i ^ (2 * k)) for i in range(n_dp)])
        for k, m in enumerate(parts)
        if k
    ]
    accs = []
    for first in (0, features // 2):
        accs += call(
            functools.partial(accumulate, first),
            [like((hidden, features // 2), f32)],
            main_t, errors, activations, x_first, x_second,
            in_specs=[vmem_spec, hbm_spec] + [anywhere] * 3,
            scratch=[
                pltpu.VMEM((main, features // 2), bf16),
                pltpu.VMEM((hidden, features // 2), bf16),
                pltpu.SemaphoreType.DMA(()),
                pltpu.SemaphoreType.DMA((3,)),
            ],
            vmem=12,
        )
    (mine,) = call(pack, [like((half, rows + 256), f32)], parts[0], *arrived, gram)
    mine = after(mine, x_second)
    z1, z2, z3 = along_t(mine)
    to_outer_3 = move(x_first, [(1, 0), (2, 3)], z1, z2, z3)
    to_inner_3 = move(activations, [(1, 2), (2, 1)], z1, z2, z3)
    mine, gram = call(unpack, [like((half, rows), f32), like((rank, rank), f32)], mine, z1, z2, z3)
    (linv,) = call(invert_cholesky, [like((rank, rank), f32)], gram)
    near = [mine] + along_xy(mine)
    near[1] = after(near[1], linv)
    far = [partners(v, "dp", n_dp, (1,))[0] for v in near]
    new_factor, new_error = call(
        functools.partial(rebuild, n_dp),
        [like((rank, rows), f32), like((hidden, features), bf16)],
        place, linv, p_total, rest_t, *near, *far, *accs, to_outer_3, to_inner_3,
        in_specs=[smem_spec] + [vmem_spec] * 13 + [anywhere] * 2,
        out_specs=[vmem_spec, anywhere],
        scratch=[
            pltpu.VMEM((4, 2, half, rows), f32),
            pltpu.VMEM((n_t, rank, rows), f32),
            pltpu.VMEM((hidden, tokens + 3 * rank), bf16),
            pltpu.VMEM((tokens + 3 * rank, features), bf16),
            pltpu.VMEM((2, hidden, 640), bf16),
            pltpu.SemaphoreType.DMA((1,)),
            pltpu.SemaphoreType.DMA((2,)),
        ],
    )
    return (new_error[None], new_factor.T)


def solution(mesh):
    placed = (
        P(("dp", "tensor"), None),
        P("dp", "tensor"),
        P("dp", "tensor", None),
        P("tensor", None),
    )
    fits = mesh.shape["dp"] == 8 and mesh.shape["tensor"] == 4
    return jax.shard_map(
        body if fits else plain_body,
        mesh=mesh,
        in_specs=placed,
        out_specs=(P("dp", "tensor", None), P("tensor", None)),
        check_vma=False,
    )
```

time: 114 us -> 104 us (0.912)
  the two profiles are of different devices: /device:TPU:0 before, /device:TPU:11 now
where the time goes in v2:
time: 104 us; the launch traced here: 103 us
  starting transfers between devices  41.7 us (40%)
  Pallas kernels  37.9 us (36%)
  waiting for transfers between devices  20.2 us (19%)
  local copies, waits for them, and re-layouts  1.44 us (1%)
  between operations  1.08 us (1%)
  other arithmetic  1.07 us (1%)
    pallas_call x14, Pallas kernels, call(): pl.pallas_call(kernel, out_shape=list(outs), in_specs=in_specs, out_specs...  37.9 us
    ppermute x22, starting transfers between devices, partners(): lax.ppermute(value, axis, [(i, i ^ k) for i in range(size)])  32.7 us
    ppermute x4, waiting for transfers between devices, move(): return lax.ppermute(after(value, *when), 'tensor', perm)  10.6 us
    ppermute x22, waiting for transfers between devices, partners(): lax.ppermute(value, axis, [(i, i ^ k) for i in range(size)])  6.99 us
    ppermute x4, starting transfers between devices, move(): return lax.ppermute(after(value, *when), 'tensor', perm)  6.23 us
    ppermute x3, starting transfers between devices, body(): lax.ppermute(m, 'dp', [(i, i ^ 2 * k) for i in range(n_dp)])  2.71 us
    ppermute x3, waiting for transfers between devices, body(): lax.ppermute(m, 'dp', [(i, i ^ 2 * k) for i in range(n_dp)])  2.61 us
  transfers between devices with their start and end apart: 29, of which 12 were waited for; matrix products, arithmetic and copies ran while one was open for 0% of the time, Pallas kernels for 27%

profile of v2, /device:TPU:11, one launch (start us, length us, event | category | flops | bytes accessed | tf_op | source)
XLA Modules:
  0.0 103.3 jit_solution(16095837647697455051)
XLA Ops:
  0.6 0.0 copy-start.1
  0.6 1.0 convert_bitcast_fusion.own
  1.6 1.3 %collective-permute-start.2 = (bf16[32,640]{1,0:T(8,128)(2,1)S(1)}, bf16[32,640]{1,0:T(8,128)(2,1)S(1)}, u32[]{:S(2)}, u32[]{:S(2)}) collective-permute-start(bf16[32,640]{1,0:T(8,128)(2,1)S(1)} %convert_bitcast_fusion.own), channel_id=1, source_target_pairs={{0,3},{1,2},{2,1},{3,0},{4,7},{5,6},{6,5},{7,4},{8,11},{9,10},{10,... | collective-permute-start | bytes 122888 | tf_op jit(solution)/shard_map/ppermute | solution.py:326
  2.9 1.1 %collective-permute-start.1 = (bf16[32,640]{1,0:T(8,128)(2,1)S(1)}, bf16[32,640]{1,0:T(8,128)(2,1)S(1)}, u32[]{:S(2)}, u32[]{:S(2)}) collective-permute-start(bf16[32,640]{1,0:T(8,128)(2,1)S(1)} %convert_bitcast_fusion.own), channel_id=1, source_target_pairs={{0,2},{1,3},{2,0},{3,1},{4,6},{5,7},{6,4},{7,5},{8,10},{9,11},{10,... | collective-permute-start | bytes 122888 | tf_op jit(solution)/shard_map/ppermute | solution.py:326
  4.0 1.1 %collective-permute-start = (bf16[32,640]{1,0:T(8,128)(2,1)S(1)}, bf16[32,640]{1,0:T(8,128)(2,1)S(1)}, u32[]{:S(2)}, u32[]{:S(2)}) collective-permute-start(bf16[32,640]{1,0:T(8,128)(2,1)S(1)} %convert_bitcast_fusion.own), channel_id=1, source_target_pairs={{0,1},{1,0},{2,3},{3,2},{4,5},{5,4},{6,7},{7,6},{8,9},{9,8},{10,11... | collective-permute-start | bytes 122888 | tf_op jit(solution)/shard_map/ppermute | solution.py:326
  5.1 0.1 pad_add_fusion.place
  5.2 3.4 %arrange.1 = (bf16[576,1728]{1,0:T(8,128)(2,1)}, bf16[1728,432]{1,0:T(8,128)(2,1)S(1)}, bf16[1728,144]{1,0:T(8,128)(2,1)S(1)}) custom-call(s32[3]{0:T(128)S(1)} %pad_add_fusion.place, bf16[576,1728]{1,0:T(8,128)(2,1)} %dy_any.1), custom_call_target="tpu_custom_call" | custom-call | bytes 5971980 | tf_op jit(solution)/shard_map/arrange/pallas_call | solution.py:82
  8.6 0.0 collective-permute-done.2.n3
  8.7 0.0 collective-permute-done.1.n2
  8.7 0.0 copy-start
  8.7 1.4 %copy-done = bf16[144,2560]{1,0:T(8,128)(2,1)S(1)} copy-done((bf16[144,2560]{1,0:T(8,128)(2,1)S(1)}, bf16[144,2560]{1,0:T(8,128)(2,1)}, u32[]{:S(2)}) %copy-start) | copy-done | bytes 737304
  10.1 0.9 project.1
  11.0 0.4 collective-permute-start.3
  11.4 2.3 %collective-permute-start.5 = (f32[32,144]{1,0:T(8,128)S(1)}, f32[32,144]{1,0:T(8,128)S(1)}, u32[]{:S(2)}, u32[]{:S(2)}) collective-permute-start(f32[32,144]{1,0:T(8,128)S(1)} %get-tuple-element.38.own), channel_id=1, source_target_pairs={{0,3},{1,2},{2,1},{3,0},{4,7},{5,6},{6,5},{7,4},{8,11},{9,10},{10,... | collective-permute-start | bytes 55304 | tf_op jit(solution)/shard_map/ppermute | solution.py:326
  13.7 0.9 collective-permute-start.4
  14.6 7.0 %error_left.1.eq_ref = f32[32,1728]{1,0:T(8,128)S(1)} custom-call(bf16[4,32,640]{2,1,0:T(8,128)(2,1)S(1)} %get-tuple-element.37.q_ref, bf16[1728,2560]{1,0:T(8,128)(2,1)} %bitcast.8), custom_call_target="tpu_custom_call" | custom-call | bytes 9232384 | tf_op jit(solution)/shard_map/error_left/pallas_call | solution.py:82
  21.6 0.0 collective-permute-done.3.n1
  21.6 0.0 collective-permute-done.5.n3
  21.6 0.3 collective-permute-start.8
  22.0 1.0 left_factor.1
  22.9 2.4 %collective-permute-start.6 = (bf16[32,1728]{1,0:T(8,128)(2,1)S(1)}, bf16[32,1728]{1,0:T(8,128)(2,1)S(1)}, u32[]{:S(2)}, u32[]{:S(2)}) collective-permute-start(bf16[32,1728]{1,0:T(8,128)(2,1)S(1)} %left_factor.1), channel_id=1, source_target_pairs={{0,4},{4,0},{8,12},{12,8},{16,20},{20,16},{24,28},{28,24},{1,5},{5... | collective-permute-start | bytes 331784 | tf_op jit(solution)/shard_map/ppermute | solution.py:326
  25.3 1.0 collective-permute-done.6
  26.3 0.3 collective-permute-start.7
  26.7 2.2 %collective-permute-start.10 = (bf16[32,1728]{1,0:T(8,128)(2,1)S(1)}, bf16[32,1728]{1,0:T(8,128)(2,1)S(1)}, u32[]{:S(2)}, u32[]{:S(2)}) collective-permute-start(bf16[32,1728]{1,0:T(8,128)(2,1)S(1)} %add_convert_fusion.own), channel_id=1, source_target_pairs={{0,24},{4,28},{8,16},{12,20},{16,8},{20,12},{24,0},{28,4},{1,25},{... | collective-permute-start | bytes 331784 | tf_op jit(solution)/shard_map/ppermute | solution.py:326
  28.8 0.2 collective-permute-start.9
  29.0 1.7 %collective-permute-done.7.n1 = bf16[32,1728]{1,0:T(8,128)(2,1)S(1)} collective-permute-done((bf16[32,1728]{1,0:T(8,128)(2,1)S(1)}, bf16[32,1728]{1,0:T(8,128)(2,1)S(1)}, u32[]{:S(2)}, u32[]{:S(2)}) %collective-permute-start.7) | collective-permute-done | bytes 110624 | tf_op jit(solution)/shard_map/ppermute | solution.py:326
  30.8 7.7 %collective-permute-done.8.x_first = bf16[144,2560]{1,0:T(8,128)(2,1)S(1)} collective-permute-done((bf16[144,2560]{1,0:T(8,128)(2,1)S(1)}, bf16[144,2560]{1,0:T(8,128)(2,1)S(1)}, u32[]{:S(2)}, u32[]{:S(2)}) %collective-permute-start.8) | collective-permute-done | bytes 737312 | tf_op jit(solution)/shard_map/ppermute | solution.py:347
  38.5 1.3 %weigh.1 = (bf16[32,1728]{1,0:T(8,128)(2,1)S(1)}, f32[32,32]{1,0:T(8,128)S(1)}, f32[2,32,144]{2,1,0:T(8,128)S(1)}, f32[2,32,144]{2,1,0:T(8,128)S(1)}) custom-call(s32[3]{0:T(128)S(1)} %pad_add_fusion.place, bf16[32,1728]{1,0:T(8,128)(2,1)S(1)} %add_convert_fusion.own, bf16[32,1728]{1,0:T(8,128)(2,1)S(1)} %collective-permute-done.7.n1, ...), custom_call_target="tpu_custom_call" | custom-call | bytes 2621452 | tf_op jit(solution)/shard_map/weigh/pallas_call | solution.py:82
  39.7 1.3 %collective-permute-start.11 = (f32[2,32,144]{2,1,0:T(8,128)S(1)}, f32[2,32,144]{2,1,0:T(8,128)S(1)}, u32[]{:S(2)}, u32[]{:S(2)}) collective-permute-start(f32[2,32,144]{2,1,0:T(8,128)S(1)} %get-tuple-element.44), channel_id=1, source_target_pairs={{0,3},{1,2},{2,1},{3,0},{4,7},{5,6},{6,5},{7,4},{8,11},{9,10},{10,... | collective-permute-start | bytes 110600 | tf_op jit(solution)/shard_map/ppermute | solution.py:326
  41.0 5.2 %error_right.1.te_ref = f32[32,2560]{1,0:T(8,128)S(1)} custom-call(bf16[32,1728]{1,0:T(8,128)(2,1)S(1)} %get-tuple-element.45.p_ref, bf16[1728,2560]{1,0:T(8,128)(2,1)} %bitcast.9), custom_call_target="tpu_custom_call" | custom-call | bytes 9285632 | tf_op jit(solution)/shard_map/error_right/pallas_call | solution.py:82
  46.2 0.3 collective-permute-start.16
  46.5 0.9 right_term.1
  47.4 3.6 %collective-permute-start.12 = (f32[16,2560]{1,0:T(8,128)S(1)}, f32[16,2560]{1,0:T(8,128)S(1)}, u32[]{:S(2)}, u32[]{:S(2)}) collective-permute-start(f32[16,2560]{1,0:T(8,128)S(1)} %get-tuple-element.48), channel_id=1, source_target_pairs={{0,4},{4,0},{8,12},{12,8},{16,20},{20,16},{24,28},{28,24},{1,5},{5... | collective-permute-start | bytes 491528 | tf_op jit(solution)/shard_map/ppermute | solution.py:326
  51.1 1.0 collective-permute-done.12.got
  52.1 0.6 cut.1
  52.7 0.3 collective-permute-start.13
  53.0 1.2 %collective-permute-start.14 = (f32[16,640]{1,0:T(8,128)S(1)}, f32[16,640]{1,0:T(8,128)S(1)}, u32[]{:S(2)}, u32[]{:S(2)}) collective-permute-start(f32[16,640]{1,0:T(8,128)S(1)} %get-tuple-element.51), channel_id=1, source_target_pairs={{0,16},{4,20},{8,24},{12,28},{16,0},{20,4},{24,8},{28,12},{1,17},{... | collective-permute-start | bytes 122888 | tf_op jit(solution)/shard_map/ppermute | solution.py:427
  54.2 1.1 %collective-permute-start.15 = (f32[16,640]{1,0:T(8,128)S(1)}, f32[16,640]{1,0:T(8,128)S(1)}, u32[]{:S(2)}, u32[]{:S(2)}) collective-permute-start(f32[16,640]{1,0:T(8,128)S(1)} %get-tuple-element.52), channel_id=1, source_target_pairs={{0,24},{4,28},{8,16},{12,20},{16,8},{20,12},{24,0},{28,4},{1,25},{... | collective-permute-start | bytes 122888 | tf_op jit(solution)/shard_map/ppermute | solution.py:427
  55.4 0.5 collective-permute-done.13.b
  55.9 0.3 collective-permute-done.14.c
  56.1 1.9 %collective-permute-done.15.d = f32[16,640]{1,0:T(8,128)S(1)} collective-permute-done((f32[16,640]{1,0:T(8,128)S(1)}, f32[16,640]{1,0:T(8,128)S(1)}, u32[]{:S(2)}, u32[]{:S(2)}) %collective-permute-start.15) | collective-permute-done | bytes 40992 | tf_op jit(solution)/shard_map/ppermute | solution.py:427
  58.0 2.9 %collective-permute-done.16.x_second = bf16[144,2560]{1,0:T(8,128)(2,1)S(1)} collective-permute-done((bf16[144,2560]{1,0:T(8,128)(2,1)S(1)}, bf16[144,2560]{1,0:T(8,128)(2,1)S(1)}, u32[]{:S(2)}, u32[]{:S(2)}) %collective-permute-start.16) | collective-permute-done | bytes 737312 | tf_op jit(solution)/shard_map/ppermute | solution.py:347
  60.9 0.3 collective-permute-start.19
  61.2 2.7 %collective-permute-start.18 = (f32[16,896]{1,0:T(8,128)S(1)}, f32[16,896]{1,0:T(8,128)S(1)}, u32[]{:S(2)}, u32[]{:S(2)}) collective-permute-start(f32[16,896]{1,0:T(8,128)S(1)} %pack.1.a), channel_id=1, source_target_pairs={{0,2},{1,3},{2,0},{3,1},{4,6},{5,7},{6,4},{7,5},{8,10},{9,11},{10,... | collective-permute-start | bytes 172040 | tf_op jit(solution)/shard_map/ppermute | solution.py:326
  63.9 1.0 collective-permute-done.19.d
  64.9 1.3 %collective-permute-done.18.c = f32[16,896]{1,0:T(8,128)S(1)} collective-permute-done((f32[16,896]{1,0:T(8,128)S(1)}, f32[16,896]{1,0:T(8,128)S(1)}, u32[]{:S(2)}, u32[]{:S(2)}) %collective-permute-start.18) | collective-permute-done | bytes 57376 | tf_op jit(solution)/shard_map/ppermute | solution.py:326
  66.2 0.8 collective-permute-done.17.b
  67.0 3.1 %collective-permute-start.27 = (bf16[144,2560]{1,0:T(8,128)(2,1)S(1)}, bf16[144,2560]{1,0:T(8,128)(2,1)S(1)}, u32[]{:S(2)}, u32[]{:S(2)}) collective-permute-start(bf16[144,2560]{1,0:T(8,128)(2,1)S(1)} %collective-permute-done.8.x_first), channel_id=1, source_target_pairs={{1,0},{2,3},{5,4},{6,7},{9,8},{10,11},{13,12},{14,15},{17,16},{18,... | collective-permute-start | bytes 2211848 | tf_op jit(solution)/shard_map/ppermute | solution.py:347
  70.1 2.5 %collective-permute-start.28 = (bf16[144,2560]{1,0:T(8,128)(2,1)S(1)}, bf16[144,2560]{1,0:T(8,128)(2,1)S(1)}, u32[]{:S(2)}, u32[]{:S(2)}) collective-permute-start(bf16[144,2560]{1,0:T(8,128)(2,1)S(1)} %copy-done.1), channel_id=1, source_target_pairs={{1,2},{2,1},{5,6},{6,5},{9,10},{10,9},{13,14},{14,13},{17,18},{18,... | collective-permute-start | bytes 2211848 | tf_op jit(solution)/shard_map/ppermute | solution.py:347
  72.6 0.3 collective-permute-start.20
  72.9 2.2 %collective-permute-start.22 = (f32[16,640]{1,0:T(8,128)S(1)}, f32[16,640]{1,0:T(8,128)S(1)}, u32[]{:S(2)}, u32[]{:S(2)}) collective-permute-start(f32[16,640]{1,0:T(8,128)S(1)} %get-tuple-element.58.a0), channel_id=1, source_target_pairs={{0,24},{4,28},{8,16},{12,20},{16,8},{20,12},{24,0},{28,4},{1,25},{... | collective-permute-start | bytes 122888 | tf_op jit(solution)/shard_map/ppermute | solution.py:326
  75.1 0.2 collective-permute-start.21
  75.3 0.2 collective-permute-done.20.a1
  75.5 9.2 %collective-permute-start.23 = (f32[16,640]{1,0:T(8,128)S(1)}, f32[16,640]{1,0:T(8,128)S(1)}, u32[]{:S(2)}, u32[]{:S(2)}) collective-permute-start(f32[16,640]{1,0:T(8,128)S(1)} %get-tuple-element.58.a0), channel_id=1, source_target_pairs={{0,4},{4,0},{8,12},{12,8},{16,20},{20,16},{24,28},{28,24},{1,5},{5... | collective-permute-start | bytes 122888 | tf_op jit(solution)/shard_map/ppermute | solution.py:326
  84.7 2.8 %invert_cholesky.1.linv = f32[32,32]{1,0:T(8,128)S(1)} custom-call(f32[32,32]{1,0:T(8,128)S(1)} %get-tuple-element.56.g_ref), custom_call_target="tpu_custom_call" | custom-call | bytes 8192 | tf_op jit(solution)/shard_map/invert_cholesky/pallas_call | solution.py:82
  87.6 0.0 collective-permute-done.22.a3
  87.6 0.1 collective-permute-start.26
  87.7 0.0 collective-permute-done.21.a2
  87.7 0.5 collective-permute-start.25
  88.2 0.0 collective-permute-done.23.b0
  88.2 0.1 collective-permute-start.24
  88.3 3.3 %accumulate.3.acc_1 = f32[1728,1280]{1,0:T(8,128)S(1)} custom-call(bf16[1728,432]{1,0:T(8,128)(2,1)S(1)} %get-tuple-element.33.main_ref, bf16[1728,2560]{1,0:T(8,128)(2,1)S(1)} %bitcast.12, bf16[144,2560]{1,0:T(8,128)(2,1)S(1)} %copy-done.1, bf16[144,2560]{1,0:T(8,128)(2,1)S(1)} %collective-permute-done.8.x_first, ...), custom_call_target="tpu_custom_call" | custom-call | bytes 21399552 | tf_op jit(solution)/shard_map/accumulate/pallas_call | solution.py:82
  91.6 3.3 %accumulate.2.acc_0 = f32[1728,1280]{1,0:T(8,128)S(1)} custom-call(bf16[1728,432]{1,0:T(8,128)(2,1)S(1)} %get-tuple-element.33.main_ref, bf16[1728,2560]{1,0:T(8,128)(2,1)S(1)} %bitcast.13, bf16[144,2560]{1,0:T(8,128)(2,1)S(1)} %copy-done.1, bf16[144,2560]{1,0:T(8,128)(2,1)S(1)} %collective-permute-done.8.x_first, ...), custom_call_target="tpu_custom_call" | custom-call | bytes 21399552 | tf_op jit(solution)/shard_map/accumulate/pallas_call | solution.py:82
  95.0 8.1 %rebuild.1 = (f32[32,640]{1,0:T(8,128)}, bf16[1728,2560]{1,0:T(8,128)(2,1)}) custom-call(s32[3]{0:T(128)S(1)} %pad_add_fusion.place, f32[32,32]{1,0:T(8,128)S(1)} %invert_cholesky.1.linv, bf16[32,1728]{1,0:T(8,128)(2,1)S(1)} %get-tuple-element.45.p_ref, bf16[1728,144]{1,0:T(8,128)(2,1)S(1)} %copy-done.4, f32[16,640]{1,0:T(8,128)S(1)} %get-tuple-element.58.a0, ...), custom_call_target="tpu_custom_call" | custom-call | bytes 29038604 | tf_op jit(solution)/shard_map/rebuild/pallas_call | solution.py:82
  (28 shorter events, 0.1 us)
Async XLA Ops:
  0.6 21.0 %copy-start.1 = (bf16[144,2560]{1,0:T(8,128)(2,1)S(1)}, bf16[144,2560]{1,0:T(8,128)(2,1)}, u32[]{:S(2)}) copy-start(bf16[144,2560]{1,0:T(8,128)(2,1)} %x_own.5) | copy-start | bytes 2211844
  1.6 7.0 %collective-permute-start.2 = (bf16[32,640]{1,0:T(8,128)(2,1)S(1)}, bf16[32,640]{1,0:T(8,128)(2,1)S(1)}, u32[]{:S(2)}, u32[]{:S(2)}) collective-permute-start(bf16[32,640]{1,0:T(8,128)(2,1)S(1)} %convert_bitcast_fusion.own), channel_id=1, source_target_pairs={{0,3},{1,2},{2,1},{3,0},{4,7},{5,6},{6,5},{7,4},{8,11},{9,10},{10,... | collective-permute-start | bytes 122888 | tf_op jit(solution)/shard_map/ppermute | solution.py:326
  2.9 5.8 %collective-permute-start.1 = (bf16[32,640]{1,0:T(8,128)(2,1)S(1)}, bf16[32,640]{1,0:T(8,128)(2,1)S(1)}, u32[]{:S(2)}, u32[]{:S(2)}) collective-permute-start(bf16[32,640]{1,0:T(8,128)(2,1)S(1)} %convert_bitcast_fusion.own), channel_id=1, source_target_pairs={{0,2},{1,3},{2,0},{3,1},{4,6},{5,7},{6,4},{7,5},{8,10},{9,11},{10,... | collective-permute-start | bytes 122888 | tf_op jit(solution)/shard_map/ppermute | solution.py:326
  4.0 4.7 %collective-permute-start = (bf16[32,640]{1,0:T(8,128)(2,1)S(1)}, bf16[32,640]{1,0:T(8,128)(2,1)S(1)}, u32[]{:S(2)}, u32[]{:S(2)}) collective-permute-start(bf16[32,640]{1,0:T(8,128)(2,1)S(1)} %convert_bitcast_fusion.own), channel_id=1, source_target_pairs={{0,1},{1,0},{2,3},{3,2},{4,5},{5,4},{6,7},{7,6},{8,9},{9,8},{10,11... | collective-permute-start | bytes 122888 | tf_op jit(solution)/shard_map/ppermute | solution.py:326
  8.6 5.9 %copy-start.3 = (bf16[1728,144]{1,0:T(8,128)(2,1)}, bf16[1728,144]{1,0:T(8,128)(2,1)S(1)}, u32[]{:S(2)}) copy-start(bf16[1728,144]{1,0:T(8,128)(2,1)S(1)} %get-tuple-element.57.rest_ref) | copy-start | bytes 1492996
  8.7 1.4 %copy-start = (bf16[144,2560]{1,0:T(8,128)(2,1)S(1)}, bf16[144,2560]{1,0:T(8,128)(2,1)}, u32[]{:S(2)}) copy-start(bf16[144,2560]{1,0:T(8,128)(2,1)} %x_own.5) | copy-start | bytes 2211844
  10.1 11.9 %copy-start.2 = (bf16[576,1728]{1,0:T(8,128)(2,1)S(1)}, bf16[576,1728]{1,0:T(8,128)(2,1)}, u32[]{:S(2)}) copy-start(bf16[576,1728]{1,0:T(8,128)(2,1)} %get-tuple-element.40.dy_ref) | copy-start | bytes 5971972
  11.0 10.6 %collective-permute-start.3 = (f32[32,144]{1,0:T(8,128)S(1)}, f32[32,144]{1,0:T(8,128)S(1)}, u32[]{:S(2)}, u32[]{:S(2)}) collective-permute-start(f32[32,144]{1,0:T(8,128)S(1)} %get-tuple-element.38.own), channel_id=1, source_target_pairs={{0,1},{1,0},{2,3},{3,2},{4,5},{5,4},{6,7},{7,6},{8,9},{9,8},{10,11... | collective-permute-start | bytes 55304 | tf_op jit(solution)/shard_map/ppermute | solution.py:326
  11.4 10.2 %collective-permute-start.5 = (f32[32,144]{1,0:T(8,128)S(1)}, f32[32,144]{1,0:T(8,128)S(1)}, u32[]{:S(2)}, u32[]{:S(2)}) collective-permute-start(f32[32,144]{1,0:T(8,128)S(1)} %get-tuple-element.38.own), channel_id=1, source_target_pairs={{0,3},{1,2},{2,1},{3,0},{4,7},{5,6},{6,5},{7,4},{8,11},{9,10},{10,... | collective-permute-start | bytes 55304 | tf_op jit(solution)/shard_map/ppermute | solution.py:326
  13.7 7.9 %collective-permute-start.4 = (f32[32,144]{1,0:T(8,128)S(1)}, f32[32,144]{1,0:T(8,128)S(1)}, u32[]{:S(2)}, u32[]{:S(2)}) collective-permute-start(f32[32,144]{1,0:T(8,128)S(1)} %get-tuple-element.38.own), channel_id=1, source_target_pairs={{0,2},{1,3},{2,0},{3,1},{4,6},{5,7},{6,4},{7,5},{8,10},{9,11},{10,... | collective-permute-start | bytes 55304 | tf_op jit(solution)/shard_map/ppermute | solution.py:326
  14.6 73.7 %slice-start = ((s8[8847360]{0:T(1024)(128)(4,1)}), s8[4194304]{0:T(1024)(128)(4,1)S(1)}, s32[]{:S(2)}) async-start(s8[8847360]{0:T(1024)(128)(4,1)} %bitcast.10), calls=%async_computation | async-start | bytes 8388608
  14.6 73.7 %slice-start.1 = ((s8[8847360]{0:T(1024)(128)(4,1)}), s8[4194304]{0:T(1024)(128)(4,1)S(1)}, s32[]{:S(2)}) async-start(s8[8847360]{0:T(1024)(128)(4,1)} %bitcast.10), calls=%async_computation.1 | async-start | bytes 8388608
  21.6 16.9 %collective-permute-start.8 = (bf16[144,2560]{1,0:T(8,128)(2,1)S(1)}, bf16[144,2560]{1,0:T(8,128)(2,1)S(1)}, u32[]{:S(2)}, u32[]{:S(2)}) collective-permute-start(bf16[144,2560]{1,0:T(8,128)(2,1)S(1)} %copy-done.1), channel_id=1, source_target_pairs={{0,2},{2,3},{3,1},{1,0},{4,6},{6,7},{7,5},{5,4},{8,10},{10,11},{11... | collective-permute-start | bytes 2211848 | tf_op jit(solution)/shard_map/ppermute | solution.py:347
  22.9 3.4 %collective-permute-start.6 = (bf16[32,1728]{1,0:T(8,128)(2,1)S(1)}, bf16[32,1728]{1,0:T(8,128)(2,1)S(1)}, u32[]{:S(2)}, u32[]{:S(2)}) collective-permute-start(bf16[32,1728]{1,0:T(8,128)(2,1)S(1)} %left_factor.1), channel_id=1, source_target_pairs={{0,4},{4,0},{8,12},{12,8},{16,20},{20,16},{24,28},{28,24},{1,5},{5... | collective-permute-start | bytes 331784 | tf_op jit(solution)/shard_map/ppermute | solution.py:326
  26.3 4.4 %collective-permute-start.7 = (bf16[32,1728]{1,0:T(8,128)(2,1)S(1)}, bf16[32,1728]{1,0:T(8,128)(2,1)S(1)}, u32[]{:S(2)}, u32[]{:S(2)}) collective-permute-start(bf16[32,1728]{1,0:T(8,128)(2,1)S(1)} %add_convert_fusion.own), channel_id=1, source_target_pairs={{0,8},{4,12},{8,0},{12,4},{16,24},{20,28},{24,16},{28,20},{1,9},{5... | collective-permute-start | bytes 331784 | tf_op jit(solution)/shard_map/ppermute | solution.py:326
  26.7 11.8 %collective-permute-start.10 = (bf16[32,1728]{1,0:T(8,128)(2,1)S(1)}, bf16[32,1728]{1,0:T(8,128)(2,1)S(1)}, u32[]{:S(2)}, u32[]{:S(2)}) collective-permute-start(bf16[32,1728]{1,0:T(8,128)(2,1)S(1)} %add_convert_fusion.own), channel_id=1, source_target_pairs={{0,24},{4,28},{8,16},{12,20},{16,8},{20,12},{24,0},{28,4},{1,25},{... | collective-permute-start | bytes 331784 | tf_op jit(solution)/shard_map/ppermute | solution.py:326
  28.8 9.7 %collective-permute-start.9 = (bf16[32,1728]{1,0:T(8,128)(2,1)S(1)}, bf16[32,1728]{1,0:T(8,128)(2,1)S(1)}, u32[]{:S(2)}, u32[]{:S(2)}) collective-permute-start(bf16[32,1728]{1,0:T(8,128)(2,1)S(1)} %add_convert_fusion.own), channel_id=1, source_target_pairs={{0,16},{4,20},{8,24},{12,28},{16,0},{20,4},{24,8},{28,12},{1,17},{... | collective-permute-start | bytes 331784 | tf_op jit(solution)/shard_map/ppermute | solution.py:326
  39.7 6.5 %collective-permute-start.11 = (f32[2,32,144]{2,1,0:T(8,128)S(1)}, f32[2,32,144]{2,1,0:T(8,128)S(1)}, u32[]{:S(2)}, u32[]{:S(2)}) collective-permute-start(f32[2,32,144]{2,1,0:T(8,128)S(1)} %get-tuple-element.44), channel_id=1, source_target_pairs={{0,3},{1,2},{2,1},{3,0},{4,7},{5,6},{6,5},{7,4},{8,11},{9,10},{10,... | collective-permute-start | bytes 110600 | tf_op jit(solution)/shard_map/ppermute | solution.py:326
  41.0 47.3 %slice-start.2 = ((s8[8847360]{0:T(1024)(128)(4,1)}), s8[458752]{0:T(1024)(128)(4,1)S(1)}, s32[]{:S(2)}) async-start(s8[8847360]{0:T(1024)(128)(4,1)} %bitcast.10), calls=%async_computation.2 | async-start | bytes 917504
  46.2 14.7 %collective-permute-start.16 = (bf16[144,2560]{1,0:T(8,128)(2,1)S(1)}, bf16[144,2560]{1,0:T(8,128)(2,1)S(1)}, u32[]{:S(2)}, u32[]{:S(2)}) collective-permute-start(bf16[144,2560]{1,0:T(8,128)(2,1)S(1)} %copy-done.1), channel_id=1, source_target_pairs={{0,1},{1,3},{3,2},{2,0},{4,5},{5,7},{7,6},{6,4},{8,9},{9,11},{11,1... | collective-permute-start | bytes 2211848 | tf_op jit(solution)/shard_map/ppermute | solution.py:347
  47.4 4.6 %collective-permute-start.12 = (f32[16,2560]{1,0:T(8,128)S(1)}, f32[16,2560]{1,0:T(8,128)S(1)}, u32[]{:S(2)}, u32[]{:S(2)}) collective-permute-start(f32[16,2560]{1,0:T(8,128)S(1)} %get-tuple-element.48), channel_id=1, source_target_pairs={{0,4},{4,0},{8,12},{12,8},{16,20},{20,16},{24,28},{28,24},{1,5},{5... | collective-permute-start | bytes 491528 | tf_op jit(solution)/shard_map/ppermute | solution.py:326
  52.7 3.2 %collective-permute-start.13 = (f32[16,640]{1,0:T(8,128)S(1)}, f32[16,640]{1,0:T(8,128)S(1)}, u32[]{:S(2)}, u32[]{:S(2)}) collective-permute-start(f32[16,640]{1,0:T(8,128)S(1)} %get-tuple-element.50), channel_id=1, source_target_pairs={{0,8},{4,12},{8,0},{12,4},{16,24},{20,28},{24,16},{28,20},{1,9},{5... | collective-permute-start | bytes 122888 | tf_op jit(solution)/shard_map/ppermute | solution.py:427
  53.0 3.1 %collective-permute-start.14 = (f32[16,640]{1,0:T(8,128)S(1)}, f32[16,640]{1,0:T(8,128)S(1)}, u32[]{:S(2)}, u32[]{:S(2)}) collective-permute-start(f32[16,640]{1,0:T(8,128)S(1)} %get-tuple-element.51), channel_id=1, source_target_pairs={{0,16},{4,20},{8,24},{12,28},{16,0},{20,4},{24,8},{28,12},{1,17},{... | collective-permute-start | bytes 122888 | tf_op jit(solution)/shard_map/ppermute | solution.py:427
  54.2 3.8 %collective-permute-start.15 = (f32[16,640]{1,0:T(8,128)S(1)}, f32[16,640]{1,0:T(8,128)S(1)}, u32[]{:S(2)}, u32[]{:S(2)}) collective-permute-start(f32[16,640]{1,0:T(8,128)S(1)} %get-tuple-element.52), channel_id=1, source_target_pairs={{0,24},{4,28},{8,16},{12,20},{16,8},{20,12},{24,0},{28,4},{1,25},{... | collective-permute-start | bytes 122888 | tf_op jit(solution)/shard_map/ppermute | solution.py:427
  60.9 4.0 %collective-permute-start.19 = (f32[16,896]{1,0:T(8,128)S(1)}, f32[16,896]{1,0:T(8,128)S(1)}, u32[]{:S(2)}, u32[]{:S(2)}) collective-permute-start(f32[16,896]{1,0:T(8,128)S(1)} %pack.1.a), channel_id=1, source_target_pairs={{0,3},{1,2},{2,1},{3,0},{4,7},{5,6},{6,5},{7,4},{8,11},{9,10},{10,... | collective-permute-start | bytes 172040 | tf_op jit(solution)/shard_map/ppermute | solution.py:326
  61.2 5.0 %collective-permute-start.18 = (f32[16,896]{1,0:T(8,128)S(1)}, f32[16,896]{1,0:T(8,128)S(1)}, u32[]{:S(2)}, u32[]{:S(2)}) collective-permute-start(f32[16,896]{1,0:T(8,128)S(1)} %pack.1.a), channel_id=1, source_target_pairs={{0,2},{1,3},{2,0},{3,1},{4,6},{5,7},{6,4},{7,5},{8,10},{9,11},{10,... | collective-permute-start | bytes 172040 | tf_op jit(solution)/shard_map/ppermute | solution.py:326
  63.9 3.0 %collective-permute-start.17 = (f32[16,896]{1,0:T(8,128)S(1)}, f32[16,896]{1,0:T(8,128)S(1)}, u32[]{:S(2)}, u32[]{:S(2)}) collective-permute-start(f32[16,896]{1,0:T(8,128)S(1)} %pack.1.a), channel_id=1, source_target_pairs={{0,1},{1,0},{2,3},{3,2},{4,5},{5,4},{6,7},{7,6},{8,9},{9,8},{10,11... | collective-permute-start | bytes 172040 | tf_op jit(solution)/shard_map/ppermute | solution.py:326
  67.0 28.0 %collective-permute-start.27 = (bf16[144,2560]{1,0:T(8,128)(2,1)S(1)}, bf16[144,2560]{1,0:T(8,128)(2,1)S(1)}, u32[]{:S(2)}, u32[]{:S(2)}) collective-permute-start(bf16[144,2560]{1,0:T(8,128)(2,1)S(1)} %collective-permute-done.8.x_first), channel_id=1, source_target_pairs={{1,0},{2,3},{5,4},{6,7},{9,8},{10,11},{13,12},{14,15},{17,16},{18,... | collective-permute-start | bytes 2211848 | tf_op jit(solution)/shard_map/ppermute | solution.py:347
  70.1 24.9 %collective-permute-start.28 = (bf16[144,2560]{1,0:T(8,128)(2,1)S(1)}, bf16[144,2560]{1,0:T(8,128)(2,1)S(1)}, u32[]{:S(2)}, u32[]{:S(2)}) collective-permute-start(bf16[144,2560]{1,0:T(8,128)(2,1)S(1)} %copy-done.1), channel_id=1, source_target_pairs={{1,2},{2,1},{5,6},{6,5},{9,10},{10,9},{13,14},{14,13},{17,18},{18,... | collective-permute-start | bytes 2211848 | tf_op jit(solution)/shard_map/ppermute | solution.py:347
  72.6 2.9 %collective-permute-start.20 = (f32[16,640]{1,0:T(8,128)S(1)}, f32[16,640]{1,0:T(8,128)S(1)}, u32[]{:S(2)}, u32[]{:S(2)}) collective-permute-start(f32[16,640]{1,0:T(8,128)S(1)} %get-tuple-element.58.a0), channel_id=1, source_target_pairs={{0,8},{4,12},{8,0},{12,4},{16,24},{20,28},{24,16},{28,20},{1,9},{5... | collective-permute-start | bytes 122888 | tf_op jit(solution)/shard_map/ppermute | solution.py:326
  72.9 14.7 %collective-permute-start.22 = (f32[16,640]{1,0:T(8,128)S(1)}, f32[16,640]{1,0:T(8,128)S(1)}, u32[]{:S(2)}, u32[]{:S(2)}) collective-permute-start(f32[16,640]{1,0:T(8,128)S(1)} %get-tuple-element.58.a0), channel_id=1, source_target_pairs={{0,24},{4,28},{8,16},{12,20},{16,8},{20,12},{24,0},{28,4},{1,25},{... | collective-permute-start | bytes 122888 | tf_op jit(solution)/shard_map/ppermute | solution.py:326
  75.1 12.6 %collective-permute-start.21 = (f32[16,640]{1,0:T(8,128)S(1)}, f32[16,640]{1,0:T(8,128)S(1)}, u32[]{:S(2)}, u32[]{:S(2)}) collective-permute-start(f32[16,640]{1,0:T(8,128)S(1)} %get-tuple-element.58.a0), channel_id=1, source_target_pairs={{0,16},{4,20},{8,24},{12,28},{16,0},{20,4},{24,8},{28,12},{1,17},{... | collective-permute-start | bytes 122888 | tf_op jit(solution)/shard_map/ppermute | solution.py:326
  75.5 12.7 %collective-permute-start.23 = (f32[16,640]{1,0:T(8,128)S(1)}, f32[16,640]{1,0:T(8,128)S(1)}, u32[]{:S(2)}, u32[]{:S(2)}) collective-permute-start(f32[16,640]{1,0:T(8,128)S(1)} %get-tuple-element.58.a0), channel_id=1, source_target_pairs={{0,4},{4,0},{8,12},{12,8},{16,20},{20,16},{24,28},{28,24},{1,5},{5... | collective-permute-start | bytes 122888 | tf_op jit(solution)/shard_map/ppermute | solution.py:326
  87.6 7.4 %collective-permute-start.26 = (f32[16,640]{1,0:T(8,128)S(1)}, f32[16,640]{1,0:T(8,128)S(1)}, u32[]{:S(2)}, u32[]{:S(2)}) collective-permute-start(f32[16,640]{1,0:T(8,128)S(1)} %collective-permute-done.22.a3), channel_id=1, source_target_pairs={{0,4},{4,0},{8,12},{12,8},{16,20},{20,16},{24,28},{28,24},{1,5},{5... | collective-permute-start | bytes 122888 | tf_op jit(solution)/shard_map/ppermute | solution.py:326
  87.7 7.3 %collective-permute-start.25 = (f32[16,640]{1,0:T(8,128)S(1)}, f32[16,640]{1,0:T(8,128)S(1)}, u32[]{:S(2)}, u32[]{:S(2)}) collective-permute-start(f32[16,640]{1,0:T(8,128)S(1)} %collective-permute-done.21.a2), channel_id=1, source_target_pairs={{0,4},{4,0},{8,12},{12,8},{16,20},{20,16},{24,28},{28,24},{1,5},{5... | collective-permute-start | bytes 122888 | tf_op jit(solution)/shard_map/ppermute | solution.py:326
  88.2 6.8 %collective-permute-start.24 = (f32[16,640]{1,0:T(8,128)S(1)}, f32[16,640]{1,0:T(8,128)S(1)}, u32[]{:S(2)}, u32[]{:S(2)}) collective-permute-start(f32[16,640]{1,0:T(8,128)S(1)} %collective-permute-done.20.a1), channel_id=1, source_target_pairs={{0,4},{4,0},{8,12},{12,8},{16,20},{20,16},{24,28},{28,24},{1,5},{5... | collective-permute-start | bytes 122888 | tf_op jit(solution)/shard_map/ppermute | solution.py:326
  91.6 3.4 %copy-start.4 = (bf16[1728,144]{1,0:T(8,128)(2,1)S(1)}, bf16[1728,144]{1,0:T(8,128)(2,1)}, u32[]{:S(2)}) copy-start(bf16[1728,144]{1,0:T(8,128)(2,1)} %copy-done.3) | copy-start | bytes 1492996

commit v3 on v2

--- a/solution.py
+++ b/solution.py
@@ -11,6 +11,7 @@
 column_block = 8
 bf16, f32 = jnp.bfloat16, jnp.float32
 MIB = 1 << 20
+KA, KB, KP = 1_000_000_000, 5_500_000_000, 3_500_000_000
 
 
 def plain_body(activations, out_grad, error_state, right_factor):
@@ -108,16 +109,25 @@
     y_ref[...] = total
 
 
-def error_left(q_ref, e_ref, out_ref):
-    term = dot(q_ref[0], e_ref[...], contract_last)
-
-    @pl.when(pl.program_id(0) == 0)
-    def _():
-        out_ref[...] = term
-
-    @pl.when(pl.program_id(0) > 0)
-    def _():
-        out_ref[...] += term
+def error_left(q_ref, e_any, out_ref, e_0, e_1, sems):
+    parts, _, width = q_ref.shape
+    half = parts // 2
+
+    def place_of(k):
+        return (e_0, e_1)[k // half].at[:, pl.ds(k % half * width, width)]
+
+    def load(k):
+        return pltpu.make_async_copy(e_any.at[:, pl.ds(k * width, width)], place_of(k), sems.at[k])
+
+    for k in range(parts):
+        load(k).start()
+    for k in range(parts):
+        load(k).wait()
+        term = dot(q_ref[k], place_of(k)[...], contract_last)
+        if k:
+            out_ref[...] += term
+        else:
+            out_ref[...] = term
 
 
 def left_factor(place, eq_ref, own, n1, n2, n3, dy_ref, out_ref, y4):
@@ -153,8 +163,12 @@
     far_ref[1] = held[t ^ 3 ^ step]
 
 
-def error_right(p_ref, e_ref, out_ref):
-    out_ref[...] = dot(p_ref[...], e_ref[...])
+def error_right(p_ref, e_0, e_1, out_ref):
+    width = e_0.shape[1]
+    step = 640
+    for k, e_ref in enumerate((e_0, e_1)):
+        for c in range(0, width, step):
+            out_ref[:, k * width + c : k * width + c + step] = dot(p_ref[...], e_ref[:, c : c + step])
 
 
 def right_term(place, near_ref, got_ref, te_ref, x_own, x_first, keep_ref, send_ref, held):
@@ -215,13 +229,10 @@
     out_ref[...] = inverse * lax.rsqrt(diagonal)
 
 
-def arrange(place, dy_any, dy_ref, main_ref, rest_ref, held, sem):
-    copy = pltpu.make_async_copy(dy_any, dy_ref, sem)
-    copy.start()
+def arrange(place, dy_ref, main_ref, rest_ref, held):
     t = place[0]
     step = first_partner(t)
     tokens = rest_ref.shape[1]
-    copy.wait()
     for k, source in enumerate((t, t ^ step, t ^ 3 ^ step, t ^ 3)):
         held[k * tokens : (k + 1) * tokens, :] = dy_ref[pl.ds(pl.multiple_of(source * tokens, tokens), tokens), :]
     main = main_ref.shape[1]
@@ -229,14 +240,13 @@
     rest_ref[...] = held[main:, :].T
 
 
-def accumulate(first, main_ref, e_any, x_own, x_first, x_second, acc_ref, x_ref, e_ref, e_sem, sems):
+def accumulate(first, main_ref, e_ref, x_own, x_first, x_second, acc_ref, x_ref, sems):
     width = acc_ref.shape[1]
-    tokens = x_own.shape[0]
-    copies = [pltpu.make_async_copy(e_any.at[:, pl.ds(first, width)], e_ref, e_sem)]
-    for k, source in enumerate((x_own, x_first, x_second)):
-        copies.append(
-            pltpu.make_async_copy(source.at[:, pl.ds(first, width)], x_ref.at[pl.ds(k * tokens, tokens), :], sems.at[k])
-        )
+    rows = x_own.shape[0]
+    copies = [
+        pltpu.make_async_copy(source.at[:, pl.ds(first, width)], x_ref.at[pl.ds(k * rows, rows), :], sems.at[k])
+        for k, source in enumerate((x_own, x_first, x_second))
+    ]
     for copy in copies:
         copy.start()
     for copy in copies:
@@ -249,44 +259,48 @@
             acc_ref[at, cols] = dot(main_ref[at, :], x_ref[:, cols]) + e_ref[at, cols].astype(f32)
 
 
-def rebuild(replicas, place, linv, p_ref, rest_ref, a0, a1, a2, a3, b0, b1, b2, b3, acc_0, acc_1, outer, inner,
-            new_ref, out_any, held, nf4, left_ref, buffer, staged, sems, out_sems):
-    rows = inner.shape[0]
+def finish(replicas, place, linv, p_ref, rest_ref, a0, a1, a2, a3, b0, b1, b2, b3, new_ref, left_ref, right_ref, held, nf4):
     t, core, chip = place[0], place[1], place[2]
-    is_inner = (t == 1) | (t == 2)
-
-    def fetch(source):
-        return pltpu.make_async_copy(source, buffer.at[pl.ds(0, rows), :], sems.at[0])
-
-    @pl.when(is_inner)
-    def _():
-        fetch(inner).start()
-
-    @pl.when(jnp.logical_not(is_inner))
-    def _():
-        fetch(outer).start()
-
     for k, (a, b) in enumerate(((a0, b0), (a1, b1), (a2, b2), (a3, b3))):
         held[chip ^ k, core] = a[...]
         held[chip ^ k, 1 - core] = b[...]
     highest = lax.Precision.HIGHEST
     parts, _, half, width = held.shape
     rank = 2 * half
-    base = rows
     scaled = linv[...] * (1.0 / replicas)
     for s in range(parts):
         nf = dot(scaled, held[s].reshape(rank, width), precision=highest)
         nf4[s] = nf
         high, low = split(nf)
         at = slice(s * width, (s + 1) * width)
-        buffer[base : base + rank, at] = high
-        buffer[base + rank : base + 2 * rank, at] = high
-        buffer[base + 2 * rank :, at] = low
+        right_ref[:rank, at] = high
+        right_ref[rank : 2 * rank, at] = high
+        right_ref[2 * rank :, at] = low
     new_ref[...] = nf4[t]
     basis = dot(linv[...], p_ref[...].astype(f32), precision=highest)
     high, low = split(-basis)
+    base = rest_ref.shape[1]
     left_ref[:, :base] = rest_ref[...]
     left_ref[:, base:] = jnp.concatenate((high, low, high), axis=0).T
+
+
+def rebuild(place, left_ref, right_ref, acc_0, acc_1, outer, inner, out_any, buffer, staged, sems, out_sems):
+    t = place[0]
+    rows = inner.shape[0]
+    is_inner = (t == 1) | (t == 2)
+
+    def fetch(source):
+        return pltpu.make_async_copy(source, buffer.at[pl.ds(0, rows), :], sems.at[0])
+
+    @pl.when(is_inner)
+    def _():
+        fetch(inner).start()
+
+    @pl.when(jnp.logical_not(is_inner))
+    def _():
+        fetch(outer).start()
+
+    buffer[rows:, :] = right_ref[...]
     fetch(inner).wait()
     width = staged.shape[2]
     count = acc_0.shape[1] // width
@@ -350,39 +364,35 @@
     q_parts = along_t(q_own)
 
     main = 3 * tokens
-    grads, main_t, rest_t = call(
+    main_t, rest_t = call(
         arrange,
-        [like((all_tokens, hidden), bf16), like((hidden, main), bf16), like((hidden, tokens), bf16)],
+        [like((hidden, main), bf16), like((hidden, all_tokens - main), bf16)],
         place, out_grad,
-        in_specs=[smem_spec, hbm_spec],
-        scratch=[pltpu.VMEM((all_tokens, hidden), bf16), pltpu.SemaphoreType.DMA(())],
-        vmem=50,
+        scratch=[pltpu.VMEM((all_tokens, hidden), bf16)],
     )
     q_parts, _ = lax.optimization_barrier((q_parts, main_t))
+    way_1, way_2 = [(0, 2), (2, 3), (3, 1), (1, 0)], [(0, 1), (1, 3), (3, 2), (2, 0)]
     q_full, y_own = call(
         project,
         [like((n_t, rank, rows), bf16), like((rank, tokens), f32)],
         place, q_own, *q_parts, activations,
     )
     y_parts = along_t(y_own)
-    (eq,) = call(
+    eq, *held_errors = call(
         error_left,
-        [like((rank, hidden), f32)],
+        [like((rank, hidden), f32)] + [like((hidden, features // 2), bf16)] * 2,
         q_full, errors,
-        grid=(n_t,),
-        in_specs=[
-            pl.BlockSpec((1, rank, rows), lambda k: (k, 0, 0)),
-            pl.BlockSpec((hidden, rows), lambda k: (0, k)),
-        ],
-        out_specs=[pl.BlockSpec((rank, hidden), lambda k: (0, 0))],
-        vmem=50,
+        in_specs=[vmem_spec, hbm_spec],
+        scratch=[pltpu.SemaphoreType.DMA((n_t,))],
+        vmem=40,
     )
     y_parts[0] = after(y_parts[0], eq)
-    x_first = move(activations, [(0, 2), (2, 3), (3, 1), (1, 0)], *y_parts)
+    x_first = move(activations, way_1, *y_parts)
     (p_local,) = call(
         left_factor,
         [like((rank, hidden), bf16)],
-        place, eq, y_own, *y_parts, grads,
+        place, eq, y_own, *y_parts, out_grad,
+        flops=KA,
         scratch=[pltpu.VMEM((n_t, rank, tokens), f32)],
     )
     (p_other,) = partners(p_local, "dp", n_dp, (1,))
@@ -392,22 +402,11 @@
     p_total, gram, near_w, far_w = call(
         weigh,
         [like((rank, hidden), bf16), like((rank, rank), f32), like((2, rank, tokens), f32), like((2, rank, tokens), f32)],
-        place, p_chip, *p_parts, grads,
+        place, p_chip, *p_parts, out_grad,
         scratch=[pltpu.VMEM((n_t, rank, tokens), f32)],
     )
     (got_w,) = partners(far_w, "tensor", n_t, (3,))
-    (te,) = call(
-        error_right,
-        [like((rank, features), f32)],
-        p_total, errors,
-        grid=(n_t,),
-        in_specs=[
-            pl.BlockSpec((rank, hidden), lambda k: (0, 0)),
-            pl.BlockSpec((hidden, rows), lambda k: (0, k)),
-        ],
-        out_specs=[pl.BlockSpec((rank, rows), lambda k: (0, k))],
-        vmem=50,
-    )
+    (te,) = call(error_right, [like((rank, features), f32)], p_total, *held_errors)
     got_w = after(got_w, te)
     keep, given = call(
         right_term,
@@ -415,12 +414,28 @@
         place, near_w, got_w, te, activations, x_first,
         scratch=[pltpu.VMEM((2, half, features), f32)],
     )
-    x_second = move(activations, [(0, 1), (1, 3), (3, 2), (2, 0)], got_w)
+    x_second = move(activations, way_2, p_total)
+    got_w = after(got_w, te)
+    keep, given = call(
+        right_term,
+        [like((half, features), f32), like((half, features), f32)],
+        place, near_w, got_w, te, activations, x_first,
+        scratch=[pltpu.VMEM((2, half, features), f32)],
+    )
+    cut_at = tokens // 32 * 16 + 16
+    to_outer, to_inner = [], []
+
+    def third_step(part, *when):
+        to_outer.append(move(x_first[part], [(1, 0), (2, 3)], *when))
+        to_inner.append(move(activations[part], [(1, 2), (2, 1)], *when))
+
+    third_step(slice(0, cut_at), got_w)
     (got,) = partners(given, "dp", n_dp, (1,))
     parts = call(
         cut,
         [like((half, rows), f32)] * 4,
         place, keep, got,
+        flops=KB,
         scratch=[pltpu.VMEM((n_t, half, rows), f32)],
     )
     arrived = [
@@ -429,40 +444,38 @@
         if k
     ]
     accs = []
-    for first in (0, features // 2):
+    for k, e_held in enumerate(held_errors):
         accs += call(
-            functools.partial(accumulate, first),
+            functools.partial(accumulate, k * (features // 2)),
             [like((hidden, features // 2), f32)],
-            main_t, errors, activations, x_first, x_second,
-            in_specs=[vmem_spec, hbm_spec] + [anywhere] * 3,
-            scratch=[
-                pltpu.VMEM((main, features // 2), bf16),
-                pltpu.VMEM((hidden, features // 2), bf16),
-                pltpu.SemaphoreType.DMA(()),
-                pltpu.SemaphoreType.DMA((3,)),
-            ],
-            vmem=12,
+            main_t, e_held, activations, x_first, x_second,
+            flops=KP,
+            in_specs=[vmem_spec, vmem_spec] + [anywhere] * 3,
+            scratch=[pltpu.VMEM((main, features // 2), bf16), pltpu.SemaphoreType.DMA((3,))],
         )
     (mine,) = call(pack, [like((half, rows + 256), f32)], parts[0], *arrived, gram)
     mine = after(mine, x_second)
     z1, z2, z3 = along_t(mine)
-    to_outer_3 = move(x_first, [(1, 0), (2, 3)], z1, z2, z3)
-    to_inner_3 = move(activations, [(1, 2), (2, 1)], z1, z2, z3)
+    x_outer = move(x_first, [(1, 0), (2, 3)], mine)
+    x_inner = move(activations, [(1, 2), (2, 1)], mine)
     mine, gram = call(unpack, [like((half, rows), f32), like((rank, rank), f32)], mine, z1, z2, z3)
     (linv,) = call(invert_cholesky, [like((rank, rank), f32)], gram)
     near = [mine] + along_xy(mine)
     near[1] = after(near[1], linv)
     far = [partners(v, "dp", n_dp, (1,))[0] for v in near]
-    new_factor, new_error = call(
-        functools.partial(rebuild, n_dp),
-        [like((rank, rows), f32), like((hidden, features), bf16)],
-        place, linv, p_total, rest_t, *near, *far, *accs, to_outer_3, to_inner_3,
-        in_specs=[smem_spec] + [vmem_spec] * 13 + [anywhere] * 2,
-        out_specs=[vmem_spec, anywhere],
+    new_factor, left, right = call(
+        functools.partial(finish, n_dp),
+        [like((rank, rows), f32), like((hidden, tokens + 3 * rank), bf16), like((3 * rank, features), bf16)],
+        place, linv, p_total, rest_t, *near, *far,
+        scratch=[pltpu.VMEM((4, 2, half, rows), f32), pltpu.VMEM((n_t, rank, rows), f32)],
+    )
+    (new_error,) = call(
+        rebuild,
+        [like((hidden, features), bf16)],
+        place, left, right, *accs, x_outer, x_inner,
+        in_specs=[smem_spec] + [vmem_spec] * 4 + [anywhere] * 2,
+        out_specs=[anywhere],
         scratch=[
-            pltpu.VMEM((4, 2, half, rows), f32),
-            pltpu.VMEM((n_t, rank, rows), f32),
-            pltpu.VMEM((hidden, tokens + 3 * rank), bf16),
             pltpu.VMEM((tokens + 3 * rank, features), bf16),
             pltpu.VMEM((2, hidden, 640), bf16),
             pltpu.SemaphoreType.DMA((1,)),

time: 104 us -> 94.3 us (0.907)
  the two profiles are of different devices: /device:TPU:11 before, /device:TPU:0 now
where the time goes in v3:
time: 94.3 us; the launch traced here: 92.8 us
  starting transfers between devices  34.7 us (37%)
  Pallas kernels  29.8 us (32%)
  waiting for transfers between devices  23.5 us (25%)
  local copies, waits for them, and re-layouts  2.71 us (3%)
  other arithmetic  1.07 us (1%)
  between operations  1.01 us (1%)
    pallas_call x15, Pallas kernels, call(): pl.pallas_call(kernel, out_shape=list(outs), in_specs=in_specs, out_specs...  29.8 us
    ppermute x22, starting transfers between devices, partners(): lax.ppermute(value, axis, [(i, i ^ k) for i in range(size)])  24.6 us
    ppermute x22, waiting for transfers between devices, partners(): lax.ppermute(value, axis, [(i, i ^ k) for i in range(size)])  10.1 us
    ppermute x4, waiting for transfers between devices, move(): return lax.ppermute(after(value, *when), 'tensor', perm)  9.03 us
    ppermute x4, starting transfers between devices, move(): return lax.ppermute(after(value, *when), 'tensor', perm)  6.45 us
    ppermute x3, waiting for transfers between devices, body(): lax.ppermute(m, 'dp', [(i, i ^ 2 * k) for i in range(n_dp)])  4.41 us
    ppermute x3, starting transfers between devices, body(): lax.ppermute(m, 'dp', [(i, i ^ 2 * k) for i in range(n_dp)])  3.55 us
    unnamed x8, local copies, waits for them, and re-layouts  2.71 us
  transfers between devices with their start and end apart: 29, of which 13 were waited for; matrix products, arithmetic and copies ran while one was open for 0% of the time, Pallas kernels for 23%

profile of v3, /device:TPU:0, one launch (start us, length us, event | category | flops | bytes accessed | tf_op | source)
XLA Modules:
  0.0 92.8 jit_solution(7433082087484477910)
XLA Ops:
  0.6 0.0 copy-start.1
  0.6 1.0 %convert_bitcast_fusion.own = bf16[32,640]{1,0:T(8,128)(2,1)S(1)} fusion(f32[640,32]{0,1:T(8,128)} %param.7), kind=kLoop, calls=%fused_computation.1 | loop fusion | flops 20480 | bytes 122880 | tf_op jit(solution)/shard_map/convert_element_type | solution.py:363
  1.6 5.0 %collective-permute-start.2 = (bf16[32,640]{1,0:T(8,128)(2,1)S(1)}, bf16[32,640]{1,0:T(8,128)(2,1)S(1)}, u32[]{:S(2)}, u32[]{:S(2)}) collective-permute-start(bf16[32,640]{1,0:T(8,128)(2,1)S(1)} %convert_bitcast_fusion.own), channel_id=1, source_target_pairs={{0,3},{1,2},{2,1},{3,0},{4,7},{5,6},{6,5},{7,4},{8,11},{9,10},{10,... | collective-permute-start | bytes 122888 | tf_op jit(solution)/shard_map/ppermute | solution.py:340
  6.7 0.0 collective-permute-start.1
  6.7 0.6 collective-permute-start
  7.3 0.1 pad_add_fusion.place
  7.4 1.6 %copy-done.2 = bf16[576,1728]{1,0:T(8,128)(2,1)S(1)} copy-done((bf16[576,1728]{1,0:T(8,128)(2,1)S(1)}, bf16[576,1728]{1,0:T(8,128)(2,1)}, u32[]{:S(2)}) %copy-start.2) | copy-done | bytes 1990680
  8.9 1.3 %arrange.1 = (bf16[1728,432]{1,0:T(8,128)(2,1)S(1)}, bf16[1728,144]{1,0:T(8,128)(2,1)S(1)}) custom-call(s32[3]{0:T(128)S(1)} %pad_add_fusion.place, bf16[576,1728]{1,0:T(8,128)(2,1)S(1)} %copy-done.2), custom_call_target="tpu_custom_call" | custom-call | bytes 3981324 | tf_op jit(solution)/shard_map/arrange/pallas_call | solution.py:83
  10.3 0.0 collective-permute-done.2.n3
  10.3 1.3 %collective-permute-done.1.n2 = bf16[32,640]{1,0:T(8,128)(2,1)S(1)} collective-permute-done((bf16[32,640]{1,0:T(8,128)(2,1)S(1)}, bf16[32,640]{1,0:T(8,128)(2,1)S(1)}, u32[]{:S(2)}, u32[]{:S(2)}) %collective-permute-start.1) | collective-permute-done | bytes 40992 | tf_op jit(solution)/shard_map/ppermute | solution.py:340
  11.6 0.0 collective-permute-done.n1
  11.6 1.1 %copy-done = bf16[144,2560]{1,0:T(8,128)(2,1)S(1)} copy-done((bf16[144,2560]{1,0:T(8,128)(2,1)S(1)}, bf16[144,2560]{1,0:T(8,128)(2,1)}, u32[]{:S(2)}) %copy-start) | copy-done | bytes 737304
  12.7 0.9 project.1
  13.6 0.2 collective-permute-start.3
  13.8 3.3 %collective-permute-start.5 = (f32[32,144]{1,0:T(8,128)S(1)}, f32[32,144]{1,0:T(8,128)S(1)}, u32[]{:S(2)}, u32[]{:S(2)}) collective-permute-start(f32[32,144]{1,0:T(8,128)S(1)} %get-tuple-element.43.own), channel_id=1, source_target_pairs={{0,3},{1,2},{2,1},{3,0},{4,7},{5,6},{6,5},{7,4},{8,11},{9,10},{10,... | collective-permute-start | bytes 55304 | tf_op jit(solution)/shard_map/ppermute | solution.py:340
  17.1 0.0 collective-permute-start.4
  17.1 5.0 %error_left.1 = (f32[32,1728]{1,0:T(8,128)S(1)}, bf16[1728,1280]{1,0:T(8,128)(2,1)S(1)}, bf16[1728,1280]{1,0:T(8,128)(2,1)S(1)}) custom-call(bf16[4,32,640]{2,1,0:T(8,128)(2,1)S(1)} %get-tuple-element.41.q_ref, bf16[1728,2560]{1,0:T(8,128)(2,1)} %bitcast.9), custom_call_target="tpu_custom_call" | custom-call | bytes 18079744 | tf_op jit(solution)/shard_map/error_left/pallas_call | solution.py:83
  22.2 0.0 collective-permute-done.3.n1
  22.2 0.0 collective-permute-done.4.n2
  22.2 3.0 %collective-permute-start.8 = (bf16[144,2560]{1,0:T(8,128)(2,1)S(1)}, bf16[144,2560]{1,0:T(8,128)(2,1)S(1)}, u32[]{:S(2)}, u32[]{:S(2)}) collective-permute-start(bf16[144,2560]{1,0:T(8,128)(2,1)S(1)} %copy-done.1), channel_id=1, source_target_pairs={{0,2},{2,3},{3,1},{1,0},{4,6},{6,7},{7,5},{5,4},{8,10},{10,11},{11... | collective-permute-start | bytes 2211848 | tf_op jit(solution)/shard_map/ppermute | solution.py:361
  25.2 1.0 %left_factor.1 = bf16[32,1728]{1,0:T(8,128)(2,1)S(1)} custom-call(s32[3]{0:T(128)S(1)} %pad_add_fusion.place, f32[32,1728]{1,0:T(8,128)S(1)} %get-tuple-element.42.eq_ref, f32[32,144]{1,0:T(8,128)S(1)} %get-tuple-element.43.own, f32[32,144]{1,0:T(8,128)S(1)} %collective-permute-done.3.n1, f32[32,144]{1,0:T(8,128)S(1)} %collective-permute-done.4.n2, ...), custom_call_target="tpu_custom_call" | custom-call | flops 1000000000 | bytes 2396172 | tf_op jit(solution)/shard_map/left_factor/pallas_call | solution.py:83
  26.1 0.1 collective-permute-start.6
  26.2 1.3 %collective-permute-done.6 = bf16[32,1728]{1,0:T(8,128)(2,1)S(1)} collective-permute-done((bf16[32,1728]{1,0:T(8,128)(2,1)S(1)}, bf16[32,1728]{1,0:T(8,128)(2,1)S(1)}, u32[]{:S(2)}, u32[]{:S(2)}) %collective-permute-start.6) | collective-permute-done | bytes 110624 | tf_op jit(solution)/shard_map/ppermute | solution.py:340
  27.6 1.6 %collective-permute-start.7 = (bf16[32,1728]{1,0:T(8,128)(2,1)S(1)}, bf16[32,1728]{1,0:T(8,128)(2,1)S(1)}, u32[]{:S(2)}, u32[]{:S(2)}) collective-permute-start(bf16[32,1728]{1,0:T(8,128)(2,1)S(1)} %add_convert_fusion.own), channel_id=1, source_target_pairs={{0,8},{4,12},{8,0},{12,4},{16,24},{20,28},{24,16},{28,20},{1,9},{5... | collective-permute-start | bytes 331784 | tf_op jit(solution)/shard_map/ppermute | solution.py:340
  29.1 1.5 %collective-permute-start.10 = (bf16[32,1728]{1,0:T(8,128)(2,1)S(1)}, bf16[32,1728]{1,0:T(8,128)(2,1)S(1)}, u32[]{:S(2)}, u32[]{:S(2)}) collective-permute-start(bf16[32,1728]{1,0:T(8,128)(2,1)S(1)} %add_convert_fusion.own), channel_id=1, source_target_pairs={{0,24},{4,28},{8,16},{12,20},{16,8},{20,12},{24,0},{28,4},{1,25},{... | collective-permute-start | bytes 331784 | tf_op jit(solution)/shard_map/ppermute | solution.py:340
  30.6 0.5 collective-permute-start.9
  31.1 2.0 %collective-permute-done.7.n1 = bf16[32,1728]{1,0:T(8,128)(2,1)S(1)} collective-permute-done((bf16[32,1728]{1,0:T(8,128)(2,1)S(1)}, bf16[32,1728]{1,0:T(8,128)(2,1)S(1)}, u32[]{:S(2)}, u32[]{:S(2)}) %collective-permute-start.7) | collective-permute-done | bytes 110624 | tf_op jit(solution)/shard_map/ppermute | solution.py:340
  33.1 5.6 %collective-permute-done.8.x_first = bf16[144,2560]{1,0:T(8,128)(2,1)S(1)} collective-permute-done((bf16[144,2560]{1,0:T(8,128)(2,1)S(1)}, bf16[144,2560]{1,0:T(8,128)(2,1)S(1)}, u32[]{:S(2)}, u32[]{:S(2)}) %collective-permute-start.8) | collective-permute-done | bytes 737312 | tf_op jit(solution)/shard_map/ppermute | solution.py:361
  38.7 0.0 collective-permute-done.10.n3
  38.7 1.3 %weigh.1 = (bf16[32,1728]{1,0:T(8,128)(2,1)S(1)}, f32[32,32]{1,0:T(8,128)S(1)}, f32[2,32,144]{2,1,0:T(8,128)S(1)}, f32[2,32,144]{2,1,0:T(8,128)S(1)}) custom-call(s32[3]{0:T(128)S(1)} %pad_add_fusion.place, bf16[32,1728]{1,0:T(8,128)(2,1)S(1)} %add_convert_fusion.own, bf16[32,1728]{1,0:T(8,128)(2,1)S(1)} %collective-permute-done.7.n1, ...), custom_call_target="tpu_custom_call" | custom-call | bytes 2621452 | tf_op jit(solution)/shard_map/weigh/pallas_call | solution.py:83
  39.9 2.7 %collective-permute-start.11 = (f32[2,32,144]{2,1,0:T(8,128)S(1)}, f32[2,32,144]{2,1,0:T(8,128)S(1)}, u32[]{:S(2)}, u32[]{:S(2)}) collective-permute-start(f32[2,32,144]{2,1,0:T(8,128)S(1)} %get-tuple-element.48), channel_id=1, source_target_pairs={{0,3},{1,2},{2,1},{3,0},{4,7},{5,6},{6,5},{7,4},{8,11},{9,10},{10,... | collective-permute-start | bytes 110600 | tf_op jit(solution)/shard_map/ppermute | solution.py:340
  42.6 1.3 %collective-permute-start.16 = (bf16[144,2560]{1,0:T(8,128)(2,1)S(1)}, bf16[144,2560]{1,0:T(8,128)(2,1)S(1)}, u32[]{:S(2)}, u32[]{:S(2)}) collective-permute-start(bf16[144,2560]{1,0:T(8,128)(2,1)S(1)} %copy-done.1), channel_id=1, source_target_pairs={{0,1},{1,3},{3,2},{2,0},{4,5},{5,7},{7,6},{6,4},{8,9},{9,11},{11,1... | collective-permute-start | bytes 2211848 | tf_op jit(solution)/shard_map/ppermute | solution.py:361
  43.9 1.4 %error_right.1.te_ref = f32[32,2560]{1,0:T(8,128)S(1)} custom-call(bf16[32,1728]{1,0:T(8,128)(2,1)S(1)} %get-tuple-element.49.p_ref, bf16[1728,1280]{1,0:T(8,128)(2,1)S(1)} %get-tuple-element.50.e_0.e_ref, bf16[1728,1280]{1,0:T(8,128)(2,1)S(1)} %get-tuple-element.51.e_1.e_ref), custom_call_target="tpu_custom_call" | custom-call | bytes 9285632 | tf_op jit(solution)/shard_map/error_right/pallas_call | solution.py:83
  45.4 1.5 %collective-permute-done.11.got_ref = f32[2,32,144]{2,1,0:T(8,128)S(1)} collective-permute-done((f32[2,32,144]{2,1,0:T(8,128)S(1)}, f32[2,32,144]{2,1,0:T(8,128)S(1)}, u32[]{:S(2)}, u32[]{:S(2)}) %collective-permute-start.11) | collective-permute-done | bytes 36896 | tf_op jit(solution)/shard_map/ppermute | solution.py:340
  46.8 0.9 right_term.1
  47.8 0.1 collective-permute-start.12
  47.8 1.4 %collective-permute-done.12.got = f32[16,2560]{1,0:T(8,128)S(1)} collective-permute-done((f32[16,2560]{1,0:T(8,128)S(1)}, f32[16,2560]{1,0:T(8,128)S(1)}, u32[]{:S(2)}, u32[]{:S(2)}) %collective-permute-start.12) | collective-permute-done | bytes 163872 | tf_op jit(solution)/shard_map/ppermute | solution.py:340
  49.2 0.6 cut.1
  49.8 1.5 %collective-permute-start.13 = (f32[16,640]{1,0:T(8,128)S(1)}, f32[16,640]{1,0:T(8,128)S(1)}, u32[]{:S(2)}, u32[]{:S(2)}) collective-permute-start(f32[16,640]{1,0:T(8,128)S(1)} %get-tuple-element.57), channel_id=1, source_target_pairs={{0,8},{4,12},{8,0},{12,4},{16,24},{20,28},{24,16},{28,20},{1,9},{5... | collective-permute-start | bytes 122888 | tf_op jit(solution)/shard_map/ppermute | solution.py:442
  51.3 1.5 %collective-permute-start.14 = (f32[16,640]{1,0:T(8,128)S(1)}, f32[16,640]{1,0:T(8,128)S(1)}, u32[]{:S(2)}, u32[]{:S(2)}) collective-permute-start(f32[16,640]{1,0:T(8,128)S(1)} %get-tuple-element.58), channel_id=1, source_target_pairs={{0,16},{4,20},{8,24},{12,28},{16,0},{20,4},{24,8},{28,12},{1,17},{... | collective-permute-start | bytes 122888 | tf_op jit(solution)/shard_map/ppermute | solution.py:442
  52.9 0.5 collective-permute-start.15
  53.4 0.5 collective-permute-done.13.b
  53.9 1.5 %collective-permute-done.14.c = f32[16,640]{1,0:T(8,128)S(1)} collective-permute-done((f32[16,640]{1,0:T(8,128)S(1)}, f32[16,640]{1,0:T(8,128)S(1)}, u32[]{:S(2)}, u32[]{:S(2)}) %collective-permute-start.14) | collective-permute-done | bytes 40992 | tf_op jit(solution)/shard_map/ppermute | solution.py:442
  55.4 2.4 %collective-permute-done.15.d = f32[16,640]{1,0:T(8,128)S(1)} collective-permute-done((f32[16,640]{1,0:T(8,128)S(1)}, f32[16,640]{1,0:T(8,128)S(1)}, u32[]{:S(2)}, u32[]{:S(2)}) %collective-permute-start.15) | collective-permute-done | bytes 40992 | tf_op jit(solution)/shard_map/ppermute | solution.py:442
  57.8 3.4 %collective-permute-done.16.x_second = bf16[144,2560]{1,0:T(8,128)(2,1)S(1)} collective-permute-done((bf16[144,2560]{1,0:T(8,128)(2,1)S(1)}, bf16[144,2560]{1,0:T(8,128)(2,1)S(1)}, u32[]{:S(2)}, u32[]{:S(2)}) %collective-permute-start.16) | collective-permute-done | bytes 737312 | tf_op jit(solution)/shard_map/ppermute | solution.py:361
  61.2 1.7 %collective-permute-start.19 = (f32[16,896]{1,0:T(8,128)S(1)}, f32[16,896]{1,0:T(8,128)S(1)}, u32[]{:S(2)}, u32[]{:S(2)}) collective-permute-start(f32[16,896]{1,0:T(8,128)S(1)} %pack.1.a), channel_id=1, source_target_pairs={{0,3},{1,2},{2,1},{3,0},{4,7},{5,6},{6,5},{7,4},{8,11},{9,10},{10,... | collective-permute-start | bytes 172040 | tf_op jit(solution)/shard_map/ppermute | solution.py:340
  63.0 2.6 %collective-permute-start.17 = (f32[16,896]{1,0:T(8,128)S(1)}, f32[16,896]{1,0:T(8,128)S(1)}, u32[]{:S(2)}, u32[]{:S(2)}) collective-permute-start(f32[16,896]{1,0:T(8,128)S(1)} %pack.1.a), channel_id=1, source_target_pairs={{0,1},{1,0},{2,3},{3,2},{4,5},{5,4},{6,7},{7,6},{8,9},{9,8},{10,11... | collective-permute-start | bytes 172040 | tf_op jit(solution)/shard_map/ppermute | solution.py:340
  65.6 1.3 %collective-permute-start.27 = (bf16[144,2560]{1,0:T(8,128)(2,1)S(1)}, bf16[144,2560]{1,0:T(8,128)(2,1)S(1)}, u32[]{:S(2)}, u32[]{:S(2)}) collective-permute-start(bf16[144,2560]{1,0:T(8,128)(2,1)S(1)} %collective-permute-done.8.x_first), channel_id=1, source_target_pairs={{1,0},{2,3},{5,4},{6,7},{9,8},{10,11},{13,12},{14,15},{17,16},{18,... | collective-permute-start | bytes 2211848 | tf_op jit(solution)/shard_map/ppermute | solution.py:361
  66.9 0.9 collective-permute-start.28
  67.8 0.7 collective-permute-done.18.c
  68.5 0.7 collective-permute-done.17.b
  69.2 1.6 %collective-permute-start.20 = (f32[16,640]{1,0:T(8,128)S(1)}, f32[16,640]{1,0:T(8,128)S(1)}, u32[]{:S(2)}, u32[]{:S(2)}) collective-permute-start(f32[16,640]{1,0:T(8,128)S(1)} %get-tuple-element.65.a0), channel_id=1, source_target_pairs={{0,8},{4,12},{8,0},{12,4},{16,24},{20,28},{24,16},{28,20},{1,9},{5... | collective-permute-start | bytes 122888 | tf_op jit(solution)/shard_map/ppermute | solution.py:340
  70.7 1.2 %collective-permute-start.22 = (f32[16,640]{1,0:T(8,128)S(1)}, f32[16,640]{1,0:T(8,128)S(1)}, u32[]{:S(2)}, u32[]{:S(2)}) collective-permute-start(f32[16,640]{1,0:T(8,128)S(1)} %get-tuple-element.65.a0), channel_id=1, source_target_pairs={{0,24},{4,28},{8,16},{12,20},{16,8},{20,12},{24,0},{28,4},{1,25},{... | collective-permute-start | bytes 122888 | tf_op jit(solution)/shard_map/ppermute | solution.py:340
  71.9 1.3 %collective-permute-done.20.a1 = f32[16,640]{1,0:T(8,128)S(1)} collective-permute-done((f32[16,640]{1,0:T(8,128)S(1)}, f32[16,640]{1,0:T(8,128)S(1)}, u32[]{:S(2)}, u32[]{:S(2)}) %collective-permute-start.20) | collective-permute-done | bytes 40992 | tf_op jit(solution)/shard_map/ppermute | solution.py:340
  73.2 1.2 %collective-permute-start.21 = (f32[16,640]{1,0:T(8,128)S(1)}, f32[16,640]{1,0:T(8,128)S(1)}, u32[]{:S(2)}, u32[]{:S(2)}) collective-permute-start(f32[16,640]{1,0:T(8,128)S(1)} %get-tuple-element.65.a0), channel_id=1, source_target_pairs={{0,16},{4,20},{8,24},{12,28},{16,0},{20,4},{24,8},{28,12},{1,17},{... | collective-permute-start | bytes 122888 | tf_op jit(solution)/shard_map/ppermute | solution.py:340
  74.5 3.0 %accumulate.3.acc_1 = f32[1728,1280]{1,0:T(8,128)S(1)} custom-call(bf16[1728,432]{1,0:T(8,128)(2,1)S(1)} %get-tuple-element.37.main_ref, bf16[1728,1280]{1,0:T(8,128)(2,1)S(1)} %get-tuple-element.51.e_1.e_ref, bf16[144,2560]{1,0:T(8,128)(2,1)S(1)} %copy-done.1, bf16[144,2560]{1,0:T(8,128)(2,1)S(1)} %collective-permute-done.8.x_first, ...), custom_call_target="tpu_custom_call" | custom-call | flops 3500000000 | bytes 16975872 | tf_op jit(solution)/shard_map/accumulate/pallas_call | solution.py:83
  77.5 2.8 %invert_cholesky.1.linv = f32[32,32]{1,0:T(8,128)S(1)} custom-call(f32[32,32]{1,0:T(8,128)S(1)} %get-tuple-element.63.g_ref), custom_call_target="tpu_custom_call" | custom-call | bytes 8192 | tf_op jit(solution)/shard_map/invert_cholesky/pallas_call | solution.py:83
  80.4 0.0 collective-permute-done.23.b0
  80.4 0.1 collective-permute-start.24
  80.5 0.5 collective-permute-start.26
  81.0 0.1 collective-permute-start.25
  81.0 3.0 %accumulate.2.acc_0 = f32[1728,1280]{1,0:T(8,128)S(1)} custom-call(bf16[1728,432]{1,0:T(8,128)(2,1)S(1)} %get-tuple-element.37.main_ref, bf16[1728,1280]{1,0:T(8,128)(2,1)S(1)} %get-tuple-element.50.e_0.e_ref, bf16[144,2560]{1,0:T(8,128)(2,1)S(1)} %copy-done.1, bf16[144,2560]{1,0:T(8,128)(2,1)S(1)} %collective-permute-done.8.x_first, ...), custom_call_target="tpu_custom_call" | custom-call | flops 3500000000 | bytes 16975872 | tf_op jit(solution)/shard_map/accumulate/pallas_call | solution.py:83
  84.1 2.2 %finish.1 = (f32[32,640]{1,0:T(8,128)}, bf16[1728,240]{1,0:T(8,128)(2,1)S(1)}, bf16[96,2560]{1,0:T(8,128)(2,1)S(1)}) custom-call(s32[3]{0:T(128)S(1)} %pad_add_fusion.place, f32[32,32]{1,0:T(8,128)S(1)} %invert_cholesky.1.linv, bf16[32,1728]{1,0:T(8,128)(2,1)S(1)} %get-tuple-element.49.p_ref, bf16[1728,144]{1,0:T(8,128)(2,1)S(1)} %get-tuple-element.64.rest_ref, ...), custom_call_target="tpu_custom_call" | custom-call | bytes 2342924 | tf_op jit(solution)/shard_map/finish/pallas_call | solution.py:83
  86.3 6.3 %rebuild.1 = bf16[1728,2560]{1,0:T(8,128)(2,1)} custom-call(s32[3]{0:T(128)S(1)} %pad_add_fusion.place, bf16[1728,240]{1,0:T(8,128)(2,1)S(1)} %get-tuple-element.67.left_ref, bf16[96,2560]{1,0:T(8,128)(2,1)S(1)} %get-tuple-element.68.right_ref, f32[1728,1280]{1,0:T(8,128)S(1)} %accumulate.2.acc_0, f32[1728,1280]{1,0:T(8,128)S(1)} %accumulate.3.acc_1, ...), custom_call_target="tpu_custom_call" | custom-call | bytes 29337612 | tf_op jit(solution)/shard_map/rebuild/pallas_call | solution.py:83
  (20 shorter events, 0.1 us)
Async XLA Ops:
  0.6 21.6 %copy-start.1 = (bf16[144,2560]{1,0:T(8,128)(2,1)S(1)}, bf16[144,2560]{1,0:T(8,128)(2,1)}, u32[]{:S(2)}) copy-start(bf16[144,2560]{1,0:T(8,128)(2,1)} %x_own.5) | copy-start | bytes 2211844
  1.6 8.7 %collective-permute-start.2 = (bf16[32,640]{1,0:T(8,128)(2,1)S(1)}, bf16[32,640]{1,0:T(8,128)(2,1)S(1)}, u32[]{:S(2)}, u32[]{:S(2)}) collective-permute-start(bf16[32,640]{1,0:T(8,128)(2,1)S(1)} %convert_bitcast_fusion.own), channel_id=1, source_target_pairs={{0,3},{1,2},{2,1},{3,0},{4,7},{5,6},{6,5},{7,4},{8,11},{9,10},{10,... | collective-permute-start | bytes 122888 | tf_op jit(solution)/shard_map/ppermute | solution.py:340
  6.7 4.9 %collective-permute-start.1 = (bf16[32,640]{1,0:T(8,128)(2,1)S(1)}, bf16[32,640]{1,0:T(8,128)(2,1)S(1)}, u32[]{:S(2)}, u32[]{:S(2)}) collective-permute-start(bf16[32,640]{1,0:T(8,128)(2,1)S(1)} %convert_bitcast_fusion.own), channel_id=1, source_target_pairs={{0,2},{1,3},{2,0},{3,1},{4,6},{5,7},{6,4},{7,5},{8,10},{9,11},{10,... | collective-permute-start | bytes 122888 | tf_op jit(solution)/shard_map/ppermute | solution.py:340
  6.7 4.9 %collective-permute-start = (bf16[32,640]{1,0:T(8,128)(2,1)S(1)}, bf16[32,640]{1,0:T(8,128)(2,1)S(1)}, u32[]{:S(2)}, u32[]{:S(2)}) collective-permute-start(bf16[32,640]{1,0:T(8,128)(2,1)S(1)} %convert_bitcast_fusion.own), channel_id=1, source_target_pairs={{0,1},{1,0},{2,3},{3,2},{4,5},{5,4},{6,7},{7,6},{8,9},{9,8},{10,11... | collective-permute-start | bytes 122888 | tf_op jit(solution)/shard_map/ppermute | solution.py:340
  7.4 1.6 %copy-start.2 = (bf16[576,1728]{1,0:T(8,128)(2,1)S(1)}, bf16[576,1728]{1,0:T(8,128)(2,1)}, u32[]{:S(2)}) copy-start(bf16[576,1728]{1,0:T(8,128)(2,1)} %dy_ref.5) | copy-start | bytes 5971972
  11.6 1.1 %copy-start = (bf16[144,2560]{1,0:T(8,128)(2,1)S(1)}, bf16[144,2560]{1,0:T(8,128)(2,1)}, u32[]{:S(2)}) copy-start(bf16[144,2560]{1,0:T(8,128)(2,1)} %x_own.5) | copy-start | bytes 2211844
  12.7 12.5 %copy-start.3 = (bf16[576,1728]{1,0:T(8,128)(2,1)S(1)}, bf16[576,1728]{1,0:T(8,128)(2,1)}, u32[]{:S(2)}) copy-start(bf16[576,1728]{1,0:T(8,128)(2,1)} %dy_ref.5) | copy-start | bytes 5971972
  13.6 8.6 %collective-permute-start.3 = (f32[32,144]{1,0:T(8,128)S(1)}, f32[32,144]{1,0:T(8,128)S(1)}, u32[]{:S(2)}, u32[]{:S(2)}) collective-permute-start(f32[32,144]{1,0:T(8,128)S(1)} %get-tuple-element.43.own), channel_id=1, source_target_pairs={{0,1},{1,0},{2,3},{3,2},{4,5},{5,4},{6,7},{7,6},{8,9},{9,8},{10,11... | collective-permute-start | bytes 55304 | tf_op jit(solution)/shard_map/ppermute | solution.py:340
  13.8 8.4 %collective-permute-start.5 = (f32[32,144]{1,0:T(8,128)S(1)}, f32[32,144]{1,0:T(8,128)S(1)}, u32[]{:S(2)}, u32[]{:S(2)}) collective-permute-start(f32[32,144]{1,0:T(8,128)S(1)} %get-tuple-element.43.own), channel_id=1, source_target_pairs={{0,3},{1,2},{2,1},{3,0},{4,7},{5,6},{6,5},{7,4},{8,11},{9,10},{10,... | collective-permute-start | bytes 55304 | tf_op jit(solution)/shard_map/ppermute | solution.py:340
  17.1 5.1 %collective-permute-start.4 = (f32[32,144]{1,0:T(8,128)S(1)}, f32[32,144]{1,0:T(8,128)S(1)}, u32[]{:S(2)}, u32[]{:S(2)}) collective-permute-start(f32[32,144]{1,0:T(8,128)S(1)} %get-tuple-element.43.own), channel_id=1, source_target_pairs={{0,2},{1,3},{2,0},{3,1},{4,6},{5,7},{6,4},{7,5},{8,10},{9,11},{10,... | collective-permute-start | bytes 55304 | tf_op jit(solution)/shard_map/ppermute | solution.py:340
  22.2 16.5 %collective-permute-start.8 = (bf16[144,2560]{1,0:T(8,128)(2,1)S(1)}, bf16[144,2560]{1,0:T(8,128)(2,1)S(1)}, u32[]{:S(2)}, u32[]{:S(2)}) collective-permute-start(bf16[144,2560]{1,0:T(8,128)(2,1)S(1)} %copy-done.1), channel_id=1, source_target_pairs={{0,2},{2,3},{3,1},{1,0},{4,6},{6,7},{7,5},{5,4},{8,10},{10,11},{11... | collective-permute-start | bytes 2211848 | tf_op jit(solution)/shard_map/ppermute | solution.py:361
  26.1 1.4 %collective-permute-start.6 = (bf16[32,1728]{1,0:T(8,128)(2,1)S(1)}, bf16[32,1728]{1,0:T(8,128)(2,1)S(1)}, u32[]{:S(2)}, u32[]{:S(2)}) collective-permute-start(bf16[32,1728]{1,0:T(8,128)(2,1)S(1)} %left_factor.1), channel_id=1, source_target_pairs={{0,4},{4,0},{8,12},{12,8},{16,20},{20,16},{24,28},{28,24},{1,5},{5... | collective-permute-start | bytes 331784 | tf_op jit(solution)/shard_map/ppermute | solution.py:340
  27.6 5.5 %collective-permute-start.7 = (bf16[32,1728]{1,0:T(8,128)(2,1)S(1)}, bf16[32,1728]{1,0:T(8,128)(2,1)S(1)}, u32[]{:S(2)}, u32[]{:S(2)}) collective-permute-start(bf16[32,1728]{1,0:T(8,128)(2,1)S(1)} %add_convert_fusion.own), channel_id=1, source_target_pairs={{0,8},{4,12},{8,0},{12,4},{16,24},{20,28},{24,16},{28,20},{1,9},{5... | collective-permute-start | bytes 331784 | tf_op jit(solution)/shard_map/ppermute | solution.py:340
  29.1 9.6 %collective-permute-start.10 = (bf16[32,1728]{1,0:T(8,128)(2,1)S(1)}, bf16[32,1728]{1,0:T(8,128)(2,1)S(1)}, u32[]{:S(2)}, u32[]{:S(2)}) collective-permute-start(bf16[32,1728]{1,0:T(8,128)(2,1)S(1)} %add_convert_fusion.own), channel_id=1, source_target_pairs={{0,24},{4,28},{8,16},{12,20},{16,8},{20,12},{24,0},{28,4},{1,25},{... | collective-permute-start | bytes 331784 | tf_op jit(solution)/shard_map/ppermute | solution.py:340
  30.6 8.1 %collective-permute-start.9 = (bf16[32,1728]{1,0:T(8,128)(2,1)S(1)}, bf16[32,1728]{1,0:T(8,128)(2,1)S(1)}, u32[]{:S(2)}, u32[]{:S(2)}) collective-permute-start(bf16[32,1728]{1,0:T(8,128)(2,1)S(1)} %add_convert_fusion.own), channel_id=1, source_target_pairs={{0,16},{4,20},{8,24},{12,28},{16,0},{20,4},{24,8},{28,12},{1,17},{... | collective-permute-start | bytes 331784 | tf_op jit(solution)/shard_map/ppermute | solution.py:340
  39.9 6.9 %collective-permute-start.11 = (f32[2,32,144]{2,1,0:T(8,128)S(1)}, f32[2,32,144]{2,1,0:T(8,128)S(1)}, u32[]{:S(2)}, u32[]{:S(2)}) collective-permute-start(f32[2,32,144]{2,1,0:T(8,128)S(1)} %get-tuple-element.48), channel_id=1, source_target_pairs={{0,3},{1,2},{2,1},{3,0},{4,7},{5,6},{6,5},{7,4},{8,11},{9,10},{10,... | collective-permute-start | bytes 110600 | tf_op jit(solution)/shard_map/ppermute | solution.py:340
  42.6 18.6 %collective-permute-start.16 = (bf16[144,2560]{1,0:T(8,128)(2,1)S(1)}, bf16[144,2560]{1,0:T(8,128)(2,1)S(1)}, u32[]{:S(2)}, u32[]{:S(2)}) collective-permute-start(bf16[144,2560]{1,0:T(8,128)(2,1)S(1)} %copy-done.1), channel_id=1, source_target_pairs={{0,1},{1,3},{3,2},{2,0},{4,5},{5,7},{7,6},{6,4},{8,9},{9,11},{11,1... | collective-permute-start | bytes 2211848 | tf_op jit(solution)/shard_map/ppermute | solution.py:361
  47.8 1.5 %collective-permute-start.12 = (f32[16,2560]{1,0:T(8,128)S(1)}, f32[16,2560]{1,0:T(8,128)S(1)}, u32[]{:S(2)}, u32[]{:S(2)}) collective-permute-start(f32[16,2560]{1,0:T(8,128)S(1)} %get-tuple-element.55), channel_id=1, source_target_pairs={{0,4},{4,0},{8,12},{12,8},{16,20},{20,16},{24,28},{28,24},{1,5},{5... | collective-permute-start | bytes 491528 | tf_op jit(solution)/shard_map/ppermute | solution.py:340
  49.8 4.1 %collective-permute-start.13 = (f32[16,640]{1,0:T(8,128)S(1)}, f32[16,640]{1,0:T(8,128)S(1)}, u32[]{:S(2)}, u32[]{:S(2)}) collective-permute-start(f32[16,640]{1,0:T(8,128)S(1)} %get-tuple-element.57), channel_id=1, source_target_pairs={{0,8},{4,12},{8,0},{12,4},{16,24},{20,28},{24,16},{28,20},{1,9},{5... | collective-permute-start | bytes 122888 | tf_op jit(solution)/shard_map/ppermute | solution.py:442
  51.3 4.0 %collective-permute-start.14 = (f32[16,640]{1,0:T(8,128)S(1)}, f32[16,640]{1,0:T(8,128)S(1)}, u32[]{:S(2)}, u32[]{:S(2)}) collective-permute-start(f32[16,640]{1,0:T(8,128)S(1)} %get-tuple-element.58), channel_id=1, source_target_pairs={{0,16},{4,20},{8,24},{12,28},{16,0},{20,4},{24,8},{28,12},{1,17},{... | collective-permute-start | bytes 122888 | tf_op jit(solution)/shard_map/ppermute | solution.py:442
  52.9 4.9 %collective-permute-start.15 = (f32[16,640]{1,0:T(8,128)S(1)}, f32[16,640]{1,0:T(8,128)S(1)}, u32[]{:S(2)}, u32[]{:S(2)}) collective-permute-start(f32[16,640]{1,0:T(8,128)S(1)} %get-tuple-element.59), channel_id=1, source_target_pairs={{0,24},{4,28},{8,16},{12,20},{16,8},{20,12},{24,0},{28,4},{1,25},{... | collective-permute-start | bytes 122888 | tf_op jit(solution)/shard_map/ppermute | solution.py:442
  61.2 6.6 %collective-permute-start.19 = (f32[16,896]{1,0:T(8,128)S(1)}, f32[16,896]{1,0:T(8,128)S(1)}, u32[]{:S(2)}, u32[]{:S(2)}) collective-permute-start(f32[16,896]{1,0:T(8,128)S(1)} %pack.1.a), channel_id=1, source_target_pairs={{0,3},{1,2},{2,1},{3,0},{4,7},{5,6},{6,5},{7,4},{8,11},{9,10},{10,... | collective-permute-start | bytes 172040 | tf_op jit(solution)/shard_map/ppermute | solution.py:340
  63.0 5.5 %collective-permute-start.18 = (f32[16,896]{1,0:T(8,128)S(1)}, f32[16,896]{1,0:T(8,128)S(1)}, u32[]{:S(2)}, u32[]{:S(2)}) collective-permute-start(f32[16,896]{1,0:T(8,128)S(1)} %pack.1.a), channel_id=1, source_target_pairs={{0,2},{1,3},{2,0},{3,1},{4,6},{5,7},{6,4},{7,5},{8,10},{9,11},{10,... | collective-permute-start | bytes 172040 | tf_op jit(solution)/shard_map/ppermute | solution.py:340
  63.0 6.2 %collective-permute-start.17 = (f32[16,896]{1,0:T(8,128)S(1)}, f32[16,896]{1,0:T(8,128)S(1)}, u32[]{:S(2)}, u32[]{:S(2)}) collective-permute-start(f32[16,896]{1,0:T(8,128)S(1)} %pack.1.a), channel_id=1, source_target_pairs={{0,1},{1,0},{2,3},{3,2},{4,5},{5,4},{6,7},{7,6},{8,9},{9,8},{10,11... | collective-permute-start | bytes 172040 | tf_op jit(solution)/shard_map/ppermute | solution.py:340
  65.6 20.7 %collective-permute-start.27 = (bf16[144,2560]{1,0:T(8,128)(2,1)S(1)}, bf16[144,2560]{1,0:T(8,128)(2,1)S(1)}, u32[]{:S(2)}, u32[]{:S(2)}) collective-permute-start(bf16[144,2560]{1,0:T(8,128)(2,1)S(1)} %collective-permute-done.8.x_first), channel_id=1, source_target_pairs={{1,0},{2,3},{5,4},{6,7},{9,8},{10,11},{13,12},{14,15},{17,16},{18,... | collective-permute-start | bytes 2211848 | tf_op jit(solution)/shard_map/ppermute | solution.py:361
  66.9 19.4 %collective-permute-start.28 = (bf16[144,2560]{1,0:T(8,128)(2,1)S(1)}, bf16[144,2560]{1,0:T(8,128)(2,1)S(1)}, u32[]{:S(2)}, u32[]{:S(2)}) collective-permute-start(bf16[144,2560]{1,0:T(8,128)(2,1)S(1)} %copy-done.1), channel_id=1, source_target_pairs={{1,2},{2,1},{5,6},{6,5},{9,10},{10,9},{13,14},{14,13},{17,18},{18,... | collective-permute-start | bytes 2211848 | tf_op jit(solution)/shard_map/ppermute | solution.py:361
  69.2 4.1 %collective-permute-start.20 = (f32[16,640]{1,0:T(8,128)S(1)}, f32[16,640]{1,0:T(8,128)S(1)}, u32[]{:S(2)}, u32[]{:S(2)}) collective-permute-start(f32[16,640]{1,0:T(8,128)S(1)} %get-tuple-element.65.a0), channel_id=1, source_target_pairs={{0,8},{4,12},{8,0},{12,4},{16,24},{20,28},{24,16},{28,20},{1,9},{5... | collective-permute-start | bytes 122888 | tf_op jit(solution)/shard_map/ppermute | solution.py:340
  70.7 9.6 %collective-permute-start.23 = (f32[16,640]{1,0:T(8,128)S(1)}, f32[16,640]{1,0:T(8,128)S(1)}, u32[]{:S(2)}, u32[]{:S(2)}) collective-permute-start(f32[16,640]{1,0:T(8,128)S(1)} %get-tuple-element.65.a0), channel_id=1, source_target_pairs={{0,4},{4,0},{8,12},{12,8},{16,20},{20,16},{24,28},{28,24},{1,5},{5... | collective-permute-start | bytes 122888 | tf_op jit(solution)/shard_map/ppermute | solution.py:340
  70.7 9.7 %collective-permute-start.22 = (f32[16,640]{1,0:T(8,128)S(1)}, f32[16,640]{1,0:T(8,128)S(1)}, u32[]{:S(2)}, u32[]{:S(2)}) collective-permute-start(f32[16,640]{1,0:T(8,128)S(1)} %get-tuple-element.65.a0), channel_id=1, source_target_pairs={{0,24},{4,28},{8,16},{12,20},{16,8},{20,12},{24,0},{28,4},{1,25},{... | collective-permute-start | bytes 122888 | tf_op jit(solution)/shard_map/ppermute | solution.py:340
  73.2 7.7 %collective-permute-start.21 = (f32[16,640]{1,0:T(8,128)S(1)}, f32[16,640]{1,0:T(8,128)S(1)}, u32[]{:S(2)}, u32[]{:S(2)}) collective-permute-start(f32[16,640]{1,0:T(8,128)S(1)} %get-tuple-element.65.a0), channel_id=1, source_target_pairs={{0,16},{4,20},{8,24},{12,28},{16,0},{20,4},{24,8},{28,12},{1,17},{... | collective-permute-start | bytes 122888 | tf_op jit(solution)/shard_map/ppermute | solution.py:340
  80.4 3.7 %collective-permute-start.24 = (f32[16,640]{1,0:T(8,128)S(1)}, f32[16,640]{1,0:T(8,128)S(1)}, u32[]{:S(2)}, u32[]{:S(2)}) collective-permute-start(f32[16,640]{1,0:T(8,128)S(1)} %collective-permute-done.20.a1), channel_id=1, source_target_pairs={{0,4},{4,0},{8,12},{12,8},{16,20},{20,16},{24,28},{28,24},{1,5},{5... | collective-permute-start | bytes 122888 | tf_op jit(solution)/shard_map/ppermute | solution.py:340
  80.5 3.6 %collective-permute-start.26 = (f32[16,640]{1,0:T(8,128)S(1)}, f32[16,640]{1,0:T(8,128)S(1)}, u32[]{:S(2)}, u32[]{:S(2)}) collective-permute-start(f32[16,640]{1,0:T(8,128)S(1)} %collective-permute-done.22.a3), channel_id=1, source_target_pairs={{0,4},{4,0},{8,12},{12,8},{16,20},{20,16},{24,28},{28,24},{1,5},{5... | collective-permute-start | bytes 122888 | tf_op jit(solution)/shard_map/ppermute | solution.py:340
  81.0 3.1 %collective-permute-start.25 = (f32[16,640]{1,0:T(8,128)S(1)}, f32[16,640]{1,0:T(8,128)S(1)}, u32[]{:S(2)}, u32[]{:S(2)}) collective-permute-start(f32[16,640]{1,0:T(8,128)S(1)} %collective-permute-done.21.a2), channel_id=1, source_target_pairs={{0,4},{4,0},{8,12},{12,8},{16,20},{20,16},{24,28},{28,24},{1,5},{5... | collective-permute-start | bytes 122888 | tf_op jit(solution)/shard_map/ppermute | solution.py:340

commit v4 on v3

--- a/solution.py
+++ b/solution.py
@@ -11,7 +11,7 @@
 column_block = 8
 bf16, f32 = jnp.bfloat16, jnp.float32
 MIB = 1 << 20
-KA, KB, KP = 1_000_000_000, 5_500_000_000, 3_500_000_000
+KA, KB, KP = 0, 3_900_000_000, 3_500_000_000
 
 
 def plain_body(activations, out_grad, error_state, right_factor):
@@ -219,12 +219,18 @@
     cols = lax.broadcasted_iota(jnp.int32, (n, n), 1)
     a = g_ref[...]
     inverse = jnp.where(rows == cols, 1.0, 0.0).astype(f32)
-    for j in range(n):
-        column = jnp.sum(jnp.where(cols == j, a, 0.0), axis=1, keepdims=True)
-        pivot = column[j : j + 1, :]
-        factor = jnp.where(rows[:, :1] > j, column / pivot, 0.0)
-        a = a - factor * a[j : j + 1, :]
-        inverse = inverse - factor * inverse[j : j + 1, :]
+    for j in range(0, n, 2):
+        first = jnp.sum(jnp.where(cols == j, a, 0.0), axis=1, keepdims=True)
+        second = jnp.sum(jnp.where(cols == j + 1, a, 0.0), axis=1, keepdims=True)
+        row, row_inverse = a[j : j + 1, :], inverse[j : j + 1, :]
+        factor = jnp.where(rows[:, :1] > j, first / first[j : j + 1, :], 0.0)
+        step = factor[j + 1 : j + 2, :]
+        next_row = a[j + 1 : j + 2, :] - step * row
+        next_inverse = inverse[j + 1 : j + 2, :] - step * row_inverse
+        second = second - factor * first[j + 1 : j + 2, :]
+        next_factor = jnp.where(rows[:, :1] > j + 1, second / second[j + 1 : j + 2, :], 0.0)
+        a = a - factor * row - next_factor * next_row
+        inverse = inverse - factor * row_inverse - next_factor * next_inverse
     diagonal = jnp.sum(jnp.where(rows == cols, a, 0.0), axis=1, keepdims=True)
     out_ref[...] = inverse * lax.rsqrt(diagonal)
 
@@ -240,23 +246,25 @@
     rest_ref[...] = held[main:, :].T
 
 
-def accumulate(first, main_ref, e_ref, x_own, x_first, x_second, acc_ref, x_ref, sems):
+def accumulate(first, lane, spans, main_ref, base_ref, *rest):
+    sources, (acc_ref, x_ref, sems) = rest[: len(spans)], rest[len(spans) :]
     width = acc_ref.shape[1]
-    rows = x_own.shape[0]
-    copies = [
-        pltpu.make_async_copy(source.at[:, pl.ds(first, width)], x_ref.at[pl.ds(k * rows, rows), :], sems.at[k])
-        for k, source in enumerate((x_own, x_first, x_second))
-    ]
+    copies, at = [], 0
+    for k, (source, (begin, end)) in enumerate(zip(sources, spans)):
+        part = source.at[pl.ds(begin, end - begin), pl.ds(first, width)]
+        copies.append(pltpu.make_async_copy(part, x_ref.at[pl.ds(at, end - begin), :], sems.at[k]))
+        at += end - begin
     for copy in copies:
         copy.start()
     for copy in copies:
         copy.wait()
-    step, block = 640, 432
+    step, block = 256, acc_ref.shape[0] // 4
     for c in range(0, width, step):
         cols = slice(c, c + step)
         for r in range(0, acc_ref.shape[0], block):
-            at = slice(r, r + block)
-            acc_ref[at, cols] = dot(main_ref[at, :], x_ref[:, cols]) + e_ref[at, cols].astype(f32)
+            here = slice(r, r + block)
+            term = dot(main_ref[here, lane : lane + at], x_ref[:, cols])
+            acc_ref[here, cols] = term + base_ref[here, cols].astype(f32)
 
 
 def finish(replicas, place, linv, p_ref, rest_ref, a0, a1, a2, a3, b0, b1, b2, b3, new_ref, left_ref, right_ref, held, nf4):
@@ -264,12 +272,14 @@
     for k, (a, b) in enumerate(((a0, b0), (a1, b1), (a2, b2), (a3, b3))):
         held[chip ^ k, core] = a[...]
         held[chip ^ k, 1 - core] = b[...]
-    highest = lax.Precision.HIGHEST
     parts, _, half, width = held.shape
     rank = 2 * half
-    scaled = linv[...] * (1.0 / replicas)
+    l_high, l_low = split(linv[...])
+    both = jnp.concatenate((l_high, l_low), axis=0)
     for s in range(parts):
-        nf = dot(scaled, held[s].reshape(rank, width), precision=highest)
+        t_high, t_low = split(held[s].reshape(rank, width))
+        term = dot(both, t_high)
+        nf = (term[:rank] + (term[rank:] + dot(l_high, t_low))) * (1.0 / replicas)
         nf4[s] = nf
         high, low = split(nf)
         at = slice(s * width, (s + 1) * width)
@@ -277,8 +287,8 @@
         right_ref[rank : 2 * rank, at] = high
         right_ref[2 * rank :, at] = low
     new_ref[...] = nf4[t]
-    basis = dot(linv[...], p_ref[...].astype(f32), precision=highest)
-    high, low = split(-basis)
+    term = dot(both, p_ref[...])
+    high, low = split(-(term[:rank] + term[rank:]))
     base = rest_ref.shape[1]
     left_ref[:, :base] = rest_ref[...]
     left_ref[:, base:] = jnp.concatenate((high, low, high), axis=0).T
@@ -302,34 +312,25 @@
 
     buffer[rows:, :] = right_ref[...]
     fetch(inner).wait()
-    width = staged.shape[2]
+    slots, hidden, width = staged.shape
     count = acc_0.shape[1] // width
 
-    def put(i, slot):
-        return pltpu.make_async_copy(staged.at[slot], out_any.at[:, pl.ds(pl.multiple_of(i * width, width), width)], out_sems.at[slot])
-
-    for part, acc_ref in enumerate((acc_0, acc_1)):
-
-        @pl.loop(0, count)
-        def _(c):
-            i = part * count + c
-            slot = lax.rem(i, 2)
-
-            @pl.when(i >= 2)
-            def _():
-                put(i - 2, slot).wait()
-
-            here = pl.ds(pl.multiple_of(c * width, width), width)
-            cols = pl.ds(pl.multiple_of(i * width, width), width)
-            block = 432
-            for r in range(0, acc_ref.shape[0], block):
-                at = slice(r, r + block)
-                total = acc_ref[at, here] + dot(left_ref[at, :], buffer[:, cols])
-                staged[slot, at, :] = total.astype(bf16)
-            put(i, slot).start()
-
-    for i in (2 * count - 2, 2 * count - 1):
-        put(i, i % 2).wait()
+    def put(i):
+        columns = out_any.at[:, pl.ds(i * width, width)]
+        return pltpu.make_async_copy(staged.at[i % slots], columns, out_sems.at[i % slots])
+
+    block = hidden // 4
+    for i in range(2 * count):
+        if i >= slots:
+            put(i - slots).wait()
+        acc_ref, first = (acc_0, acc_1)[i // count], i % count * width
+        for r in range(0, hidden, block):
+            at = slice(r, r + block)
+            total = acc_ref[at, first : first + width] + dot(left_ref[at, :], buffer[:, i * width : (i + 1) * width])
+            staged[i % slots, at, :] = total.astype(bf16)
+        put(i).start()
+    for i in range(2 * count - slots, 2 * count):
+        put(i).wait()
 
 
 def after(value, *others):
@@ -398,7 +399,6 @@
     (p_other,) = partners(p_local, "dp", n_dp, (1,))
     p_chip = (p_local.astype(f32) + p_other.astype(f32)).astype(bf16)
     p_parts = along_xy(p_chip)
-    p_parts[0] = after(p_parts[0], x_first)
     p_total, gram, near_w, far_w = call(
         weigh,
         [like((rank, hidden), bf16), like((rank, rank), f32), like((2, rank, tokens), f32), like((2, rank, tokens), f32)],
@@ -443,21 +443,31 @@
         for k, m in enumerate(parts)
         if k
     ]
-    accs = []
-    for k, e_held in enumerate(held_errors):
-        accs += call(
-            functools.partial(accumulate, k * (features // 2)),
+    def add_tokens(k, cost, lane, base, spans, *sources):
+        count = sum(end - begin for begin, end in spans)
+        return call(
+            functools.partial(accumulate, k * (features // 2), lane, spans),
             [like((hidden, features // 2), f32)],
-            main_t, e_held, activations, x_first, x_second,
-            flops=KP,
-            in_specs=[vmem_spec, vmem_spec] + [anywhere] * 3,
-            scratch=[pltpu.VMEM((main, features // 2), bf16), pltpu.SemaphoreType.DMA((3,))],
-        )
+            main_t, base, *sources,
+            flops=cost,
+            in_specs=[vmem_spec, vmem_spec] + [anywhere] * len(sources),
+            scratch=[pltpu.VMEM((count, features // 2), bf16), pltpu.SemaphoreType.DMA((len(spans),))],
+        )[0]
+
+    early = 256 - tokens
+    accs = [
+        add_tokens(k, 0, 0, e_held, ((0, tokens), (0, early)), activations, x_first)
+        for k, e_held in enumerate(held_errors)
+    ]
     (mine,) = call(pack, [like((half, rows + 256), f32)], parts[0], *arrived, gram)
-    mine = after(mine, x_second)
+    mine = after(mine, *accs)
     z1, z2, z3 = along_t(mine)
     x_outer = move(x_first, [(1, 0), (2, 3)], mine)
     x_inner = move(activations, [(1, 2), (2, 1)], mine)
+    accs = [
+        add_tokens(k, KP, 256, acc, ((early, tokens), (0, tokens)), x_first, x_second)
+        for k, acc in enumerate(accs)
+    ]
     mine, gram = call(unpack, [like((half, rows), f32), like((rank, rank), f32)], mine, z1, z2, z3)
     (linv,) = call(invert_cholesky, [like((rank, rank), f32)], gram)
     near = [mine] + along_xy(mine)
@@ -477,9 +487,9 @@
         out_specs=[anywhere],
         scratch=[
             pltpu.VMEM((tokens + 3 * rank, features), bf16),
-            pltpu.VMEM((2, hidden, 640), bf16),
+            pltpu.VMEM((4, hidden, 256), bf16),
             pltpu.SemaphoreType.DMA((1,)),
-            pltpu.SemaphoreType.DMA((2,)),
+            pltpu.SemaphoreType.DMA((4,)),
         ],
     )
     return (new_error[None], new_factor.T)

time: 94.3 us -> 84.5 us (0.90); the launches traced: 92.8 us -> 84.2 us
  starting transfers between devices: 34.7 us -> 30.8 us
  Pallas kernels: 29.8 us -> 26.6 us
  waiting for transfers between devices: 23.5 us -> 22 us
    ppermute x22, waiting for transfers between devices: 10.1 us -> 17.4 us  [partners(): lax.ppermute(value, axis, [(i, i ^ k) for i in range(size)])]
    ppermute x4, waiting for transfers between devices: 9.03 us -> 3.98 us  [move(): return lax.ppermute(after(value, *when), 'tensor', perm)]
    ppermute x3, waiting for transfers between devices: 4.41 us -> 0.64 us  [body(): lax.ppermute(m, 'dp', [(i, i ^ 2 * k) for i in range(n_dp)])]
    ppermute x4, starting transfers between devices: 6.45 us -> 2.86 us  [move(): return lax.ppermute(after(value, *when), 'tensor', perm)]
    pallas_call x15 -> x17, Pallas kernels: 29.8 us -> 26.6 us  [call(): pl.pallas_call(kernel, out_shape=list(outs), in_specs=in_specs, out_specs...]
  transfers between devices with their start and end apart: 29 -> 29, of which waited for: 13 -> 12; matrix products, arithmetic and copies ran while one was open for 0% -> 0% of each run, Pallas kernels for 23% -> 24%
where the time goes in v4:
time: 84.5 us; the launch traced here: 84.2 us
  starting transfers between devices  30.8 us (36%)
  Pallas kernels  26.6 us (31%)
  waiting for transfers between devices  22 us (26%)
  local copies, waits for them, and re-layouts  2.7 us (3%)
  between operations  1.04 us (1%)
  other arithmetic  1 us (1%)
    pallas_call x17, Pallas kernels, call(): pl.pallas_call(kernel, out_shape=list(outs), in_specs=in_specs, out_specs...  26.6 us
    ppermute x22, starting transfers between devices, partners(): lax.ppermute(value, axis, [(i, i ^ k) for i in range(size)])  24.4 us
    ppermute x22, waiting for transfers between devices, partners(): lax.ppermute(value, axis, [(i, i ^ k) for i in range(size)])  17.4 us
    ppermute x4, waiting for transfers between devices, move(): return lax.ppermute(after(value, *when), 'tensor', perm)  3.98 us
    ppermute x3, starting transfers between devices, body(): lax.ppermute(m, 'dp', [(i, i ^ 2 * k) for i in range(n_dp)])  3.55 us
    ppermute x4, starting transfers between devices, move(): return lax.ppermute(after(value, *when), 'tensor', perm)  2.86 us
    unnamed x8, local copies, waits for them, and re-layouts  2.7 us
  transfers between devices with their start and end apart: 29, of which 12 were waited for; matrix products, arithmetic and copies ran while one was open for 0% of the time, Pallas kernels for 24%

profile of v4, /device:TPU:0, one launch (start us, length us, event | category | flops | bytes accessed | tf_op | source)
XLA Modules:
  0.0 84.2 jit_solution(12256686463659062074)
XLA Ops:
  0.6 0.9 %convert_bitcast_fusion.own = bf16[32,640]{1,0:T(8,128)(2,1)S(1)} fusion(f32[640,32]{0,1:T(8,128)} %param.7), kind=kLoop, calls=%fused_computation.1 | loop fusion | flops 20480 | bytes 122880 | tf_op jit(solution)/shard_map/convert_element_type | solution.py:364
  1.5 3.0 %collective-permute-start = (bf16[32,640]{1,0:T(8,128)(2,1)S(1)}, bf16[32,640]{1,0:T(8,128)(2,1)S(1)}, u32[]{:S(2)}, u32[]{:S(2)}) collective-permute-start(bf16[32,640]{1,0:T(8,128)(2,1)S(1)} %convert_bitcast_fusion.own), channel_id=1, source_target_pairs={{0,1},{1,0},{2,3},{3,2},{4,5},{5,4},{6,7},{7,6},{8,9},{9,8},{10,11... | collective-permute-start | bytes 122888 | tf_op jit(solution)/shard_map/ppermute | solution.py:341
  4.5 2.6 %collective-permute-start.1 = (bf16[32,640]{1,0:T(8,128)(2,1)S(1)}, bf16[32,640]{1,0:T(8,128)(2,1)S(1)}, u32[]{:S(2)}, u32[]{:S(2)}) collective-permute-start(bf16[32,640]{1,0:T(8,128)(2,1)S(1)} %convert_bitcast_fusion.own), channel_id=1, source_target_pairs={{0,2},{1,3},{2,0},{3,1},{4,6},{5,7},{6,4},{7,5},{8,10},{9,11},{10,... | collective-permute-start | bytes 122888 | tf_op jit(solution)/shard_map/ppermute | solution.py:341
  7.1 0.1 pad_add_fusion.place
  7.2 1.6 %copy-done = bf16[576,1728]{1,0:T(8,128)(2,1)S(1)} copy-done((bf16[576,1728]{1,0:T(8,128)(2,1)S(1)}, bf16[576,1728]{1,0:T(8,128)(2,1)}, u32[]{:S(2)}) %copy-start) | copy-done | bytes 1990680
  8.8 1.3 %arrange.1 = (bf16[1728,432]{1,0:T(8,128)(2,1)S(1)}, bf16[1728,144]{1,0:T(8,128)(2,1)S(1)}) custom-call(s32[3]{0:T(128)S(1)} %pad_add_fusion.place, bf16[576,1728]{1,0:T(8,128)(2,1)S(1)} %copy-done), custom_call_target="tpu_custom_call" | custom-call | bytes 3981324 | tf_op jit(solution)/shard_map/arrange/pallas_call | solution.py:83
  10.1 0.0 collective-permute-done.n1
  10.1 0.1 collective-permute-done.1.n2
  10.2 2.7 %collective-permute-done.2.n3 = bf16[32,640]{1,0:T(8,128)(2,1)S(1)} collective-permute-done((bf16[32,640]{1,0:T(8,128)(2,1)S(1)}, bf16[32,640]{1,0:T(8,128)(2,1)S(1)}, u32[]{:S(2)}, u32[]{:S(2)}) %collective-permute-start.2) | collective-permute-done | bytes 40992 | tf_op jit(solution)/shard_map/ppermute | solution.py:341
  12.9 1.1 %copy-done.2 = bf16[144,2560]{1,0:T(8,128)(2,1)S(1)} copy-done((bf16[144,2560]{1,0:T(8,128)(2,1)S(1)}, bf16[144,2560]{1,0:T(8,128)(2,1)}, u32[]{:S(2)}) %copy-start.2) | copy-done | bytes 737304
  14.1 0.9 %project.1 = (bf16[4,32,640]{2,1,0:T(8,128)(2,1)S(1)}, f32[32,144]{1,0:T(8,128)S(1)}) custom-call(s32[3]{0:T(128)S(1)} %pad_add_fusion.place, bf16[32,640]{1,0:T(8,128)(2,1)S(1)} %convert_bitcast_fusion.own, bf16[32,640]{1,0:T(8,128)(2,1)S(1)} %collective-permute-done.n1, bf16[32,640]{1,0:T(8,128)(2,1)S(1)} %collective-permute-done.1.n2, ...), custom_call_target="tpu_custom_call" | custom-call | bytes 1083404 | tf_op jit(solution)/shard_map/project/pallas_call | solution.py:83
  14.9 0.0 collective-permute-start.3
  15.0 1.6 %collective-permute-start.4 = (f32[32,144]{1,0:T(8,128)S(1)}, f32[32,144]{1,0:T(8,128)S(1)}, u32[]{:S(2)}, u32[]{:S(2)}) collective-permute-start(f32[32,144]{1,0:T(8,128)S(1)} %get-tuple-element.42.own), channel_id=1, source_target_pairs={{0,2},{1,3},{2,0},{3,1},{4,6},{5,7},{6,4},{7,5},{8,10},{9,11},{10,... | collective-permute-start | bytes 55304 | tf_op jit(solution)/shard_map/ppermute | solution.py:341
  16.6 2.8 %collective-permute-start.5 = (f32[32,144]{1,0:T(8,128)S(1)}, f32[32,144]{1,0:T(8,128)S(1)}, u32[]{:S(2)}, u32[]{:S(2)}) collective-permute-start(f32[32,144]{1,0:T(8,128)S(1)} %get-tuple-element.42.own), channel_id=1, source_target_pairs={{0,3},{1,2},{2,1},{3,0},{4,7},{5,6},{6,5},{7,4},{8,11},{9,10},{10,... | collective-permute-start | bytes 55304 | tf_op jit(solution)/shard_map/ppermute | solution.py:341
  19.4 5.0 %error_left.1 = (f32[32,1728]{1,0:T(8,128)S(1)}, bf16[1728,1280]{1,0:T(8,128)(2,1)S(1)}, bf16[1728,1280]{1,0:T(8,128)(2,1)S(1)}) custom-call(bf16[4,32,640]{2,1,0:T(8,128)(2,1)S(1)} %get-tuple-element.40.q_ref, bf16[1728,2560]{1,0:T(8,128)(2,1)} %bitcast.9), custom_call_target="tpu_custom_call" | custom-call | bytes 18079744 | tf_op jit(solution)/shard_map/error_left/pallas_call | solution.py:83
  24.4 0.0 collective-permute-done.3.n1
  24.4 0.0 collective-permute-done.4.n2
  24.5 0.1 collective-permute-start.11
  24.6 1.0 %left_factor.1 = bf16[32,1728]{1,0:T(8,128)(2,1)S(1)} custom-call(s32[3]{0:T(128)S(1)} %pad_add_fusion.place, f32[32,1728]{1,0:T(8,128)S(1)} %get-tuple-element.41.eq_ref, f32[32,144]{1,0:T(8,128)S(1)} %get-tuple-element.42.own, f32[32,144]{1,0:T(8,128)S(1)} %collective-permute-done.3.n1, f32[32,144]{1,0:T(8,128)S(1)} %collective-permute-done.4.n2, ...), custom_call_target="tpu_custom_call" | custom-call | bytes 2396172 | tf_op jit(solution)/shard_map/left_factor/pallas_call | solution.py:83
  25.5 0.1 collective-permute-start.6
  25.6 1.3 %collective-permute-done.6 = bf16[32,1728]{1,0:T(8,128)(2,1)S(1)} collective-permute-done((bf16[32,1728]{1,0:T(8,128)(2,1)S(1)}, bf16[32,1728]{1,0:T(8,128)(2,1)S(1)}, u32[]{:S(2)}, u32[]{:S(2)}) %collective-permute-start.6) | collective-permute-done | bytes 110624 | tf_op jit(solution)/shard_map/ppermute | solution.py:341
  26.9 1.6 %collective-permute-start.7 = (bf16[32,1728]{1,0:T(8,128)(2,1)S(1)}, bf16[32,1728]{1,0:T(8,128)(2,1)S(1)}, u32[]{:S(2)}, u32[]{:S(2)}) collective-permute-start(bf16[32,1728]{1,0:T(8,128)(2,1)S(1)} %add_convert_fusion.own), channel_id=1, source_target_pairs={{0,8},{4,12},{8,0},{12,4},{16,24},{20,28},{24,16},{28,20},{1,9},{5... | collective-permute-start | bytes 331784 | tf_op jit(solution)/shard_map/ppermute | solution.py:341
  28.5 1.5 %collective-permute-start.8 = (bf16[32,1728]{1,0:T(8,128)(2,1)S(1)}, bf16[32,1728]{1,0:T(8,128)(2,1)S(1)}, u32[]{:S(2)}, u32[]{:S(2)}) collective-permute-start(bf16[32,1728]{1,0:T(8,128)(2,1)S(1)} %add_convert_fusion.own), channel_id=1, source_target_pairs={{0,16},{4,20},{8,24},{12,28},{16,0},{20,4},{24,8},{28,12},{1,17},{... | collective-permute-start | bytes 331784 | tf_op jit(solution)/shard_map/ppermute | solution.py:341
  30.0 0.5 collective-permute-start.9
  30.5 1.7 %collective-permute-done.7.n1 = bf16[32,1728]{1,0:T(8,128)(2,1)S(1)} collective-permute-done((bf16[32,1728]{1,0:T(8,128)(2,1)S(1)}, bf16[32,1728]{1,0:T(8,128)(2,1)S(1)}, u32[]{:S(2)}, u32[]{:S(2)}) %collective-permute-start.7) | collective-permute-done | bytes 110624 | tf_op jit(solution)/shard_map/ppermute | solution.py:341
  32.2 3.7 %collective-permute-done.8.n2 = bf16[32,1728]{1,0:T(8,128)(2,1)S(1)} collective-permute-done((bf16[32,1728]{1,0:T(8,128)(2,1)S(1)}, bf16[32,1728]{1,0:T(8,128)(2,1)S(1)}, u32[]{:S(2)}, u32[]{:S(2)}) %collective-permute-start.8) | collective-permute-done | bytes 110624 | tf_op jit(solution)/shard_map/ppermute | solution.py:341
  35.9 1.3 %weigh.1 = (bf16[32,1728]{1,0:T(8,128)(2,1)S(1)}, f32[32,32]{1,0:T(8,128)S(1)}, f32[2,32,144]{2,1,0:T(8,128)S(1)}, f32[2,32,144]{2,1,0:T(8,128)S(1)}) custom-call(s32[3]{0:T(128)S(1)} %pad_add_fusion.place, bf16[32,1728]{1,0:T(8,128)(2,1)S(1)} %add_convert_fusion.own, bf16[32,1728]{1,0:T(8,128)(2,1)S(1)} %collective-permute-done.7.n1, ...), custom_call_target="tpu_custom_call" | custom-call | bytes 2621452 | tf_op jit(solution)/shard_map/weigh/pallas_call | solution.py:83
  37.1 1.6 %collective-permute-start.10 = (f32[2,32,144]{2,1,0:T(8,128)S(1)}, f32[2,32,144]{2,1,0:T(8,128)S(1)}, u32[]{:S(2)}, u32[]{:S(2)}) collective-permute-start(f32[2,32,144]{2,1,0:T(8,128)S(1)} %get-tuple-element.45), channel_id=1, source_target_pairs={{0,3},{1,2},{2,1},{3,0},{4,7},{5,6},{6,5},{7,4},{8,11},{9,10},{10,... | collective-permute-start | bytes 110600 | tf_op jit(solution)/shard_map/ppermute | solution.py:341
  38.7 0.6 collective-permute-start.26
  39.4 1.4 %error_right.1.te_ref = f32[32,2560]{1,0:T(8,128)S(1)} custom-call(bf16[32,1728]{1,0:T(8,128)(2,1)S(1)} %get-tuple-element.46.p_ref, bf16[1728,1280]{1,0:T(8,128)(2,1)S(1)} %get-tuple-element.47.e_0.base_ref, bf16[1728,1280]{1,0:T(8,128)(2,1)S(1)} %get-tuple-element.48.e_1.base_ref), custom_call_target="tpu_custom_call" | custom-call | bytes 9285632 | tf_op jit(solution)/shard_map/error_right/pallas_call | solution.py:83
  40.8 3.3 %collective-permute-done.10.got_ref = f32[2,32,144]{2,1,0:T(8,128)S(1)} collective-permute-done((f32[2,32,144]{2,1,0:T(8,128)S(1)}, f32[2,32,144]{2,1,0:T(8,128)S(1)}, u32[]{:S(2)}, u32[]{:S(2)}) %collective-permute-start.10) | collective-permute-done | bytes 36896 | tf_op jit(solution)/shard_map/ppermute | solution.py:341
  44.0 0.0 collective-permute-done.11.x_first.rest_1_.rest_0_
  44.0 0.9 %right_term.1 = (f32[16,2560]{1,0:T(8,128)S(1)}, f32[16,2560]{1,0:T(8,128)S(1)}) custom-call(s32[3]{0:T(128)S(1)} %pad_add_fusion.place, f32[2,32,144]{2,1,0:T(8,128)S(1)} %get-tuple-element.44.near_ref, f32[2,32,144]{2,1,0:T(8,128)S(1)} %collective-permute-done.10.got_ref, f32[32,2560]{1,0:T(8,128)S(1)} %error_right.1.te_ref, ...), custom_call_target="tpu_custom_call" | custom-call | bytes 2203660 | tf_op jit(solution)/shard_map/right_term/pallas_call | solution.py:83
  45.0 0.1 collective-permute-start.12
  45.0 1.4 %collective-permute-done.12.got = f32[16,2560]{1,0:T(8,128)S(1)} collective-permute-done((f32[16,2560]{1,0:T(8,128)S(1)}, f32[16,2560]{1,0:T(8,128)S(1)}, u32[]{:S(2)}, u32[]{:S(2)}) %collective-permute-start.12) | collective-permute-done | bytes 163872 | tf_op jit(solution)/shard_map/ppermute | solution.py:341
  46.4 0.6 cut.1
  47.0 1.2 %collective-permute-start.13 = (f32[16,640]{1,0:T(8,128)S(1)}, f32[16,640]{1,0:T(8,128)S(1)}, u32[]{:S(2)}, u32[]{:S(2)}) collective-permute-start(f32[16,640]{1,0:T(8,128)S(1)} %get-tuple-element.55), channel_id=1, source_target_pairs={{0,8},{4,12},{8,0},{12,4},{16,24},{20,28},{24,16},{28,20},{1,9},{5... | collective-permute-start | bytes 122888 | tf_op jit(solution)/shard_map/ppermute | solution.py:442
  48.2 0.9 %collective-permute-start.14 = (f32[16,640]{1,0:T(8,128)S(1)}, f32[16,640]{1,0:T(8,128)S(1)}, u32[]{:S(2)}, u32[]{:S(2)}) collective-permute-start(f32[16,640]{1,0:T(8,128)S(1)} %get-tuple-element.56), channel_id=1, source_target_pairs={{0,16},{4,20},{8,24},{12,28},{16,0},{20,4},{24,8},{28,12},{1,17},{... | collective-permute-start | bytes 122888 | tf_op jit(solution)/shard_map/ppermute | solution.py:442
  49.1 1.4 %collective-permute-start.15 = (f32[16,640]{1,0:T(8,128)S(1)}, f32[16,640]{1,0:T(8,128)S(1)}, u32[]{:S(2)}, u32[]{:S(2)}) collective-permute-start(f32[16,640]{1,0:T(8,128)S(1)} %get-tuple-element.57), channel_id=1, source_target_pairs={{0,24},{4,28},{8,16},{12,20},{16,8},{20,12},{24,0},{28,4},{1,25},{... | collective-permute-start | bytes 122888 | tf_op jit(solution)/shard_map/ppermute | solution.py:442
  50.6 1.4 %accumulate.4.base_ref = f32[1728,1280]{1,0:T(8,128)S(1)} custom-call(bf16[1728,432]{1,0:T(8,128)(2,1)S(1)} %get-tuple-element.36.main_ref, bf16[1728,1280]{1,0:T(8,128)(2,1)S(1)} %get-tuple-element.47.e_0.base_ref, bf16[144,2560]{1,0:T(8,128)(2,1)S(1)} %copy-done.3, bf16[144,2560]{1,0:T(8,128)(2,1)S(1)} %collective-permute-done.11.x_first.rest_1_.rest_0_), custom_call_target="tpu_custom_call" | custom-call | bytes 16238592 | tf_op jit(solution)/shard_map/accumulate/pallas_call | solution.py:83
  52.0 1.4 %accumulate.5.base_ref = f32[1728,1280]{1,0:T(8,128)S(1)} custom-call(bf16[1728,432]{1,0:T(8,128)(2,1)S(1)} %get-tuple-element.36.main_ref, bf16[1728,1280]{1,0:T(8,128)(2,1)S(1)} %get-tuple-element.48.e_1.base_ref, bf16[144,2560]{1,0:T(8,128)(2,1)S(1)} %copy-done.3, bf16[144,2560]{1,0:T(8,128)(2,1)S(1)} %collective-permute-done.11.x_first.rest_1_.rest_0_), custom_call_target="tpu_custom_call" | custom-call | bytes 16238592 | tf_op jit(solution)/shard_map/accumulate/pallas_call | solution.py:83
  53.4 0.0 collective-permute-done.13.b
  53.4 0.6 collective-permute-done.15.d
  54.0 0.9 %collective-permute-start.16 = (f32[16,896]{1,0:T(8,128)S(1)}, f32[16,896]{1,0:T(8,128)S(1)}, u32[]{:S(2)}, u32[]{:S(2)}) collective-permute-start(f32[16,896]{1,0:T(8,128)S(1)} %pack.1.a), channel_id=1, source_target_pairs={{0,1},{1,0},{2,3},{3,2},{4,5},{5,4},{6,7},{7,6},{8,9},{9,8},{10,11... | collective-permute-start | bytes 172040 | tf_op jit(solution)/shard_map/ppermute | solution.py:341
  54.9 1.7 %collective-permute-start.17 = (f32[16,896]{1,0:T(8,128)S(1)}, f32[16,896]{1,0:T(8,128)S(1)}, u32[]{:S(2)}, u32[]{:S(2)}) collective-permute-start(f32[16,896]{1,0:T(8,128)S(1)} %pack.1.a), channel_id=1, source_target_pairs={{0,2},{1,3},{2,0},{3,1},{4,6},{5,7},{6,4},{7,5},{8,10},{9,11},{10,... | collective-permute-start | bytes 172040 | tf_op jit(solution)/shard_map/ppermute | solution.py:341
  56.6 1.9 %collective-permute-start.18 = (f32[16,896]{1,0:T(8,128)S(1)}, f32[16,896]{1,0:T(8,128)S(1)}, u32[]{:S(2)}, u32[]{:S(2)}) collective-permute-start(f32[16,896]{1,0:T(8,128)S(1)} %pack.1.a), channel_id=1, source_target_pairs={{0,3},{1,2},{2,1},{3,0},{4,7},{5,6},{6,5},{7,4},{8,11},{9,10},{10,... | collective-permute-start | bytes 172040 | tf_op jit(solution)/shard_map/ppermute | solution.py:341
  58.5 1.3 %collective-permute-start.27 = (bf16[144,2560]{1,0:T(8,128)(2,1)S(1)}, bf16[144,2560]{1,0:T(8,128)(2,1)S(1)}, u32[]{:S(2)}, u32[]{:S(2)}) collective-permute-start(bf16[144,2560]{1,0:T(8,128)(2,1)S(1)} %collective-permute-done.11.x_first.rest_1_.rest_0_), channel_id=1, source_target_pairs={{1,0},{2,3},{5,4},{6,7},{9,8},{10,11},{13,12},{14,15},{17,16},{18,... | collective-permute-start | bytes 2211848 | tf_op jit(solution)/shard_map/ppermute | solution.py:362
  59.8 0.9 %collective-permute-done.16.b = f32[16,896]{1,0:T(8,128)S(1)} collective-permute-done((f32[16,896]{1,0:T(8,128)S(1)}, f32[16,896]{1,0:T(8,128)S(1)}, u32[]{:S(2)}, u32[]{:S(2)}) %collective-permute-start.16) | collective-permute-done | bytes 57376 | tf_op jit(solution)/shard_map/ppermute | solution.py:341
  60.7 0.9 %collective-permute-start.28 = (bf16[144,2560]{1,0:T(8,128)(2,1)S(1)}, bf16[144,2560]{1,0:T(8,128)(2,1)S(1)}, u32[]{:S(2)}, u32[]{:S(2)}) collective-permute-start(bf16[144,2560]{1,0:T(8,128)(2,1)S(1)} %copy-done.3), channel_id=1, source_target_pairs={{1,2},{2,1},{5,6},{6,5},{9,10},{10,9},{13,14},{14,13},{17,18},{18,... | collective-permute-start | bytes 2211848 | tf_op jit(solution)/shard_map/ppermute | solution.py:362
  61.6 1.8 %collective-permute-done.17.c = f32[16,896]{1,0:T(8,128)S(1)} collective-permute-done((f32[16,896]{1,0:T(8,128)S(1)}, f32[16,896]{1,0:T(8,128)S(1)}, u32[]{:S(2)}, u32[]{:S(2)}) %collective-permute-start.17) | collective-permute-done | bytes 57376 | tf_op jit(solution)/shard_map/ppermute | solution.py:341
  63.4 1.5 %collective-permute-start.19 = (f32[16,640]{1,0:T(8,128)S(1)}, f32[16,640]{1,0:T(8,128)S(1)}, u32[]{:S(2)}, u32[]{:S(2)}) collective-permute-start(f32[16,640]{1,0:T(8,128)S(1)} %get-tuple-element.62.a0), channel_id=1, source_target_pairs={{0,8},{4,12},{8,0},{12,4},{16,24},{20,28},{24,16},{28,20},{1,9},{5... | collective-permute-start | bytes 122888 | tf_op jit(solution)/shard_map/ppermute | solution.py:341
  64.9 1.1 %collective-permute-start.20 = (f32[16,640]{1,0:T(8,128)S(1)}, f32[16,640]{1,0:T(8,128)S(1)}, u32[]{:S(2)}, u32[]{:S(2)}) collective-permute-start(f32[16,640]{1,0:T(8,128)S(1)} %get-tuple-element.62.a0), channel_id=1, source_target_pairs={{0,16},{4,20},{8,24},{12,28},{16,0},{20,4},{24,8},{28,12},{1,17},{... | collective-permute-start | bytes 122888 | tf_op jit(solution)/shard_map/ppermute | solution.py:341
  66.0 0.9 %collective-permute-start.21 = (f32[16,640]{1,0:T(8,128)S(1)}, f32[16,640]{1,0:T(8,128)S(1)}, u32[]{:S(2)}, u32[]{:S(2)}) collective-permute-start(f32[16,640]{1,0:T(8,128)S(1)} %get-tuple-element.62.a0), channel_id=1, source_target_pairs={{0,24},{4,28},{8,16},{12,20},{16,8},{20,12},{24,0},{28,4},{1,25},{... | collective-permute-start | bytes 122888 | tf_op jit(solution)/shard_map/ppermute | solution.py:341
  67.0 0.5 collective-permute-done.19.a1
  67.5 1.4 %accumulate.6.acc_0 = f32[1728,1280]{1,0:T(8,128)S(1)} custom-call(bf16[1728,432]{1,0:T(8,128)(2,1)S(1)} %get-tuple-element.36.main_ref, f32[1728,1280]{1,0:T(8,128)S(1)} %accumulate.4.base_ref, bf16[144,2560]{1,0:T(8,128)(2,1)S(1)} %collective-permute-done.11.x_first.rest_1_.rest_0_, bf16[144,2560]{1,0:T(8,128)(2,1)S(1)} %collective-permute-done.26.rest_1_), custom_call_target="tpu_custom_call" | custom-call | flops 3500000000 | bytes 20662272 | tf_op jit(solution)/shard_map/accumulate/pallas_call | solution.py:83
  68.9 1.7 %invert_cholesky.1.linv = f32[32,32]{1,0:T(8,128)S(1)} custom-call(f32[32,32]{1,0:T(8,128)S(1)} %get-tuple-element.60.g_ref), custom_call_target="tpu_custom_call" | custom-call | bytes 8192 | tf_op jit(solution)/shard_map/invert_cholesky/pallas_call | solution.py:83
  70.5 0.0 collective-permute-done.20.a2
  70.6 0.6 collective-permute-start.23
  71.1 0.1 collective-permute-start.24
  71.2 0.4 collective-permute-start.25
  71.6 1.4 %accumulate.7.acc_1 = f32[1728,1280]{1,0:T(8,128)S(1)} custom-call(bf16[1728,432]{1,0:T(8,128)(2,1)S(1)} %get-tuple-element.36.main_ref, f32[1728,1280]{1,0:T(8,128)S(1)} %accumulate.5.base_ref, bf16[144,2560]{1,0:T(8,128)(2,1)S(1)} %collective-permute-done.11.x_first.rest_1_.rest_0_, bf16[144,2560]{1,0:T(8,128)(2,1)S(1)} %collective-permute-done.26.rest_1_), custom_call_target="tpu_custom_call" | custom-call | flops 3500000000 | bytes 20662272 | tf_op jit(solution)/shard_map/accumulate/pallas_call | solution.py:83
  73.0 1.5 %finish.1 = (f32[32,640]{1,0:T(8,128)}, bf16[1728,240]{1,0:T(8,128)(2,1)S(1)}, bf16[96,2560]{1,0:T(8,128)(2,1)S(1)}) custom-call(s32[3]{0:T(128)S(1)} %pad_add_fusion.place, f32[32,32]{1,0:T(8,128)S(1)} %invert_cholesky.1.linv, bf16[32,1728]{1,0:T(8,128)(2,1)S(1)} %get-tuple-element.46.p_ref, bf16[1728,144]{1,0:T(8,128)(2,1)S(1)} %get-tuple-element.61.rest_ref, ...), custom_call_target="tpu_custom_call" | custom-call | bytes 2342924 | tf_op jit(solution)/shard_map/finish/pallas_call | solution.py:83
  74.5 4.0 %collective-permute-done.27.outer = bf16[144,2560]{1,0:T(8,128)(2,1)S(1)} collective-permute-done((bf16[144,2560]{1,0:T(8,128)(2,1)S(1)}, bf16[144,2560]{1,0:T(8,128)(2,1)S(1)}, u32[]{:S(2)}, u32[]{:S(2)}) %collective-permute-start.27) | collective-permute-done | bytes 737312 | tf_op jit(solution)/shard_map/ppermute | solution.py:362
  78.5 5.5 %rebuild.1 = bf16[1728,2560]{1,0:T(8,128)(2,1)} custom-call(s32[3]{0:T(128)S(1)} %pad_add_fusion.place, bf16[1728,240]{1,0:T(8,128)(2,1)S(1)} %get-tuple-element.64.left_ref, bf16[96,2560]{1,0:T(8,128)(2,1)S(1)} %get-tuple-element.65.right_ref, f32[1728,1280]{1,0:T(8,128)S(1)} %accumulate.6.acc_0, f32[1728,1280]{1,0:T(8,128)S(1)} %accumulate.7.acc_1, ...), custom_call_target="tpu_custom_call" | custom-call | bytes 29337612 | tf_op jit(solution)/shard_map/rebuild/pallas_call | solution.py:83
  (22 shorter events, 0.1 us)
Async XLA Ops:
  1.5 8.6 %collective-permute-start = (bf16[32,640]{1,0:T(8,128)(2,1)S(1)}, bf16[32,640]{1,0:T(8,128)(2,1)S(1)}, u32[]{:S(2)}, u32[]{:S(2)}) collective-permute-start(bf16[32,640]{1,0:T(8,128)(2,1)S(1)} %convert_bitcast_fusion.own), channel_id=1, source_target_pairs={{0,1},{1,0},{2,3},{3,2},{4,5},{5,4},{6,7},{7,6},{8,9},{9,8},{10,11... | collective-permute-start | bytes 122888 | tf_op jit(solution)/shard_map/ppermute | solution.py:341
  4.5 5.7 %collective-permute-start.1 = (bf16[32,640]{1,0:T(8,128)(2,1)S(1)}, bf16[32,640]{1,0:T(8,128)(2,1)S(1)}, u32[]{:S(2)}, u32[]{:S(2)}) collective-permute-start(bf16[32,640]{1,0:T(8,128)(2,1)S(1)} %convert_bitcast_fusion.own), channel_id=1, source_target_pairs={{0,2},{1,3},{2,0},{3,1},{4,6},{5,7},{6,4},{7,5},{8,10},{9,11},{10,... | collective-permute-start | bytes 122888 | tf_op jit(solution)/shard_map/ppermute | solution.py:341
  7.1 5.8 %collective-permute-start.2 = (bf16[32,640]{1,0:T(8,128)(2,1)S(1)}, bf16[32,640]{1,0:T(8,128)(2,1)S(1)}, u32[]{:S(2)}, u32[]{:S(2)}) collective-permute-start(bf16[32,640]{1,0:T(8,128)(2,1)S(1)} %convert_bitcast_fusion.own), channel_id=1, source_target_pairs={{0,3},{1,2},{2,1},{3,0},{4,7},{5,6},{6,5},{7,4},{8,11},{9,10},{10,... | collective-permute-start | bytes 122888 | tf_op jit(solution)/shard_map/ppermute | solution.py:341
  7.2 1.6 %copy-start = (bf16[576,1728]{1,0:T(8,128)(2,1)S(1)}, bf16[576,1728]{1,0:T(8,128)(2,1)}, u32[]{:S(2)}) copy-start(bf16[576,1728]{1,0:T(8,128)(2,1)} %dy_ref.5) | copy-start | bytes 5971972
  8.8 15.7 %copy-start.1 = (bf16[576,1728]{1,0:T(8,128)(2,1)S(1)}, bf16[576,1728]{1,0:T(8,128)(2,1)}, u32[]{:S(2)}) copy-start(bf16[576,1728]{1,0:T(8,128)(2,1)} %dy_ref.5) | copy-start | bytes 5971972
  12.9 1.1 %copy-start.2 = (bf16[144,2560]{1,0:T(8,128)(2,1)S(1)}, bf16[144,2560]{1,0:T(8,128)(2,1)}, u32[]{:S(2)}) copy-start(bf16[144,2560]{1,0:T(8,128)(2,1)} %rest_0_.3) | copy-start | bytes 2211844
  14.1 10.4 %copy-start.3 = (bf16[144,2560]{1,0:T(8,128)(2,1)S(1)}, bf16[144,2560]{1,0:T(8,128)(2,1)}, u32[]{:S(2)}) copy-start(bf16[144,2560]{1,0:T(8,128)(2,1)} %rest_0_.3) | copy-start | bytes 2211844
  14.9 9.5 %collective-permute-start.3 = (f32[32,144]{1,0:T(8,128)S(1)}, f32[32,144]{1,0:T(8,128)S(1)}, u32[]{:S(2)}, u32[]{:S(2)}) collective-permute-start(f32[32,144]{1,0:T(8,128)S(1)} %get-tuple-element.42.own), channel_id=1, source_target_pairs={{0,1},{1,0},{2,3},{3,2},{4,5},{5,4},{6,7},{7,6},{8,9},{9,8},{10,11... | collective-permute-start | bytes 55304 | tf_op jit(solution)/shard_map/ppermute | solution.py:341
  15.0 9.4 %collective-permute-start.4 = (f32[32,144]{1,0:T(8,128)S(1)}, f32[32,144]{1,0:T(8,128)S(1)}, u32[]{:S(2)}, u32[]{:S(2)}) collective-permute-start(f32[32,144]{1,0:T(8,128)S(1)} %get-tuple-element.42.own), channel_id=1, source_target_pairs={{0,2},{1,3},{2,0},{3,1},{4,6},{5,7},{6,4},{7,5},{8,10},{9,11},{10,... | collective-permute-start | bytes 55304 | tf_op jit(solution)/shard_map/ppermute | solution.py:341
  16.6 7.9 %collective-permute-start.5 = (f32[32,144]{1,0:T(8,128)S(1)}, f32[32,144]{1,0:T(8,128)S(1)}, u32[]{:S(2)}, u32[]{:S(2)}) collective-permute-start(f32[32,144]{1,0:T(8,128)S(1)} %get-tuple-element.42.own), channel_id=1, source_target_pairs={{0,3},{1,2},{2,1},{3,0},{4,7},{5,6},{6,5},{7,4},{8,11},{9,10},{10,... | collective-permute-start | bytes 55304 | tf_op jit(solution)/shard_map/ppermute | solution.py:341
  24.5 19.6 %collective-permute-start.11 = (bf16[144,2560]{1,0:T(8,128)(2,1)S(1)}, bf16[144,2560]{1,0:T(8,128)(2,1)S(1)}, u32[]{:S(2)}, u32[]{:S(2)}) collective-permute-start(bf16[144,2560]{1,0:T(8,128)(2,1)S(1)} %copy-done.3), channel_id=1, source_target_pairs={{0,2},{2,3},{3,1},{1,0},{4,6},{6,7},{7,5},{5,4},{8,10},{10,11},{11... | collective-permute-start | bytes 2211848 | tf_op jit(solution)/shard_map/ppermute | solution.py:362
  25.5 1.4 %collective-permute-start.6 = (bf16[32,1728]{1,0:T(8,128)(2,1)S(1)}, bf16[32,1728]{1,0:T(8,128)(2,1)S(1)}, u32[]{:S(2)}, u32[]{:S(2)}) collective-permute-start(bf16[32,1728]{1,0:T(8,128)(2,1)S(1)} %left_factor.1), channel_id=1, source_target_pairs={{0,4},{4,0},{8,12},{12,8},{16,20},{20,16},{24,28},{28,24},{1,5},{5... | collective-permute-start | bytes 331784 | tf_op jit(solution)/shard_map/ppermute | solution.py:341
  26.9 5.3 %collective-permute-start.7 = (bf16[32,1728]{1,0:T(8,128)(2,1)S(1)}, bf16[32,1728]{1,0:T(8,128)(2,1)S(1)}, u32[]{:S(2)}, u32[]{:S(2)}) collective-permute-start(bf16[32,1728]{1,0:T(8,128)(2,1)S(1)} %add_convert_fusion.own), channel_id=1, source_target_pairs={{0,8},{4,12},{8,0},{12,4},{16,24},{20,28},{24,16},{28,20},{1,9},{5... | collective-permute-start | bytes 331784 | tf_op jit(solution)/shard_map/ppermute | solution.py:341
  28.5 7.4 %collective-permute-start.8 = (bf16[32,1728]{1,0:T(8,128)(2,1)S(1)}, bf16[32,1728]{1,0:T(8,128)(2,1)S(1)}, u32[]{:S(2)}, u32[]{:S(2)}) collective-permute-start(bf16[32,1728]{1,0:T(8,128)(2,1)S(1)} %add_convert_fusion.own), channel_id=1, source_target_pairs={{0,16},{4,20},{8,24},{12,28},{16,0},{20,4},{24,8},{28,12},{1,17},{... | collective-permute-start | bytes 331784 | tf_op jit(solution)/shard_map/ppermute | solution.py:341
  30.0 5.9 %collective-permute-start.9 = (bf16[32,1728]{1,0:T(8,128)(2,1)S(1)}, bf16[32,1728]{1,0:T(8,128)(2,1)S(1)}, u32[]{:S(2)}, u32[]{:S(2)}) collective-permute-start(bf16[32,1728]{1,0:T(8,128)(2,1)S(1)} %add_convert_fusion.own), channel_id=1, source_target_pairs={{0,24},{4,28},{8,16},{12,20},{16,8},{20,12},{24,0},{28,4},{1,25},{... | collective-permute-start | bytes 331784 | tf_op jit(solution)/shard_map/ppermute | solution.py:341
  37.1 6.9 %collective-permute-start.10 = (f32[2,32,144]{2,1,0:T(8,128)S(1)}, f32[2,32,144]{2,1,0:T(8,128)S(1)}, u32[]{:S(2)}, u32[]{:S(2)}) collective-permute-start(f32[2,32,144]{2,1,0:T(8,128)S(1)} %get-tuple-element.45), channel_id=1, source_target_pairs={{0,3},{1,2},{2,1},{3,0},{4,7},{5,6},{6,5},{7,4},{8,11},{9,10},{10,... | collective-permute-start | bytes 110600 | tf_op jit(solution)/shard_map/ppermute | solution.py:341
  38.7 27.3 %collective-permute-start.26 = (bf16[144,2560]{1,0:T(8,128)(2,1)S(1)}, bf16[144,2560]{1,0:T(8,128)(2,1)S(1)}, u32[]{:S(2)}, u32[]{:S(2)}) collective-permute-start(bf16[144,2560]{1,0:T(8,128)(2,1)S(1)} %copy-done.3), channel_id=1, source_target_pairs={{0,1},{1,3},{3,2},{2,0},{4,5},{5,7},{7,6},{6,4},{8,9},{9,11},{11,1... | collective-permute-start | bytes 2211848 | tf_op jit(solution)/shard_map/ppermute | solution.py:362
  45.0 1.5 %collective-permute-start.12 = (f32[16,2560]{1,0:T(8,128)S(1)}, f32[16,2560]{1,0:T(8,128)S(1)}, u32[]{:S(2)}, u32[]{:S(2)}) collective-permute-start(f32[16,2560]{1,0:T(8,128)S(1)} %get-tuple-element.53), channel_id=1, source_target_pairs={{0,4},{4,0},{8,12},{12,8},{16,20},{20,16},{24,28},{28,24},{1,5},{5... | collective-permute-start | bytes 491528 | tf_op jit(solution)/shard_map/ppermute | solution.py:341
  47.0 6.4 %collective-permute-start.13 = (f32[16,640]{1,0:T(8,128)S(1)}, f32[16,640]{1,0:T(8,128)S(1)}, u32[]{:S(2)}, u32[]{:S(2)}) collective-permute-start(f32[16,640]{1,0:T(8,128)S(1)} %get-tuple-element.55), channel_id=1, source_target_pairs={{0,8},{4,12},{8,0},{12,4},{16,24},{20,28},{24,16},{28,20},{1,9},{5... | collective-permute-start | bytes 122888 | tf_op jit(solution)/shard_map/ppermute | solution.py:442
  48.2 5.2 %collective-permute-start.14 = (f32[16,640]{1,0:T(8,128)S(1)}, f32[16,640]{1,0:T(8,128)S(1)}, u32[]{:S(2)}, u32[]{:S(2)}) collective-permute-start(f32[16,640]{1,0:T(8,128)S(1)} %get-tuple-element.56), channel_id=1, source_target_pairs={{0,16},{4,20},{8,24},{12,28},{16,0},{20,4},{24,8},{28,12},{1,17},{... | collective-permute-start | bytes 122888 | tf_op jit(solution)/shard_map/ppermute | solution.py:442
  49.1 4.9 %collective-permute-start.15 = (f32[16,640]{1,0:T(8,128)S(1)}, f32[16,640]{1,0:T(8,128)S(1)}, u32[]{:S(2)}, u32[]{:S(2)}) collective-permute-start(f32[16,640]{1,0:T(8,128)S(1)} %get-tuple-element.57), channel_id=1, source_target_pairs={{0,24},{4,28},{8,16},{12,20},{16,8},{20,12},{24,0},{28,4},{1,25},{... | collective-permute-start | bytes 122888 | tf_op jit(solution)/shard_map/ppermute | solution.py:442
  54.0 6.7 %collective-permute-start.16 = (f32[16,896]{1,0:T(8,128)S(1)}, f32[16,896]{1,0:T(8,128)S(1)}, u32[]{:S(2)}, u32[]{:S(2)}) collective-permute-start(f32[16,896]{1,0:T(8,128)S(1)} %pack.1.a), channel_id=1, source_target_pairs={{0,1},{1,0},{2,3},{3,2},{4,5},{5,4},{6,7},{7,6},{8,9},{9,8},{10,11... | collective-permute-start | bytes 172040 | tf_op jit(solution)/shard_map/ppermute | solution.py:341
  54.9 8.5 %collective-permute-start.17 = (f32[16,896]{1,0:T(8,128)S(1)}, f32[16,896]{1,0:T(8,128)S(1)}, u32[]{:S(2)}, u32[]{:S(2)}) collective-permute-start(f32[16,896]{1,0:T(8,128)S(1)} %pack.1.a), channel_id=1, source_target_pairs={{0,2},{1,3},{2,0},{3,1},{4,6},{5,7},{6,4},{7,5},{8,10},{9,11},{10,... | collective-permute-start | bytes 172040 | tf_op jit(solution)/shard_map/ppermute | solution.py:341
  56.6 6.8 %collective-permute-start.18 = (f32[16,896]{1,0:T(8,128)S(1)}, f32[16,896]{1,0:T(8,128)S(1)}, u32[]{:S(2)}, u32[]{:S(2)}) collective-permute-start(f32[16,896]{1,0:T(8,128)S(1)} %pack.1.a), channel_id=1, source_target_pairs={{0,3},{1,2},{2,1},{3,0},{4,7},{5,6},{6,5},{7,4},{8,11},{9,10},{10,... | collective-permute-start | bytes 172040 | tf_op jit(solution)/shard_map/ppermute | solution.py:341
  58.5 20.0 %collective-permute-start.27 = (bf16[144,2560]{1,0:T(8,128)(2,1)S(1)}, bf16[144,2560]{1,0:T(8,128)(2,1)S(1)}, u32[]{:S(2)}, u32[]{:S(2)}) collective-permute-start(bf16[144,2560]{1,0:T(8,128)(2,1)S(1)} %collective-permute-done.11.x_first.rest_1_.rest_0_), channel_id=1, source_target_pairs={{1,0},{2,3},{5,4},{6,7},{9,8},{10,11},{13,12},{14,15},{17,16},{18,... | collective-permute-start | bytes 2211848 | tf_op jit(solution)/shard_map/ppermute | solution.py:362
  60.7 17.8 %collective-permute-start.28 = (bf16[144,2560]{1,0:T(8,128)(2,1)S(1)}, bf16[144,2560]{1,0:T(8,128)(2,1)S(1)}, u32[]{:S(2)}, u32[]{:S(2)}) collective-permute-start(bf16[144,2560]{1,0:T(8,128)(2,1)S(1)} %copy-done.3), channel_id=1, source_target_pairs={{1,2},{2,1},{5,6},{6,5},{9,10},{10,9},{13,14},{14,13},{17,18},{18,... | collective-permute-start | bytes 2211848 | tf_op jit(solution)/shard_map/ppermute | solution.py:362
  63.4 4.1 %collective-permute-start.19 = (f32[16,640]{1,0:T(8,128)S(1)}, f32[16,640]{1,0:T(8,128)S(1)}, u32[]{:S(2)}, u32[]{:S(2)}) collective-permute-start(f32[16,640]{1,0:T(8,128)S(1)} %get-tuple-element.62.a0), channel_id=1, source_target_pairs={{0,8},{4,12},{8,0},{12,4},{16,24},{20,28},{24,16},{28,20},{1,9},{5... | collective-permute-start | bytes 122888 | tf_op jit(solution)/shard_map/ppermute | solution.py:341
  64.9 5.6 %collective-permute-start.20 = (f32[16,640]{1,0:T(8,128)S(1)}, f32[16,640]{1,0:T(8,128)S(1)}, u32[]{:S(2)}, u32[]{:S(2)}) collective-permute-start(f32[16,640]{1,0:T(8,128)S(1)} %get-tuple-element.62.a0), channel_id=1, source_target_pairs={{0,16},{4,20},{8,24},{12,28},{16,0},{20,4},{24,8},{28,12},{1,17},{... | collective-permute-start | bytes 122888 | tf_op jit(solution)/shard_map/ppermute | solution.py:341
  66.0 5.1 %collective-permute-start.21 = (f32[16,640]{1,0:T(8,128)S(1)}, f32[16,640]{1,0:T(8,128)S(1)}, u32[]{:S(2)}, u32[]{:S(2)}) collective-permute-start(f32[16,640]{1,0:T(8,128)S(1)} %get-tuple-element.62.a0), channel_id=1, source_target_pairs={{0,24},{4,28},{8,16},{12,20},{16,8},{20,12},{24,0},{28,4},{1,25},{... | collective-permute-start | bytes 122888 | tf_op jit(solution)/shard_map/ppermute | solution.py:341
  67.5 3.7 %collective-permute-start.22 = (f32[16,640]{1,0:T(8,128)S(1)}, f32[16,640]{1,0:T(8,128)S(1)}, u32[]{:S(2)}, u32[]{:S(2)}) collective-permute-start(f32[16,640]{1,0:T(8,128)S(1)} %get-tuple-element.62.a0), channel_id=1, source_target_pairs={{0,4},{4,0},{8,12},{12,8},{16,20},{20,16},{24,28},{28,24},{1,5},{5... | collective-permute-start | bytes 122888 | tf_op jit(solution)/shard_map/ppermute | solution.py:341
  70.6 2.4 %collective-permute-start.23 = (f32[16,640]{1,0:T(8,128)S(1)}, f32[16,640]{1,0:T(8,128)S(1)}, u32[]{:S(2)}, u32[]{:S(2)}) collective-permute-start(f32[16,640]{1,0:T(8,128)S(1)} %collective-permute-done.19.a1), channel_id=1, source_target_pairs={{0,4},{4,0},{8,12},{12,8},{16,20},{20,16},{24,28},{28,24},{1,5},{5... | collective-permute-start | bytes 122888 | tf_op jit(solution)/shard_map/ppermute | solution.py:341
  71.1 1.9 %collective-permute-start.24 = (f32[16,640]{1,0:T(8,128)S(1)}, f32[16,640]{1,0:T(8,128)S(1)}, u32[]{:S(2)}, u32[]{:S(2)}) collective-permute-start(f32[16,640]{1,0:T(8,128)S(1)} %collective-permute-done.20.a2), channel_id=1, source_target_pairs={{0,4},{4,0},{8,12},{12,8},{16,20},{20,16},{24,28},{28,24},{1,5},{5... | collective-permute-start | bytes 122888 | tf_op jit(solution)/shard_map/ppermute | solution.py:341
  71.2 1.8 %collective-permute-start.25 = (f32[16,640]{1,0:T(8,128)S(1)}, f32[16,640]{1,0:T(8,128)S(1)}, u32[]{:S(2)}, u32[]{:S(2)}) collective-permute-start(f32[16,640]{1,0:T(8,128)S(1)} %collective-permute-done.21.a3), channel_id=1, source_target_pairs={{0,4},{4,0},{8,12},{12,8},{16,20},{20,16},{24,28},{28,24},{1,5},{5... | collective-permute-start | bytes 122888 | tf_op jit(solution)/shard_map/ppermute | solution.py:341

commit v5 on v4

--- a/solution.py
+++ b/solution.py
@@ -11,7 +11,7 @@
 column_block = 8
 bf16, f32 = jnp.bfloat16, jnp.float32
 MIB = 1 << 20
-KA, KB, KP = 0, 3_900_000_000, 3_500_000_000
+CUT_COST, ACC_COST = 1_600_000_000, 2_000_000_000
 
 
 def plain_body(activations, out_grad, error_state, right_factor):
@@ -159,8 +159,8 @@
     step = first_partner(t)
     near_ref[0] = held[t]
     near_ref[1] = held[t ^ step]
-    far_ref[0] = held[t ^ 3]
-    far_ref[1] = held[t ^ 3 ^ step]
+    far_ref[0] = held[t ^ 3].astype(bf16)
+    far_ref[1] = held[t ^ 3 ^ step].astype(bf16)
 
 
 def error_right(p_ref, e_0, e_1, out_ref):
@@ -176,7 +176,7 @@
     rank = te_ref.shape[0]
     total = te_ref[...]
     for k, x_ref in enumerate((x_own, x_first)):
-        both = jnp.concatenate(split(near_ref[k] + got_ref[k]), axis=0)
+        both = jnp.concatenate(split(near_ref[k] + got_ref[k].astype(f32)), axis=0)
         term = dot(both, x_ref[...])
         total += term[:rank] + term[rank:]
     held[0] = total[: rank // 2]
@@ -192,25 +192,33 @@
     for s in range(held.shape[0]):
         held[s] = total[:, s * width : (s + 1) * width]
     for k, out in enumerate((o0, o1, o2, o3)):
-        out[...] = held[chip ^ k]
+        out[...] = held[chip ^ k].astype(out.dtype)
 
 
 def pack(a, b, c, d, gram_ref, out_ref):
     half, width = a.shape
     rank = 2 * half
-    out_ref[...] = jnp.zeros_like(out_ref)
-    out_ref[:, :width] = (a[...] + b[...]) + (c[...] + d[...])
-    out_ref[:, width : width + rank] = gram_ref[:half, :]
-    out_ref[:, width + 128 : width + 128 + rank] = gram_ref[half:, :]
+    total = (a[...] + b[...].astype(f32)) + (c[...].astype(f32) + d[...].astype(f32))
+    out_ref[:, :width] = total.astype(bf16)
+    left = jnp.concatenate((gram_ref[:half, :], gram_ref[half:, :]), axis=1)
+    for k in range(3):
+        term = left.astype(bf16)
+        left = left - term.astype(f32)
+        out_ref[:, width + k * 128 : width + k * 128 + 2 * rank] = term
 
 
 def unpack(a, b, c, d, out_ref, gram_ref):
     half, width = out_ref.shape
     rank = 2 * half
-    total = (a[...] + b[...]) + (c[...] + d[...])
-    out_ref[...] = total[:, :width]
-    gram_ref[:half, :] = total[:, width : width + rank]
-    gram_ref[half:, :] = total[:, width + 128 : width + 128 + rank]
+
+    def part(ref, at, count):
+        return ref[:, at : at + count].astype(f32)
+
+    out_ref[...] = (part(a, 0, width) + part(b, 0, width)) + (part(c, 0, width) + part(d, 0, width))
+    grams = [sum(part(ref, width + k * 128, 2 * rank) for k in range(3)) for ref in (a, b, c, d)]
+    total = (grams[0] + grams[1]) + (grams[2] + grams[3])
+    gram_ref[:half, :] = total[:, :rank]
+    gram_ref[half:, :] = total[:, rank:]
 
 
 def invert_cholesky(g_ref, out_ref):
@@ -294,24 +302,12 @@
     left_ref[:, base:] = jnp.concatenate((high, low, high), axis=0).T
 
 
-def rebuild(place, left_ref, right_ref, acc_0, acc_1, outer, inner, out_any, buffer, staged, sems, out_sems):
-    t = place[0]
-    rows = inner.shape[0]
-    is_inner = (t == 1) | (t == 2)
-
-    def fetch(source):
-        return pltpu.make_async_copy(source, buffer.at[pl.ds(0, rows), :], sems.at[0])
-
-    @pl.when(is_inner)
-    def _():
-        fetch(inner).start()
-
-    @pl.when(jnp.logical_not(is_inner))
-    def _():
-        fetch(outer).start()
-
+def rebuild(left_ref, right_ref, acc_0, acc_1, x_any, out_any, buffer, staged, sem, out_sems):
+    rows = x_any.shape[0]
+    fetch = pltpu.make_async_copy(x_any, buffer.at[pl.ds(0, rows), :], sem)
+    fetch.start()
     buffer[rows:, :] = right_ref[...]
-    fetch(inner).wait()
+    fetch.wait()
     slots, hidden, width = staged.shape
     count = acc_0.shape[1] // width
 
@@ -393,7 +389,6 @@
         left_factor,
         [like((rank, hidden), bf16)],
         place, eq, y_own, *y_parts, out_grad,
-        flops=KA,
         scratch=[pltpu.VMEM((n_t, rank, tokens), f32)],
     )
     (p_other,) = partners(p_local, "dp", n_dp, (1,))
@@ -401,7 +396,7 @@
     p_parts = along_xy(p_chip)
     p_total, gram, near_w, far_w = call(
         weigh,
-        [like((rank, hidden), bf16), like((rank, rank), f32), like((2, rank, tokens), f32), like((2, rank, tokens), f32)],
+        [like((rank, hidden), bf16), like((rank, rank), f32), like((2, rank, tokens), f32), like((2, rank, tokens), bf16)],
         place, p_chip, *p_parts, out_grad,
         scratch=[pltpu.VMEM((n_t, rank, tokens), f32)],
     )
@@ -422,20 +417,12 @@
         place, near_w, got_w, te, activations, x_first,
         scratch=[pltpu.VMEM((2, half, features), f32)],
     )
-    cut_at = tokens // 32 * 16 + 16
-    to_outer, to_inner = [], []
-
-    def third_step(part, *when):
-        to_outer.append(move(x_first[part], [(1, 0), (2, 3)], *when))
-        to_inner.append(move(activations[part], [(1, 2), (2, 1)], *when))
-
-    third_step(slice(0, cut_at), got_w)
     (got,) = partners(given, "dp", n_dp, (1,))
     parts = call(
         cut,
-        [like((half, rows), f32)] * 4,
+        [like((half, rows), f32)] + [like((half, rows), bf16)] * 3,
         place, keep, got,
-        flops=KB,
+        flops=CUT_COST,
         scratch=[pltpu.VMEM((n_t, half, rows), f32)],
     )
     arrived = [
@@ -459,13 +446,12 @@
         add_tokens(k, 0, 0, e_held, ((0, tokens), (0, early)), activations, x_first)
         for k, e_held in enumerate(held_errors)
     ]
-    (mine,) = call(pack, [like((half, rows + 256), f32)], parts[0], *arrived, gram)
+    (mine,) = call(pack, [like((half, rows + 384), bf16)], parts[0], *arrived, gram)
     mine = after(mine, *accs)
     z1, z2, z3 = along_t(mine)
-    x_outer = move(x_first, [(1, 0), (2, 3)], mine)
-    x_inner = move(activations, [(1, 2), (2, 1)], mine)
+    x_third = move(x_first, way_1, z1, z2, z3)
     accs = [
-        add_tokens(k, KP, 256, acc, ((early, tokens), (0, tokens)), x_first, x_second)
+        add_tokens(k, ACC_COST, 256, acc, ((early, tokens), (0, tokens)), x_first, x_second)
         for k, acc in enumerate(accs)
     ]
     mine, gram = call(unpack, [like((half, rows), f32), like((rank, rank), f32)], mine, z1, z2, z3)
@@ -482,13 +468,13 @@
     (new_error,) = call(
         rebuild,
         [like((hidden, features), bf16)],
-        place, left, right, *accs, x_outer, x_inner,
-        in_specs=[smem_spec] + [vmem_spec] * 4 + [anywhere] * 2,
+        left, right, *accs, x_third,
+        in_specs=[vmem_spec] * 4 + [anywhere],
         out_specs=[anywhere],
         scratch=[
             pltpu.VMEM((tokens + 3 * rank, features), bf16),
             pltpu.VMEM((4, hidden, 256), bf16),
-            pltpu.SemaphoreType.DMA((1,)),
+            pltpu.SemaphoreType.DMA(()),
             pltpu.SemaphoreType.DMA((4,)),
         ],
     )

time: 84.5 us -> 82.5 us (0.976)
  starting transfers between devices: 30.8 us -> 28.1 us
  waiting for transfers between devices: 22 us -> 23.2 us
    ppermute x4 -> x3, starting transfers between devices: 2.86 us -> 0.71 us  [move(): return lax.ppermute(after(value, *when), 'tensor', perm)]
    ppermute x4 -> x3, waiting for transfers between devices: 3.98 us -> 4.69 us  [move(): return lax.ppermute(after(value, *when), 'tensor', perm)]
  transfers between devices with their start and end apart: 29 -> 28, of which waited for: 12 -> 13; matrix products, arithmetic and copies ran while one was open for 0% -> 0% of each run, Pallas kernels for 24% -> 25%
where the time goes in v5:
time: 82.5 us; the launch traced here: 82.2 us
  starting transfers between devices  28.1 us (34%)
  Pallas kernels  26.2 us (32%)
  waiting for transfers between devices  23.2 us (28%)
  local copies, waits for them, and re-layouts  2.7 us (3%)
  between operations  1.04 us (1%)
  other arithmetic  1 us (1%)
    pallas_call x17, Pallas kernels, call(): pl.pallas_call(kernel, out_shape=list(outs), in_specs=in_specs, out_specs...  26.2 us
    ppermute x22, starting transfers between devices, partners(): lax.ppermute(value, axis, [(i, i ^ k) for i in range(size)])  23.9 us
    ppermute x22, waiting for transfers between devices, partners(): lax.ppermute(value, axis, [(i, i ^ k) for i in range(size)])  18.1 us
    ppermute x3, waiting for transfers between devices, move(): return lax.ppermute(after(value, *when), 'tensor', perm)  4.69 us
    ppermute x3, starting transfers between devices, body(): lax.ppermute(m, 'dp', [(i, i ^ 2 * k) for i in range(n_dp)])  3.55 us
    unnamed x8, local copies, waits for them, and re-layouts  2.7 us
  transfers between devices with their start and end apart: 28, of which 13 were waited for; matrix products, arithmetic and copies ran while one was open for 0% of the time, Pallas kernels for 25%

profile of v5, /device:TPU:0, one launch (start us, length us, event | category | flops | bytes accessed | tf_op | source)
XLA Modules:
  0.0 82.2 jit_solution(8426599927904469775)
XLA Ops:
  0.6 0.9 %convert_bitcast_fusion.own = bf16[32,640]{1,0:T(8,128)(2,1)S(1)} fusion(f32[640,32]{0,1:T(8,128)} %param.7), kind=kLoop, calls=%fused_computation.1 | loop fusion | flops 20480 | bytes 122880 | tf_op jit(solution)/shard_map/convert_element_type | solution.py:360
  1.5 3.0 %collective-permute-start = (bf16[32,640]{1,0:T(8,128)(2,1)S(1)}, bf16[32,640]{1,0:T(8,128)(2,1)S(1)}, u32[]{:S(2)}, u32[]{:S(2)}) collective-permute-start(bf16[32,640]{1,0:T(8,128)(2,1)S(1)} %convert_bitcast_fusion.own), channel_id=1, source_target_pairs={{0,1},{1,0},{2,3},{3,2},{4,5},{5,4},{6,7},{7,6},{8,9},{9,8},{10,11... | collective-permute-start | bytes 122888 | tf_op jit(solution)/shard_map/ppermute | solution.py:337
  4.5 2.6 %collective-permute-start.1 = (bf16[32,640]{1,0:T(8,128)(2,1)S(1)}, bf16[32,640]{1,0:T(8,128)(2,1)S(1)}, u32[]{:S(2)}, u32[]{:S(2)}) collective-permute-start(bf16[32,640]{1,0:T(8,128)(2,1)S(1)} %convert_bitcast_fusion.own), channel_id=1, source_target_pairs={{0,2},{1,3},{2,0},{3,1},{4,6},{5,7},{6,4},{7,5},{8,10},{9,11},{10,... | collective-permute-start | bytes 122888 | tf_op jit(solution)/shard_map/ppermute | solution.py:337
  7.1 0.1 pad_add_fusion.place
  7.2 1.6 %copy-done = bf16[576,1728]{1,0:T(8,128)(2,1)S(1)} copy-done((bf16[576,1728]{1,0:T(8,128)(2,1)S(1)}, bf16[576,1728]{1,0:T(8,128)(2,1)}, u32[]{:S(2)}) %copy-start) | copy-done | bytes 1990680
  8.8 1.3 %arrange.1 = (bf16[1728,432]{1,0:T(8,128)(2,1)S(1)}, bf16[1728,144]{1,0:T(8,128)(2,1)S(1)}) custom-call(s32[3]{0:T(128)S(1)} %pad_add_fusion.place, bf16[576,1728]{1,0:T(8,128)(2,1)S(1)} %copy-done), custom_call_target="tpu_custom_call" | custom-call | bytes 3981324 | tf_op jit(solution)/shard_map/arrange/pallas_call | solution.py:83
  10.1 0.0 collective-permute-done.n1
  10.1 0.1 collective-permute-done.1.n2
  10.2 2.7 %collective-permute-done.2.n3 = bf16[32,640]{1,0:T(8,128)(2,1)S(1)} collective-permute-done((bf16[32,640]{1,0:T(8,128)(2,1)S(1)}, bf16[32,640]{1,0:T(8,128)(2,1)S(1)}, u32[]{:S(2)}, u32[]{:S(2)}) %collective-permute-start.2) | collective-permute-done | bytes 40992 | tf_op jit(solution)/shard_map/ppermute | solution.py:337
  12.9 1.1 %copy-done.2 = bf16[144,2560]{1,0:T(8,128)(2,1)S(1)} copy-done((bf16[144,2560]{1,0:T(8,128)(2,1)S(1)}, bf16[144,2560]{1,0:T(8,128)(2,1)}, u32[]{:S(2)}) %copy-start.2) | copy-done | bytes 737304
  14.1 0.9 %project.1 = (bf16[4,32,640]{2,1,0:T(8,128)(2,1)S(1)}, f32[32,144]{1,0:T(8,128)S(1)}) custom-call(s32[3]{0:T(128)S(1)} %pad_add_fusion.place, bf16[32,640]{1,0:T(8,128)(2,1)S(1)} %convert_bitcast_fusion.own, bf16[32,640]{1,0:T(8,128)(2,1)S(1)} %collective-permute-done.n1, bf16[32,640]{1,0:T(8,128)(2,1)S(1)} %collective-permute-done.1.n2, ...), custom_call_target="tpu_custom_call" | custom-call | bytes 1083404 | tf_op jit(solution)/shard_map/project/pallas_call | solution.py:83
  14.9 0.0 collective-permute-start.3
  15.0 1.6 %collective-permute-start.4 = (f32[32,144]{1,0:T(8,128)S(1)}, f32[32,144]{1,0:T(8,128)S(1)}, u32[]{:S(2)}, u32[]{:S(2)}) collective-permute-start(f32[32,144]{1,0:T(8,128)S(1)} %get-tuple-element.41.own), channel_id=1, source_target_pairs={{0,2},{1,3},{2,0},{3,1},{4,6},{5,7},{6,4},{7,5},{8,10},{9,11},{10,... | collective-permute-start | bytes 55304 | tf_op jit(solution)/shard_map/ppermute | solution.py:337
  16.6 2.8 %collective-permute-start.5 = (f32[32,144]{1,0:T(8,128)S(1)}, f32[32,144]{1,0:T(8,128)S(1)}, u32[]{:S(2)}, u32[]{:S(2)}) collective-permute-start(f32[32,144]{1,0:T(8,128)S(1)} %get-tuple-element.41.own), channel_id=1, source_target_pairs={{0,3},{1,2},{2,1},{3,0},{4,7},{5,6},{6,5},{7,4},{8,11},{9,10},{10,... | collective-permute-start | bytes 55304 | tf_op jit(solution)/shard_map/ppermute | solution.py:337
  19.4 5.0 %error_left.1 = (f32[32,1728]{1,0:T(8,128)S(1)}, bf16[1728,1280]{1,0:T(8,128)(2,1)S(1)}, bf16[1728,1280]{1,0:T(8,128)(2,1)S(1)}) custom-call(bf16[4,32,640]{2,1,0:T(8,128)(2,1)S(1)} %get-tuple-element.39.q_ref, bf16[1728,2560]{1,0:T(8,128)(2,1)} %bitcast.9), custom_call_target="tpu_custom_call" | custom-call | bytes 18079744 | tf_op jit(solution)/shard_map/error_left/pallas_call | solution.py:83
  24.4 0.0 collective-permute-done.3.n1
  24.4 0.0 collective-permute-done.4.n2
  24.5 0.1 collective-permute-start.11
  24.6 1.0 %left_factor.1 = bf16[32,1728]{1,0:T(8,128)(2,1)S(1)} custom-call(s32[3]{0:T(128)S(1)} %pad_add_fusion.place, f32[32,1728]{1,0:T(8,128)S(1)} %get-tuple-element.40.eq_ref, f32[32,144]{1,0:T(8,128)S(1)} %get-tuple-element.41.own, f32[32,144]{1,0:T(8,128)S(1)} %collective-permute-done.3.n1, f32[32,144]{1,0:T(8,128)S(1)} %collective-permute-done.4.n2, ...), custom_call_target="tpu_custom_call" | custom-call | bytes 2396172 | tf_op jit(solution)/shard_map/left_factor/pallas_call | solution.py:83
  25.5 0.1 collective-permute-start.6
  25.6 1.3 %collective-permute-done.6 = bf16[32,1728]{1,0:T(8,128)(2,1)S(1)} collective-permute-done((bf16[32,1728]{1,0:T(8,128)(2,1)S(1)}, bf16[32,1728]{1,0:T(8,128)(2,1)S(1)}, u32[]{:S(2)}, u32[]{:S(2)}) %collective-permute-start.6) | collective-permute-done | bytes 110624 | tf_op jit(solution)/shard_map/ppermute | solution.py:337
  26.9 1.6 %collective-permute-start.7 = (bf16[32,1728]{1,0:T(8,128)(2,1)S(1)}, bf16[32,1728]{1,0:T(8,128)(2,1)S(1)}, u32[]{:S(2)}, u32[]{:S(2)}) collective-permute-start(bf16[32,1728]{1,0:T(8,128)(2,1)S(1)} %add_convert_fusion.own), channel_id=1, source_target_pairs={{0,8},{4,12},{8,0},{12,4},{16,24},{20,28},{24,16},{28,20},{1,9},{5... | collective-permute-start | bytes 331784 | tf_op jit(solution)/shard_map/ppermute | solution.py:337
  28.5 1.5 %collective-permute-start.8 = (bf16[32,1728]{1,0:T(8,128)(2,1)S(1)}, bf16[32,1728]{1,0:T(8,128)(2,1)S(1)}, u32[]{:S(2)}, u32[]{:S(2)}) collective-permute-start(bf16[32,1728]{1,0:T(8,128)(2,1)S(1)} %add_convert_fusion.own), channel_id=1, source_target_pairs={{0,16},{4,20},{8,24},{12,28},{16,0},{20,4},{24,8},{28,12},{1,17},{... | collective-permute-start | bytes 331784 | tf_op jit(solution)/shard_map/ppermute | solution.py:337
  30.0 0.5 collective-permute-start.9
  30.5 1.7 %collective-permute-done.7.n1 = bf16[32,1728]{1,0:T(8,128)(2,1)S(1)} collective-permute-done((bf16[32,1728]{1,0:T(8,128)(2,1)S(1)}, bf16[32,1728]{1,0:T(8,128)(2,1)S(1)}, u32[]{:S(2)}, u32[]{:S(2)}) %collective-permute-start.7) | collective-permute-done | bytes 110624 | tf_op jit(solution)/shard_map/ppermute | solution.py:337
  32.2 3.7 %collective-permute-done.8.n2 = bf16[32,1728]{1,0:T(8,128)(2,1)S(1)} collective-permute-done((bf16[32,1728]{1,0:T(8,128)(2,1)S(1)}, bf16[32,1728]{1,0:T(8,128)(2,1)S(1)}, u32[]{:S(2)}, u32[]{:S(2)}) %collective-permute-start.8) | collective-permute-done | bytes 110624 | tf_op jit(solution)/shard_map/ppermute | solution.py:337
  35.9 1.3 %weigh.1 = (bf16[32,1728]{1,0:T(8,128)(2,1)S(1)}, f32[32,32]{1,0:T(8,128)S(1)}, f32[2,32,144]{2,1,0:T(8,128)S(1)}, bf16[2,32,144]{2,1,0:T(8,128)(2,1)S(1)}) custom-call(s32[3]{0:T(128)S(1)} %pad_add_fusion.place, bf16[32,1728]{1,0:T(8,128)(2,1)S(1)} %add_convert_fusion.own, bf16[32,1728]{1,0:T(8,128)(2,1)S(1)} %collective-permute-done.7.n1, ...), custom_call_target="tpu_custom_call" | custom-call | bytes 2603020 | tf_op jit(solution)/shard_map/weigh/pallas_call | solution.py:83
  37.1 1.6 %collective-permute-start.10 = (bf16[2,32,144]{2,1,0:T(8,128)(2,1)S(1)}, bf16[2,32,144]{2,1,0:T(8,128)(2,1)S(1)}, u32[]{:S(2)}, u32[]{:S(2)}) collective-permute-start(bf16[2,32,144]{2,1,0:T(8,128)(2,1)S(1)} %get-tuple-element.44), channel_id=1, source_target_pairs={{0,3},{1,2},{2,1},{3,0},{4,7},{5,6},{6,5},{7,4},{8,11},{9,10},{10,... | collective-permute-start | bytes 55304 | tf_op jit(solution)/shard_map/ppermute | solution.py:337
  38.7 0.6 collective-permute-start.26
  39.4 1.4 %error_right.1.te_ref = f32[32,2560]{1,0:T(8,128)S(1)} custom-call(bf16[32,1728]{1,0:T(8,128)(2,1)S(1)} %get-tuple-element.45.p_ref, bf16[1728,1280]{1,0:T(8,128)(2,1)S(1)} %get-tuple-element.46.e_0.base_ref, bf16[1728,1280]{1,0:T(8,128)(2,1)S(1)} %get-tuple-element.47.e_1.base_ref), custom_call_target="tpu_custom_call" | custom-call | bytes 9285632 | tf_op jit(solution)/shard_map/error_right/pallas_call | solution.py:83
  40.8 2.6 %collective-permute-done.10.got_ref = bf16[2,32,144]{2,1,0:T(8,128)(2,1)S(1)} collective-permute-done((bf16[2,32,144]{2,1,0:T(8,128)(2,1)S(1)}, bf16[2,32,144]{2,1,0:T(8,128)(2,1)S(1)}, u32[]{:S(2)}, u32[]{:S(2)}) %collective-permute-start.10) | collective-permute-done | bytes 18464 | tf_op jit(solution)/shard_map/ppermute | solution.py:337
  43.3 0.9 %right_term.1 = (f32[16,2560]{1,0:T(8,128)S(1)}, f32[16,2560]{1,0:T(8,128)S(1)}) custom-call(s32[3]{0:T(128)S(1)} %pad_add_fusion.place, f32[2,32,144]{2,1,0:T(8,128)S(1)} %get-tuple-element.43.near_ref, bf16[2,32,144]{2,1,0:T(8,128)(2,1)S(1)} %collective-permute-done.10.got_ref, f32[32,2560]{1,0:T(8,128)S(1)} %error_right.1.te_ref, ...), custom_call_target="tpu_custom_call" | custom-call | bytes 2185228 | tf_op jit(solution)/shard_map/right_term/pallas_call | solution.py:83
  44.3 0.1 collective-permute-start.12
  44.3 1.4 %collective-permute-done.12.got = f32[16,2560]{1,0:T(8,128)S(1)} collective-permute-done((f32[16,2560]{1,0:T(8,128)S(1)}, f32[16,2560]{1,0:T(8,128)S(1)}, u32[]{:S(2)}, u32[]{:S(2)}) %collective-permute-start.12) | collective-permute-done | bytes 163872 | tf_op jit(solution)/shard_map/ppermute | solution.py:337
  45.7 0.6 cut.1
  46.3 1.2 %collective-permute-start.13 = (bf16[16,640]{1,0:T(8,128)(2,1)S(1)}, bf16[16,640]{1,0:T(8,128)(2,1)S(1)}, u32[]{:S(2)}, u32[]{:S(2)}) collective-permute-start(bf16[16,640]{1,0:T(8,128)(2,1)S(1)} %get-tuple-element.54), channel_id=1, source_target_pairs={{0,8},{4,12},{8,0},{12,4},{16,24},{20,28},{24,16},{28,20},{1,9},{5... | collective-permute-start | bytes 61448 | tf_op jit(solution)/shard_map/ppermute | solution.py:429
  47.5 0.9 %collective-permute-start.14 = (bf16[16,640]{1,0:T(8,128)(2,1)S(1)}, bf16[16,640]{1,0:T(8,128)(2,1)S(1)}, u32[]{:S(2)}, u32[]{:S(2)}) collective-permute-start(bf16[16,640]{1,0:T(8,128)(2,1)S(1)} %get-tuple-element.55), channel_id=1, source_target_pairs={{0,16},{4,20},{8,24},{12,28},{16,0},{20,4},{24,8},{28,12},{1,17},{... | collective-permute-start | bytes 61448 | tf_op jit(solution)/shard_map/ppermute | solution.py:429
  48.4 1.5 %collective-permute-start.15 = (bf16[16,640]{1,0:T(8,128)(2,1)S(1)}, bf16[16,640]{1,0:T(8,128)(2,1)S(1)}, u32[]{:S(2)}, u32[]{:S(2)}) collective-permute-start(bf16[16,640]{1,0:T(8,128)(2,1)S(1)} %get-tuple-element.56), channel_id=1, source_target_pairs={{0,24},{4,28},{8,16},{12,20},{16,8},{20,12},{24,0},{28,4},{1,25},{... | collective-permute-start | bytes 61448 | tf_op jit(solution)/shard_map/ppermute | solution.py:429
  49.9 1.4 %accumulate.4.base_ref = f32[1728,1280]{1,0:T(8,128)S(1)} custom-call(bf16[1728,432]{1,0:T(8,128)(2,1)S(1)} %get-tuple-element.35.main_ref, bf16[1728,1280]{1,0:T(8,128)(2,1)S(1)} %get-tuple-element.46.e_0.base_ref, bf16[144,2560]{1,0:T(8,128)(2,1)S(1)} %copy-done.3, bf16[144,2560]{1,0:T(8,128)(2,1)S(1)} %collective-permute-done.11.x_first.rest_1_.rest_0_), custom_call_target="tpu_custom_call" | custom-call | bytes 16238592 | tf_op jit(solution)/shard_map/accumulate/pallas_call | solution.py:83
  51.2 1.4 %accumulate.5.base_ref = f32[1728,1280]{1,0:T(8,128)S(1)} custom-call(bf16[1728,432]{1,0:T(8,128)(2,1)S(1)} %get-tuple-element.35.main_ref, bf16[1728,1280]{1,0:T(8,128)(2,1)S(1)} %get-tuple-element.47.e_1.base_ref, bf16[144,2560]{1,0:T(8,128)(2,1)S(1)} %copy-done.3, bf16[144,2560]{1,0:T(8,128)(2,1)S(1)} %collective-permute-done.11.x_first.rest_1_.rest_0_), custom_call_target="tpu_custom_call" | custom-call | bytes 16238592 | tf_op jit(solution)/shard_map/accumulate/pallas_call | solution.py:83
  52.7 0.4 collective-permute-done.15.d
  53.0 0.1 pack.1.a
  53.1 0.6 collective-permute-start.16
  53.7 1.9 %collective-permute-start.17 = (bf16[16,1024]{1,0:T(8,128)(2,1)S(1)}, bf16[16,1024]{1,0:T(8,128)(2,1)S(1)}, u32[]{:S(2)}, u32[]{:S(2)}) collective-permute-start(bf16[16,1024]{1,0:T(8,128)(2,1)S(1)} %pack.1.a), channel_id=1, source_target_pairs={{0,2},{1,3},{2,0},{3,1},{4,6},{5,7},{6,4},{7,5},{8,10},{9,11},{10,... | collective-permute-start | bytes 98312 | tf_op jit(solution)/shard_map/ppermute | solution.py:337
  55.6 1.9 %collective-permute-start.18 = (bf16[16,1024]{1,0:T(8,128)(2,1)S(1)}, bf16[16,1024]{1,0:T(8,128)(2,1)S(1)}, u32[]{:S(2)}, u32[]{:S(2)}) collective-permute-start(bf16[16,1024]{1,0:T(8,128)(2,1)S(1)} %pack.1.a), channel_id=1, source_target_pairs={{0,3},{1,2},{2,1},{3,0},{4,7},{5,6},{6,5},{7,4},{8,11},{9,10},{10,... | collective-permute-start | bytes 98312 | tf_op jit(solution)/shard_map/ppermute | solution.py:337
  57.5 0.2 collective-permute-done.16.b
  57.8 2.0 %collective-permute-done.17.c = bf16[16,1024]{1,0:T(8,128)(2,1)S(1)} collective-permute-done((bf16[16,1024]{1,0:T(8,128)(2,1)S(1)}, bf16[16,1024]{1,0:T(8,128)(2,1)S(1)}, u32[]{:S(2)}, u32[]{:S(2)}) %collective-permute-start.17) | collective-permute-done | bytes 32800 | tf_op jit(solution)/shard_map/ppermute | solution.py:337
  59.7 1.6 %collective-permute-done.18.d = bf16[16,1024]{1,0:T(8,128)(2,1)S(1)} collective-permute-done((bf16[16,1024]{1,0:T(8,128)(2,1)S(1)}, bf16[16,1024]{1,0:T(8,128)(2,1)S(1)}, u32[]{:S(2)}, u32[]{:S(2)}) %collective-permute-start.18) | collective-permute-done | bytes 32800 | tf_op jit(solution)/shard_map/ppermute | solution.py:337
  61.4 0.0 collective-permute-start.27
  61.4 0.1 unpack.1
  61.5 1.3 %collective-permute-start.19 = (f32[16,640]{1,0:T(8,128)S(1)}, f32[16,640]{1,0:T(8,128)S(1)}, u32[]{:S(2)}, u32[]{:S(2)}) collective-permute-start(f32[16,640]{1,0:T(8,128)S(1)} %get-tuple-element.61.a0), channel_id=1, source_target_pairs={{0,8},{4,12},{8,0},{12,4},{16,24},{20,28},{24,16},{28,20},{1,9},{5... | collective-permute-start | bytes 122888 | tf_op jit(solution)/shard_map/ppermute | solution.py:337
  62.8 1.9 %collective-permute-start.20 = (f32[16,640]{1,0:T(8,128)S(1)}, f32[16,640]{1,0:T(8,128)S(1)}, u32[]{:S(2)}, u32[]{:S(2)}) collective-permute-start(f32[16,640]{1,0:T(8,128)S(1)} %get-tuple-element.61.a0), channel_id=1, source_target_pairs={{0,16},{4,20},{8,24},{12,28},{16,0},{20,4},{24,8},{28,12},{1,17},{... | collective-permute-start | bytes 122888 | tf_op jit(solution)/shard_map/ppermute | solution.py:337
  64.7 0.3 collective-permute-start.21
  65.0 1.7 %invert_cholesky.1.linv = f32[32,32]{1,0:T(8,128)S(1)} custom-call(f32[32,32]{1,0:T(8,128)S(1)} %get-tuple-element.59.g_ref), custom_call_target="tpu_custom_call" | custom-call | bytes 8192 | tf_op jit(solution)/shard_map/invert_cholesky/pallas_call | solution.py:83
  66.6 0.0 collective-permute-done.26.rest_1_
  66.6 0.1 collective-permute-start.22
  66.7 1.4 %accumulate.6.acc_0 = f32[1728,1280]{1,0:T(8,128)S(1)} custom-call(bf16[1728,432]{1,0:T(8,128)(2,1)S(1)} %get-tuple-element.35.main_ref, f32[1728,1280]{1,0:T(8,128)S(1)} %accumulate.4.base_ref, bf16[144,2560]{1,0:T(8,128)(2,1)S(1)} %collective-permute-done.11.x_first.rest_1_.rest_0_, bf16[144,2560]{1,0:T(8,128)(2,1)S(1)} %collective-permute-done.26.rest_1_), custom_call_target="tpu_custom_call" | custom-call | flops 2000000000 | bytes 20662272 | tf_op jit(solution)/shard_map/accumulate/pallas_call | solution.py:83
  68.1 0.5 collective-permute-start.23
  68.7 0.1 collective-permute-start.24
  68.8 0.8 collective-permute-done.21.a3
  69.6 1.4 %accumulate.7.acc_1 = f32[1728,1280]{1,0:T(8,128)S(1)} custom-call(bf16[1728,432]{1,0:T(8,128)(2,1)S(1)} %get-tuple-element.35.main_ref, f32[1728,1280]{1,0:T(8,128)S(1)} %accumulate.5.base_ref, bf16[144,2560]{1,0:T(8,128)(2,1)S(1)} %collective-permute-done.11.x_first.rest_1_.rest_0_, bf16[144,2560]{1,0:T(8,128)(2,1)S(1)} %collective-permute-done.26.rest_1_), custom_call_target="tpu_custom_call" | custom-call | flops 2000000000 | bytes 20662272 | tf_op jit(solution)/shard_map/accumulate/pallas_call | solution.py:83
  71.0 1.5 %finish.1 = (f32[32,640]{1,0:T(8,128)}, bf16[1728,240]{1,0:T(8,128)(2,1)S(1)}, bf16[96,2560]{1,0:T(8,128)(2,1)S(1)}) custom-call(s32[3]{0:T(128)S(1)} %pad_add_fusion.place, f32[32,32]{1,0:T(8,128)S(1)} %invert_cholesky.1.linv, bf16[32,1728]{1,0:T(8,128)(2,1)S(1)} %get-tuple-element.45.p_ref, bf16[1728,144]{1,0:T(8,128)(2,1)S(1)} %get-tuple-element.60.rest_ref, ...), custom_call_target="tpu_custom_call" | custom-call | bytes 2342924 | tf_op jit(solution)/shard_map/finish/pallas_call | solution.py:83
  72.5 4.7 %collective-permute-done.27.x_any = bf16[144,2560]{1,0:T(8,128)(2,1)S(1)} collective-permute-done((bf16[144,2560]{1,0:T(8,128)(2,1)S(1)}, bf16[144,2560]{1,0:T(8,128)(2,1)S(1)}, u32[]{:S(2)}, u32[]{:S(2)}) %collective-permute-start.27) | collective-permute-done | bytes 737312 | tf_op jit(solution)/shard_map/ppermute | solution.py:358
  77.2 4.9 %rebuild.1 = bf16[1728,2560]{1,0:T(8,128)(2,1)} custom-call(bf16[1728,240]{1,0:T(8,128)(2,1)S(1)} %get-tuple-element.63.left_ref, bf16[96,2560]{1,0:T(8,128)(2,1)S(1)} %get-tuple-element.64.right_ref, f32[1728,1280]{1,0:T(8,128)S(1)} %accumulate.6.acc_0, f32[1728,1280]{1,0:T(8,128)S(1)} %accumulate.7.acc_1, bf16[144,2560]{1,0:T(8,128)(2,1)S(1)} %collective-permute-done.27.x_any), custom_call_target="tpu_custom_call" | custom-call | bytes 28600320 | tf_op jit(solution)/shard_map/rebuild/pallas_call | solution.py:83
  (20 shorter events, 0.1 us)
Async XLA Ops:
  1.5 8.6 %collective-permute-start = (bf16[32,640]{1,0:T(8,128)(2,1)S(1)}, bf16[32,640]{1,0:T(8,128)(2,1)S(1)}, u32[]{:S(2)}, u32[]{:S(2)}) collective-permute-start(bf16[32,640]{1,0:T(8,128)(2,1)S(1)} %convert_bitcast_fusion.own), channel_id=1, source_target_pairs={{0,1},{1,0},{2,3},{3,2},{4,5},{5,4},{6,7},{7,6},{8,9},{9,8},{10,11... | collective-permute-start | bytes 122888 | tf_op jit(solution)/shard_map/ppermute | solution.py:337
  4.5 5.7 %collective-permute-start.1 = (bf16[32,640]{1,0:T(8,128)(2,1)S(1)}, bf16[32,640]{1,0:T(8,128)(2,1)S(1)}, u32[]{:S(2)}, u32[]{:S(2)}) collective-permute-start(bf16[32,640]{1,0:T(8,128)(2,1)S(1)} %convert_bitcast_fusion.own), channel_id=1, source_target_pairs={{0,2},{1,3},{2,0},{3,1},{4,6},{5,7},{6,4},{7,5},{8,10},{9,11},{10,... | collective-permute-start | bytes 122888 | tf_op jit(solution)/shard_map/ppermute | solution.py:337
  7.1 5.8 %collective-permute-start.2 = (bf16[32,640]{1,0:T(8,128)(2,1)S(1)}, bf16[32,640]{1,0:T(8,128)(2,1)S(1)}, u32[]{:S(2)}, u32[]{:S(2)}) collective-permute-start(bf16[32,640]{1,0:T(8,128)(2,1)S(1)} %convert_bitcast_fusion.own), channel_id=1, source_target_pairs={{0,3},{1,2},{2,1},{3,0},{4,7},{5,6},{6,5},{7,4},{8,11},{9,10},{10,... | collective-permute-start | bytes 122888 | tf_op jit(solution)/shard_map/ppermute | solution.py:337
  7.2 1.6 %copy-start = (bf16[576,1728]{1,0:T(8,128)(2,1)S(1)}, bf16[576,1728]{1,0:T(8,128)(2,1)}, u32[]{:S(2)}) copy-start(bf16[576,1728]{1,0:T(8,128)(2,1)} %dy_ref.5) | copy-start | bytes 5971972
  8.8 15.7 %copy-start.1 = (bf16[576,1728]{1,0:T(8,128)(2,1)S(1)}, bf16[576,1728]{1,0:T(8,128)(2,1)}, u32[]{:S(2)}) copy-start(bf16[576,1728]{1,0:T(8,128)(2,1)} %dy_ref.5) | copy-start | bytes 5971972
  12.9 1.1 %copy-start.2 = (bf16[144,2560]{1,0:T(8,128)(2,1)S(1)}, bf16[144,2560]{1,0:T(8,128)(2,1)}, u32[]{:S(2)}) copy-start(bf16[144,2560]{1,0:T(8,128)(2,1)} %rest_0_.3) | copy-start | bytes 2211844
  14.1 10.4 %copy-start.3 = (bf16[144,2560]{1,0:T(8,128)(2,1)S(1)}, bf16[144,2560]{1,0:T(8,128)(2,1)}, u32[]{:S(2)}) copy-start(bf16[144,2560]{1,0:T(8,128)(2,1)} %rest_0_.3) | copy-start | bytes 2211844
  14.9 9.5 %collective-permute-start.3 = (f32[32,144]{1,0:T(8,128)S(1)}, f32[32,144]{1,0:T(8,128)S(1)}, u32[]{:S(2)}, u32[]{:S(2)}) collective-permute-start(f32[32,144]{1,0:T(8,128)S(1)} %get-tuple-element.41.own), channel_id=1, source_target_pairs={{0,1},{1,0},{2,3},{3,2},{4,5},{5,4},{6,7},{7,6},{8,9},{9,8},{10,11... | collective-permute-start | bytes 55304 | tf_op jit(solution)/shard_map/ppermute | solution.py:337
  15.0 9.4 %collective-permute-start.4 = (f32[32,144]{1,0:T(8,128)S(1)}, f32[32,144]{1,0:T(8,128)S(1)}, u32[]{:S(2)}, u32[]{:S(2)}) collective-permute-start(f32[32,144]{1,0:T(8,128)S(1)} %get-tuple-element.41.own), channel_id=1, source_target_pairs={{0,2},{1,3},{2,0},{3,1},{4,6},{5,7},{6,4},{7,5},{8,10},{9,11},{10,... | collective-permute-start | bytes 55304 | tf_op jit(solution)/shard_map/ppermute | solution.py:337
  16.6 7.9 %collective-permute-start.5 = (f32[32,144]{1,0:T(8,128)S(1)}, f32[32,144]{1,0:T(8,128)S(1)}, u32[]{:S(2)}, u32[]{:S(2)}) collective-permute-start(f32[32,144]{1,0:T(8,128)S(1)} %get-tuple-element.41.own), channel_id=1, source_target_pairs={{0,3},{1,2},{2,1},{3,0},{4,7},{5,6},{6,5},{7,4},{8,11},{9,10},{10,... | collective-permute-start | bytes 55304 | tf_op jit(solution)/shard_map/ppermute | solution.py:337
  24.5 18.9 %collective-permute-start.11 = (bf16[144,2560]{1,0:T(8,128)(2,1)S(1)}, bf16[144,2560]{1,0:T(8,128)(2,1)S(1)}, u32[]{:S(2)}, u32[]{:S(2)}) collective-permute-start(bf16[144,2560]{1,0:T(8,128)(2,1)S(1)} %copy-done.3), channel_id=1, source_target_pairs={{0,2},{2,3},{3,1},{1,0},{4,6},{6,7},{7,5},{5,4},{8,10},{10,11},{11... | collective-permute-start | bytes 2211848 | tf_op jit(solution)/shard_map/ppermute | solution.py:358
  25.5 1.4 %collective-permute-start.6 = (bf16[32,1728]{1,0:T(8,128)(2,1)S(1)}, bf16[32,1728]{1,0:T(8,128)(2,1)S(1)}, u32[]{:S(2)}, u32[]{:S(2)}) collective-permute-start(bf16[32,1728]{1,0:T(8,128)(2,1)S(1)} %left_factor.1), channel_id=1, source_target_pairs={{0,4},{4,0},{8,12},{12,8},{16,20},{20,16},{24,28},{28,24},{1,5},{5... | collective-permute-start | bytes 331784 | tf_op jit(solution)/shard_map/ppermute | solution.py:337
  26.9 5.3 %collective-permute-start.7 = (bf16[32,1728]{1,0:T(8,128)(2,1)S(1)}, bf16[32,1728]{1,0:T(8,128)(2,1)S(1)}, u32[]{:S(2)}, u32[]{:S(2)}) collective-permute-start(bf16[32,1728]{1,0:T(8,128)(2,1)S(1)} %add_convert_fusion.own), channel_id=1, source_target_pairs={{0,8},{4,12},{8,0},{12,4},{16,24},{20,28},{24,16},{28,20},{1,9},{5... | collective-permute-start | bytes 331784 | tf_op jit(solution)/shard_map/ppermute | solution.py:337
  28.5 7.4 %collective-permute-start.8 = (bf16[32,1728]{1,0:T(8,128)(2,1)S(1)}, bf16[32,1728]{1,0:T(8,128)(2,1)S(1)}, u32[]{:S(2)}, u32[]{:S(2)}) collective-permute-start(bf16[32,1728]{1,0:T(8,128)(2,1)S(1)} %add_convert_fusion.own), channel_id=1, source_target_pairs={{0,16},{4,20},{8,24},{12,28},{16,0},{20,4},{24,8},{28,12},{1,17},{... | collective-permute-start | bytes 331784 | tf_op jit(solution)/shard_map/ppermute | solution.py:337
  30.0 5.9 %collective-permute-start.9 = (bf16[32,1728]{1,0:T(8,128)(2,1)S(1)}, bf16[32,1728]{1,0:T(8,128)(2,1)S(1)}, u32[]{:S(2)}, u32[]{:S(2)}) collective-permute-start(bf16[32,1728]{1,0:T(8,128)(2,1)S(1)} %add_convert_fusion.own), channel_id=1, source_target_pairs={{0,24},{4,28},{8,16},{12,20},{16,8},{20,12},{24,0},{28,4},{1,25},{... | collective-permute-start | bytes 331784 | tf_op jit(solution)/shard_map/ppermute | solution.py:337
  37.1 6.2 %collective-permute-start.10 = (bf16[2,32,144]{2,1,0:T(8,128)(2,1)S(1)}, bf16[2,32,144]{2,1,0:T(8,128)(2,1)S(1)}, u32[]{:S(2)}, u32[]{:S(2)}) collective-permute-start(bf16[2,32,144]{2,1,0:T(8,128)(2,1)S(1)} %get-tuple-element.44), channel_id=1, source_target_pairs={{0,3},{1,2},{2,1},{3,0},{4,7},{5,6},{6,5},{7,4},{8,11},{9,10},{10,... | collective-permute-start | bytes 55304 | tf_op jit(solution)/shard_map/ppermute | solution.py:337
  38.7 27.9 %collective-permute-start.26 = (bf16[144,2560]{1,0:T(8,128)(2,1)S(1)}, bf16[144,2560]{1,0:T(8,128)(2,1)S(1)}, u32[]{:S(2)}, u32[]{:S(2)}) collective-permute-start(bf16[144,2560]{1,0:T(8,128)(2,1)S(1)} %copy-done.3), channel_id=1, source_target_pairs={{0,1},{1,3},{3,2},{2,0},{4,5},{5,7},{7,6},{6,4},{8,9},{9,11},{11,1... | collective-permute-start | bytes 2211848 | tf_op jit(solution)/shard_map/ppermute | solution.py:358
  44.3 1.5 %collective-permute-start.12 = (f32[16,2560]{1,0:T(8,128)S(1)}, f32[16,2560]{1,0:T(8,128)S(1)}, u32[]{:S(2)}, u32[]{:S(2)}) collective-permute-start(f32[16,2560]{1,0:T(8,128)S(1)} %get-tuple-element.52), channel_id=1, source_target_pairs={{0,4},{4,0},{8,12},{12,8},{16,20},{20,16},{24,28},{28,24},{1,5},{5... | collective-permute-start | bytes 491528 | tf_op jit(solution)/shard_map/ppermute | solution.py:337
  46.3 6.4 %collective-permute-start.13 = (bf16[16,640]{1,0:T(8,128)(2,1)S(1)}, bf16[16,640]{1,0:T(8,128)(2,1)S(1)}, u32[]{:S(2)}, u32[]{:S(2)}) collective-permute-start(bf16[16,640]{1,0:T(8,128)(2,1)S(1)} %get-tuple-element.54), channel_id=1, source_target_pairs={{0,8},{4,12},{8,0},{12,4},{16,24},{20,28},{24,16},{28,20},{1,9},{5... | collective-permute-start | bytes 61448 | tf_op jit(solution)/shard_map/ppermute | solution.py:429
  47.5 5.2 %collective-permute-start.14 = (bf16[16,640]{1,0:T(8,128)(2,1)S(1)}, bf16[16,640]{1,0:T(8,128)(2,1)S(1)}, u32[]{:S(2)}, u32[]{:S(2)}) collective-permute-start(bf16[16,640]{1,0:T(8,128)(2,1)S(1)} %get-tuple-element.55), channel_id=1, source_target_pairs={{0,16},{4,20},{8,24},{12,28},{16,0},{20,4},{24,8},{28,12},{1,17},{... | collective-permute-start | bytes 61448 | tf_op jit(solution)/shard_map/ppermute | solution.py:429
  48.4 4.7 %collective-permute-start.15 = (bf16[16,640]{1,0:T(8,128)(2,1)S(1)}, bf16[16,640]{1,0:T(8,128)(2,1)S(1)}, u32[]{:S(2)}, u32[]{:S(2)}) collective-permute-start(bf16[16,640]{1,0:T(8,128)(2,1)S(1)} %get-tuple-element.56), channel_id=1, source_target_pairs={{0,24},{4,28},{8,16},{12,20},{16,8},{20,12},{24,0},{28,4},{1,25},{... | collective-permute-start | bytes 61448 | tf_op jit(solution)/shard_map/ppermute | solution.py:429
  53.1 4.6 %collective-permute-start.16 = (bf16[16,1024]{1,0:T(8,128)(2,1)S(1)}, bf16[16,1024]{1,0:T(8,128)(2,1)S(1)}, u32[]{:S(2)}, u32[]{:S(2)}) collective-permute-start(bf16[16,1024]{1,0:T(8,128)(2,1)S(1)} %pack.1.a), channel_id=1, source_target_pairs={{0,1},{1,0},{2,3},{3,2},{4,5},{5,4},{6,7},{7,6},{8,9},{9,8},{10,11... | collective-permute-start | bytes 98312 | tf_op jit(solution)/shard_map/ppermute | solution.py:337
  53.7 6.0 %collective-permute-start.17 = (bf16[16,1024]{1,0:T(8,128)(2,1)S(1)}, bf16[16,1024]{1,0:T(8,128)(2,1)S(1)}, u32[]{:S(2)}, u32[]{:S(2)}) collective-permute-start(bf16[16,1024]{1,0:T(8,128)(2,1)S(1)} %pack.1.a), channel_id=1, source_target_pairs={{0,2},{1,3},{2,0},{3,1},{4,6},{5,7},{6,4},{7,5},{8,10},{9,11},{10,... | collective-permute-start | bytes 98312 | tf_op jit(solution)/shard_map/ppermute | solution.py:337
  55.6 5.7 %collective-permute-start.18 = (bf16[16,1024]{1,0:T(8,128)(2,1)S(1)}, bf16[16,1024]{1,0:T(8,128)(2,1)S(1)}, u32[]{:S(2)}, u32[]{:S(2)}) collective-permute-start(bf16[16,1024]{1,0:T(8,128)(2,1)S(1)} %pack.1.a), channel_id=1, source_target_pairs={{0,3},{1,2},{2,1},{3,0},{4,7},{5,6},{6,5},{7,4},{8,11},{9,10},{10,... | collective-permute-start | bytes 98312 | tf_op jit(solution)/shard_map/ppermute | solution.py:337
  61.4 15.8 %collective-permute-start.27 = (bf16[144,2560]{1,0:T(8,128)(2,1)S(1)}, bf16[144,2560]{1,0:T(8,128)(2,1)S(1)}, u32[]{:S(2)}, u32[]{:S(2)}) collective-permute-start(bf16[144,2560]{1,0:T(8,128)(2,1)S(1)} %collective-permute-done.11.x_first.rest_1_.rest_0_), channel_id=1, source_target_pairs={{0,2},{2,3},{3,1},{1,0},{4,6},{6,7},{7,5},{5,4},{8,10},{10,11},{11... | collective-permute-start | bytes 2211848 | tf_op jit(solution)/shard_map/ppermute | solution.py:358
  61.5 6.7 %collective-permute-start.19 = (f32[16,640]{1,0:T(8,128)S(1)}, f32[16,640]{1,0:T(8,128)S(1)}, u32[]{:S(2)}, u32[]{:S(2)}) collective-permute-start(f32[16,640]{1,0:T(8,128)S(1)} %get-tuple-element.61.a0), channel_id=1, source_target_pairs={{0,8},{4,12},{8,0},{12,4},{16,24},{20,28},{24,16},{28,20},{1,9},{5... | collective-permute-start | bytes 122888 | tf_op jit(solution)/shard_map/ppermute | solution.py:337
  62.8 5.9 %collective-permute-start.20 = (f32[16,640]{1,0:T(8,128)S(1)}, f32[16,640]{1,0:T(8,128)S(1)}, u32[]{:S(2)}, u32[]{:S(2)}) collective-permute-start(f32[16,640]{1,0:T(8,128)S(1)} %get-tuple-element.61.a0), channel_id=1, source_target_pairs={{0,16},{4,20},{8,24},{12,28},{16,0},{20,4},{24,8},{28,12},{1,17},{... | collective-permute-start | bytes 122888 | tf_op jit(solution)/shard_map/ppermute | solution.py:337
  64.7 4.9 %collective-permute-start.21 = (f32[16,640]{1,0:T(8,128)S(1)}, f32[16,640]{1,0:T(8,128)S(1)}, u32[]{:S(2)}, u32[]{:S(2)}) collective-permute-start(f32[16,640]{1,0:T(8,128)S(1)} %get-tuple-element.61.a0), channel_id=1, source_target_pairs={{0,24},{4,28},{8,16},{12,20},{16,8},{20,12},{24,0},{28,4},{1,25},{... | collective-permute-start | bytes 122888 | tf_op jit(solution)/shard_map/ppermute | solution.py:337
  66.6 4.3 %collective-permute-start.22 = (f32[16,640]{1,0:T(8,128)S(1)}, f32[16,640]{1,0:T(8,128)S(1)}, u32[]{:S(2)}, u32[]{:S(2)}) collective-permute-start(f32[16,640]{1,0:T(8,128)S(1)} %get-tuple-element.61.a0), channel_id=1, source_target_pairs={{0,4},{4,0},{8,12},{12,8},{16,20},{20,16},{24,28},{28,24},{1,5},{5... | collective-permute-start | bytes 122888 | tf_op jit(solution)/shard_map/ppermute | solution.py:337
  68.1 2.8 %collective-permute-start.23 = (f32[16,640]{1,0:T(8,128)S(1)}, f32[16,640]{1,0:T(8,128)S(1)}, u32[]{:S(2)}, u32[]{:S(2)}) collective-permute-start(f32[16,640]{1,0:T(8,128)S(1)} %collective-permute-done.19.a1), channel_id=1, source_target_pairs={{0,4},{4,0},{8,12},{12,8},{16,20},{20,16},{24,28},{28,24},{1,5},{5... | collective-permute-start | bytes 122888 | tf_op jit(solution)/shard_map/ppermute | solution.py:337
  68.7 2.3 %collective-permute-start.24 = (f32[16,640]{1,0:T(8,128)S(1)}, f32[16,640]{1,0:T(8,128)S(1)}, u32[]{:S(2)}, u32[]{:S(2)}) collective-permute-start(f32[16,640]{1,0:T(8,128)S(1)} %collective-permute-done.20.a2), channel_id=1, source_target_pairs={{0,4},{4,0},{8,12},{12,8},{16,20},{20,16},{24,28},{28,24},{1,5},{5... | collective-permute-start | bytes 122888 | tf_op jit(solution)/shard_map/ppermute | solution.py:337
  69.6 1.4 %collective-permute-start.25 = (f32[16,640]{1,0:T(8,128)S(1)}, f32[16,640]{1,0:T(8,128)S(1)}, u32[]{:S(2)}, u32[]{:S(2)}) collective-permute-start(f32[16,640]{1,0:T(8,128)S(1)} %collective-permute-done.21.a3), channel_id=1, source_target_pairs={{0,4},{4,0},{8,12},{12,8},{16,20},{20,16},{24,28},{28,24},{1,5},{5... | collective-permute-start | bytes 122888 | tf_op jit(solution)/shard_map/ppermute | solution.py:337

commit v6 on v5

--- a/solution.py
+++ b/solution.py
@@ -109,25 +109,30 @@
     y_ref[...] = total
 
 
-def error_left(q_ref, e_any, out_ref, e_0, e_1, sems):
+def load_half(e_any, e_ref, sem):
+    copy = pltpu.make_async_copy(e_any.at[:, pl.ds(0, e_ref.shape[1])], e_ref, sem)
+    copy.start()
+    copy.wait()
+
+
+def error_left(q_ref, e_0, e_any, out_ref, e_1, sems):
     parts, _, width = q_ref.shape
     half = parts // 2
 
-    def place_of(k):
-        return (e_0, e_1)[k // half].at[:, pl.ds(k % half * width, width)]
-
     def load(k):
-        return pltpu.make_async_copy(e_any.at[:, pl.ds(k * width, width)], place_of(k), sems.at[k])
-
-    for k in range(parts):
+        return pltpu.make_async_copy(
+            e_any.at[:, pl.ds((half + k) * width, width)], e_1.at[:, pl.ds(k * width, width)], sems.at[k]
+        )
+
+    for k in range(half):
         load(k).start()
-    for k in range(parts):
+    total = dot(q_ref[0], e_0[:, :width], contract_last)
+    for k in range(1, half):
+        total += dot(q_ref[k], e_0[:, k * width : (k + 1) * width], contract_last)
+    for k in range(half):
         load(k).wait()
-        term = dot(q_ref[k], place_of(k)[...], contract_last)
-        if k:
-            out_ref[...] += term
-        else:
-            out_ref[...] = term
+        total += dot(q_ref[half + k], e_1[:, k * width : (k + 1) * width], contract_last)
+    out_ref[...] = total
 
 
 def left_factor(place, eq_ref, own, n1, n2, n3, dy_ref, out_ref, y4):
@@ -367,7 +372,15 @@
         place, out_grad,
         scratch=[pltpu.VMEM((all_tokens, hidden), bf16)],
     )
-    q_parts, _ = lax.optimization_barrier((q_parts, main_t))
+    (e_0,) = call(
+        load_half,
+        [like((hidden, features // 2), bf16)],
+        errors,
+        in_specs=[hbm_spec],
+        scratch=[pltpu.SemaphoreType.DMA(())],
+        vmem=46,
+    )
+    q_parts, _, e_0 = lax.optimization_barrier((q_parts, main_t, e_0))
     way_1, way_2 = [(0, 2), (2, 3), (3, 1), (1, 0)], [(0, 1), (1, 3), (3, 2), (2, 0)]
     q_full, y_own = call(
         project,
@@ -375,14 +388,15 @@
         place, q_own, *q_parts, activations,
     )
     y_parts = along_t(y_own)
-    eq, *held_errors = call(
+    eq, e_1 = call(
         error_left,
-        [like((rank, hidden), f32)] + [like((hidden, features // 2), bf16)] * 2,
-        q_full, errors,
-        in_specs=[vmem_spec, hbm_spec],
-        scratch=[pltpu.SemaphoreType.DMA((n_t,))],
+        [like((rank, hidden), f32), like((hidden, features // 2), bf16)],
+        q_full, e_0, errors,
+        in_specs=[vmem_spec, vmem_spec, hbm_spec],
+        scratch=[pltpu.SemaphoreType.DMA((n_t // 2,))],
         vmem=40,
     )
+    held_errors = (e_0, e_1)
     y_parts[0] = after(y_parts[0], eq)
     x_first = move(activations, way_1, *y_parts)
     (p_local,) = call(

time: 82.5 us -> 80.2 us (0.972)
  local copies, waits for them, and re-layouts: 2.7 us -> 0.01 us
  waiting for transfers between devices: 23.2 us -> 22 us
  starting transfers between devices: 28.1 us -> 29.2 us
    unnamed x8 -> x4, local copies, waits for them, and re-layouts: 2.7 us -> 0.01 us
    ppermute x22, waiting for transfers between devices: 18.1 us -> 16.7 us  [partners(): lax.ppermute(value, axis, [(i, i ^ k) for i in range(size)])]
    pallas_call x17 -> x18, Pallas kernels: 26.2 us -> 26.6 us  [call(): pl.pallas_call(kernel, out_shape=list(outs), in_specs=in_specs, out_specs...]
  transfers between devices with their start and end apart: 28 -> 28, of which waited for: 13 -> 13; matrix products, arithmetic and copies ran while one was open for 0% -> 0% of each run, Pallas kernels for 25% -> 26%
where the time goes in v6:
time: 80.2 us; the launch traced here: 80 us
  starting transfers between devices  29.2 us (36%)
  Pallas kernels  26.6 us (33%)
  waiting for transfers between devices  22 us (27%)
  other arithmetic  1.15 us (1%)
  between operations  1.05 us (1%)
    pallas_call x18, Pallas kernels, call(): pl.pallas_call(kernel, out_shape=list(outs), in_specs=in_specs, out_specs...  26.6 us
    ppermute x22, starting transfers between devices, partners(): lax.ppermute(value, axis, [(i, i ^ k) for i in range(size)])  24.6 us
    ppermute x22, waiting for transfers between devices, partners(): lax.ppermute(value, axis, [(i, i ^ k) for i in range(size)])  16.7 us
    ppermute x3, waiting for transfers between devices, move(): return lax.ppermute(after(value, *when), 'tensor', perm)  4.89 us
    ppermute x3, starting transfers between devices, body(): lax.ppermute(m, 'dp', [(i, i ^ 2 * k) for i in range(n_dp)])  3.55 us
  transfers between devices with their start and end apart: 28, of which 13 were waited for; matrix products, arithmetic and copies ran while one was open for 0% of the time, Pallas kernels for 26%

profile of v6, /device:TPU:0, one launch (start us, length us, event | category | flops | bytes accessed | tf_op | source)
XLA Modules:
  0.0 80.0 jit_solution(9692149413393498096)
XLA Ops:
  0.6 1.0 %convert_bitcast_fusion.own = bf16[32,640]{1,0:T(8,128)(2,1)S(1)} fusion(f32[640,32]{0,1:T(8,128)} %param.7), kind=kLoop, calls=%fused_computation.1 | loop fusion | flops 20480 | bytes 122880 | tf_op jit(solution)/shard_map/convert_element_type | solution.py:365
  1.7 3.0 %collective-permute-start = (bf16[32,640]{1,0:T(8,128)(2,1)S(1)}, bf16[32,640]{1,0:T(8,128)(2,1)S(1)}, u32[]{:S(2)}, u32[]{:S(2)}) collective-permute-start(bf16[32,640]{1,0:T(8,128)(2,1)S(1)} %convert_bitcast_fusion.own), channel_id=1, source_target_pairs={{0,1},{1,0},{2,3},{3,2},{4,5},{5,4},{6,7},{7,6},{8,9},{9,8},{10,11... | collective-permute-start | bytes 122888 | tf_op jit(solution)/shard_map/ppermute | solution.py:342
  4.7 2.6 %collective-permute-start.1 = (bf16[32,640]{1,0:T(8,128)(2,1)S(1)}, bf16[32,640]{1,0:T(8,128)(2,1)S(1)}, u32[]{:S(2)}, u32[]{:S(2)}) collective-permute-start(bf16[32,640]{1,0:T(8,128)(2,1)S(1)} %convert_bitcast_fusion.own), channel_id=1, source_target_pairs={{0,2},{1,3},{2,0},{3,1},{4,6},{5,7},{6,4},{7,5},{8,10},{9,11},{10,... | collective-permute-start | bytes 122888 | tf_op jit(solution)/shard_map/ppermute | solution.py:342
  7.3 0.0 collective-permute-start.2
  7.3 0.1 pad_add_fusion.place
  7.4 2.3 %load_half.1.e_0.base_ref = bf16[1728,1280]{1,0:T(8,128)(2,1)S(1)} custom-call(bf16[1728,2560]{1,0:T(8,128)(2,1)} %bitcast.8), custom_call_target="tpu_custom_call" | custom-call | bytes 13271040 | tf_op jit(solution)/shard_map/load_half/pallas_call | solution.py:83
  9.7 1.3 %arrange.1 = (bf16[1728,432]{1,0:T(8,128)(2,1)S(1)}, bf16[1728,144]{1,0:T(8,128)(2,1)S(1)}) custom-call(s32[3]{0:T(128)S(1)} %pad_add_fusion.place, bf16[576,1728]{1,0:T(8,128)(2,1)S(1)} %copy-done), custom_call_target="tpu_custom_call" | custom-call | bytes 3981324 | tf_op jit(solution)/shard_map/arrange/pallas_call | solution.py:83
  11.0 0.0 collective-permute-done.n1
  11.0 0.0 collective-permute-done.1.n2
  11.0 2.1 %collective-permute-done.2.n3 = bf16[32,640]{1,0:T(8,128)(2,1)S(1)} collective-permute-done((bf16[32,640]{1,0:T(8,128)(2,1)S(1)}, bf16[32,640]{1,0:T(8,128)(2,1)S(1)}, u32[]{:S(2)}, u32[]{:S(2)}) %collective-permute-start.2) | collective-permute-done | bytes 40992 | tf_op jit(solution)/shard_map/ppermute | solution.py:342
  13.1 0.9 %project.1 = (bf16[4,32,640]{2,1,0:T(8,128)(2,1)S(1)}, f32[32,144]{1,0:T(8,128)S(1)}) custom-call(s32[3]{0:T(128)S(1)} %pad_add_fusion.place, bf16[32,640]{1,0:T(8,128)(2,1)S(1)} %convert_bitcast_fusion.own, bf16[32,640]{1,0:T(8,128)(2,1)S(1)} %collective-permute-done.n1, bf16[32,640]{1,0:T(8,128)(2,1)S(1)} %collective-permute-done.1.n2, ...), custom_call_target="tpu_custom_call" | custom-call | bytes 1083404 | tf_op jit(solution)/shard_map/project/pallas_call | solution.py:83
  14.0 0.0 collective-permute-start.3
  14.0 2.3 %collective-permute-start.4 = (f32[32,144]{1,0:T(8,128)S(1)}, f32[32,144]{1,0:T(8,128)S(1)}, u32[]{:S(2)}, u32[]{:S(2)}) collective-permute-start(f32[32,144]{1,0:T(8,128)S(1)} %get-tuple-element.42.own), channel_id=1, source_target_pairs={{0,2},{1,3},{2,0},{3,1},{4,6},{5,7},{6,4},{7,5},{8,10},{9,11},{10,... | collective-permute-start | bytes 55304 | tf_op jit(solution)/shard_map/ppermute | solution.py:342
  16.4 2.1 %collective-permute-start.5 = (f32[32,144]{1,0:T(8,128)S(1)}, f32[32,144]{1,0:T(8,128)S(1)}, u32[]{:S(2)}, u32[]{:S(2)}) collective-permute-start(f32[32,144]{1,0:T(8,128)S(1)} %get-tuple-element.42.own), channel_id=1, source_target_pairs={{0,3},{1,2},{2,1},{3,0},{4,7},{5,6},{6,5},{7,4},{8,11},{9,10},{10,... | collective-permute-start | bytes 55304 | tf_op jit(solution)/shard_map/ppermute | solution.py:342
  18.4 3.2 %error_left.1 = (f32[32,1728]{1,0:T(8,128)S(1)}, bf16[1728,1280]{1,0:T(8,128)(2,1)S(1)}) custom-call(bf16[4,32,640]{2,1,0:T(8,128)(2,1)S(1)} %get-tuple-element.39.q_ref, bf16[1728,1280]{1,0:T(8,128)(2,1)S(1)} %load_half.1.e_0.base_ref, bf16[1728,2560]{1,0:T(8,128)(2,1)} %bitcast.9), custom_call_target="tpu_custom_call" | custom-call | bytes 18079744 | tf_op jit(solution)/shard_map/error_left/pallas_call | solution.py:83
  21.6 0.0 collective-permute-done.3.n1
  21.6 0.5 collective-permute-done.5.n3
  22.1 0.0 collective-permute-start.11
  22.1 1.0 %left_factor.1 = bf16[32,1728]{1,0:T(8,128)(2,1)S(1)} custom-call(s32[3]{0:T(128)S(1)} %pad_add_fusion.place, f32[32,1728]{1,0:T(8,128)S(1)} %get-tuple-element.41.eq_ref, f32[32,144]{1,0:T(8,128)S(1)} %get-tuple-element.42.own, f32[32,144]{1,0:T(8,128)S(1)} %collective-permute-done.3.n1, f32[32,144]{1,0:T(8,128)S(1)} %collective-permute-done.4.n2, ...), custom_call_target="tpu_custom_call" | custom-call | bytes 2396172 | tf_op jit(solution)/shard_map/left_factor/pallas_call | solution.py:83
  23.0 0.1 collective-permute-start.6
  23.1 1.3 %collective-permute-done.6 = bf16[32,1728]{1,0:T(8,128)(2,1)S(1)} collective-permute-done((bf16[32,1728]{1,0:T(8,128)(2,1)S(1)}, bf16[32,1728]{1,0:T(8,128)(2,1)S(1)}, u32[]{:S(2)}, u32[]{:S(2)}) %collective-permute-start.6) | collective-permute-done | bytes 110624 | tf_op jit(solution)/shard_map/ppermute | solution.py:342
  24.5 1.6 %collective-permute-start.7 = (bf16[32,1728]{1,0:T(8,128)(2,1)S(1)}, bf16[32,1728]{1,0:T(8,128)(2,1)S(1)}, u32[]{:S(2)}, u32[]{:S(2)}) collective-permute-start(bf16[32,1728]{1,0:T(8,128)(2,1)S(1)} %add_convert_fusion.own), channel_id=1, source_target_pairs={{0,8},{4,12},{8,0},{12,4},{16,24},{20,28},{24,16},{28,20},{1,9},{5... | collective-permute-start | bytes 331784 | tf_op jit(solution)/shard_map/ppermute | solution.py:342
  26.0 1.5 %collective-permute-start.8 = (bf16[32,1728]{1,0:T(8,128)(2,1)S(1)}, bf16[32,1728]{1,0:T(8,128)(2,1)S(1)}, u32[]{:S(2)}, u32[]{:S(2)}) collective-permute-start(bf16[32,1728]{1,0:T(8,128)(2,1)S(1)} %add_convert_fusion.own), channel_id=1, source_target_pairs={{0,16},{4,20},{8,24},{12,28},{16,0},{20,4},{24,8},{28,12},{1,17},{... | collective-permute-start | bytes 331784 | tf_op jit(solution)/shard_map/ppermute | solution.py:342
  27.5 0.5 collective-permute-start.9
  28.0 1.7 %collective-permute-done.7.n1 = bf16[32,1728]{1,0:T(8,128)(2,1)S(1)} collective-permute-done((bf16[32,1728]{1,0:T(8,128)(2,1)S(1)}, bf16[32,1728]{1,0:T(8,128)(2,1)S(1)}, u32[]{:S(2)}, u32[]{:S(2)}) %collective-permute-start.7) | collective-permute-done | bytes 110624 | tf_op jit(solution)/shard_map/ppermute | solution.py:342
  29.7 3.7 %collective-permute-done.8.n2 = bf16[32,1728]{1,0:T(8,128)(2,1)S(1)} collective-permute-done((bf16[32,1728]{1,0:T(8,128)(2,1)S(1)}, bf16[32,1728]{1,0:T(8,128)(2,1)S(1)}, u32[]{:S(2)}, u32[]{:S(2)}) %collective-permute-start.8) | collective-permute-done | bytes 110624 | tf_op jit(solution)/shard_map/ppermute | solution.py:342
  33.4 1.3 %weigh.1 = (bf16[32,1728]{1,0:T(8,128)(2,1)S(1)}, f32[32,32]{1,0:T(8,128)S(1)}, f32[2,32,144]{2,1,0:T(8,128)S(1)}, bf16[2,32,144]{2,1,0:T(8,128)(2,1)S(1)}) custom-call(s32[3]{0:T(128)S(1)} %pad_add_fusion.place, bf16[32,1728]{1,0:T(8,128)(2,1)S(1)} %add_convert_fusion.own, bf16[32,1728]{1,0:T(8,128)(2,1)S(1)} %collective-permute-done.7.n1, ...), custom_call_target="tpu_custom_call" | custom-call | bytes 2603020 | tf_op jit(solution)/shard_map/weigh/pallas_call | solution.py:83
  34.7 2.2 %collective-permute-start.10 = (bf16[2,32,144]{2,1,0:T(8,128)(2,1)S(1)}, bf16[2,32,144]{2,1,0:T(8,128)(2,1)S(1)}, u32[]{:S(2)}, u32[]{:S(2)}) collective-permute-start(bf16[2,32,144]{2,1,0:T(8,128)(2,1)S(1)} %get-tuple-element.45), channel_id=1, source_target_pairs={{0,3},{1,2},{2,1},{3,0},{4,7},{5,6},{6,5},{7,4},{8,11},{9,10},{10,... | collective-permute-start | bytes 55304 | tf_op jit(solution)/shard_map/ppermute | solution.py:342
  36.9 1.1 %collective-permute-start.26 = (bf16[144,2560]{1,0:T(8,128)(2,1)S(1)}, bf16[144,2560]{1,0:T(8,128)(2,1)S(1)}, u32[]{:S(2)}, u32[]{:S(2)}) collective-permute-start(bf16[144,2560]{1,0:T(8,128)(2,1)S(1)} %copy-done.1), channel_id=1, source_target_pairs={{0,1},{1,3},{3,2},{2,0},{4,5},{5,7},{7,6},{6,4},{8,9},{9,11},{11,1... | collective-permute-start | bytes 2211848 | tf_op jit(solution)/shard_map/ppermute | solution.py:363
  38.0 1.4 %error_right.1.te_ref = f32[32,2560]{1,0:T(8,128)S(1)} custom-call(bf16[32,1728]{1,0:T(8,128)(2,1)S(1)} %get-tuple-element.46.p_ref, bf16[1728,1280]{1,0:T(8,128)(2,1)S(1)} %load_half.1.e_0.base_ref, bf16[1728,1280]{1,0:T(8,128)(2,1)S(1)} %get-tuple-element.47.e_1.base_ref), custom_call_target="tpu_custom_call" | custom-call | bytes 9285632 | tf_op jit(solution)/shard_map/error_right/pallas_call | solution.py:83
  39.4 1.4 %collective-permute-done.10.got_ref = bf16[2,32,144]{2,1,0:T(8,128)(2,1)S(1)} collective-permute-done((bf16[2,32,144]{2,1,0:T(8,128)(2,1)S(1)}, bf16[2,32,144]{2,1,0:T(8,128)(2,1)S(1)}, u32[]{:S(2)}, u32[]{:S(2)}) %collective-permute-start.10) | collective-permute-done | bytes 18464 | tf_op jit(solution)/shard_map/ppermute | solution.py:342
  40.9 0.9 %right_term.1 = (f32[16,2560]{1,0:T(8,128)S(1)}, f32[16,2560]{1,0:T(8,128)S(1)}) custom-call(s32[3]{0:T(128)S(1)} %pad_add_fusion.place, f32[2,32,144]{2,1,0:T(8,128)S(1)} %get-tuple-element.44.near_ref, bf16[2,32,144]{2,1,0:T(8,128)(2,1)S(1)} %collective-permute-done.10.got_ref, f32[32,2560]{1,0:T(8,128)S(1)} %error_right.1.te_ref, ...), custom_call_target="tpu_custom_call" | custom-call | bytes 2185228 | tf_op jit(solution)/shard_map/right_term/pallas_call | solution.py:83
  41.8 0.1 collective-permute-start.12
  41.9 1.4 %collective-permute-done.12.got = f32[16,2560]{1,0:T(8,128)S(1)} collective-permute-done((f32[16,2560]{1,0:T(8,128)S(1)}, f32[16,2560]{1,0:T(8,128)S(1)}, u32[]{:S(2)}, u32[]{:S(2)}) %collective-permute-start.12) | collective-permute-done | bytes 163872 | tf_op jit(solution)/shard_map/ppermute | solution.py:342
  43.2 0.6 cut.1
  43.8 1.2 %collective-permute-start.13 = (bf16[16,640]{1,0:T(8,128)(2,1)S(1)}, bf16[16,640]{1,0:T(8,128)(2,1)S(1)}, u32[]{:S(2)}, u32[]{:S(2)}) collective-permute-start(bf16[16,640]{1,0:T(8,128)(2,1)S(1)} %get-tuple-element.54), channel_id=1, source_target_pairs={{0,8},{4,12},{8,0},{12,4},{16,24},{20,28},{24,16},{28,20},{1,9},{5... | collective-permute-start | bytes 61448 | tf_op jit(solution)/shard_map/ppermute | solution.py:443
  45.0 0.9 %collective-permute-start.14 = (bf16[16,640]{1,0:T(8,128)(2,1)S(1)}, bf16[16,640]{1,0:T(8,128)(2,1)S(1)}, u32[]{:S(2)}, u32[]{:S(2)}) collective-permute-start(bf16[16,640]{1,0:T(8,128)(2,1)S(1)} %get-tuple-element.55), channel_id=1, source_target_pairs={{0,16},{4,20},{8,24},{12,28},{16,0},{20,4},{24,8},{28,12},{1,17},{... | collective-permute-start | bytes 61448 | tf_op jit(solution)/shard_map/ppermute | solution.py:443
  45.9 1.5 %collective-permute-start.15 = (bf16[16,640]{1,0:T(8,128)(2,1)S(1)}, bf16[16,640]{1,0:T(8,128)(2,1)S(1)}, u32[]{:S(2)}, u32[]{:S(2)}) collective-permute-start(bf16[16,640]{1,0:T(8,128)(2,1)S(1)} %get-tuple-element.56), channel_id=1, source_target_pairs={{0,24},{4,28},{8,16},{12,20},{16,8},{20,12},{24,0},{28,4},{1,25},{... | collective-permute-start | bytes 61448 | tf_op jit(solution)/shard_map/ppermute | solution.py:443
  47.4 1.4 %accumulate.4.base_ref = f32[1728,1280]{1,0:T(8,128)S(1)} custom-call(bf16[1728,432]{1,0:T(8,128)(2,1)S(1)} %get-tuple-element.35.main_ref, bf16[1728,1280]{1,0:T(8,128)(2,1)S(1)} %load_half.1.e_0.base_ref, bf16[144,2560]{1,0:T(8,128)(2,1)S(1)} %copy-done.1, bf16[144,2560]{1,0:T(8,128)(2,1)S(1)} %collective-permute-done.11.x_first.rest_1_.rest_0_), custom_call_target="tpu_custom_call" | custom-call | bytes 16238592 | tf_op jit(solution)/shard_map/accumulate/pallas_call | solution.py:83
  48.8 1.4 %accumulate.5.base_ref = f32[1728,1280]{1,0:T(8,128)S(1)} custom-call(bf16[1728,432]{1,0:T(8,128)(2,1)S(1)} %get-tuple-element.35.main_ref, bf16[1728,1280]{1,0:T(8,128)(2,1)S(1)} %get-tuple-element.47.e_1.base_ref, bf16[144,2560]{1,0:T(8,128)(2,1)S(1)} %copy-done.1, bf16[144,2560]{1,0:T(8,128)(2,1)S(1)} %collective-permute-done.11.x_first.rest_1_.rest_0_), custom_call_target="tpu_custom_call" | custom-call | bytes 16238592 | tf_op jit(solution)/shard_map/accumulate/pallas_call | solution.py:83
  50.2 0.4 collective-permute-done.15.d
  50.6 0.1 pack.1.a
  50.6 0.8 %collective-permute-start.16 = (bf16[16,1024]{1,0:T(8,128)(2,1)S(1)}, bf16[16,1024]{1,0:T(8,128)(2,1)S(1)}, u32[]{:S(2)}, u32[]{:S(2)}) collective-permute-start(bf16[16,1024]{1,0:T(8,128)(2,1)S(1)} %pack.1.a), channel_id=1, source_target_pairs={{0,1},{1,0},{2,3},{3,2},{4,5},{5,4},{6,7},{7,6},{8,9},{9,8},{10,11... | collective-permute-start | bytes 98312 | tf_op jit(solution)/shard_map/ppermute | solution.py:342
  51.4 1.9 %collective-permute-start.17 = (bf16[16,1024]{1,0:T(8,128)(2,1)S(1)}, bf16[16,1024]{1,0:T(8,128)(2,1)S(1)}, u32[]{:S(2)}, u32[]{:S(2)}) collective-permute-start(bf16[16,1024]{1,0:T(8,128)(2,1)S(1)} %pack.1.a), channel_id=1, source_target_pairs={{0,2},{1,3},{2,0},{3,1},{4,6},{5,7},{6,4},{7,5},{8,10},{9,11},{10,... | collective-permute-start | bytes 98312 | tf_op jit(solution)/shard_map/ppermute | solution.py:342
  53.4 1.7 %collective-permute-start.18 = (bf16[16,1024]{1,0:T(8,128)(2,1)S(1)}, bf16[16,1024]{1,0:T(8,128)(2,1)S(1)}, u32[]{:S(2)}, u32[]{:S(2)}) collective-permute-start(bf16[16,1024]{1,0:T(8,128)(2,1)S(1)} %pack.1.a), channel_id=1, source_target_pairs={{0,3},{1,2},{2,1},{3,0},{4,7},{5,6},{6,5},{7,4},{8,11},{9,10},{10,... | collective-permute-start | bytes 98312 | tf_op jit(solution)/shard_map/ppermute | solution.py:342
  55.0 0.3 collective-permute-done.16.b
  55.4 2.2 %collective-permute-done.17.c = bf16[16,1024]{1,0:T(8,128)(2,1)S(1)} collective-permute-done((bf16[16,1024]{1,0:T(8,128)(2,1)S(1)}, bf16[16,1024]{1,0:T(8,128)(2,1)S(1)}, u32[]{:S(2)}, u32[]{:S(2)}) %collective-permute-start.17) | collective-permute-done | bytes 32800 | tf_op jit(solution)/shard_map/ppermute | solution.py:342
  57.6 1.5 %collective-permute-done.18.d = bf16[16,1024]{1,0:T(8,128)(2,1)S(1)} collective-permute-done((bf16[16,1024]{1,0:T(8,128)(2,1)S(1)}, bf16[16,1024]{1,0:T(8,128)(2,1)S(1)}, u32[]{:S(2)}, u32[]{:S(2)}) %collective-permute-start.18) | collective-permute-done | bytes 32800 | tf_op jit(solution)/shard_map/ppermute | solution.py:342
  59.1 0.0 collective-permute-start.27
  59.1 0.1 unpack.1
  59.2 1.5 %collective-permute-start.19 = (f32[16,640]{1,0:T(8,128)S(1)}, f32[16,640]{1,0:T(8,128)S(1)}, u32[]{:S(2)}, u32[]{:S(2)}) collective-permute-start(f32[16,640]{1,0:T(8,128)S(1)} %get-tuple-element.61.a0), channel_id=1, source_target_pairs={{0,8},{4,12},{8,0},{12,4},{16,24},{20,28},{24,16},{28,20},{1,9},{5... | collective-permute-start | bytes 122888 | tf_op jit(solution)/shard_map/ppermute | solution.py:342
  60.7 1.5 %collective-permute-start.20 = (f32[16,640]{1,0:T(8,128)S(1)}, f32[16,640]{1,0:T(8,128)S(1)}, u32[]{:S(2)}, u32[]{:S(2)}) collective-permute-start(f32[16,640]{1,0:T(8,128)S(1)} %get-tuple-element.61.a0), channel_id=1, source_target_pairs={{0,16},{4,20},{8,24},{12,28},{16,0},{20,4},{24,8},{28,12},{1,17},{... | collective-permute-start | bytes 122888 | tf_op jit(solution)/shard_map/ppermute | solution.py:342
  62.2 0.5 collective-permute-start.21
  62.7 1.7 %invert_cholesky.1.linv = f32[32,32]{1,0:T(8,128)S(1)} custom-call(f32[32,32]{1,0:T(8,128)S(1)} %get-tuple-element.59.g_ref), custom_call_target="tpu_custom_call" | custom-call | bytes 8192 | tf_op jit(solution)/shard_map/invert_cholesky/pallas_call | solution.py:83
  64.4 0.0 collective-permute-done.26.rest_1_
  64.4 0.1 collective-permute-start.22
  64.5 1.4 %accumulate.6.acc_0 = f32[1728,1280]{1,0:T(8,128)S(1)} custom-call(bf16[1728,432]{1,0:T(8,128)(2,1)S(1)} %get-tuple-element.35.main_ref, f32[1728,1280]{1,0:T(8,128)S(1)} %accumulate.4.base_ref, bf16[144,2560]{1,0:T(8,128)(2,1)S(1)} %collective-permute-done.11.x_first.rest_1_.rest_0_, bf16[144,2560]{1,0:T(8,128)(2,1)S(1)} %collective-permute-done.26.rest_1_), custom_call_target="tpu_custom_call" | custom-call | flops 2000000000 | bytes 20662272 | tf_op jit(solution)/shard_map/accumulate/pallas_call | solution.py:83
  65.9 0.5 collective-permute-start.23
  66.4 0.1 collective-permute-start.24
  66.5 0.6 collective-permute-done.21.a3
  67.1 1.4 %accumulate.7.acc_1 = f32[1728,1280]{1,0:T(8,128)S(1)} custom-call(bf16[1728,432]{1,0:T(8,128)(2,1)S(1)} %get-tuple-element.35.main_ref, f32[1728,1280]{1,0:T(8,128)S(1)} %accumulate.5.base_ref, bf16[144,2560]{1,0:T(8,128)(2,1)S(1)} %collective-permute-done.11.x_first.rest_1_.rest_0_, bf16[144,2560]{1,0:T(8,128)(2,1)S(1)} %collective-permute-done.26.rest_1_), custom_call_target="tpu_custom_call" | custom-call | flops 2000000000 | bytes 20662272 | tf_op jit(solution)/shard_map/accumulate/pallas_call | solution.py:83
  68.5 1.5 %finish.1 = (f32[32,640]{1,0:T(8,128)}, bf16[1728,240]{1,0:T(8,128)(2,1)S(1)}, bf16[96,2560]{1,0:T(8,128)(2,1)S(1)}) custom-call(s32[3]{0:T(128)S(1)} %pad_add_fusion.place, f32[32,32]{1,0:T(8,128)S(1)} %invert_cholesky.1.linv, bf16[32,1728]{1,0:T(8,128)(2,1)S(1)} %get-tuple-element.46.p_ref, bf16[1728,144]{1,0:T(8,128)(2,1)S(1)} %get-tuple-element.60.rest_ref, ...), custom_call_target="tpu_custom_call" | custom-call | bytes 2342924 | tf_op jit(solution)/shard_map/finish/pallas_call | solution.py:83
  70.0 4.9 %collective-permute-done.27.x_any = bf16[144,2560]{1,0:T(8,128)(2,1)S(1)} collective-permute-done((bf16[144,2560]{1,0:T(8,128)(2,1)S(1)}, bf16[144,2560]{1,0:T(8,128)(2,1)S(1)}, u32[]{:S(2)}, u32[]{:S(2)}) %collective-permute-start.27) | collective-permute-done | bytes 737312 | tf_op jit(solution)/shard_map/ppermute | solution.py:363
  74.9 4.9 %rebuild.1 = bf16[1728,2560]{1,0:T(8,128)(2,1)} custom-call(bf16[1728,240]{1,0:T(8,128)(2,1)S(1)} %get-tuple-element.63.left_ref, bf16[96,2560]{1,0:T(8,128)(2,1)S(1)} %get-tuple-element.64.right_ref, f32[1728,1280]{1,0:T(8,128)S(1)} %accumulate.6.acc_0, f32[1728,1280]{1,0:T(8,128)S(1)} %accumulate.7.acc_1, bf16[144,2560]{1,0:T(8,128)(2,1)S(1)} %collective-permute-done.27.x_any), custom_call_target="tpu_custom_call" | custom-call | bytes 28600320 | tf_op jit(solution)/shard_map/rebuild/pallas_call | solution.py:83
  (17 shorter events, 0.1 us)
Async XLA Ops:
  0.6 9.0 %copy-start = (bf16[576,1728]{1,0:T(8,128)(2,1)S(1)}, bf16[576,1728]{1,0:T(8,128)(2,1)}, u32[]{:S(2)}) copy-start(bf16[576,1728]{1,0:T(8,128)(2,1)} %dy_ref.5) | copy-start | bytes 5971972
  0.6 12.5 %copy-start.1 = (bf16[144,2560]{1,0:T(8,128)(2,1)S(1)}, bf16[144,2560]{1,0:T(8,128)(2,1)}, u32[]{:S(2)}) copy-start(bf16[144,2560]{1,0:T(8,128)(2,1)} %rest_0_.3) | copy-start | bytes 2211844
  1.7 9.3 %collective-permute-start = (bf16[32,640]{1,0:T(8,128)(2,1)S(1)}, bf16[32,640]{1,0:T(8,128)(2,1)S(1)}, u32[]{:S(2)}, u32[]{:S(2)}) collective-permute-start(bf16[32,640]{1,0:T(8,128)(2,1)S(1)} %convert_bitcast_fusion.own), channel_id=1, source_target_pairs={{0,1},{1,0},{2,3},{3,2},{4,5},{5,4},{6,7},{7,6},{8,9},{9,8},{10,11... | collective-permute-start | bytes 122888 | tf_op jit(solution)/shard_map/ppermute | solution.py:342
  4.7 6.3 %collective-permute-start.1 = (bf16[32,640]{1,0:T(8,128)(2,1)S(1)}, bf16[32,640]{1,0:T(8,128)(2,1)S(1)}, u32[]{:S(2)}, u32[]{:S(2)}) collective-permute-start(bf16[32,640]{1,0:T(8,128)(2,1)S(1)} %convert_bitcast_fusion.own), channel_id=1, source_target_pairs={{0,2},{1,3},{2,0},{3,1},{4,6},{5,7},{6,4},{7,5},{8,10},{9,11},{10,... | collective-permute-start | bytes 122888 | tf_op jit(solution)/shard_map/ppermute | solution.py:342
  7.3 5.8 %collective-permute-start.2 = (bf16[32,640]{1,0:T(8,128)(2,1)S(1)}, bf16[32,640]{1,0:T(8,128)(2,1)S(1)}, u32[]{:S(2)}, u32[]{:S(2)}) collective-permute-start(bf16[32,640]{1,0:T(8,128)(2,1)S(1)} %convert_bitcast_fusion.own), channel_id=1, source_target_pairs={{0,3},{1,2},{2,1},{3,0},{4,7},{5,6},{6,5},{7,4},{8,11},{9,10},{10,... | collective-permute-start | bytes 122888 | tf_op jit(solution)/shard_map/ppermute | solution.py:342
  14.0 7.6 %collective-permute-start.3 = (f32[32,144]{1,0:T(8,128)S(1)}, f32[32,144]{1,0:T(8,128)S(1)}, u32[]{:S(2)}, u32[]{:S(2)}) collective-permute-start(f32[32,144]{1,0:T(8,128)S(1)} %get-tuple-element.42.own), channel_id=1, source_target_pairs={{0,1},{1,0},{2,3},{3,2},{4,5},{5,4},{6,7},{7,6},{8,9},{9,8},{10,11... | collective-permute-start | bytes 55304 | tf_op jit(solution)/shard_map/ppermute | solution.py:342
  14.0 7.6 %collective-permute-start.4 = (f32[32,144]{1,0:T(8,128)S(1)}, f32[32,144]{1,0:T(8,128)S(1)}, u32[]{:S(2)}, u32[]{:S(2)}) collective-permute-start(f32[32,144]{1,0:T(8,128)S(1)} %get-tuple-element.42.own), channel_id=1, source_target_pairs={{0,2},{1,3},{2,0},{3,1},{4,6},{5,7},{6,4},{7,5},{8,10},{9,11},{10,... | collective-permute-start | bytes 55304 | tf_op jit(solution)/shard_map/ppermute | solution.py:342
  16.4 5.7 %collective-permute-start.5 = (f32[32,144]{1,0:T(8,128)S(1)}, f32[32,144]{1,0:T(8,128)S(1)}, u32[]{:S(2)}, u32[]{:S(2)}) collective-permute-start(f32[32,144]{1,0:T(8,128)S(1)} %get-tuple-element.42.own), channel_id=1, source_target_pairs={{0,3},{1,2},{2,1},{3,0},{4,7},{5,6},{6,5},{7,4},{8,11},{9,10},{10,... | collective-permute-start | bytes 55304 | tf_op jit(solution)/shard_map/ppermute | solution.py:342
  22.1 18.8 %collective-permute-start.11 = (bf16[144,2560]{1,0:T(8,128)(2,1)S(1)}, bf16[144,2560]{1,0:T(8,128)(2,1)S(1)}, u32[]{:S(2)}, u32[]{:S(2)}) collective-permute-start(bf16[144,2560]{1,0:T(8,128)(2,1)S(1)} %copy-done.1), channel_id=1, source_target_pairs={{0,2},{2,3},{3,1},{1,0},{4,6},{6,7},{7,5},{5,4},{8,10},{10,11},{11... | collective-permute-start | bytes 2211848 | tf_op jit(solution)/shard_map/ppermute | solution.py:363
  23.0 1.4 %collective-permute-start.6 = (bf16[32,1728]{1,0:T(8,128)(2,1)S(1)}, bf16[32,1728]{1,0:T(8,128)(2,1)S(1)}, u32[]{:S(2)}, u32[]{:S(2)}) collective-permute-start(bf16[32,1728]{1,0:T(8,128)(2,1)S(1)} %left_factor.1), channel_id=1, source_target_pairs={{0,4},{4,0},{8,12},{12,8},{16,20},{20,16},{24,28},{28,24},{1,5},{5... | collective-permute-start | bytes 331784 | tf_op jit(solution)/shard_map/ppermute | solution.py:342
  24.5 5.3 %collective-permute-start.7 = (bf16[32,1728]{1,0:T(8,128)(2,1)S(1)}, bf16[32,1728]{1,0:T(8,128)(2,1)S(1)}, u32[]{:S(2)}, u32[]{:S(2)}) collective-permute-start(bf16[32,1728]{1,0:T(8,128)(2,1)S(1)} %add_convert_fusion.own), channel_id=1, source_target_pairs={{0,8},{4,12},{8,0},{12,4},{16,24},{20,28},{24,16},{28,20},{1,9},{5... | collective-permute-start | bytes 331784 | tf_op jit(solution)/shard_map/ppermute | solution.py:342
  26.0 7.4 %collective-permute-start.8 = (bf16[32,1728]{1,0:T(8,128)(2,1)S(1)}, bf16[32,1728]{1,0:T(8,128)(2,1)S(1)}, u32[]{:S(2)}, u32[]{:S(2)}) collective-permute-start(bf16[32,1728]{1,0:T(8,128)(2,1)S(1)} %add_convert_fusion.own), channel_id=1, source_target_pairs={{0,16},{4,20},{8,24},{12,28},{16,0},{20,4},{24,8},{28,12},{1,17},{... | collective-permute-start | bytes 331784 | tf_op jit(solution)/shard_map/ppermute | solution.py:342
  27.5 5.9 %collective-permute-start.9 = (bf16[32,1728]{1,0:T(8,128)(2,1)S(1)}, bf16[32,1728]{1,0:T(8,128)(2,1)S(1)}, u32[]{:S(2)}, u32[]{:S(2)}) collective-permute-start(bf16[32,1728]{1,0:T(8,128)(2,1)S(1)} %add_convert_fusion.own), channel_id=1, source_target_pairs={{0,24},{4,28},{8,16},{12,20},{16,8},{20,12},{24,0},{28,4},{1,25},{... | collective-permute-start | bytes 331784 | tf_op jit(solution)/shard_map/ppermute | solution.py:342
  34.7 6.2 %collective-permute-start.10 = (bf16[2,32,144]{2,1,0:T(8,128)(2,1)S(1)}, bf16[2,32,144]{2,1,0:T(8,128)(2,1)S(1)}, u32[]{:S(2)}, u32[]{:S(2)}) collective-permute-start(bf16[2,32,144]{2,1,0:T(8,128)(2,1)S(1)} %get-tuple-element.45), channel_id=1, source_target_pairs={{0,3},{1,2},{2,1},{3,0},{4,7},{5,6},{6,5},{7,4},{8,11},{9,10},{10,... | collective-permute-start | bytes 55304 | tf_op jit(solution)/shard_map/ppermute | solution.py:342
  36.9 27.5 %collective-permute-start.26 = (bf16[144,2560]{1,0:T(8,128)(2,1)S(1)}, bf16[144,2560]{1,0:T(8,128)(2,1)S(1)}, u32[]{:S(2)}, u32[]{:S(2)}) collective-permute-start(bf16[144,2560]{1,0:T(8,128)(2,1)S(1)} %copy-done.1), channel_id=1, source_target_pairs={{0,1},{1,3},{3,2},{2,0},{4,5},{5,7},{7,6},{6,4},{8,9},{9,11},{11,1... | collective-permute-start | bytes 2211848 | tf_op jit(solution)/shard_map/ppermute | solution.py:363
  41.8 1.5 %collective-permute-start.12 = (f32[16,2560]{1,0:T(8,128)S(1)}, f32[16,2560]{1,0:T(8,128)S(1)}, u32[]{:S(2)}, u32[]{:S(2)}) collective-permute-start(f32[16,2560]{1,0:T(8,128)S(1)} %get-tuple-element.52), channel_id=1, source_target_pairs={{0,4},{4,0},{8,12},{12,8},{16,20},{20,16},{24,28},{28,24},{1,5},{5... | collective-permute-start | bytes 491528 | tf_op jit(solution)/shard_map/ppermute | solution.py:342
  43.8 6.4 %collective-permute-start.13 = (bf16[16,640]{1,0:T(8,128)(2,1)S(1)}, bf16[16,640]{1,0:T(8,128)(2,1)S(1)}, u32[]{:S(2)}, u32[]{:S(2)}) collective-permute-start(bf16[16,640]{1,0:T(8,128)(2,1)S(1)} %get-tuple-element.54), channel_id=1, source_target_pairs={{0,8},{4,12},{8,0},{12,4},{16,24},{20,28},{24,16},{28,20},{1,9},{5... | collective-permute-start | bytes 61448 | tf_op jit(solution)/shard_map/ppermute | solution.py:443
  45.0 5.2 %collective-permute-start.14 = (bf16[16,640]{1,0:T(8,128)(2,1)S(1)}, bf16[16,640]{1,0:T(8,128)(2,1)S(1)}, u32[]{:S(2)}, u32[]{:S(2)}) collective-permute-start(bf16[16,640]{1,0:T(8,128)(2,1)S(1)} %get-tuple-element.55), channel_id=1, source_target_pairs={{0,16},{4,20},{8,24},{12,28},{16,0},{20,4},{24,8},{28,12},{1,17},{... | collective-permute-start | bytes 61448 | tf_op jit(solution)/shard_map/ppermute | solution.py:443
  45.9 4.7 %collective-permute-start.15 = (bf16[16,640]{1,0:T(8,128)(2,1)S(1)}, bf16[16,640]{1,0:T(8,128)(2,1)S(1)}, u32[]{:S(2)}, u32[]{:S(2)}) collective-permute-start(bf16[16,640]{1,0:T(8,128)(2,1)S(1)} %get-tuple-element.56), channel_id=1, source_target_pairs={{0,24},{4,28},{8,16},{12,20},{16,8},{20,12},{24,0},{28,4},{1,25},{... | collective-permute-start | bytes 61448 | tf_op jit(solution)/shard_map/ppermute | solution.py:443
  50.6 4.7 %collective-permute-start.16 = (bf16[16,1024]{1,0:T(8,128)(2,1)S(1)}, bf16[16,1024]{1,0:T(8,128)(2,1)S(1)}, u32[]{:S(2)}, u32[]{:S(2)}) collective-permute-start(bf16[16,1024]{1,0:T(8,128)(2,1)S(1)} %pack.1.a), channel_id=1, source_target_pairs={{0,1},{1,0},{2,3},{3,2},{4,5},{5,4},{6,7},{7,6},{8,9},{9,8},{10,11... | collective-permute-start | bytes 98312 | tf_op jit(solution)/shard_map/ppermute | solution.py:342
  51.4 6.2 %collective-permute-start.17 = (bf16[16,1024]{1,0:T(8,128)(2,1)S(1)}, bf16[16,1024]{1,0:T(8,128)(2,1)S(1)}, u32[]{:S(2)}, u32[]{:S(2)}) collective-permute-start(bf16[16,1024]{1,0:T(8,128)(2,1)S(1)} %pack.1.a), channel_id=1, source_target_pairs={{0,2},{1,3},{2,0},{3,1},{4,6},{5,7},{6,4},{7,5},{8,10},{9,11},{10,... | collective-permute-start | bytes 98312 | tf_op jit(solution)/shard_map/ppermute | solution.py:342
  53.4 5.7 %collective-permute-start.18 = (bf16[16,1024]{1,0:T(8,128)(2,1)S(1)}, bf16[16,1024]{1,0:T(8,128)(2,1)S(1)}, u32[]{:S(2)}, u32[]{:S(2)}) collective-permute-start(bf16[16,1024]{1,0:T(8,128)(2,1)S(1)} %pack.1.a), channel_id=1, source_target_pairs={{0,3},{1,2},{2,1},{3,0},{4,7},{5,6},{6,5},{7,4},{8,11},{9,10},{10,... | collective-permute-start | bytes 98312 | tf_op jit(solution)/shard_map/ppermute | solution.py:342
  59.1 15.8 %collective-permute-start.27 = (bf16[144,2560]{1,0:T(8,128)(2,1)S(1)}, bf16[144,2560]{1,0:T(8,128)(2,1)S(1)}, u32[]{:S(2)}, u32[]{:S(2)}) collective-permute-start(bf16[144,2560]{1,0:T(8,128)(2,1)S(1)} %collective-permute-done.11.x_first.rest_1_.rest_0_), channel_id=1, source_target_pairs={{0,2},{2,3},{3,1},{1,0},{4,6},{6,7},{7,5},{5,4},{8,10},{10,11},{11... | collective-permute-start | bytes 2211848 | tf_op jit(solution)/shard_map/ppermute | solution.py:363
  59.2 6.7 %collective-permute-start.19 = (f32[16,640]{1,0:T(8,128)S(1)}, f32[16,640]{1,0:T(8,128)S(1)}, u32[]{:S(2)}, u32[]{:S(2)}) collective-permute-start(f32[16,640]{1,0:T(8,128)S(1)} %get-tuple-element.61.a0), channel_id=1, source_target_pairs={{0,8},{4,12},{8,0},{12,4},{16,24},{20,28},{24,16},{28,20},{1,9},{5... | collective-permute-start | bytes 122888 | tf_op jit(solution)/shard_map/ppermute | solution.py:342
  60.7 5.7 %collective-permute-start.20 = (f32[16,640]{1,0:T(8,128)S(1)}, f32[16,640]{1,0:T(8,128)S(1)}, u32[]{:S(2)}, u32[]{:S(2)}) collective-permute-start(f32[16,640]{1,0:T(8,128)S(1)} %get-tuple-element.61.a0), channel_id=1, source_target_pairs={{0,16},{4,20},{8,24},{12,28},{16,0},{20,4},{24,8},{28,12},{1,17},{... | collective-permute-start | bytes 122888 | tf_op jit(solution)/shard_map/ppermute | solution.py:342
  62.2 4.9 %collective-permute-start.21 = (f32[16,640]{1,0:T(8,128)S(1)}, f32[16,640]{1,0:T(8,128)S(1)}, u32[]{:S(2)}, u32[]{:S(2)}) collective-permute-start(f32[16,640]{1,0:T(8,128)S(1)} %get-tuple-element.61.a0), channel_id=1, source_target_pairs={{0,24},{4,28},{8,16},{12,20},{16,8},{20,12},{24,0},{28,4},{1,25},{... | collective-permute-start | bytes 122888 | tf_op jit(solution)/shard_map/ppermute | solution.py:342
  64.4 4.1 %collective-permute-start.22 = (f32[16,640]{1,0:T(8,128)S(1)}, f32[16,640]{1,0:T(8,128)S(1)}, u32[]{:S(2)}, u32[]{:S(2)}) collective-permute-start(f32[16,640]{1,0:T(8,128)S(1)} %get-tuple-element.61.a0), channel_id=1, source_target_pairs={{0,4},{4,0},{8,12},{12,8},{16,20},{20,16},{24,28},{28,24},{1,5},{5... | collective-permute-start | bytes 122888 | tf_op jit(solution)/shard_map/ppermute | solution.py:342
  65.9 2.6 %collective-permute-start.23 = (f32[16,640]{1,0:T(8,128)S(1)}, f32[16,640]{1,0:T(8,128)S(1)}, u32[]{:S(2)}, u32[]{:S(2)}) collective-permute-start(f32[16,640]{1,0:T(8,128)S(1)} %collective-permute-done.19.a1), channel_id=1, source_target_pairs={{0,4},{4,0},{8,12},{12,8},{16,20},{20,16},{24,28},{28,24},{1,5},{5... | collective-permute-start | bytes 122888 | tf_op jit(solution)/shard_map/ppermute | solution.py:342
  66.4 2.1 %collective-permute-start.24 = (f32[16,640]{1,0:T(8,128)S(1)}, f32[16,640]{1,0:T(8,128)S(1)}, u32[]{:S(2)}, u32[]{:S(2)}) collective-permute-start(f32[16,640]{1,0:T(8,128)S(1)} %collective-permute-done.20.a2), channel_id=1, source_target_pairs={{0,4},{4,0},{8,12},{12,8},{16,20},{20,16},{24,28},{28,24},{1,5},{5... | collective-permute-start | bytes 122888 | tf_op jit(solution)/shard_map/ppermute | solution.py:342
  67.1 1.4 %collective-permute-start.25 = (f32[16,640]{1,0:T(8,128)S(1)}, f32[16,640]{1,0:T(8,128)S(1)}, u32[]{:S(2)}, u32[]{:S(2)}) collective-permute-start(f32[16,640]{1,0:T(8,128)S(1)} %collective-permute-done.21.a3), channel_id=1, source_target_pairs={{0,4},{4,0},{8,12},{12,8},{16,20},{20,16},{24,28},{28,24},{1,5},{5... | collective-permute-start | bytes 122888 | tf_op jit(solution)/shard_map/ppermute | solution.py:342

commit v7 on v6

--- a/solution.py
+++ b/solution.py
@@ -67,7 +67,7 @@
     return high, (v - high.astype(f32)).astype(bf16)
 
 
-def call(kernel, outs, *args, scratch=(), grid=None, in_specs=None, out_specs=None, vmem=8, flops=0, moved=0):
+def call(kernel, outs, *args, scratch=(), in_specs=None, out_specs=None, vmem=8, flops=0):
     vmem_spec = pl.BlockSpec(memory_space=pltpu.VMEM)
     if in_specs is None:
         in_specs = [
@@ -76,7 +76,6 @@
         ]
     if out_specs is None:
         out_specs = [vmem_spec] * len(outs)
-    extra = {} if grid is None else {"grid": grid}
     size = sum(a.size * a.dtype.itemsize for a in args) + sum(
         o.size * o.dtype.itemsize for o in outs
     )
@@ -88,7 +87,6 @@
         scratch_shapes=list(scratch),
         compiler_params=pltpu.CompilerParams(vmem_limit_bytes=vmem * MIB),
         cost_estimate=pl.CostEstimate(flops=flops, bytes_accessed=size, transcendentals=0),
-        **extra,
         name=kernel.__name__ if hasattr(kernel, "__name__") else kernel.func.__name__,
     )(*args)
     return result
@@ -206,10 +204,12 @@
     total = (a[...] + b[...].astype(f32)) + (c[...].astype(f32) + d[...].astype(f32))
     out_ref[:, :width] = total.astype(bf16)
     left = jnp.concatenate((gram_ref[:half, :], gram_ref[half:, :]), axis=1)
-    for k in range(3):
-        term = left.astype(bf16)
-        left = left - term.astype(f32)
-        out_ref[:, width + k * 128 : width + k * 128 + 2 * rank] = term
+    terms = []
+    for _ in range(3):
+        terms.append(left.astype(bf16).astype(f32))
+        left = left - terms[-1]
+    terms.append(jnp.zeros_like(left))
+    out_ref[:, width:] = jnp.concatenate(terms, axis=1).astype(bf16)
 
 
 def unpack(a, b, c, d, out_ref, gram_ref):
@@ -220,7 +220,10 @@
         return ref[:, at : at + count].astype(f32)
 
     out_ref[...] = (part(a, 0, width) + part(b, 0, width)) + (part(c, 0, width) + part(d, 0, width))
-    grams = [sum(part(ref, width + k * 128, 2 * rank) for k in range(3)) for ref in (a, b, c, d)]
+    grams = []
+    for ref in (a, b, c, d):
+        terms = part(ref, width, 8 * rank)
+        grams.append(terms[:, : 2 * rank] + (terms[:, 2 * rank : 4 * rank] + terms[:, 4 * rank : 6 * rank]))
     total = (grams[0] + grams[1]) + (grams[2] + grams[3])
     gram_ref[:half, :] = total[:, :rank]
     gram_ref[half:, :] = total[:, rank:]
@@ -460,7 +463,7 @@
         add_tokens(k, 0, 0, e_held, ((0, tokens), (0, early)), activations, x_first)
         for k, e_held in enumerate(held_errors)
     ]
-    (mine,) = call(pack, [like((half, rows + 384), bf16)], parts[0], *arrived, gram)
+    (mine,) = call(pack, [like((half, rows + 8 * rank), bf16)], parts[0], *arrived, gram)
     mine = after(mine, *accs)
     z1, z2, z3 = along_t(mine)
     x_third = move(x_first, way_1, z1, z2, z3)
@@ -487,9 +490,9 @@
         out_specs=[anywhere],
         scratch=[
             pltpu.VMEM((tokens + 3 * rank, features), bf16),
-            pltpu.VMEM((4, hidden, 256), bf16),
+            pltpu.VMEM((5, hidden, 256), bf16),
             pltpu.SemaphoreType.DMA(()),
-            pltpu.SemaphoreType.DMA((4,)),
+            pltpu.SemaphoreType.DMA((5,)),
         ],
     )
     return (new_error[None], new_factor.T)

time: 80.2 us -> 79.8 us (level)
  transfers between devices with their start and end apart: 28 -> 28, of which waited for: 13 -> 12; matrix products, arithmetic and copies ran while one was open for 0% -> 0% of each run, Pallas kernels for 26% -> 26%
where the time goes in v7:
time: 79.8 us; the launch traced here: 79.7 us
  starting transfers between devices  29.7 us (37%)
  Pallas kernels  26.4 us (33%)
  waiting for transfers between devices  21.4 us (27%)
  other arithmetic  1.15 us (1%)
  between operations  1.05 us (1%)
    pallas_call x18, Pallas kernels, call(): pl.pallas_call(kernel, out_shape=list(outs), in_specs=in_specs, out_specs...  26.4 us
    ppermute x22, starting transfers between devices, partners(): lax.ppermute(value, axis, [(i, i ^ k) for i in range(size)])  25 us
    ppermute x22, waiting for transfers between devices, partners(): lax.ppermute(value, axis, [(i, i ^ k) for i in range(size)])  16.2 us
    ppermute x3, waiting for transfers between devices, move(): return lax.ppermute(after(value, *when), 'tensor', perm)  4.85 us
    ppermute x3, starting transfers between devices, body(): lax.ppermute(m, 'dp', [(i, i ^ 2 * k) for i in range(n_dp)])  3.55 us
  transfers between devices with their start and end apart: 28, of which 12 were waited for; matrix products, arithmetic and copies ran while one was open for 0% of the time, Pallas kernels for 26%

profile of v7, /device:TPU:0, one launch (start us, length us, event | category | flops | bytes accessed | tf_op | source)
XLA Modules:
  0.0 79.7 jit_solution(8044442078761913335)
XLA Ops:
  0.6 1.0 %convert_bitcast_fusion.own = bf16[32,640]{1,0:T(8,128)(2,1)S(1)} fusion(f32[640,32]{0,1:T(8,128)} %param.7), kind=kLoop, calls=%fused_computation.1 | loop fusion | flops 20480 | bytes 122880 | tf_op jit(solution)/shard_map/convert_element_type | solution.py:368
  1.7 3.0 %collective-permute-start = (bf16[32,640]{1,0:T(8,128)(2,1)S(1)}, bf16[32,640]{1,0:T(8,128)(2,1)S(1)}, u32[]{:S(2)}, u32[]{:S(2)}) collective-permute-start(bf16[32,640]{1,0:T(8,128)(2,1)S(1)} %convert_bitcast_fusion.own), channel_id=1, source_target_pairs={{0,1},{1,0},{2,3},{3,2},{4,5},{5,4},{6,7},{7,6},{8,9},{9,8},{10,11... | collective-permute-start | bytes 122888 | tf_op jit(solution)/shard_map/ppermute | solution.py:345
  4.7 2.6 %collective-permute-start.1 = (bf16[32,640]{1,0:T(8,128)(2,1)S(1)}, bf16[32,640]{1,0:T(8,128)(2,1)S(1)}, u32[]{:S(2)}, u32[]{:S(2)}) collective-permute-start(bf16[32,640]{1,0:T(8,128)(2,1)S(1)} %convert_bitcast_fusion.own), channel_id=1, source_target_pairs={{0,2},{1,3},{2,0},{3,1},{4,6},{5,7},{6,4},{7,5},{8,10},{9,11},{10,... | collective-permute-start | bytes 122888 | tf_op jit(solution)/shard_map/ppermute | solution.py:345
  7.3 0.0 collective-permute-start.2
  7.3 0.1 pad_add_fusion.place
  7.4 2.3 %load_half.1.e_0.base_ref = bf16[1728,1280]{1,0:T(8,128)(2,1)S(1)} custom-call(bf16[1728,2560]{1,0:T(8,128)(2,1)} %bitcast.8), custom_call_target="tpu_custom_call" | custom-call | bytes 13271040 | tf_op jit(solution)/shard_map/load_half/pallas_call | solution.py:82
  9.7 1.3 %arrange.1 = (bf16[1728,432]{1,0:T(8,128)(2,1)S(1)}, bf16[1728,144]{1,0:T(8,128)(2,1)S(1)}) custom-call(s32[3]{0:T(128)S(1)} %pad_add_fusion.place, bf16[576,1728]{1,0:T(8,128)(2,1)S(1)} %copy-done), custom_call_target="tpu_custom_call" | custom-call | bytes 3981324 | tf_op jit(solution)/shard_map/arrange/pallas_call | solution.py:82
  11.0 0.0 collective-permute-done.1.n2
  11.0 2.1 %collective-permute-done.2.n3 = bf16[32,640]{1,0:T(8,128)(2,1)S(1)} collective-permute-done((bf16[32,640]{1,0:T(8,128)(2,1)S(1)}, bf16[32,640]{1,0:T(8,128)(2,1)S(1)}, u32[]{:S(2)}, u32[]{:S(2)}) %collective-permute-start.2) | collective-permute-done | bytes 40992 | tf_op jit(solution)/shard_map/ppermute | solution.py:345
  13.1 0.9 %project.1 = (bf16[4,32,640]{2,1,0:T(8,128)(2,1)S(1)}, f32[32,144]{1,0:T(8,128)S(1)}) custom-call(s32[3]{0:T(128)S(1)} %pad_add_fusion.place, bf16[32,640]{1,0:T(8,128)(2,1)S(1)} %convert_bitcast_fusion.own, bf16[32,640]{1,0:T(8,128)(2,1)S(1)} %collective-permute-done.n1, bf16[32,640]{1,0:T(8,128)(2,1)S(1)} %collective-permute-done.1.n2, ...), custom_call_target="tpu_custom_call" | custom-call | bytes 1083404 | tf_op jit(solution)/shard_map/project/pallas_call | solution.py:82
  14.0 0.0 collective-permute-start.3
  14.0 2.3 %collective-permute-start.4 = (f32[32,144]{1,0:T(8,128)S(1)}, f32[32,144]{1,0:T(8,128)S(1)}, u32[]{:S(2)}, u32[]{:S(2)}) collective-permute-start(f32[32,144]{1,0:T(8,128)S(1)} %get-tuple-element.42.own), channel_id=1, source_target_pairs={{0,2},{1,3},{2,0},{3,1},{4,6},{5,7},{6,4},{7,5},{8,10},{9,11},{10,... | collective-permute-start | bytes 55304 | tf_op jit(solution)/shard_map/ppermute | solution.py:345
  16.4 2.1 %collective-permute-start.5 = (f32[32,144]{1,0:T(8,128)S(1)}, f32[32,144]{1,0:T(8,128)S(1)}, u32[]{:S(2)}, u32[]{:S(2)}) collective-permute-start(f32[32,144]{1,0:T(8,128)S(1)} %get-tuple-element.42.own), channel_id=1, source_target_pairs={{0,3},{1,2},{2,1},{3,0},{4,7},{5,6},{6,5},{7,4},{8,11},{9,10},{10,... | collective-permute-start | bytes 55304 | tf_op jit(solution)/shard_map/ppermute | solution.py:345
  18.4 3.2 %error_left.1 = (f32[32,1728]{1,0:T(8,128)S(1)}, bf16[1728,1280]{1,0:T(8,128)(2,1)S(1)}) custom-call(bf16[4,32,640]{2,1,0:T(8,128)(2,1)S(1)} %get-tuple-element.39.q_ref, bf16[1728,1280]{1,0:T(8,128)(2,1)S(1)} %load_half.1.e_0.base_ref, bf16[1728,2560]{1,0:T(8,128)(2,1)} %bitcast.9), custom_call_target="tpu_custom_call" | custom-call | bytes 18079744 | tf_op jit(solution)/shard_map/error_left/pallas_call | solution.py:82
  21.6 0.0 collective-permute-done.3.n1
  21.6 0.0 collective-permute-done.4.n2
  21.6 0.5 collective-permute-done.5.n3
  22.1 0.0 collective-permute-start.11
  22.1 1.0 %left_factor.1 = bf16[32,1728]{1,0:T(8,128)(2,1)S(1)} custom-call(s32[3]{0:T(128)S(1)} %pad_add_fusion.place, f32[32,1728]{1,0:T(8,128)S(1)} %get-tuple-element.41.eq_ref, f32[32,144]{1,0:T(8,128)S(1)} %get-tuple-element.42.own, f32[32,144]{1,0:T(8,128)S(1)} %collective-permute-done.3.n1, f32[32,144]{1,0:T(8,128)S(1)} %collective-permute-done.4.n2, ...), custom_call_target="tpu_custom_call" | custom-call | bytes 2396172 | tf_op jit(solution)/shard_map/left_factor/pallas_call | solution.py:82
  23.0 0.1 collective-permute-start.6
  23.1 1.3 %collective-permute-done.6 = bf16[32,1728]{1,0:T(8,128)(2,1)S(1)} collective-permute-done((bf16[32,1728]{1,0:T(8,128)(2,1)S(1)}, bf16[32,1728]{1,0:T(8,128)(2,1)S(1)}, u32[]{:S(2)}, u32[]{:S(2)}) %collective-permute-start.6) | collective-permute-done | bytes 110624 | tf_op jit(solution)/shard_map/ppermute | solution.py:345
  24.5 1.6 %collective-permute-start.7 = (bf16[32,1728]{1,0:T(8,128)(2,1)S(1)}, bf16[32,1728]{1,0:T(8,128)(2,1)S(1)}, u32[]{:S(2)}, u32[]{:S(2)}) collective-permute-start(bf16[32,1728]{1,0:T(8,128)(2,1)S(1)} %add_convert_fusion.own), channel_id=1, source_target_pairs={{0,8},{4,12},{8,0},{12,4},{16,24},{20,28},{24,16},{28,20},{1,9},{5... | collective-permute-start | bytes 331784 | tf_op jit(solution)/shard_map/ppermute | solution.py:345
  26.0 1.5 %collective-permute-start.8 = (bf16[32,1728]{1,0:T(8,128)(2,1)S(1)}, bf16[32,1728]{1,0:T(8,128)(2,1)S(1)}, u32[]{:S(2)}, u32[]{:S(2)}) collective-permute-start(bf16[32,1728]{1,0:T(8,128)(2,1)S(1)} %add_convert_fusion.own), channel_id=1, source_target_pairs={{0,16},{4,20},{8,24},{12,28},{16,0},{20,4},{24,8},{28,12},{1,17},{... | collective-permute-start | bytes 331784 | tf_op jit(solution)/shard_map/ppermute | solution.py:345
  27.5 0.5 collective-permute-start.9
  28.0 1.7 %collective-permute-done.7.n1 = bf16[32,1728]{1,0:T(8,128)(2,1)S(1)} collective-permute-done((bf16[32,1728]{1,0:T(8,128)(2,1)S(1)}, bf16[32,1728]{1,0:T(8,128)(2,1)S(1)}, u32[]{:S(2)}, u32[]{:S(2)}) %collective-permute-start.7) | collective-permute-done | bytes 110624 | tf_op jit(solution)/shard_map/ppermute | solution.py:345
  29.7 3.7 %collective-permute-done.8.n2 = bf16[32,1728]{1,0:T(8,128)(2,1)S(1)} collective-permute-done((bf16[32,1728]{1,0:T(8,128)(2,1)S(1)}, bf16[32,1728]{1,0:T(8,128)(2,1)S(1)}, u32[]{:S(2)}, u32[]{:S(2)}) %collective-permute-start.8) | collective-permute-done | bytes 110624 | tf_op jit(solution)/shard_map/ppermute | solution.py:345
  33.4 1.3 %weigh.1 = (bf16[32,1728]{1,0:T(8,128)(2,1)S(1)}, f32[32,32]{1,0:T(8,128)S(1)}, f32[2,32,144]{2,1,0:T(8,128)S(1)}, bf16[2,32,144]{2,1,0:T(8,128)(2,1)S(1)}) custom-call(s32[3]{0:T(128)S(1)} %pad_add_fusion.place, bf16[32,1728]{1,0:T(8,128)(2,1)S(1)} %add_convert_fusion.own, bf16[32,1728]{1,0:T(8,128)(2,1)S(1)} %collective-permute-done.7.n1, ...), custom_call_target="tpu_custom_call" | custom-call | bytes 2603020 | tf_op jit(solution)/shard_map/weigh/pallas_call | solution.py:82
  34.7 2.2 %collective-permute-start.10 = (bf16[2,32,144]{2,1,0:T(8,128)(2,1)S(1)}, bf16[2,32,144]{2,1,0:T(8,128)(2,1)S(1)}, u32[]{:S(2)}, u32[]{:S(2)}) collective-permute-start(bf16[2,32,144]{2,1,0:T(8,128)(2,1)S(1)} %get-tuple-element.45), channel_id=1, source_target_pairs={{0,3},{1,2},{2,1},{3,0},{4,7},{5,6},{6,5},{7,4},{8,11},{9,10},{10,... | collective-permute-start | bytes 55304 | tf_op jit(solution)/shard_map/ppermute | solution.py:345
  36.9 1.1 %collective-permute-start.26 = (bf16[144,2560]{1,0:T(8,128)(2,1)S(1)}, bf16[144,2560]{1,0:T(8,128)(2,1)S(1)}, u32[]{:S(2)}, u32[]{:S(2)}) collective-permute-start(bf16[144,2560]{1,0:T(8,128)(2,1)S(1)} %copy-done.1), channel_id=1, source_target_pairs={{0,1},{1,3},{3,2},{2,0},{4,5},{5,7},{7,6},{6,4},{8,9},{9,11},{11,1... | collective-permute-start | bytes 2211848 | tf_op jit(solution)/shard_map/ppermute | solution.py:366
  38.0 1.4 %error_right.1.te_ref = f32[32,2560]{1,0:T(8,128)S(1)} custom-call(bf16[32,1728]{1,0:T(8,128)(2,1)S(1)} %get-tuple-element.46.p_ref, bf16[1728,1280]{1,0:T(8,128)(2,1)S(1)} %load_half.1.e_0.base_ref, bf16[1728,1280]{1,0:T(8,128)(2,1)S(1)} %get-tuple-element.47.e_1.base_ref), custom_call_target="tpu_custom_call" | custom-call | bytes 9285632 | tf_op jit(solution)/shard_map/error_right/pallas_call | solution.py:82
  39.4 1.4 %collective-permute-done.10.got_ref = bf16[2,32,144]{2,1,0:T(8,128)(2,1)S(1)} collective-permute-done((bf16[2,32,144]{2,1,0:T(8,128)(2,1)S(1)}, bf16[2,32,144]{2,1,0:T(8,128)(2,1)S(1)}, u32[]{:S(2)}, u32[]{:S(2)}) %collective-permute-start.10) | collective-permute-done | bytes 18464 | tf_op jit(solution)/shard_map/ppermute | solution.py:345
  40.9 0.9 %right_term.1 = (f32[16,2560]{1,0:T(8,128)S(1)}, f32[16,2560]{1,0:T(8,128)S(1)}) custom-call(s32[3]{0:T(128)S(1)} %pad_add_fusion.place, f32[2,32,144]{2,1,0:T(8,128)S(1)} %get-tuple-element.44.near_ref, bf16[2,32,144]{2,1,0:T(8,128)(2,1)S(1)} %collective-permute-done.10.got_ref, f32[32,2560]{1,0:T(8,128)S(1)} %error_right.1.te_ref, ...), custom_call_target="tpu_custom_call" | custom-call | bytes 2185228 | tf_op jit(solution)/shard_map/right_term/pallas_call | solution.py:82
  41.8 0.1 collective-permute-start.12
  41.9 1.4 %collective-permute-done.12.got = f32[16,2560]{1,0:T(8,128)S(1)} collective-permute-done((f32[16,2560]{1,0:T(8,128)S(1)}, f32[16,2560]{1,0:T(8,128)S(1)}, u32[]{:S(2)}, u32[]{:S(2)}) %collective-permute-start.12) | collective-permute-done | bytes 163872 | tf_op jit(solution)/shard_map/ppermute | solution.py:345
  43.2 0.6 cut.1
  43.8 1.2 %collective-permute-start.13 = (bf16[16,640]{1,0:T(8,128)(2,1)S(1)}, bf16[16,640]{1,0:T(8,128)(2,1)S(1)}, u32[]{:S(2)}, u32[]{:S(2)}) collective-permute-start(bf16[16,640]{1,0:T(8,128)(2,1)S(1)} %get-tuple-element.54), channel_id=1, source_target_pairs={{0,8},{4,12},{8,0},{12,4},{16,24},{20,28},{24,16},{28,20},{1,9},{5... | collective-permute-start | bytes 61448 | tf_op jit(solution)/shard_map/ppermute | solution.py:446
  45.0 0.9 %collective-permute-start.14 = (bf16[16,640]{1,0:T(8,128)(2,1)S(1)}, bf16[16,640]{1,0:T(8,128)(2,1)S(1)}, u32[]{:S(2)}, u32[]{:S(2)}) collective-permute-start(bf16[16,640]{1,0:T(8,128)(2,1)S(1)} %get-tuple-element.55), channel_id=1, source_target_pairs={{0,16},{4,20},{8,24},{12,28},{16,0},{20,4},{24,8},{28,12},{1,17},{... | collective-permute-start | bytes 61448 | tf_op jit(solution)/shard_map/ppermute | solution.py:446
  45.9 1.5 %collective-permute-start.15 = (bf16[16,640]{1,0:T(8,128)(2,1)S(1)}, bf16[16,640]{1,0:T(8,128)(2,1)S(1)}, u32[]{:S(2)}, u32[]{:S(2)}) collective-permute-start(bf16[16,640]{1,0:T(8,128)(2,1)S(1)} %get-tuple-element.56), channel_id=1, source_target_pairs={{0,24},{4,28},{8,16},{12,20},{16,8},{20,12},{24,0},{28,4},{1,25},{... | collective-permute-start | bytes 61448 | tf_op jit(solution)/shard_map/ppermute | solution.py:446
  47.4 1.4 %accumulate.4.base_ref = f32[1728,1280]{1,0:T(8,128)S(1)} custom-call(bf16[1728,432]{1,0:T(8,128)(2,1)S(1)} %get-tuple-element.35.main_ref, bf16[1728,1280]{1,0:T(8,128)(2,1)S(1)} %load_half.1.e_0.base_ref, bf16[144,2560]{1,0:T(8,128)(2,1)S(1)} %copy-done.1, bf16[144,2560]{1,0:T(8,128)(2,1)S(1)} %collective-permute-done.11.x_first.rest_1_.rest_0_), custom_call_target="tpu_custom_call" | custom-call | bytes 16238592 | tf_op jit(solution)/shard_map/accumulate/pallas_call | solution.py:82
  48.8 1.4 %accumulate.5.base_ref = f32[1728,1280]{1,0:T(8,128)S(1)} custom-call(bf16[1728,432]{1,0:T(8,128)(2,1)S(1)} %get-tuple-element.35.main_ref, bf16[1728,1280]{1,0:T(8,128)(2,1)S(1)} %get-tuple-element.47.e_1.base_ref, bf16[144,2560]{1,0:T(8,128)(2,1)S(1)} %copy-done.1, bf16[144,2560]{1,0:T(8,128)(2,1)S(1)} %collective-permute-done.11.x_first.rest_1_.rest_0_), custom_call_target="tpu_custom_call" | custom-call | bytes 16238592 | tf_op jit(solution)/shard_map/accumulate/pallas_call | solution.py:82
  50.2 0.4 collective-permute-done.15.d
  50.6 0.1 pack.1.a
  50.7 0.8 collective-permute-start.16
  51.5 1.9 %collective-permute-start.17 = (bf16[16,896]{1,0:T(8,128)(2,1)S(1)}, bf16[16,896]{1,0:T(8,128)(2,1)S(1)}, u32[]{:S(2)}, u32[]{:S(2)}) collective-permute-start(bf16[16,896]{1,0:T(8,128)(2,1)S(1)} %pack.1.a), channel_id=1, source_target_pairs={{0,2},{1,3},{2,0},{3,1},{4,6},{5,7},{6,4},{7,5},{8,10},{9,11},{10,... | collective-permute-start | bytes 86024 | tf_op jit(solution)/shard_map/ppermute | solution.py:345
  53.5 1.7 %collective-permute-start.18 = (bf16[16,896]{1,0:T(8,128)(2,1)S(1)}, bf16[16,896]{1,0:T(8,128)(2,1)S(1)}, u32[]{:S(2)}, u32[]{:S(2)}) collective-permute-start(bf16[16,896]{1,0:T(8,128)(2,1)S(1)} %pack.1.a), channel_id=1, source_target_pairs={{0,3},{1,2},{2,1},{3,0},{4,7},{5,6},{6,5},{7,4},{8,11},{9,10},{10,... | collective-permute-start | bytes 86024 | tf_op jit(solution)/shard_map/ppermute | solution.py:345
  55.1 0.2 collective-permute-done.16.b
  55.3 2.0 %collective-permute-done.17.c = bf16[16,896]{1,0:T(8,128)(2,1)S(1)} collective-permute-done((bf16[16,896]{1,0:T(8,128)(2,1)S(1)}, bf16[16,896]{1,0:T(8,128)(2,1)S(1)}, u32[]{:S(2)}, u32[]{:S(2)}) %collective-permute-start.17) | collective-permute-done | bytes 28704 | tf_op jit(solution)/shard_map/ppermute | solution.py:345
  57.3 1.9 %collective-permute-done.18.d = bf16[16,896]{1,0:T(8,128)(2,1)S(1)} collective-permute-done((bf16[16,896]{1,0:T(8,128)(2,1)S(1)}, bf16[16,896]{1,0:T(8,128)(2,1)S(1)}, u32[]{:S(2)}, u32[]{:S(2)}) %collective-permute-start.18) | collective-permute-done | bytes 28704 | tf_op jit(solution)/shard_map/ppermute | solution.py:345
  59.2 0.0 collective-permute-start.27
  59.2 0.2 unpack.1
  59.5 1.4 %collective-permute-start.19 = (f32[16,640]{1,0:T(8,128)S(1)}, f32[16,640]{1,0:T(8,128)S(1)}, u32[]{:S(2)}, u32[]{:S(2)}) collective-permute-start(f32[16,640]{1,0:T(8,128)S(1)} %get-tuple-element.61.a0), channel_id=1, source_target_pairs={{0,8},{4,12},{8,0},{12,4},{16,24},{20,28},{24,16},{28,20},{1,9},{5... | collective-permute-start | bytes 122888 | tf_op jit(solution)/shard_map/ppermute | solution.py:345
  60.9 0.8 %collective-permute-start.20 = (f32[16,640]{1,0:T(8,128)S(1)}, f32[16,640]{1,0:T(8,128)S(1)}, u32[]{:S(2)}, u32[]{:S(2)}) collective-permute-start(f32[16,640]{1,0:T(8,128)S(1)} %get-tuple-element.61.a0), channel_id=1, source_target_pairs={{0,16},{4,20},{8,24},{12,28},{16,0},{20,4},{24,8},{28,12},{1,17},{... | collective-permute-start | bytes 122888 | tf_op jit(solution)/shard_map/ppermute | solution.py:345
  61.7 1.3 %collective-permute-start.21 = (f32[16,640]{1,0:T(8,128)S(1)}, f32[16,640]{1,0:T(8,128)S(1)}, u32[]{:S(2)}, u32[]{:S(2)}) collective-permute-start(f32[16,640]{1,0:T(8,128)S(1)} %get-tuple-element.61.a0), channel_id=1, source_target_pairs={{0,24},{4,28},{8,16},{12,20},{16,8},{20,12},{24,0},{28,4},{1,25},{... | collective-permute-start | bytes 122888 | tf_op jit(solution)/shard_map/ppermute | solution.py:345
  62.9 1.7 %invert_cholesky.1.linv = f32[32,32]{1,0:T(8,128)S(1)} custom-call(f32[32,32]{1,0:T(8,128)S(1)} %get-tuple-element.59.g_ref), custom_call_target="tpu_custom_call" | custom-call | bytes 8192 | tf_op jit(solution)/shard_map/invert_cholesky/pallas_call | solution.py:82
  64.6 0.0 collective-permute-done.26.rest_1_
  64.6 0.1 collective-permute-start.22
  64.7 1.4 %accumulate.6.acc_0 = f32[1728,1280]{1,0:T(8,128)S(1)} custom-call(bf16[1728,432]{1,0:T(8,128)(2,1)S(1)} %get-tuple-element.35.main_ref, f32[1728,1280]{1,0:T(8,128)S(1)} %accumulate.4.base_ref, bf16[144,2560]{1,0:T(8,128)(2,1)S(1)} %collective-permute-done.11.x_first.rest_1_.rest_0_, bf16[144,2560]{1,0:T(8,128)(2,1)S(1)} %collective-permute-done.26.rest_1_), custom_call_target="tpu_custom_call" | custom-call | flops 2000000000 | bytes 20662272 | tf_op jit(solution)/shard_map/accumulate/pallas_call | solution.py:82
  66.1 0.5 collective-permute-start.23
  66.7 0.1 collective-permute-start.24
  66.8 0.4 collective-permute-start.25
  67.2 1.4 %accumulate.7.acc_1 = f32[1728,1280]{1,0:T(8,128)S(1)} custom-call(bf16[1728,432]{1,0:T(8,128)(2,1)S(1)} %get-tuple-element.35.main_ref, f32[1728,1280]{1,0:T(8,128)S(1)} %accumulate.5.base_ref, bf16[144,2560]{1,0:T(8,128)(2,1)S(1)} %collective-permute-done.11.x_first.rest_1_.rest_0_, bf16[144,2560]{1,0:T(8,128)(2,1)S(1)} %collective-permute-done.26.rest_1_), custom_call_target="tpu_custom_call" | custom-call | flops 2000000000 | bytes 20662272 | tf_op jit(solution)/shard_map/accumulate/pallas_call | solution.py:82
  68.6 1.5 %finish.1 = (f32[32,640]{1,0:T(8,128)}, bf16[1728,240]{1,0:T(8,128)(2,1)S(1)}, bf16[96,2560]{1,0:T(8,128)(2,1)S(1)}) custom-call(s32[3]{0:T(128)S(1)} %pad_add_fusion.place, f32[32,32]{1,0:T(8,128)S(1)} %invert_cholesky.1.linv, bf16[32,1728]{1,0:T(8,128)(2,1)S(1)} %get-tuple-element.46.p_ref, bf16[1728,144]{1,0:T(8,128)(2,1)S(1)} %get-tuple-element.60.rest_ref, ...), custom_call_target="tpu_custom_call" | custom-call | bytes 2342924 | tf_op jit(solution)/shard_map/finish/pallas_call | solution.py:82
  70.1 4.8 %collective-permute-done.27.x_any = bf16[144,2560]{1,0:T(8,128)(2,1)S(1)} collective-permute-done((bf16[144,2560]{1,0:T(8,128)(2,1)S(1)}, bf16[144,2560]{1,0:T(8,128)(2,1)S(1)}, u32[]{:S(2)}, u32[]{:S(2)}) %collective-permute-start.27) | collective-permute-done | bytes 737312 | tf_op jit(solution)/shard_map/ppermute | solution.py:366
  74.9 4.6 %rebuild.1 = bf16[1728,2560]{1,0:T(8,128)(2,1)} custom-call(bf16[1728,240]{1,0:T(8,128)(2,1)S(1)} %get-tuple-element.63.left_ref, bf16[96,2560]{1,0:T(8,128)(2,1)S(1)} %get-tuple-element.64.right_ref, f32[1728,1280]{1,0:T(8,128)S(1)} %accumulate.6.acc_0, f32[1728,1280]{1,0:T(8,128)S(1)} %accumulate.7.acc_1, bf16[144,2560]{1,0:T(8,128)(2,1)S(1)} %collective-permute-done.27.x_any), custom_call_target="tpu_custom_call" | custom-call | bytes 28600320 | tf_op jit(solution)/shard_map/rebuild/pallas_call | solution.py:82
  (17 shorter events, 0.1 us)
Async XLA Ops:
  0.6 9.0 %copy-start = (bf16[576,1728]{1,0:T(8,128)(2,1)S(1)}, bf16[576,1728]{1,0:T(8,128)(2,1)}, u32[]{:S(2)}) copy-start(bf16[576,1728]{1,0:T(8,128)(2,1)} %dy_ref.5) | copy-start | bytes 5971972
  0.6 12.5 %copy-start.1 = (bf16[144,2560]{1,0:T(8,128)(2,1)S(1)}, bf16[144,2560]{1,0:T(8,128)(2,1)}, u32[]{:S(2)}) copy-start(bf16[144,2560]{1,0:T(8,128)(2,1)} %rest_0_.3) | copy-start | bytes 2211844
  1.7 9.3 %collective-permute-start = (bf16[32,640]{1,0:T(8,128)(2,1)S(1)}, bf16[32,640]{1,0:T(8,128)(2,1)S(1)}, u32[]{:S(2)}, u32[]{:S(2)}) collective-permute-start(bf16[32,640]{1,0:T(8,128)(2,1)S(1)} %convert_bitcast_fusion.own), channel_id=1, source_target_pairs={{0,1},{1,0},{2,3},{3,2},{4,5},{5,4},{6,7},{7,6},{8,9},{9,8},{10,11... | collective-permute-start | bytes 122888 | tf_op jit(solution)/shard_map/ppermute | solution.py:345
  4.7 6.3 %collective-permute-start.1 = (bf16[32,640]{1,0:T(8,128)(2,1)S(1)}, bf16[32,640]{1,0:T(8,128)(2,1)S(1)}, u32[]{:S(2)}, u32[]{:S(2)}) collective-permute-start(bf16[32,640]{1,0:T(8,128)(2,1)S(1)} %convert_bitcast_fusion.own), channel_id=1, source_target_pairs={{0,2},{1,3},{2,0},{3,1},{4,6},{5,7},{6,4},{7,5},{8,10},{9,11},{10,... | collective-permute-start | bytes 122888 | tf_op jit(solution)/shard_map/ppermute | solution.py:345
  7.3 5.8 %collective-permute-start.2 = (bf16[32,640]{1,0:T(8,128)(2,1)S(1)}, bf16[32,640]{1,0:T(8,128)(2,1)S(1)}, u32[]{:S(2)}, u32[]{:S(2)}) collective-permute-start(bf16[32,640]{1,0:T(8,128)(2,1)S(1)} %convert_bitcast_fusion.own), channel_id=1, source_target_pairs={{0,3},{1,2},{2,1},{3,0},{4,7},{5,6},{6,5},{7,4},{8,11},{9,10},{10,... | collective-permute-start | bytes 122888 | tf_op jit(solution)/shard_map/ppermute | solution.py:345
  14.0 7.6 %collective-permute-start.3 = (f32[32,144]{1,0:T(8,128)S(1)}, f32[32,144]{1,0:T(8,128)S(1)}, u32[]{:S(2)}, u32[]{:S(2)}) collective-permute-start(f32[32,144]{1,0:T(8,128)S(1)} %get-tuple-element.42.own), channel_id=1, source_target_pairs={{0,1},{1,0},{2,3},{3,2},{4,5},{5,4},{6,7},{7,6},{8,9},{9,8},{10,11... | collective-permute-start | bytes 55304 | tf_op jit(solution)/shard_map/ppermute | solution.py:345
  14.0 7.6 %collective-permute-start.4 = (f32[32,144]{1,0:T(8,128)S(1)}, f32[32,144]{1,0:T(8,128)S(1)}, u32[]{:S(2)}, u32[]{:S(2)}) collective-permute-start(f32[32,144]{1,0:T(8,128)S(1)} %get-tuple-element.42.own), channel_id=1, source_target_pairs={{0,2},{1,3},{2,0},{3,1},{4,6},{5,7},{6,4},{7,5},{8,10},{9,11},{10,... | collective-permute-start | bytes 55304 | tf_op jit(solution)/shard_map/ppermute | solution.py:345
  16.4 5.7 %collective-permute-start.5 = (f32[32,144]{1,0:T(8,128)S(1)}, f32[32,144]{1,0:T(8,128)S(1)}, u32[]{:S(2)}, u32[]{:S(2)}) collective-permute-start(f32[32,144]{1,0:T(8,128)S(1)} %get-tuple-element.42.own), channel_id=1, source_target_pairs={{0,3},{1,2},{2,1},{3,0},{4,7},{5,6},{6,5},{7,4},{8,11},{9,10},{10,... | collective-permute-start | bytes 55304 | tf_op jit(solution)/shard_map/ppermute | solution.py:345
  22.1 18.8 %collective-permute-start.11 = (bf16[144,2560]{1,0:T(8,128)(2,1)S(1)}, bf16[144,2560]{1,0:T(8,128)(2,1)S(1)}, u32[]{:S(2)}, u32[]{:S(2)}) collective-permute-start(bf16[144,2560]{1,0:T(8,128)(2,1)S(1)} %copy-done.1), channel_id=1, source_target_pairs={{0,2},{2,3},{3,1},{1,0},{4,6},{6,7},{7,5},{5,4},{8,10},{10,11},{11... | collective-permute-start | bytes 2211848 | tf_op jit(solution)/shard_map/ppermute | solution.py:366
  23.0 1.4 %collective-permute-start.6 = (bf16[32,1728]{1,0:T(8,128)(2,1)S(1)}, bf16[32,1728]{1,0:T(8,128)(2,1)S(1)}, u32[]{:S(2)}, u32[]{:S(2)}) collective-permute-start(bf16[32,1728]{1,0:T(8,128)(2,1)S(1)} %left_factor.1), channel_id=1, source_target_pairs={{0,4},{4,0},{8,12},{12,8},{16,20},{20,16},{24,28},{28,24},{1,5},{5... | collective-permute-start | bytes 331784 | tf_op jit(solution)/shard_map/ppermute | solution.py:345
  24.5 5.3 %collective-permute-start.7 = (bf16[32,1728]{1,0:T(8,128)(2,1)S(1)}, bf16[32,1728]{1,0:T(8,128)(2,1)S(1)}, u32[]{:S(2)}, u32[]{:S(2)}) collective-permute-start(bf16[32,1728]{1,0:T(8,128)(2,1)S(1)} %add_convert_fusion.own), channel_id=1, source_target_pairs={{0,8},{4,12},{8,0},{12,4},{16,24},{20,28},{24,16},{28,20},{1,9},{5... | collective-permute-start | bytes 331784 | tf_op jit(solution)/shard_map/ppermute | solution.py:345
  26.0 7.4 %collective-permute-start.8 = (bf16[32,1728]{1,0:T(8,128)(2,1)S(1)}, bf16[32,1728]{1,0:T(8,128)(2,1)S(1)}, u32[]{:S(2)}, u32[]{:S(2)}) collective-permute-start(bf16[32,1728]{1,0:T(8,128)(2,1)S(1)} %add_convert_fusion.own), channel_id=1, source_target_pairs={{0,16},{4,20},{8,24},{12,28},{16,0},{20,4},{24,8},{28,12},{1,17},{... | collective-permute-start | bytes 331784 | tf_op jit(solution)/shard_map/ppermute | solution.py:345
  27.5 5.9 %collective-permute-start.9 = (bf16[32,1728]{1,0:T(8,128)(2,1)S(1)}, bf16[32,1728]{1,0:T(8,128)(2,1)S(1)}, u32[]{:S(2)}, u32[]{:S(2)}) collective-permute-start(bf16[32,1728]{1,0:T(8,128)(2,1)S(1)} %add_convert_fusion.own), channel_id=1, source_target_pairs={{0,24},{4,28},{8,16},{12,20},{16,8},{20,12},{24,0},{28,4},{1,25},{... | collective-permute-start | bytes 331784 | tf_op jit(solution)/shard_map/ppermute | solution.py:345
  34.7 6.2 %collective-permute-start.10 = (bf16[2,32,144]{2,1,0:T(8,128)(2,1)S(1)}, bf16[2,32,144]{2,1,0:T(8,128)(2,1)S(1)}, u32[]{:S(2)}, u32[]{:S(2)}) collective-permute-start(bf16[2,32,144]{2,1,0:T(8,128)(2,1)S(1)} %get-tuple-element.45), channel_id=1, source_target_pairs={{0,3},{1,2},{2,1},{3,0},{4,7},{5,6},{6,5},{7,4},{8,11},{9,10},{10,... | collective-permute-start | bytes 55304 | tf_op jit(solution)/shard_map/ppermute | solution.py:345
  36.9 27.7 %collective-permute-start.26 = (bf16[144,2560]{1,0:T(8,128)(2,1)S(1)}, bf16[144,2560]{1,0:T(8,128)(2,1)S(1)}, u32[]{:S(2)}, u32[]{:S(2)}) collective-permute-start(bf16[144,2560]{1,0:T(8,128)(2,1)S(1)} %copy-done.1), channel_id=1, source_target_pairs={{0,1},{1,3},{3,2},{2,0},{4,5},{5,7},{7,6},{6,4},{8,9},{9,11},{11,1... | collective-permute-start | bytes 2211848 | tf_op jit(solution)/shard_map/ppermute | solution.py:366
  41.8 1.5 %collective-permute-start.12 = (f32[16,2560]{1,0:T(8,128)S(1)}, f32[16,2560]{1,0:T(8,128)S(1)}, u32[]{:S(2)}, u32[]{:S(2)}) collective-permute-start(f32[16,2560]{1,0:T(8,128)S(1)} %get-tuple-element.52), channel_id=1, source_target_pairs={{0,4},{4,0},{8,12},{12,8},{16,20},{20,16},{24,28},{28,24},{1,5},{5... | collective-permute-start | bytes 491528 | tf_op jit(solution)/shard_map/ppermute | solution.py:345
  43.8 6.4 %collective-permute-start.13 = (bf16[16,640]{1,0:T(8,128)(2,1)S(1)}, bf16[16,640]{1,0:T(8,128)(2,1)S(1)}, u32[]{:S(2)}, u32[]{:S(2)}) collective-permute-start(bf16[16,640]{1,0:T(8,128)(2,1)S(1)} %get-tuple-element.54), channel_id=1, source_target_pairs={{0,8},{4,12},{8,0},{12,4},{16,24},{20,28},{24,16},{28,20},{1,9},{5... | collective-permute-start | bytes 61448 | tf_op jit(solution)/shard_map/ppermute | solution.py:446
  45.0 5.2 %collective-permute-start.14 = (bf16[16,640]{1,0:T(8,128)(2,1)S(1)}, bf16[16,640]{1,0:T(8,128)(2,1)S(1)}, u32[]{:S(2)}, u32[]{:S(2)}) collective-permute-start(bf16[16,640]{1,0:T(8,128)(2,1)S(1)} %get-tuple-element.55), channel_id=1, source_target_pairs={{0,16},{4,20},{8,24},{12,28},{16,0},{20,4},{24,8},{28,12},{1,17},{... | collective-permute-start | bytes 61448 | tf_op jit(solution)/shard_map/ppermute | solution.py:446
  45.9 4.7 %collective-permute-start.15 = (bf16[16,640]{1,0:T(8,128)(2,1)S(1)}, bf16[16,640]{1,0:T(8,128)(2,1)S(1)}, u32[]{:S(2)}, u32[]{:S(2)}) collective-permute-start(bf16[16,640]{1,0:T(8,128)(2,1)S(1)} %get-tuple-element.56), channel_id=1, source_target_pairs={{0,24},{4,28},{8,16},{12,20},{16,8},{20,12},{24,0},{28,4},{1,25},{... | collective-permute-start | bytes 61448 | tf_op jit(solution)/shard_map/ppermute | solution.py:446
  50.7 4.6 %collective-permute-start.16 = (bf16[16,896]{1,0:T(8,128)(2,1)S(1)}, bf16[16,896]{1,0:T(8,128)(2,1)S(1)}, u32[]{:S(2)}, u32[]{:S(2)}) collective-permute-start(bf16[16,896]{1,0:T(8,128)(2,1)S(1)} %pack.1.a), channel_id=1, source_target_pairs={{0,1},{1,0},{2,3},{3,2},{4,5},{5,4},{6,7},{7,6},{8,9},{9,8},{10,11... | collective-permute-start | bytes 86024 | tf_op jit(solution)/shard_map/ppermute | solution.py:345
  51.5 5.8 %collective-permute-start.17 = (bf16[16,896]{1,0:T(8,128)(2,1)S(1)}, bf16[16,896]{1,0:T(8,128)(2,1)S(1)}, u32[]{:S(2)}, u32[]{:S(2)}) collective-permute-start(bf16[16,896]{1,0:T(8,128)(2,1)S(1)} %pack.1.a), channel_id=1, source_target_pairs={{0,2},{1,3},{2,0},{3,1},{4,6},{5,7},{6,4},{7,5},{8,10},{9,11},{10,... | collective-permute-start | bytes 86024 | tf_op jit(solution)/shard_map/ppermute | solution.py:345
  53.5 5.8 %collective-permute-start.18 = (bf16[16,896]{1,0:T(8,128)(2,1)S(1)}, bf16[16,896]{1,0:T(8,128)(2,1)S(1)}, u32[]{:S(2)}, u32[]{:S(2)}) collective-permute-start(bf16[16,896]{1,0:T(8,128)(2,1)S(1)} %pack.1.a), channel_id=1, source_target_pairs={{0,3},{1,2},{2,1},{3,0},{4,7},{5,6},{6,5},{7,4},{8,11},{9,10},{10,... | collective-permute-start | bytes 86024 | tf_op jit(solution)/shard_map/ppermute | solution.py:345
  59.2 15.7 %collective-permute-start.27 = (bf16[144,2560]{1,0:T(8,128)(2,1)S(1)}, bf16[144,2560]{1,0:T(8,128)(2,1)S(1)}, u32[]{:S(2)}, u32[]{:S(2)}) collective-permute-start(bf16[144,2560]{1,0:T(8,128)(2,1)S(1)} %collective-permute-done.11.x_first.rest_1_.rest_0_), channel_id=1, source_target_pairs={{0,2},{2,3},{3,1},{1,0},{4,6},{6,7},{7,5},{5,4},{8,10},{10,11},{11... | collective-permute-start | bytes 2211848 | tf_op jit(solution)/shard_map/ppermute | solution.py:366
  59.5 6.7 %collective-permute-start.19 = (f32[16,640]{1,0:T(8,128)S(1)}, f32[16,640]{1,0:T(8,128)S(1)}, u32[]{:S(2)}, u32[]{:S(2)}) collective-permute-start(f32[16,640]{1,0:T(8,128)S(1)} %get-tuple-element.61.a0), channel_id=1, source_target_pairs={{0,8},{4,12},{8,0},{12,4},{16,24},{20,28},{24,16},{28,20},{1,9},{5... | collective-permute-start | bytes 122888 | tf_op jit(solution)/shard_map/ppermute | solution.py:345
  60.9 5.8 %collective-permute-start.20 = (f32[16,640]{1,0:T(8,128)S(1)}, f32[16,640]{1,0:T(8,128)S(1)}, u32[]{:S(2)}, u32[]{:S(2)}) collective-permute-start(f32[16,640]{1,0:T(8,128)S(1)} %get-tuple-element.61.a0), channel_id=1, source_target_pairs={{0,16},{4,20},{8,24},{12,28},{16,0},{20,4},{24,8},{28,12},{1,17},{... | collective-permute-start | bytes 122888 | tf_op jit(solution)/shard_map/ppermute | solution.py:345
  61.7 5.1 %collective-permute-start.21 = (f32[16,640]{1,0:T(8,128)S(1)}, f32[16,640]{1,0:T(8,128)S(1)}, u32[]{:S(2)}, u32[]{:S(2)}) collective-permute-start(f32[16,640]{1,0:T(8,128)S(1)} %get-tuple-element.61.a0), channel_id=1, source_target_pairs={{0,24},{4,28},{8,16},{12,20},{16,8},{20,12},{24,0},{28,4},{1,25},{... | collective-permute-start | bytes 122888 | tf_op jit(solution)/shard_map/ppermute | solution.py:345
  64.6 3.9 %collective-permute-start.22 = (f32[16,640]{1,0:T(8,128)S(1)}, f32[16,640]{1,0:T(8,128)S(1)}, u32[]{:S(2)}, u32[]{:S(2)}) collective-permute-start(f32[16,640]{1,0:T(8,128)S(1)} %get-tuple-element.61.a0), channel_id=1, source_target_pairs={{0,4},{4,0},{8,12},{12,8},{16,20},{20,16},{24,28},{28,24},{1,5},{5... | collective-permute-start | bytes 122888 | tf_op jit(solution)/shard_map/ppermute | solution.py:345
  66.1 2.4 %collective-permute-start.23 = (f32[16,640]{1,0:T(8,128)S(1)}, f32[16,640]{1,0:T(8,128)S(1)}, u32[]{:S(2)}, u32[]{:S(2)}) collective-permute-start(f32[16,640]{1,0:T(8,128)S(1)} %collective-permute-done.19.a1), channel_id=1, source_target_pairs={{0,4},{4,0},{8,12},{12,8},{16,20},{20,16},{24,28},{28,24},{1,5},{5... | collective-permute-start | bytes 122888 | tf_op jit(solution)/shard_map/ppermute | solution.py:345
  66.7 1.9 %collective-permute-start.24 = (f32[16,640]{1,0:T(8,128)S(1)}, f32[16,640]{1,0:T(8,128)S(1)}, u32[]{:S(2)}, u32[]{:S(2)}) collective-permute-start(f32[16,640]{1,0:T(8,128)S(1)} %collective-permute-done.20.a2), channel_id=1, source_target_pairs={{0,4},{4,0},{8,12},{12,8},{16,20},{20,16},{24,28},{28,24},{1,5},{5... | collective-permute-start | bytes 122888 | tf_op jit(solution)/shard_map/ppermute | solution.py:345
  66.8 1.8 %collective-permute-start.25 = (f32[16,640]{1,0:T(8,128)S(1)}, f32[16,640]{1,0:T(8,128)S(1)}, u32[]{:S(2)}, u32[]{:S(2)}) collective-permute-start(f32[16,640]{1,0:T(8,128)S(1)} %collective-permute-done.21.a3), channel_id=1, source_target_pairs={{0,4},{4,0},{8,12},{12,8},{16,20},{20,16},{24,28},{28,24},{1,5},{5... | collective-permute-start | bytes 122888 | tf_op jit(solution)/shard_map/ppermute | solution.py:345

commit v8 on v7

--- a/solution.py
+++ b/solution.py
@@ -104,7 +104,7 @@
     total = dot(q_ref[0], x_ref[:, :width], contract_last)
     for k in range(1, parts):
         total += dot(q_ref[k], x_ref[:, k * width : (k + 1) * width], contract_last)
-    y_ref[...] = total
+    y_ref[...] = total.astype(bf16)
 
 
 def load_half(e_any, e_ref, sem):
@@ -140,9 +140,7 @@
     parts, rank, tokens = y4.shape
     total = eq_ref[...]
     for s in range(parts):
-        both = jnp.concatenate(split(y4[s]), axis=0)
-        term = dot(both, dy_ref[s * tokens : (s + 1) * tokens, :])
-        total += term[:rank] + term[rank:]
+        total += dot(y4[s], dy_ref[s * tokens : (s + 1) * tokens, :])
     out_ref[...] = total.astype(bf16)
 
 
@@ -387,7 +385,7 @@
     way_1, way_2 = [(0, 2), (2, 3), (3, 1), (1, 0)], [(0, 1), (1, 3), (3, 2), (2, 0)]
     q_full, y_own = call(
         project,
-        [like((n_t, rank, rows), bf16), like((rank, tokens), f32)],
+        [like((n_t, rank, rows), bf16), like((rank, tokens), bf16)],
         place, q_own, *q_parts, activations,
     )
     y_parts = along_t(y_own)
@@ -406,7 +404,7 @@
         left_factor,
         [like((rank, hidden), bf16)],
         place, eq, y_own, *y_parts, out_grad,
-        scratch=[pltpu.VMEM((n_t, rank, tokens), f32)],
+        scratch=[pltpu.VMEM((n_t, rank, tokens), bf16)],
     )
     (p_other,) = partners(p_local, "dp", n_dp, (1,))
     p_chip = (p_local.astype(f32) + p_other.astype(f32)).astype(bf16)

time: 79.8 us -> 79.6 us (level)
  no operation moved by 1% of the time
where the time goes in v8:
time: 79.6 us; the launch traced here: 79.4 us
  starting transfers between devices  29.5 us (37%)
  Pallas kernels  26.4 us (33%)
  waiting for transfers between devices  21.3 us (27%)
  other arithmetic  1.15 us (1%)
  between operations  1.06 us (1%)
    pallas_call x18, Pallas kernels, call(): pl.pallas_call(kernel, out_shape=list(outs), in_specs=in_specs, out_specs...  26.4 us
    ppermute x22, starting transfers between devices, partners(): lax.ppermute(value, axis, [(i, i ^ k) for i in range(size)])  24.8 us
    ppermute x22, waiting for transfers between devices, partners(): lax.ppermute(value, axis, [(i, i ^ k) for i in range(size)])  15.6 us
    ppermute x3, waiting for transfers between devices, move(): return lax.ppermute(after(value, *when), 'tensor', perm)  4.95 us
    ppermute x3, starting transfers between devices, body(): lax.ppermute(m, 'dp', [(i, i ^ 2 * k) for i in range(n_dp)])  3.55 us
  transfers between devices with their start and end apart: 28, of which 12 were waited for; matrix products, arithmetic and copies ran while one was open for 0% of the time, Pallas kernels for 26%

profile of v8, /device:TPU:0, one launch (start us, length us, event | category | flops | bytes accessed | tf_op | source)
XLA Modules:
  0.0 79.4 jit_solution(6647521714418487865)
XLA Ops:
  0.6 1.0 %convert_bitcast_fusion.own = bf16[32,640]{1,0:T(8,128)(2,1)S(1)} fusion(f32[640,32]{0,1:T(8,128)} %param.7), kind=kLoop, calls=%fused_computation.1 | loop fusion | flops 20480 | bytes 122880 | tf_op jit(solution)/shard_map/convert_element_type | solution.py:366
  1.7 3.0 %collective-permute-start = (bf16[32,640]{1,0:T(8,128)(2,1)S(1)}, bf16[32,640]{1,0:T(8,128)(2,1)S(1)}, u32[]{:S(2)}, u32[]{:S(2)}) collective-permute-start(bf16[32,640]{1,0:T(8,128)(2,1)S(1)} %convert_bitcast_fusion.own), channel_id=1, source_target_pairs={{0,1},{1,0},{2,3},{3,2},{4,5},{5,4},{6,7},{7,6},{8,9},{9,8},{10,11... | collective-permute-start | bytes 122888 | tf_op jit(solution)/shard_map/ppermute | solution.py:343
  4.7 2.6 %collective-permute-start.1 = (bf16[32,640]{1,0:T(8,128)(2,1)S(1)}, bf16[32,640]{1,0:T(8,128)(2,1)S(1)}, u32[]{:S(2)}, u32[]{:S(2)}) collective-permute-start(bf16[32,640]{1,0:T(8,128)(2,1)S(1)} %convert_bitcast_fusion.own), channel_id=1, source_target_pairs={{0,2},{1,3},{2,0},{3,1},{4,6},{5,7},{6,4},{7,5},{8,10},{9,11},{10,... | collective-permute-start | bytes 122888 | tf_op jit(solution)/shard_map/ppermute | solution.py:343
  7.3 0.1 pad_add_fusion.place
  7.4 2.3 %load_half.1.e_0.base_ref = bf16[1728,1280]{1,0:T(8,128)(2,1)S(1)} custom-call(bf16[1728,2560]{1,0:T(8,128)(2,1)} %bitcast.8), custom_call_target="tpu_custom_call" | custom-call | bytes 13271040 | tf_op jit(solution)/shard_map/load_half/pallas_call | solution.py:82
  9.7 1.3 %arrange.1 = (bf16[1728,432]{1,0:T(8,128)(2,1)S(1)}, bf16[1728,144]{1,0:T(8,128)(2,1)S(1)}) custom-call(s32[3]{0:T(128)S(1)} %pad_add_fusion.place, bf16[576,1728]{1,0:T(8,128)(2,1)S(1)} %copy-done), custom_call_target="tpu_custom_call" | custom-call | bytes 3981324 | tf_op jit(solution)/shard_map/arrange/pallas_call | solution.py:82
  11.0 2.1 %collective-permute-done.2.n3 = bf16[32,640]{1,0:T(8,128)(2,1)S(1)} collective-permute-done((bf16[32,640]{1,0:T(8,128)(2,1)S(1)}, bf16[32,640]{1,0:T(8,128)(2,1)S(1)}, u32[]{:S(2)}, u32[]{:S(2)}) %collective-permute-start.2) | collective-permute-done | bytes 40992 | tf_op jit(solution)/shard_map/ppermute | solution.py:343
  13.1 0.9 %project.1 = (bf16[4,32,640]{2,1,0:T(8,128)(2,1)S(1)}, bf16[32,144]{1,0:T(8,128)(2,1)S(1)}) custom-call(s32[3]{0:T(128)S(1)} %pad_add_fusion.place, bf16[32,640]{1,0:T(8,128)(2,1)S(1)} %convert_bitcast_fusion.own, bf16[32,640]{1,0:T(8,128)(2,1)S(1)} %collective-permute-done.n1, bf16[32,640]{1,0:T(8,128)(2,1)S(1)} %collective-permute-done.1.n2, ...), custom_call_target="tpu_custom_call" | custom-call | bytes 1074188 | tf_op jit(solution)/shard_map/project/pallas_call | solution.py:82
  14.0 0.0 collective-permute-start.3
  14.0 2.3 %collective-permute-start.4 = (bf16[32,144]{1,0:T(8,128)(2,1)S(1)}, bf16[32,144]{1,0:T(8,128)(2,1)S(1)}, u32[]{:S(2)}, u32[]{:S(2)}) collective-permute-start(bf16[32,144]{1,0:T(8,128)(2,1)S(1)} %get-tuple-element.42.own), channel_id=1, source_target_pairs={{0,2},{1,3},{2,0},{3,1},{4,6},{5,7},{6,4},{7,5},{8,10},{9,11},{10,... | collective-permute-start | bytes 27656 | tf_op jit(solution)/shard_map/ppermute | solution.py:343
  16.4 2.1 %collective-permute-start.5 = (bf16[32,144]{1,0:T(8,128)(2,1)S(1)}, bf16[32,144]{1,0:T(8,128)(2,1)S(1)}, u32[]{:S(2)}, u32[]{:S(2)}) collective-permute-start(bf16[32,144]{1,0:T(8,128)(2,1)S(1)} %get-tuple-element.42.own), channel_id=1, source_target_pairs={{0,3},{1,2},{2,1},{3,0},{4,7},{5,6},{6,5},{7,4},{8,11},{9,10},{10,... | collective-permute-start | bytes 27656 | tf_op jit(solution)/shard_map/ppermute | solution.py:343
  18.4 3.2 %error_left.1 = (f32[32,1728]{1,0:T(8,128)S(1)}, bf16[1728,1280]{1,0:T(8,128)(2,1)S(1)}) custom-call(bf16[4,32,640]{2,1,0:T(8,128)(2,1)S(1)} %get-tuple-element.39.q_ref, bf16[1728,1280]{1,0:T(8,128)(2,1)S(1)} %load_half.1.e_0.base_ref, bf16[1728,2560]{1,0:T(8,128)(2,1)} %bitcast.9), custom_call_target="tpu_custom_call" | custom-call | bytes 18079744 | tf_op jit(solution)/shard_map/error_left/pallas_call | solution.py:82
  21.6 0.0 collective-permute-done.3.n1
  21.6 0.3 collective-permute-done.5.n3
  21.9 0.0 collective-permute-start.11
  21.9 0.9 %left_factor.1 = bf16[32,1728]{1,0:T(8,128)(2,1)S(1)} custom-call(s32[3]{0:T(128)S(1)} %pad_add_fusion.place, f32[32,1728]{1,0:T(8,128)S(1)} %get-tuple-element.41.eq_ref, bf16[32,144]{1,0:T(8,128)(2,1)S(1)} %get-tuple-element.42.own, bf16[32,144]{1,0:T(8,128)(2,1)S(1)} %collective-permute-done.3.n1, bf16[32,144]{1,0:T(8,128)(2,1)S(1)} %collective-permute-done.4.n2, ...), custom_call_target="tpu_custom_call" | custom-call | bytes 2359308 | tf_op jit(solution)/shard_map/left_factor/pallas_call | solution.py:82
  22.9 0.1 collective-permute-start.6
  22.9 1.3 %collective-permute-done.6 = bf16[32,1728]{1,0:T(8,128)(2,1)S(1)} collective-permute-done((bf16[32,1728]{1,0:T(8,128)(2,1)S(1)}, bf16[32,1728]{1,0:T(8,128)(2,1)S(1)}, u32[]{:S(2)}, u32[]{:S(2)}) %collective-permute-start.6) | collective-permute-done | bytes 110624 | tf_op jit(solution)/shard_map/ppermute | solution.py:343
  24.3 1.6 %collective-permute-start.7 = (bf16[32,1728]{1,0:T(8,128)(2,1)S(1)}, bf16[32,1728]{1,0:T(8,128)(2,1)S(1)}, u32[]{:S(2)}, u32[]{:S(2)}) collective-permute-start(bf16[32,1728]{1,0:T(8,128)(2,1)S(1)} %add_convert_fusion.own), channel_id=1, source_target_pairs={{0,8},{4,12},{8,0},{12,4},{16,24},{20,28},{24,16},{28,20},{1,9},{5... | collective-permute-start | bytes 331784 | tf_op jit(solution)/shard_map/ppermute | solution.py:343
  25.8 1.5 %collective-permute-start.8 = (bf16[32,1728]{1,0:T(8,128)(2,1)S(1)}, bf16[32,1728]{1,0:T(8,128)(2,1)S(1)}, u32[]{:S(2)}, u32[]{:S(2)}) collective-permute-start(bf16[32,1728]{1,0:T(8,128)(2,1)S(1)} %add_convert_fusion.own), channel_id=1, source_target_pairs={{0,16},{4,20},{8,24},{12,28},{16,0},{20,4},{24,8},{28,12},{1,17},{... | collective-permute-start | bytes 331784 | tf_op jit(solution)/shard_map/ppermute | solution.py:343
  27.4 0.5 collective-permute-start.9
  27.8 1.7 %collective-permute-done.7.n1 = bf16[32,1728]{1,0:T(8,128)(2,1)S(1)} collective-permute-done((bf16[32,1728]{1,0:T(8,128)(2,1)S(1)}, bf16[32,1728]{1,0:T(8,128)(2,1)S(1)}, u32[]{:S(2)}, u32[]{:S(2)}) %collective-permute-start.7) | collective-permute-done | bytes 110624 | tf_op jit(solution)/shard_map/ppermute | solution.py:343
  29.6 3.7 %collective-permute-done.8.n2 = bf16[32,1728]{1,0:T(8,128)(2,1)S(1)} collective-permute-done((bf16[32,1728]{1,0:T(8,128)(2,1)S(1)}, bf16[32,1728]{1,0:T(8,128)(2,1)S(1)}, u32[]{:S(2)}, u32[]{:S(2)}) %collective-permute-start.8) | collective-permute-done | bytes 110624 | tf_op jit(solution)/shard_map/ppermute | solution.py:343
  33.2 1.2 %weigh.1 = (bf16[32,1728]{1,0:T(8,128)(2,1)S(1)}, f32[32,32]{1,0:T(8,128)S(1)}, f32[2,32,144]{2,1,0:T(8,128)S(1)}, bf16[2,32,144]{2,1,0:T(8,128)(2,1)S(1)}) custom-call(s32[3]{0:T(128)S(1)} %pad_add_fusion.place, bf16[32,1728]{1,0:T(8,128)(2,1)S(1)} %add_convert_fusion.own, bf16[32,1728]{1,0:T(8,128)(2,1)S(1)} %collective-permute-done.7.n1, ...), custom_call_target="tpu_custom_call" | custom-call | bytes 2603020 | tf_op jit(solution)/shard_map/weigh/pallas_call | solution.py:82
  34.5 2.1 %collective-permute-start.10 = (bf16[2,32,144]{2,1,0:T(8,128)(2,1)S(1)}, bf16[2,32,144]{2,1,0:T(8,128)(2,1)S(1)}, u32[]{:S(2)}, u32[]{:S(2)}) collective-permute-start(bf16[2,32,144]{2,1,0:T(8,128)(2,1)S(1)} %get-tuple-element.45), channel_id=1, source_target_pairs={{0,3},{1,2},{2,1},{3,0},{4,7},{5,6},{6,5},{7,4},{8,11},{9,10},{10,... | collective-permute-start | bytes 55304 | tf_op jit(solution)/shard_map/ppermute | solution.py:343
  36.6 1.1 %collective-permute-start.26 = (bf16[144,2560]{1,0:T(8,128)(2,1)S(1)}, bf16[144,2560]{1,0:T(8,128)(2,1)S(1)}, u32[]{:S(2)}, u32[]{:S(2)}) collective-permute-start(bf16[144,2560]{1,0:T(8,128)(2,1)S(1)} %copy-done.1), channel_id=1, source_target_pairs={{0,1},{1,3},{3,2},{2,0},{4,5},{5,7},{7,6},{6,4},{8,9},{9,11},{11,1... | collective-permute-start | bytes 2211848 | tf_op jit(solution)/shard_map/ppermute | solution.py:364
  37.7 1.4 %error_right.1.te_ref = f32[32,2560]{1,0:T(8,128)S(1)} custom-call(bf16[32,1728]{1,0:T(8,128)(2,1)S(1)} %get-tuple-element.46.p_ref, bf16[1728,1280]{1,0:T(8,128)(2,1)S(1)} %load_half.1.e_0.base_ref, bf16[1728,1280]{1,0:T(8,128)(2,1)S(1)} %get-tuple-element.47.e_1.base_ref), custom_call_target="tpu_custom_call" | custom-call | bytes 9285632 | tf_op jit(solution)/shard_map/error_right/pallas_call | solution.py:82
  39.2 1.5 %collective-permute-done.10.got_ref = bf16[2,32,144]{2,1,0:T(8,128)(2,1)S(1)} collective-permute-done((bf16[2,32,144]{2,1,0:T(8,128)(2,1)S(1)}, bf16[2,32,144]{2,1,0:T(8,128)(2,1)S(1)}, u32[]{:S(2)}, u32[]{:S(2)}) %collective-permute-start.10) | collective-permute-done | bytes 18464 | tf_op jit(solution)/shard_map/ppermute | solution.py:343
  40.7 0.0 collective-permute-done.11.x_first.rest_1_.rest_0_
  40.7 0.9 %right_term.1 = (f32[16,2560]{1,0:T(8,128)S(1)}, f32[16,2560]{1,0:T(8,128)S(1)}) custom-call(s32[3]{0:T(128)S(1)} %pad_add_fusion.place, f32[2,32,144]{2,1,0:T(8,128)S(1)} %get-tuple-element.44.near_ref, bf16[2,32,144]{2,1,0:T(8,128)(2,1)S(1)} %collective-permute-done.10.got_ref, f32[32,2560]{1,0:T(8,128)S(1)} %error_right.1.te_ref, ...), custom_call_target="tpu_custom_call" | custom-call | bytes 2185228 | tf_op jit(solution)/shard_map/right_term/pallas_call | solution.py:82
  41.6 0.1 collective-permute-start.12
  41.7 1.4 %collective-permute-done.12.got = f32[16,2560]{1,0:T(8,128)S(1)} collective-permute-done((f32[16,2560]{1,0:T(8,128)S(1)}, f32[16,2560]{1,0:T(8,128)S(1)}, u32[]{:S(2)}, u32[]{:S(2)}) %collective-permute-start.12) | collective-permute-done | bytes 163872 | tf_op jit(solution)/shard_map/ppermute | solution.py:343
  43.1 0.6 cut.1
  43.6 1.2 %collective-permute-start.13 = (bf16[16,640]{1,0:T(8,128)(2,1)S(1)}, bf16[16,640]{1,0:T(8,128)(2,1)S(1)}, u32[]{:S(2)}, u32[]{:S(2)}) collective-permute-start(bf16[16,640]{1,0:T(8,128)(2,1)S(1)} %get-tuple-element.54), channel_id=1, source_target_pairs={{0,8},{4,12},{8,0},{12,4},{16,24},{20,28},{24,16},{28,20},{1,9},{5... | collective-permute-start | bytes 61448 | tf_op jit(solution)/shard_map/ppermute | solution.py:444
  44.8 1.2 %collective-permute-start.14 = (bf16[16,640]{1,0:T(8,128)(2,1)S(1)}, bf16[16,640]{1,0:T(8,128)(2,1)S(1)}, u32[]{:S(2)}, u32[]{:S(2)}) collective-permute-start(bf16[16,640]{1,0:T(8,128)(2,1)S(1)} %get-tuple-element.55), channel_id=1, source_target_pairs={{0,16},{4,20},{8,24},{12,28},{16,0},{20,4},{24,8},{28,12},{1,17},{... | collective-permute-start | bytes 61448 | tf_op jit(solution)/shard_map/ppermute | solution.py:444
  46.0 1.1 %collective-permute-start.15 = (bf16[16,640]{1,0:T(8,128)(2,1)S(1)}, bf16[16,640]{1,0:T(8,128)(2,1)S(1)}, u32[]{:S(2)}, u32[]{:S(2)}) collective-permute-start(bf16[16,640]{1,0:T(8,128)(2,1)S(1)} %get-tuple-element.56), channel_id=1, source_target_pairs={{0,24},{4,28},{8,16},{12,20},{16,8},{20,12},{24,0},{28,4},{1,25},{... | collective-permute-start | bytes 61448 | tf_op jit(solution)/shard_map/ppermute | solution.py:444
  47.2 1.4 %accumulate.4.base_ref = f32[1728,1280]{1,0:T(8,128)S(1)} custom-call(bf16[1728,432]{1,0:T(8,128)(2,1)S(1)} %get-tuple-element.35.main_ref, bf16[1728,1280]{1,0:T(8,128)(2,1)S(1)} %load_half.1.e_0.base_ref, bf16[144,2560]{1,0:T(8,128)(2,1)S(1)} %copy-done.1, bf16[144,2560]{1,0:T(8,128)(2,1)S(1)} %collective-permute-done.11.x_first.rest_1_.rest_0_), custom_call_target="tpu_custom_call" | custom-call | bytes 16238592 | tf_op jit(solution)/shard_map/accumulate/pallas_call | solution.py:82
  48.6 1.4 %accumulate.5.base_ref = f32[1728,1280]{1,0:T(8,128)S(1)} custom-call(bf16[1728,432]{1,0:T(8,128)(2,1)S(1)} %get-tuple-element.35.main_ref, bf16[1728,1280]{1,0:T(8,128)(2,1)S(1)} %get-tuple-element.47.e_1.base_ref, bf16[144,2560]{1,0:T(8,128)(2,1)S(1)} %copy-done.1, bf16[144,2560]{1,0:T(8,128)(2,1)S(1)} %collective-permute-done.11.x_first.rest_1_.rest_0_), custom_call_target="tpu_custom_call" | custom-call | bytes 16238592 | tf_op jit(solution)/shard_map/accumulate/pallas_call | solution.py:82
  50.0 0.0 collective-permute-done.13.b
  50.0 0.7 collective-permute-done.15.d
  50.7 0.1 pack.1.a
  50.9 0.6 collective-permute-start.16
  51.5 1.7 %collective-permute-start.17 = (bf16[16,896]{1,0:T(8,128)(2,1)S(1)}, bf16[16,896]{1,0:T(8,128)(2,1)S(1)}, u32[]{:S(2)}, u32[]{:S(2)}) collective-permute-start(bf16[16,896]{1,0:T(8,128)(2,1)S(1)} %pack.1.a), channel_id=1, source_target_pairs={{0,2},{1,3},{2,0},{3,1},{4,6},{5,7},{6,4},{7,5},{8,10},{9,11},{10,... | collective-permute-start | bytes 86024 | tf_op jit(solution)/shard_map/ppermute | solution.py:343
  53.2 2.1 %collective-permute-start.18 = (bf16[16,896]{1,0:T(8,128)(2,1)S(1)}, bf16[16,896]{1,0:T(8,128)(2,1)S(1)}, u32[]{:S(2)}, u32[]{:S(2)}) collective-permute-start(bf16[16,896]{1,0:T(8,128)(2,1)S(1)} %pack.1.a), channel_id=1, source_target_pairs={{0,3},{1,2},{2,1},{3,0},{4,7},{5,6},{6,5},{7,4},{8,11},{9,10},{10,... | collective-permute-start | bytes 86024 | tf_op jit(solution)/shard_map/ppermute | solution.py:343
  55.3 0.2 collective-permute-done.16.b
  55.5 1.9 %collective-permute-done.17.c = bf16[16,896]{1,0:T(8,128)(2,1)S(1)} collective-permute-done((bf16[16,896]{1,0:T(8,128)(2,1)S(1)}, bf16[16,896]{1,0:T(8,128)(2,1)S(1)}, u32[]{:S(2)}, u32[]{:S(2)}) %collective-permute-start.17) | collective-permute-done | bytes 28704 | tf_op jit(solution)/shard_map/ppermute | solution.py:343
  57.3 1.5 %collective-permute-done.18.d = bf16[16,896]{1,0:T(8,128)(2,1)S(1)} collective-permute-done((bf16[16,896]{1,0:T(8,128)(2,1)S(1)}, bf16[16,896]{1,0:T(8,128)(2,1)S(1)}, u32[]{:S(2)}, u32[]{:S(2)}) %collective-permute-start.18) | collective-permute-done | bytes 28704 | tf_op jit(solution)/shard_map/ppermute | solution.py:343
  58.8 0.0 collective-permute-start.27
  58.8 0.2 unpack.1
  59.1 1.5 %collective-permute-start.19 = (f32[16,640]{1,0:T(8,128)S(1)}, f32[16,640]{1,0:T(8,128)S(1)}, u32[]{:S(2)}, u32[]{:S(2)}) collective-permute-start(f32[16,640]{1,0:T(8,128)S(1)} %get-tuple-element.61.a0), channel_id=1, source_target_pairs={{0,8},{4,12},{8,0},{12,4},{16,24},{20,28},{24,16},{28,20},{1,9},{5... | collective-permute-start | bytes 122888 | tf_op jit(solution)/shard_map/ppermute | solution.py:343
  60.6 0.9 %collective-permute-start.20 = (f32[16,640]{1,0:T(8,128)S(1)}, f32[16,640]{1,0:T(8,128)S(1)}, u32[]{:S(2)}, u32[]{:S(2)}) collective-permute-start(f32[16,640]{1,0:T(8,128)S(1)} %get-tuple-element.61.a0), channel_id=1, source_target_pairs={{0,16},{4,20},{8,24},{12,28},{16,0},{20,4},{24,8},{28,12},{1,17},{... | collective-permute-start | bytes 122888 | tf_op jit(solution)/shard_map/ppermute | solution.py:343
  61.5 1.1 %collective-permute-start.21 = (f32[16,640]{1,0:T(8,128)S(1)}, f32[16,640]{1,0:T(8,128)S(1)}, u32[]{:S(2)}, u32[]{:S(2)}) collective-permute-start(f32[16,640]{1,0:T(8,128)S(1)} %get-tuple-element.61.a0), channel_id=1, source_target_pairs={{0,24},{4,28},{8,16},{12,20},{16,8},{20,12},{24,0},{28,4},{1,25},{... | collective-permute-start | bytes 122888 | tf_op jit(solution)/shard_map/ppermute | solution.py:343
  62.6 1.7 %invert_cholesky.1.linv = f32[32,32]{1,0:T(8,128)S(1)} custom-call(f32[32,32]{1,0:T(8,128)S(1)} %get-tuple-element.59.g_ref), custom_call_target="tpu_custom_call" | custom-call | bytes 8192 | tf_op jit(solution)/shard_map/invert_cholesky/pallas_call | solution.py:82
  64.2 0.0 collective-permute-done.26.rest_1_
  64.3 0.1 collective-permute-start.22
  64.3 1.4 %accumulate.6.acc_0 = f32[1728,1280]{1,0:T(8,128)S(1)} custom-call(bf16[1728,432]{1,0:T(8,128)(2,1)S(1)} %get-tuple-element.35.main_ref, f32[1728,1280]{1,0:T(8,128)S(1)} %accumulate.4.base_ref, bf16[144,2560]{1,0:T(8,128)(2,1)S(1)} %collective-permute-done.11.x_first.rest_1_.rest_0_, bf16[144,2560]{1,0:T(8,128)(2,1)S(1)} %collective-permute-done.26.rest_1_), custom_call_target="tpu_custom_call" | custom-call | flops 2000000000 | bytes 20662272 | tf_op jit(solution)/shard_map/accumulate/pallas_call | solution.py:82
  65.7 0.5 collective-permute-start.23
  66.3 0.1 collective-permute-start.24
  66.4 0.0 collective-permute-done.21.a3
  66.4 0.4 collective-permute-start.25
  66.8 1.4 %accumulate.7.acc_1 = f32[1728,1280]{1,0:T(8,128)S(1)} custom-call(bf16[1728,432]{1,0:T(8,128)(2,1)S(1)} %get-tuple-element.35.main_ref, f32[1728,1280]{1,0:T(8,128)S(1)} %accumulate.5.base_ref, bf16[144,2560]{1,0:T(8,128)(2,1)S(1)} %collective-permute-done.11.x_first.rest_1_.rest_0_, bf16[144,2560]{1,0:T(8,128)(2,1)S(1)} %collective-permute-done.26.rest_1_), custom_call_target="tpu_custom_call" | custom-call | flops 2000000000 | bytes 20662272 | tf_op jit(solution)/shard_map/accumulate/pallas_call | solution.py:82
  68.2 1.5 %finish.1 = (f32[32,640]{1,0:T(8,128)}, bf16[1728,240]{1,0:T(8,128)(2,1)S(1)}, bf16[96,2560]{1,0:T(8,128)(2,1)S(1)}) custom-call(s32[3]{0:T(128)S(1)} %pad_add_fusion.place, f32[32,32]{1,0:T(8,128)S(1)} %invert_cholesky.1.linv, bf16[32,1728]{1,0:T(8,128)(2,1)S(1)} %get-tuple-element.46.p_ref, bf16[1728,144]{1,0:T(8,128)(2,1)S(1)} %get-tuple-element.60.rest_ref, ...), custom_call_target="tpu_custom_call" | custom-call | bytes 2342924 | tf_op jit(solution)/shard_map/finish/pallas_call | solution.py:82
  69.7 4.9 %collective-permute-done.27.x_any = bf16[144,2560]{1,0:T(8,128)(2,1)S(1)} collective-permute-done((bf16[144,2560]{1,0:T(8,128)(2,1)S(1)}, bf16[144,2560]{1,0:T(8,128)(2,1)S(1)}, u32[]{:S(2)}, u32[]{:S(2)}) %collective-permute-start.27) | collective-permute-done | bytes 737312 | tf_op jit(solution)/shard_map/ppermute | solution.py:364
  74.6 4.6 %rebuild.1 = bf16[1728,2560]{1,0:T(8,128)(2,1)} custom-call(bf16[1728,240]{1,0:T(8,128)(2,1)S(1)} %get-tuple-element.63.left_ref, bf16[96,2560]{1,0:T(8,128)(2,1)S(1)} %get-tuple-element.64.right_ref, f32[1728,1280]{1,0:T(8,128)S(1)} %accumulate.6.acc_0, f32[1728,1280]{1,0:T(8,128)S(1)} %accumulate.7.acc_1, bf16[144,2560]{1,0:T(8,128)(2,1)S(1)} %collective-permute-done.27.x_any), custom_call_target="tpu_custom_call" | custom-call | bytes 28600320 | tf_op jit(solution)/shard_map/rebuild/pallas_call | solution.py:82
  (17 shorter events, 0.1 us)
Async XLA Ops:
  0.6 9.0 %copy-start = (bf16[576,1728]{1,0:T(8,128)(2,1)S(1)}, bf16[576,1728]{1,0:T(8,128)(2,1)}, u32[]{:S(2)}) copy-start(bf16[576,1728]{1,0:T(8,128)(2,1)} %dy_ref.5) | copy-start | bytes 5971972
  0.6 12.5 %copy-start.1 = (bf16[144,2560]{1,0:T(8,128)(2,1)S(1)}, bf16[144,2560]{1,0:T(8,128)(2,1)}, u32[]{:S(2)}) copy-start(bf16[144,2560]{1,0:T(8,128)(2,1)} %rest_0_.3) | copy-start | bytes 2211844
  1.7 9.3 %collective-permute-start = (bf16[32,640]{1,0:T(8,128)(2,1)S(1)}, bf16[32,640]{1,0:T(8,128)(2,1)S(1)}, u32[]{:S(2)}, u32[]{:S(2)}) collective-permute-start(bf16[32,640]{1,0:T(8,128)(2,1)S(1)} %convert_bitcast_fusion.own), channel_id=1, source_target_pairs={{0,1},{1,0},{2,3},{3,2},{4,5},{5,4},{6,7},{7,6},{8,9},{9,8},{10,11... | collective-permute-start | bytes 122888 | tf_op jit(solution)/shard_map/ppermute | solution.py:343
  4.7 6.3 %collective-permute-start.1 = (bf16[32,640]{1,0:T(8,128)(2,1)S(1)}, bf16[32,640]{1,0:T(8,128)(2,1)S(1)}, u32[]{:S(2)}, u32[]{:S(2)}) collective-permute-start(bf16[32,640]{1,0:T(8,128)(2,1)S(1)} %convert_bitcast_fusion.own), channel_id=1, source_target_pairs={{0,2},{1,3},{2,0},{3,1},{4,6},{5,7},{6,4},{7,5},{8,10},{9,11},{10,... | collective-permute-start | bytes 122888 | tf_op jit(solution)/shard_map/ppermute | solution.py:343
  7.3 5.8 %collective-permute-start.2 = (bf16[32,640]{1,0:T(8,128)(2,1)S(1)}, bf16[32,640]{1,0:T(8,128)(2,1)S(1)}, u32[]{:S(2)}, u32[]{:S(2)}) collective-permute-start(bf16[32,640]{1,0:T(8,128)(2,1)S(1)} %convert_bitcast_fusion.own), channel_id=1, source_target_pairs={{0,3},{1,2},{2,1},{3,0},{4,7},{5,6},{6,5},{7,4},{8,11},{9,10},{10,... | collective-permute-start | bytes 122888 | tf_op jit(solution)/shard_map/ppermute | solution.py:343
  14.0 7.6 %collective-permute-start.3 = (bf16[32,144]{1,0:T(8,128)(2,1)S(1)}, bf16[32,144]{1,0:T(8,128)(2,1)S(1)}, u32[]{:S(2)}, u32[]{:S(2)}) collective-permute-start(bf16[32,144]{1,0:T(8,128)(2,1)S(1)} %get-tuple-element.42.own), channel_id=1, source_target_pairs={{0,1},{1,0},{2,3},{3,2},{4,5},{5,4},{6,7},{7,6},{8,9},{9,8},{10,11... | collective-permute-start | bytes 27656 | tf_op jit(solution)/shard_map/ppermute | solution.py:343
  14.0 7.6 %collective-permute-start.4 = (bf16[32,144]{1,0:T(8,128)(2,1)S(1)}, bf16[32,144]{1,0:T(8,128)(2,1)S(1)}, u32[]{:S(2)}, u32[]{:S(2)}) collective-permute-start(bf16[32,144]{1,0:T(8,128)(2,1)S(1)} %get-tuple-element.42.own), channel_id=1, source_target_pairs={{0,2},{1,3},{2,0},{3,1},{4,6},{5,7},{6,4},{7,5},{8,10},{9,11},{10,... | collective-permute-start | bytes 27656 | tf_op jit(solution)/shard_map/ppermute | solution.py:343
  16.4 5.5 %collective-permute-start.5 = (bf16[32,144]{1,0:T(8,128)(2,1)S(1)}, bf16[32,144]{1,0:T(8,128)(2,1)S(1)}, u32[]{:S(2)}, u32[]{:S(2)}) collective-permute-start(bf16[32,144]{1,0:T(8,128)(2,1)S(1)} %get-tuple-element.42.own), channel_id=1, source_target_pairs={{0,3},{1,2},{2,1},{3,0},{4,7},{5,6},{6,5},{7,4},{8,11},{9,10},{10,... | collective-permute-start | bytes 27656 | tf_op jit(solution)/shard_map/ppermute | solution.py:343
  21.9 18.8 %collective-permute-start.11 = (bf16[144,2560]{1,0:T(8,128)(2,1)S(1)}, bf16[144,2560]{1,0:T(8,128)(2,1)S(1)}, u32[]{:S(2)}, u32[]{:S(2)}) collective-permute-start(bf16[144,2560]{1,0:T(8,128)(2,1)S(1)} %copy-done.1), channel_id=1, source_target_pairs={{0,2},{2,3},{3,1},{1,0},{4,6},{6,7},{7,5},{5,4},{8,10},{10,11},{11... | collective-permute-start | bytes 2211848 | tf_op jit(solution)/shard_map/ppermute | solution.py:364
  22.9 1.4 %collective-permute-start.6 = (bf16[32,1728]{1,0:T(8,128)(2,1)S(1)}, bf16[32,1728]{1,0:T(8,128)(2,1)S(1)}, u32[]{:S(2)}, u32[]{:S(2)}) collective-permute-start(bf16[32,1728]{1,0:T(8,128)(2,1)S(1)} %left_factor.1), channel_id=1, source_target_pairs={{0,4},{4,0},{8,12},{12,8},{16,20},{20,16},{24,28},{28,24},{1,5},{5... | collective-permute-start | bytes 331784 | tf_op jit(solution)/shard_map/ppermute | solution.py:343
  24.3 5.3 %collective-permute-start.7 = (bf16[32,1728]{1,0:T(8,128)(2,1)S(1)}, bf16[32,1728]{1,0:T(8,128)(2,1)S(1)}, u32[]{:S(2)}, u32[]{:S(2)}) collective-permute-start(bf16[32,1728]{1,0:T(8,128)(2,1)S(1)} %add_convert_fusion.own), channel_id=1, source_target_pairs={{0,8},{4,12},{8,0},{12,4},{16,24},{20,28},{24,16},{28,20},{1,9},{5... | collective-permute-start | bytes 331784 | tf_op jit(solution)/shard_map/ppermute | solution.py:343
  25.8 7.4 %collective-permute-start.8 = (bf16[32,1728]{1,0:T(8,128)(2,1)S(1)}, bf16[32,1728]{1,0:T(8,128)(2,1)S(1)}, u32[]{:S(2)}, u32[]{:S(2)}) collective-permute-start(bf16[32,1728]{1,0:T(8,128)(2,1)S(1)} %add_convert_fusion.own), channel_id=1, source_target_pairs={{0,16},{4,20},{8,24},{12,28},{16,0},{20,4},{24,8},{28,12},{1,17},{... | collective-permute-start | bytes 331784 | tf_op jit(solution)/shard_map/ppermute | solution.py:343
  27.4 5.9 %collective-permute-start.9 = (bf16[32,1728]{1,0:T(8,128)(2,1)S(1)}, bf16[32,1728]{1,0:T(8,128)(2,1)S(1)}, u32[]{:S(2)}, u32[]{:S(2)}) collective-permute-start(bf16[32,1728]{1,0:T(8,128)(2,1)S(1)} %add_convert_fusion.own), channel_id=1, source_target_pairs={{0,24},{4,28},{8,16},{12,20},{16,8},{20,12},{24,0},{28,4},{1,25},{... | collective-permute-start | bytes 331784 | tf_op jit(solution)/shard_map/ppermute | solution.py:343
  34.5 6.2 %collective-permute-start.10 = (bf16[2,32,144]{2,1,0:T(8,128)(2,1)S(1)}, bf16[2,32,144]{2,1,0:T(8,128)(2,1)S(1)}, u32[]{:S(2)}, u32[]{:S(2)}) collective-permute-start(bf16[2,32,144]{2,1,0:T(8,128)(2,1)S(1)} %get-tuple-element.45), channel_id=1, source_target_pairs={{0,3},{1,2},{2,1},{3,0},{4,7},{5,6},{6,5},{7,4},{8,11},{9,10},{10,... | collective-permute-start | bytes 55304 | tf_op jit(solution)/shard_map/ppermute | solution.py:343
  36.6 27.6 %collective-permute-start.26 = (bf16[144,2560]{1,0:T(8,128)(2,1)S(1)}, bf16[144,2560]{1,0:T(8,128)(2,1)S(1)}, u32[]{:S(2)}, u32[]{:S(2)}) collective-permute-start(bf16[144,2560]{1,0:T(8,128)(2,1)S(1)} %copy-done.1), channel_id=1, source_target_pairs={{0,1},{1,3},{3,2},{2,0},{4,5},{5,7},{7,6},{6,4},{8,9},{9,11},{11,1... | collective-permute-start | bytes 2211848 | tf_op jit(solution)/shard_map/ppermute | solution.py:364
  41.6 1.5 %collective-permute-start.12 = (f32[16,2560]{1,0:T(8,128)S(1)}, f32[16,2560]{1,0:T(8,128)S(1)}, u32[]{:S(2)}, u32[]{:S(2)}) collective-permute-start(f32[16,2560]{1,0:T(8,128)S(1)} %get-tuple-element.52), channel_id=1, source_target_pairs={{0,4},{4,0},{8,12},{12,8},{16,20},{20,16},{24,28},{28,24},{1,5},{5... | collective-permute-start | bytes 491528 | tf_op jit(solution)/shard_map/ppermute | solution.py:343
  43.6 6.4 %collective-permute-start.13 = (bf16[16,640]{1,0:T(8,128)(2,1)S(1)}, bf16[16,640]{1,0:T(8,128)(2,1)S(1)}, u32[]{:S(2)}, u32[]{:S(2)}) collective-permute-start(bf16[16,640]{1,0:T(8,128)(2,1)S(1)} %get-tuple-element.54), channel_id=1, source_target_pairs={{0,8},{4,12},{8,0},{12,4},{16,24},{20,28},{24,16},{28,20},{1,9},{5... | collective-permute-start | bytes 61448 | tf_op jit(solution)/shard_map/ppermute | solution.py:444
  44.8 5.2 %collective-permute-start.14 = (bf16[16,640]{1,0:T(8,128)(2,1)S(1)}, bf16[16,640]{1,0:T(8,128)(2,1)S(1)}, u32[]{:S(2)}, u32[]{:S(2)}) collective-permute-start(bf16[16,640]{1,0:T(8,128)(2,1)S(1)} %get-tuple-element.55), channel_id=1, source_target_pairs={{0,16},{4,20},{8,24},{12,28},{16,0},{20,4},{24,8},{28,12},{1,17},{... | collective-permute-start | bytes 61448 | tf_op jit(solution)/shard_map/ppermute | solution.py:444
  46.0 4.7 %collective-permute-start.15 = (bf16[16,640]{1,0:T(8,128)(2,1)S(1)}, bf16[16,640]{1,0:T(8,128)(2,1)S(1)}, u32[]{:S(2)}, u32[]{:S(2)}) collective-permute-start(bf16[16,640]{1,0:T(8,128)(2,1)S(1)} %get-tuple-element.56), channel_id=1, source_target_pairs={{0,24},{4,28},{8,16},{12,20},{16,8},{20,12},{24,0},{28,4},{1,25},{... | collective-permute-start | bytes 61448 | tf_op jit(solution)/shard_map/ppermute | solution.py:444
  50.9 4.6 %collective-permute-start.16 = (bf16[16,896]{1,0:T(8,128)(2,1)S(1)}, bf16[16,896]{1,0:T(8,128)(2,1)S(1)}, u32[]{:S(2)}, u32[]{:S(2)}) collective-permute-start(bf16[16,896]{1,0:T(8,128)(2,1)S(1)} %pack.1.a), channel_id=1, source_target_pairs={{0,1},{1,0},{2,3},{3,2},{4,5},{5,4},{6,7},{7,6},{8,9},{9,8},{10,11... | collective-permute-start | bytes 86024 | tf_op jit(solution)/shard_map/ppermute | solution.py:343
  51.5 5.8 %collective-permute-start.17 = (bf16[16,896]{1,0:T(8,128)(2,1)S(1)}, bf16[16,896]{1,0:T(8,128)(2,1)S(1)}, u32[]{:S(2)}, u32[]{:S(2)}) collective-permute-start(bf16[16,896]{1,0:T(8,128)(2,1)S(1)} %pack.1.a), channel_id=1, source_target_pairs={{0,2},{1,3},{2,0},{3,1},{4,6},{5,7},{6,4},{7,5},{8,10},{9,11},{10,... | collective-permute-start | bytes 86024 | tf_op jit(solution)/shard_map/ppermute | solution.py:343
  53.2 5.7 %collective-permute-start.18 = (bf16[16,896]{1,0:T(8,128)(2,1)S(1)}, bf16[16,896]{1,0:T(8,128)(2,1)S(1)}, u32[]{:S(2)}, u32[]{:S(2)}) collective-permute-start(bf16[16,896]{1,0:T(8,128)(2,1)S(1)} %pack.1.a), channel_id=1, source_target_pairs={{0,3},{1,2},{2,1},{3,0},{4,7},{5,6},{6,5},{7,4},{8,11},{9,10},{10,... | collective-permute-start | bytes 86024 | tf_op jit(solution)/shard_map/ppermute | solution.py:343
  58.8 15.8 %collective-permute-start.27 = (bf16[144,2560]{1,0:T(8,128)(2,1)S(1)}, bf16[144,2560]{1,0:T(8,128)(2,1)S(1)}, u32[]{:S(2)}, u32[]{:S(2)}) collective-permute-start(bf16[144,2560]{1,0:T(8,128)(2,1)S(1)} %collective-permute-done.11.x_first.rest_1_.rest_0_), channel_id=1, source_target_pairs={{0,2},{2,3},{3,1},{1,0},{4,6},{6,7},{7,5},{5,4},{8,10},{10,11},{11... | collective-permute-start | bytes 2211848 | tf_op jit(solution)/shard_map/ppermute | solution.py:364
  59.1 6.7 %collective-permute-start.19 = (f32[16,640]{1,0:T(8,128)S(1)}, f32[16,640]{1,0:T(8,128)S(1)}, u32[]{:S(2)}, u32[]{:S(2)}) collective-permute-start(f32[16,640]{1,0:T(8,128)S(1)} %get-tuple-element.61.a0), channel_id=1, source_target_pairs={{0,8},{4,12},{8,0},{12,4},{16,24},{20,28},{24,16},{28,20},{1,9},{5... | collective-permute-start | bytes 122888 | tf_op jit(solution)/shard_map/ppermute | solution.py:343
  60.6 5.7 %collective-permute-start.20 = (f32[16,640]{1,0:T(8,128)S(1)}, f32[16,640]{1,0:T(8,128)S(1)}, u32[]{:S(2)}, u32[]{:S(2)}) collective-permute-start(f32[16,640]{1,0:T(8,128)S(1)} %get-tuple-element.61.a0), channel_id=1, source_target_pairs={{0,16},{4,20},{8,24},{12,28},{16,0},{20,4},{24,8},{28,12},{1,17},{... | collective-permute-start | bytes 122888 | tf_op jit(solution)/shard_map/ppermute | solution.py:343
  61.5 4.9 %collective-permute-start.21 = (f32[16,640]{1,0:T(8,128)S(1)}, f32[16,640]{1,0:T(8,128)S(1)}, u32[]{:S(2)}, u32[]{:S(2)}) collective-permute-start(f32[16,640]{1,0:T(8,128)S(1)} %get-tuple-element.61.a0), channel_id=1, source_target_pairs={{0,24},{4,28},{8,16},{12,20},{16,8},{20,12},{24,0},{28,4},{1,25},{... | collective-permute-start | bytes 122888 | tf_op jit(solution)/shard_map/ppermute | solution.py:343
  64.3 3.9 %collective-permute-start.22 = (f32[16,640]{1,0:T(8,128)S(1)}, f32[16,640]{1,0:T(8,128)S(1)}, u32[]{:S(2)}, u32[]{:S(2)}) collective-permute-start(f32[16,640]{1,0:T(8,128)S(1)} %get-tuple-element.61.a0), channel_id=1, source_target_pairs={{0,4},{4,0},{8,12},{12,8},{16,20},{20,16},{24,28},{28,24},{1,5},{5... | collective-permute-start | bytes 122888 | tf_op jit(solution)/shard_map/ppermute | solution.py:343
  65.7 2.4 %collective-permute-start.23 = (f32[16,640]{1,0:T(8,128)S(1)}, f32[16,640]{1,0:T(8,128)S(1)}, u32[]{:S(2)}, u32[]{:S(2)}) collective-permute-start(f32[16,640]{1,0:T(8,128)S(1)} %collective-permute-done.19.a1), channel_id=1, source_target_pairs={{0,4},{4,0},{8,12},{12,8},{16,20},{20,16},{24,28},{28,24},{1,5},{5... | collective-permute-start | bytes 122888 | tf_op jit(solution)/shard_map/ppermute | solution.py:343
  66.3 1.9 %collective-permute-start.24 = (f32[16,640]{1,0:T(8,128)S(1)}, f32[16,640]{1,0:T(8,128)S(1)}, u32[]{:S(2)}, u32[]{:S(2)}) collective-permute-start(f32[16,640]{1,0:T(8,128)S(1)} %collective-permute-done.20.a2), channel_id=1, source_target_pairs={{0,4},{4,0},{8,12},{12,8},{16,20},{20,16},{24,28},{28,24},{1,5},{5... | collective-permute-start | bytes 122888 | tf_op jit(solution)/shard_map/ppermute | solution.py:343
  66.4 1.8 %collective-permute-start.25 = (f32[16,640]{1,0:T(8,128)S(1)}, f32[16,640]{1,0:T(8,128)S(1)}, u32[]{:S(2)}, u32[]{:S(2)}) collective-permute-start(f32[16,640]{1,0:T(8,128)S(1)} %collective-permute-done.21.a3), channel_id=1, source_target_pairs={{0,4},{4,0},{8,12},{12,8},{16,20},{20,16},{24,28},{28,24},{1,5},{5... | collective-permute-start | bytes 122888 | tf_op jit(solution)/shard_map/ppermute | solution.py:343
